TPU v7x, 32 devices: a whole 2x2x4 slice. The times are simulated.
32 devices in a mesh: dp: 4 (over z), pipe: 2 (over core), tensor: 4 (over y, x).
Axes of the slice: x: 2, y: 2, z: 4, core: 2. Of those that a mesh axis runs over, the one named last changes fastest.
Arguments:
- tokens: bfloat16 [4, 2, 1280, 768], P('dp', None, 'tensor'), may hold values from -6 to 6
- lengths: int32 [4, 2, 3], P('dp'), may hold values from 1 to 1024, 1280 in all within a row
- qkv_weight: bfloat16 [2, 768, 3, 768], P('pipe', 'dp', None, 'tensor'), may hold values from -0.21875 to 0.21875
- out_weight: bfloat16 [2, 768, 768], P('pipe', 'tensor', 'dp'), may hold values from -0.875 to 0.875
- gate_up_weight: bfloat16 [2, 768, 2, 1152], P('pipe', 'dp', None, 'tensor'), may hold values from -0.21875 to 0.21875
- down_weight: bfloat16 [2, 1152, 768], P('pipe', 'tensor', 'dp'), may hold values from -0.25 to 0.25
- gains: float32 [2, 1536], P('pipe'), may hold values from 0.5 to 1.5
- out_cotangent: bfloat16 [4, 2, 1280, 768], P('dp', None, 'tensor'), may hold values from -6 to 6
Outputs:
- activations: bfloat16 [2, 4, 2, 1280, 768], P('pipe', 'dp', None, 'tensor')
- input_grads: float32 [2, 4, 2, 1280, 768], P('pipe', 'dp', None, 'tensor')
- qkv_grad: float32 [2, 768, 3, 768], P('pipe', 'dp', None, 'tensor')
- out_grad: float32 [2, 768, 768], P('pipe', 'tensor', 'dp')
- gate_up_grad: float32 [2, 768, 2, 1152], P('pipe', 'dp', None, 'tensor')
- down_grad: float32 [2, 1152, 768], P('pipe', 'tensor', 'dp')
- gain_grad: float32 [2, 1536], P('pipe', ('dp', 'tensor'))
Inputs may be any that keep to these rules, and one draw needn't show every extreme that they name: `lengths`: each micro-batch holds 3 whole sequences that fill its 1280 tokens in order; the longest has 1024 tokens.
All inputs are finite; a program needn't handle non-finite values.
Results may differ from a plain program's by a relative error of at most 0.029.
Values may be sent and summed in bfloat16 or wider, within the bound.
No kernel may reach another device: no remote copies, remote signals or barrier semaphores. Data moves between devices by JAX's collectives and lax.ppermute only.
A program may use at most 192 MiB of HBM per device.

v0:
```python
from functools import partial

import jax
import jax.numpy as jnp
from jax import lax
from jax.sharding import PartitionSpec as P

HEAD_DIM = 64
WINDOW = 128


def shifted(block, axis, distance):
    devices = range(lax.axis_size(axis))
    route = [(i - distance, i) for i in devices if i - distance in devices]
    return lax.ppermute(block, axis, route)


def norm_gain(stream, gain_row):
    average = jnp.mean(stream, axis=-1, keepdims=True)
    centred = stream - average
    spread = jnp.mean(centred * centred, axis=-1, keepdims=True)
    return centred * lax.rsqrt(spread + 1e-05) * gain_row


def frequencies(theta_base, half_dim):
    return theta_base ** (-(jnp.arange(half_dim, dtype=jnp.float32) * 2.0) / (2.0 * half_dim))


def layout(seq_lengths, full_rows):
    seq_ends = jnp.cumsum(seq_lengths)
    seq_starts = seq_ends - seq_lengths
    positions = jnp.arange(full_rows, dtype=jnp.int32)
    seq_of = jnp.sum((positions[:, None] >= seq_ends[None, :]).astype(jnp.int32), axis=1)
    matches = jnp.arange(seq_lengths.shape[0], dtype=jnp.int32)[None, :] == seq_of[:, None]
    first_row = jnp.sum(jnp.where(matches, seq_starts[None, :], 0), axis=1)
    return (seq_of, positions - first_row)


def angles(offset, inv_freq):
    turns = offset.astype(jnp.float32)[:, None] * inv_freq[None, :]
    turns = jnp.concatenate([turns, turns], axis=1)
    return (jnp.cos(turns), jnp.sin(turns))


def rotate(values_in, cosines, sines):
    half_dim = values_in.shape[-1] // 2
    turned = jnp.concatenate([-values_in[..., half_dim:], values_in[..., :half_dim]], axis=-1)
    return values_in * cosines[:, None, :] + turned * sines[:, None, :]


def allowed(seq_of, row_start, block_size, is_local):
    positions = jnp.arange(seq_of.shape[0], dtype=jnp.int32)
    row_ids = row_start + jnp.arange(block_size, dtype=jnp.int32)
    row_seq = lax.dynamic_slice_in_dim(seq_of, row_start, block_size, 0)
    same_seq = row_seq[:, None] == seq_of[None, :]
    near_rows = jnp.abs(row_ids[:, None] - positions[None, :]) <= WINDOW // 2
    return same_seq & (near_rows | jnp.logical_not(is_local))


def block_plan(full_rows):
    blocks = max(1, full_rows // 512)
    return (full_rows // blocks, blocks)


def geglu(gate_up):
    return jax.nn.gelu(gate_up[:, 0], approximate=False) * gate_up[:, 1]


def attend(queries, keys, values, seq_of, is_local):
    full_rows, heads, head_dim = queries.shape
    block_size, blocks = block_plan(full_rows)
    score_scale = head_dim ** (-0.5)

    def per_head(operands):
        query_head, key_head, value_head = operands

        def per_block(block_id):
            row_start = block_id * block_size
            query_rows = lax.dynamic_slice_in_dim(query_head, row_start, block_size, 0)
            scores = score_scale * jnp.einsum(
                "qd,kd->qk", query_rows, key_head, preferred_element_type=jnp.float32
            )
            scores = jnp.where(allowed(seq_of, row_start, block_size, is_local), scores, -1e30)
            row_max = jnp.max(scores, axis=1, keepdims=True)
            expos = jnp.exp(scores - row_max)
            row_sum = jnp.sum(expos, axis=1, keepdims=True)
            probabilities = (expos / row_sum).astype(jnp.bfloat16)
            mixed_rows = jnp.dot(probabilities, value_head, preferred_element_type=jnp.float32)
            return (mixed_rows, (row_max + jnp.log(row_sum))[:, 0])

        mixed_blocks, mass_blocks = lax.map(per_block, jnp.arange(blocks, dtype=jnp.int32))
        return (mixed_blocks.reshape(full_rows, head_dim), mass_blocks.reshape(full_rows))

    mixed, log_mass = lax.map(
        per_head,
        (jnp.moveaxis(queries, 1, 0), jnp.moveaxis(keys, 1, 0), jnp.moveaxis(values, 1, 0)),
    )
    return (jnp.moveaxis(mixed, 0, 1), log_mass)


def attend_back(queries, keys, values, log_mass, grad_mixed, seq_of, is_local):
    full_rows, heads, head_dim = queries.shape
    block_size, blocks = block_plan(full_rows)
    score_scale = head_dim ** (-0.5)

    def per_head(operands):
        query_head, key_head, value_head, mass_head, grad_head = operands

        def per_block(running, block_id):
            grad_k, grad_v = running
            row_start = block_id * block_size
            query_rows = lax.dynamic_slice_in_dim(query_head, row_start, block_size, 0)
            grad_rows = lax.dynamic_slice_in_dim(grad_head, row_start, block_size, 0)
            mass_rows = lax.dynamic_slice_in_dim(mass_head, row_start, block_size, 0)
            scores = score_scale * jnp.einsum(
                "qd,kd->qk", query_rows, key_head, preferred_element_type=jnp.float32
            )
            scores = jnp.where(allowed(seq_of, row_start, block_size, is_local), scores, -1e30)
            probabilities = jnp.exp(scores - mass_rows[:, None])
            grad_probs = jnp.einsum(
                "qd,kd->qk", grad_rows, value_head, preferred_element_type=jnp.float32
            )
            inner_sum = jnp.sum(probabilities * grad_probs, axis=1, keepdims=True)
            grad_scores = (probabilities * (grad_probs - inner_sum)).astype(jnp.bfloat16)
            grad_q = score_scale * jnp.dot(
                grad_scores, key_head, preferred_element_type=jnp.float32
            )
            grad_k = grad_k + score_scale * jnp.einsum(
                "qk,qd->kd", grad_scores, query_rows, preferred_element_type=jnp.float32
            )
            grad_v = grad_v + jnp.einsum(
                "qk,qd->kd",
                probabilities.astype(jnp.bfloat16),
                grad_rows,
                preferred_element_type=jnp.float32,
            )
            return ((grad_k, grad_v), grad_q)

        zero_rows = jnp.zeros((full_rows, head_dim), jnp.float32)
        (grad_k, grad_v), grad_q = lax.scan(
            per_block, (zero_rows, zero_rows), jnp.arange(blocks, dtype=jnp.int32)
        )
        return (grad_q.reshape(full_rows, head_dim), grad_k, grad_v)

    grad_q, grad_k, grad_v = lax.map(
        per_head,
        (
            jnp.moveaxis(queries, 1, 0),
            jnp.moveaxis(keys, 1, 0),
            jnp.moveaxis(values, 1, 0),
            log_mass,
            jnp.moveaxis(grad_mixed, 1, 0),
        ),
    )
    return (jnp.moveaxis(grad_q, 0, 1), jnp.moveaxis(grad_k, 0, 1), jnp.moveaxis(grad_v, 0, 1))


def fetch_weights(qkv_weight, out_weight, gate_up_weight, down_weight):
    gathered = (
        lax.all_gather(qkv_weight, "dp", axis=1, tiled=True),
        lax.all_gather(out_weight, "dp", axis=2, tiled=True),
        lax.all_gather(gate_up_weight, "dp", axis=1, tiled=True),
        lax.all_gather(down_weight, "dp", axis=2, tiled=True),
    )
    return tuple((weight[0] for weight in gathered))


def gather_rows(normed):
    return lax.all_gather(normed, "tensor", axis=0, tiled=True)


def reduce_rows(left_rows, weight):
    return lax.psum_scatter(
        jnp.dot(left_rows, weight, preferred_element_type=jnp.float32).astype(jnp.bfloat16),
        "tensor",
        scatter_dimension=0,
        tiled=True,
    ).astype(jnp.float32)


def fold_rows(grad_local, saved_full, weight):
    shard_rows = lax.all_gather(grad_local, "tensor", axis=0, tiled=True)
    part_rows = jnp.einsum("sd,fd->sf", shard_rows, weight, preferred_element_type=jnp.float32)
    weight_grad = jnp.einsum(
        "sf,sd->fd", saved_full, shard_rows, preferred_element_type=jnp.float32
    )
    return (part_rows, weight_grad)


def back_rows(grad_full, weight_full):
    full_rows = grad_full.shape[0]
    grad_flat = grad_full.reshape(full_rows, -1)
    weight_flat = weight_full.reshape(weight_full.shape[0], -1)
    return lax.psum_scatter(
        jnp.einsum("sf,df->sd", grad_flat, weight_flat, preferred_element_type=jnp.float32).astype(
            jnp.bfloat16
        ),
        "tensor",
        scatter_dimension=0,
        tiled=True,
    ).astype(jnp.float32)


def layer_forward(layer_in, weights, gain_row, seq_lengths, is_local, inv_freq):
    w_qkv, w_out, w_pair, w_down = weights
    local_rows, model_width = layer_in.shape
    stream = layer_in.astype(jnp.float32)
    normed_attn = gather_rows(norm_gain(stream, gain_row[:model_width]).astype(jnp.bfloat16))
    full_rows = normed_attn.shape[0]
    heads = w_qkv.shape[2] // HEAD_DIM
    seq_of, offset = layout(seq_lengths, full_rows)
    cosines, sines = angles(offset, inv_freq)
    projected = jnp.einsum("sd,dkf->skf", normed_attn, w_qkv, preferred_element_type=jnp.float32)
    queries = rotate(projected[:, 0].reshape(full_rows, heads, HEAD_DIM), cosines, sines).astype(
        jnp.bfloat16
    )
    keys = rotate(projected[:, 1].reshape(full_rows, heads, HEAD_DIM), cosines, sines).astype(
        jnp.bfloat16
    )
    values = projected[:, 2].reshape(full_rows, heads, HEAD_DIM).astype(jnp.bfloat16)
    mixed, log_mass = attend(queries, keys, values, seq_of, is_local)
    mixed = mixed.reshape(full_rows, heads * HEAD_DIM).astype(jnp.bfloat16)
    resid_mid = stream + reduce_rows(mixed, w_out)
    normed_mlp = gather_rows(norm_gain(resid_mid, gain_row[model_width:]).astype(jnp.bfloat16))
    gate_up = jnp.einsum("sd,dkf->skf", normed_mlp, w_pair, preferred_element_type=jnp.float32)
    geglu_out = geglu(gate_up).astype(jnp.bfloat16)
    layer_out = resid_mid + reduce_rows(geglu_out, w_down)
    saved = (
        layer_in,
        resid_mid,
        normed_attn,
        queries,
        keys,
        values,
        log_mass,
        mixed,
        normed_mlp,
        geglu_out,
    )
    return (layer_out, saved)


def layer_backward(grad_out, saved, weights, gain_row, seq_lengths, is_local, inv_freq):
    (
        layer_in,
        resid_mid,
        normed_attn,
        queries,
        keys,
        values,
        log_mass,
        mixed,
        normed_mlp,
        geglu_out,
    ) = saved
    w_qkv, w_out, w_pair, w_down = weights
    local_rows, model_width = grad_out.shape
    full_rows, heads = (normed_attn.shape[0], queries.shape[1])
    grad_geglu, grad_down = fold_rows(grad_out.astype(jnp.bfloat16), geglu_out, w_down)
    gate_up = jnp.einsum("sd,dkf->skf", normed_mlp, w_pair, preferred_element_type=jnp.float32)
    _, pair_back = jax.vjp(geglu, gate_up)
    (grad_pair,) = pair_back(grad_geglu)
    grad_pair = grad_pair.astype(jnp.bfloat16)
    grad_gate_up = jnp.einsum(
        "sd,skf->dkf", normed_mlp, grad_pair, preferred_element_type=jnp.float32
    )
    grad_normed = back_rows(grad_pair, w_pair)
    _, mlp_norm_back = jax.vjp(norm_gain, resid_mid, gain_row[model_width:])
    grad_from_norm, gain_mlp = mlp_norm_back(grad_normed)
    grad_mid = grad_out + grad_from_norm
    grad_mixed, grad_outw = fold_rows(grad_mid.astype(jnp.bfloat16), mixed, w_out)
    grad_mixed = grad_mixed.astype(jnp.bfloat16).reshape(full_rows, heads, HEAD_DIM)
    seq_of, offset = layout(seq_lengths, full_rows)
    cosines, sines = angles(offset, inv_freq)
    grad_q, grad_k, grad_v = attend_back(
        queries, keys, values, log_mass, grad_mixed, seq_of, is_local
    )
    _, turn_back = jax.vjp(partial(rotate, cosines=cosines, sines=sines), grad_q)
    (grad_q_raw,) = turn_back(grad_q)
    (grad_k_raw,) = turn_back(grad_k)
    grad_projected = jnp.stack(
        [
            grad_q_raw.reshape(full_rows, -1),
            grad_k_raw.reshape(full_rows, -1),
            grad_v.reshape(full_rows, -1),
        ],
        axis=1,
    ).astype(jnp.bfloat16)
    grad_qkv = jnp.einsum(
        "sd,skf->dkf", normed_attn, grad_projected, preferred_element_type=jnp.float32
    )
    grad_attn_in = back_rows(grad_projected, w_qkv)
    _, attn_norm_back = jax.vjp(norm_gain, layer_in.astype(jnp.float32), gain_row[:model_width])
    grad_from_attn, gain_attn = attn_norm_back(grad_attn_in)
    grad_in = grad_mid + grad_from_attn
    gain_grad = jnp.concatenate([gain_attn, gain_mlp])
    return (grad_in, (grad_qkv, grad_outw, grad_gate_up, grad_down), gain_grad)


def body(
    tokens, lengths, qkv_weight, out_weight, gate_up_weight, down_weight, gains, out_cotangent
):
    section_id = lax.axis_index("pipe")
    micro_count = tokens.shape[1]
    is_local = section_id == 0
    half_dim = HEAD_DIM // 2
    inv_freq = jnp.where(is_local, frequencies(10000.0, half_dim), frequencies(160000.0, half_dim))
    gain_row = gains[0]
    batch_tokens = tokens[0]
    batch_cots = out_cotangent[0]
    batch_lengths = lengths[0]

    def weights_now():
        return fetch_weights(qkv_weight, out_weight, gate_up_weight, down_weight)

    def forward_step(received, tick_id):
        micro_id = jnp.clip(tick_id - section_id, 0, micro_count - 1)
        own_rows = lax.dynamic_index_in_dim(batch_tokens, micro_id, 0, keepdims=False)
        layer_in = jnp.where(is_local, own_rows, received)
        seq_lengths = lax.dynamic_index_in_dim(batch_lengths, micro_id, 0, keepdims=False)
        layer_out, saved = layer_forward(
            layer_in, weights_now(), gain_row, seq_lengths, is_local, inv_freq
        )
        layer_out = layer_out.astype(jnp.bfloat16)
        passed = shifted(layer_out, "pipe", 1)
        return (passed, (layer_out, saved))

    tick_ids = jnp.arange(micro_count + 1, dtype=jnp.int32)
    _, (layer_outs, saved_all) = lax.scan(forward_step, jnp.zeros_like(batch_tokens[0]), tick_ids)
    activations = lax.dynamic_slice_in_dim(layer_outs, section_id, micro_count, 0)
    initial = tuple(
        (
            jnp.zeros(weight.shape[1:], jnp.float32)
            for weight in (qkv_weight, out_weight, gate_up_weight, down_weight)
        )
    )

    def backward_step(running, tick_id):
        received, grad_sums, gain_sums = running
        micro_pos = tick_id - 1 + section_id
        active = ((micro_pos >= 0) & (micro_pos < micro_count)).astype(jnp.float32)
        micro_id = jnp.clip(micro_pos, 0, micro_count - 1)
        slot_id = micro_id + section_id
        saved = tuple(
            (lax.dynamic_index_in_dim(stacked, slot_id, 0, keepdims=False) for stacked in saved_all)
        )
        seq_lengths = lax.dynamic_index_in_dim(batch_lengths, micro_id, 0, keepdims=False)
        cot_rows = lax.dynamic_index_in_dim(batch_cots, micro_id, 0, keepdims=False).astype(
            jnp.float32
        )
        grad_out = jnp.where(is_local, received.astype(jnp.float32), cot_rows)
        grad_in, weight_grads, gain_grad = layer_backward(
            grad_out, saved, weights_now(), gain_row, seq_lengths, is_local, inv_freq
        )
        grad_low = grad_in.astype(jnp.bfloat16)
        passed = shifted(grad_low, "pipe", -1)
        shown_grad = jnp.where(is_local, grad_in, grad_low.astype(jnp.float32))
        weight_grads = tuple((one_grad * active for one_grad in weight_grads))
        weight_grads = (
            lax.psum_scatter(
                weight_grads[0].astype(jnp.bfloat16), "dp", scatter_dimension=0, tiled=True
            ).astype(jnp.float32),
            lax.psum_scatter(
                weight_grads[1].astype(jnp.bfloat16), "dp", scatter_dimension=1, tiled=True
            ).astype(jnp.float32),
            lax.psum_scatter(
                weight_grads[2].astype(jnp.bfloat16), "dp", scatter_dimension=0, tiled=True
            ).astype(jnp.float32),
            lax.psum_scatter(
                weight_grads[3].astype(jnp.bfloat16), "dp", scatter_dimension=1, tiled=True
            ).astype(jnp.float32),
        )
        grad_sums = tuple((so_far + addend for so_far, addend in zip(grad_sums, weight_grads)))
        return ((passed, grad_sums, gain_sums + gain_grad * active), shown_grad)

    start_state = (jnp.zeros_like(batch_tokens[0]), initial, jnp.zeros_like(gain_row))
    (_, grad_sums, gain_sums), shown_all = lax.scan(backward_step, start_state, tick_ids)
    gain_part = lax.psum_scatter(gain_sums, ("dp", "tensor"), scatter_dimension=0, tiled=True)
    input_grads = lax.dynamic_slice_in_dim(shown_all, 1 - section_id, micro_count, 0)
    return (
        activations[None, None],
        input_grads[None, None],
        grad_sums[0][None],
        grad_sums[1][None],
        grad_sums[2][None],
        grad_sums[3][None],
        gain_part[None],
    )


def solution(mesh):
    return jax.shard_map(
        body,
        mesh=mesh,
        in_specs=(
            P("dp", None, "tensor", None),
            P("dp", None, None),
            P("pipe", "dp", None, "tensor"),
            P("pipe", "tensor", "dp"),
            P("pipe", "dp", None, "tensor"),
            P("pipe", "tensor", "dp"),
            P("pipe", None),
            P("dp", None, "tensor", None),
        ),
        out_specs=(
            P("pipe", "dp", None, "tensor", None),
            P("pipe", "dp", None, "tensor", None),
            P("pipe", "dp", None, "tensor"),
            P("pipe", "tensor", "dp"),
            P("pipe", "dp", None, "tensor"),
            P("pipe", "tensor", "dp"),
            P("pipe", ("dp", "tensor")),
        ),
        check_vma=False,
    )
```

profile of v0, /device:TPU:0, one launch (start us, length us, event | category | flops | bytes accessed | tf_op | source)
XLA Modules:
  0.0 2006.9 jit_solution(8662997835381272434)
XLA Ops:
  17.4 786.2 %while.168 = (s32[]{:T(128)}, bf16[320,768]{1,0:T(8,128)(2,1)}, bf16[3,320,768]{2,1,0:T(8,128)(2,1)}, bf16[3,320,768]{2,1,0:T(8,128)(2,1)S(1)}, f32[3,320,768]{2...) while((s32[]{:T(128)}, bf16[320,768]{1,0:T(8,128)(2,1)}, ...), condition=%wide.region_16.17_spmd.clone.clone, body=%wide.region_0.16_spmd.clone.clone.sunk | while | flops 3495099904 | bytes 215130320 | solution.py:329
  23.8 31.8 %all_gather.109 = bf16[1,768,3,192]{3,2,0,1:T(4,128)(2,1)S(1)} all-gather(bf16[1,192,3,192]{3,2,0,1:T(4,128)(2,1)} %get-tuple-element.3243), channel_id=1, replica_groups=mesh['dp'=4,'pipe'=2,'tensor'=4] {'dp'}, dimensions={1}, use_global_device_ids=true | all-gather | bytes 1105920 | tf_op jit(solution)/shard_map/while/body/eval_jaxpr/all_gather | solution.py:160
  105.2 36.1 %while.171 = (s32[]{:T(128)}, bf16[3,1280,64]{1,2,0:T(8,128)(2,1)S(1)}, f32[3,1280]{1,0:T(4,128)S(1)}, bf16[3,1280,64]{2,1,0:T(8,128)(2,1)}, bf16[3,1280,64]{2,1...) while((s32[]{:T(128)}, ...), condition=%wide.region_11.11_spmd, body=%wide.region_6.10_spmd.sunk | while | flops 221184000 | bytes 12858345 | solution.py:94
  143.3 33.5 %reduce-scatter.17.cloned.1.call-done = bf16[320,768]{1,0:T(8,128)(2,1)} async-done(((bf16[1280,768]{1,0:T(8,128)(2,1)}), bf16[320,768]{1,0:T(8,128)(2,1)}) %reduce-scatter.17.cloned.1.call-update) | async-done | bytes 491536 | tf_op jit(solution)/shard_map/while/body/eval_jaxpr/reduce_scatter | solution.py:173
  180.7 24.0 %all_gather.112 = bf16[1,768,2,288]{3,2,0,1:T(2,128)(2,1)S(1)} all-gather(bf16[1,192,2,288]{3,2,0,1:T(2,128)(2,1)S(1)} %copy-done.43), channel_id=1, replica_groups=mesh['dp'=4,'pipe'=2,'tensor'=4] {'dp'}, dimensions={1}, use_global_device_ids=true | all-gather | bytes 1105920 | tf_op jit(solution)/shard_map/while/body/eval_jaxpr/all_gather | solution.py:162
  207.6 23.9 %all_gather.113 = bf16[1,288,768]{1,0,2:T(2,128)(2,1)S(1)} all-gather(bf16[1,288,192]{1,0,2:T(2,128)(2,1)S(1)} %copy-done.39), channel_id=1, replica_groups=mesh['dp'=4,'pipe'=2,'tensor'=4] {'dp'}, dimensions={2}, use_global_device_ids=true | all-gather | bytes 552960 | tf_op jit(solution)/shard_map/while/body/eval_jaxpr/all_gather | solution.py:163
  288.7 29.3 %all_gather.109 = bf16[1,768,3,192]{3,2,0,1:T(4,128)(2,1)S(1)} all-gather(bf16[1,192,3,192]{3,2,0,1:T(4,128)(2,1)} %get-tuple-element.3243), channel_id=1, replica_groups=mesh['dp'=4,'pipe'=2,'tensor'=4] {'dp'}, dimensions={1}, use_global_device_ids=true | all-gather | bytes 1105920 | tf_op jit(solution)/shard_map/while/body/eval_jaxpr/all_gather | solution.py:160
  366.7 36.1 %while.171 = (s32[]{:T(128)}, bf16[3,1280,64]{1,2,0:T(8,128)(2,1)S(1)}, f32[3,1280]{1,0:T(4,128)S(1)}, bf16[3,1280,64]{2,1,0:T(8,128)(2,1)}, bf16[3,1280,64]{2,1...) while((s32[]{:T(128)}, ...), condition=%wide.region_11.11_spmd, body=%wide.region_6.10_spmd.sunk | while | flops 221184000 | bytes 12858345 | solution.py:94
  404.9 32.7 %reduce-scatter.17.cloned.1.call-done = bf16[320,768]{1,0:T(8,128)(2,1)} async-done(((bf16[1280,768]{1,0:T(8,128)(2,1)}), bf16[320,768]{1,0:T(8,128)(2,1)}) %reduce-scatter.17.cloned.1.call-update) | async-done | bytes 491536 | tf_op jit(solution)/shard_map/while/body/eval_jaxpr/reduce_scatter | solution.py:173
  441.4 24.0 %all_gather.112 = bf16[1,768,2,288]{3,2,0,1:T(2,128)(2,1)S(1)} all-gather(bf16[1,192,2,288]{3,2,0,1:T(2,128)(2,1)S(1)} %copy-done.43), channel_id=1, replica_groups=mesh['dp'=4,'pipe'=2,'tensor'=4] {'dp'}, dimensions={1}, use_global_device_ids=true | all-gather | bytes 1105920 | tf_op jit(solution)/shard_map/while/body/eval_jaxpr/all_gather | solution.py:162
  468.2 23.9 %all_gather.113 = bf16[1,288,768]{1,0,2:T(2,128)(2,1)S(1)} all-gather(bf16[1,288,192]{1,0,2:T(2,128)(2,1)S(1)} %copy-done.39), channel_id=1, replica_groups=mesh['dp'=4,'pipe'=2,'tensor'=4] {'dp'}, dimensions={2}, use_global_device_ids=true | all-gather | bytes 552960 | tf_op jit(solution)/shard_map/while/body/eval_jaxpr/all_gather | solution.py:163
  549.3 29.3 %all_gather.109 = bf16[1,768,3,192]{3,2,0,1:T(4,128)(2,1)S(1)} all-gather(bf16[1,192,3,192]{3,2,0,1:T(4,128)(2,1)} %get-tuple-element.3243), channel_id=1, replica_groups=mesh['dp'=4,'pipe'=2,'tensor'=4] {'dp'}, dimensions={1}, use_global_device_ids=true | all-gather | bytes 1105920 | tf_op jit(solution)/shard_map/while/body/eval_jaxpr/all_gather | solution.py:160
  627.3 36.1 %while.171 = (s32[]{:T(128)}, bf16[3,1280,64]{1,2,0:T(8,128)(2,1)S(1)}, f32[3,1280]{1,0:T(4,128)S(1)}, bf16[3,1280,64]{2,1,0:T(8,128)(2,1)}, bf16[3,1280,64]{2,1...) while((s32[]{:T(128)}, ...), condition=%wide.region_11.11_spmd, body=%wide.region_6.10_spmd.sunk | while | flops 221184000 | bytes 12858345 | solution.py:94
  665.5 32.6 %reduce-scatter.17.cloned.1.call-done = bf16[320,768]{1,0:T(8,128)(2,1)} async-done(((bf16[1280,768]{1,0:T(8,128)(2,1)}), bf16[320,768]{1,0:T(8,128)(2,1)}) %reduce-scatter.17.cloned.1.call-update) | async-done | bytes 491536 | tf_op jit(solution)/shard_map/while/body/eval_jaxpr/reduce_scatter | solution.py:173
  702.0 24.1 %all_gather.112 = bf16[1,768,2,288]{3,2,0,1:T(2,128)(2,1)S(1)} all-gather(bf16[1,192,2,288]{3,2,0,1:T(2,128)(2,1)S(1)} %copy-done.43), channel_id=1, replica_groups=mesh['dp'=4,'pipe'=2,'tensor'=4] {'dp'}, dimensions={1}, use_global_device_ids=true | all-gather | bytes 1105920 | tf_op jit(solution)/shard_map/while/body/eval_jaxpr/all_gather | solution.py:162
  728.9 23.9 %all_gather.113 = bf16[1,288,768]{1,0,2:T(2,128)(2,1)S(1)} all-gather(bf16[1,288,192]{1,0,2:T(2,128)(2,1)S(1)} %copy-done.39), channel_id=1, replica_groups=mesh['dp'=4,'pipe'=2,'tensor'=4] {'dp'}, dimensions={2}, use_global_device_ids=true | all-gather | bytes 552960 | tf_op jit(solution)/shard_map/while/body/eval_jaxpr/all_gather | solution.py:163
  808.9 1143.9 %while.170 = (s32[]{:T(128)}, bf16[320,768]{1,0:T(8,128)(2,1)S(1)}, f32[192,3,192]{2,0,1:T(8,128)}, f32[192,192]{1,0:T(8,128)}, f32[192,2,288]{2,0,1:T(8,128)}, ...) while((s32[]{:T(128)}, bf16[320,768]{1,0:T(8,128)(2,1)S(1)}, ...), condition=%wide.region_42.43_spmd.clone.clone.clone, body=%wide.region_17.42_spmd.clone.clone.clone.sunk | while | flops 8148989440 | bytes 269099328 | solution.py:377
  830.7 24.0 %all_gather.115 = bf16[1,288,768]{1,0,2:T(2,128)(2,1)S(1)} all-gather(bf16[1,288,192]{1,0,2:T(2,128)(2,1)S(1)} %get-tuple-element.3351), channel_id=1, replica_groups=mesh['dp'=4,'pipe'=2,'tensor'=4] {'dp'}, dimensions={2}, use_global_device_ids=true | all-gather | bytes 552960 | tf_op jit(solution)/shard_map/while/body/eval_jaxpr/all_gather | solution.py:163
  857.3 23.1 %all_gather.116 = bf16[1,768,2,288]{3,2,0,1:T(2,128)(2,1)S(1)} all-gather(bf16[1,192,2,288]{3,2,0,1:T(2,128)(2,1)S(1)} %get-tuple-element.3350), channel_id=1, replica_groups=mesh['dp'=4,'pipe'=2,'tensor'=4] {'dp'}, dimensions={1}, use_global_device_ids=true | all-gather | bytes 1105920 | tf_op jit(solution)/shard_map/while/body/eval_jaxpr/all_gather | solution.py:162
  901.3 28.2 %reduce-scatter.21.cloned.1.call-done = bf16[320,768]{1,0:T(8,128)(2,1)} async-done(((bf16[1280,768]{1,0:T(8,128)(2,1)}), bf16[320,768]{1,0:T(8,128)(2,1)}) %reduce-scatter.21.cloned.1.call-update) | async-done | bytes 491536 | tf_op jit(solution)/shard_map/while/body/eval_jaxpr/reduce_scatter | solution.py:194
  959.5 27.3 %all_gather.119 = bf16[1,768,3,192]{3,2,0,1:T(4,128)(2,1)S(1)} all-gather(bf16[1,192,3,192]{3,2,0,1:T(4,128)(2,1)} %get-tuple-element.3361), channel_id=1, replica_groups=mesh['dp'=4,'pipe'=2,'tensor'=4] {'dp'}, dimensions={1}, use_global_device_ids=true | all-gather | bytes 1105920 | tf_op jit(solution)/shard_map/while/body/eval_jaxpr/all_gather | solution.py:160
  1007.4 98.3 %while.172 = (s32[]{:T(128)}, f32[3,1280,64]{1,2,0:T(8,128)}, f32[3,1280,64]{1,2,0:T(8,128)}, bf16[3,1280,64]{1,2,0:T(8,128)(2,1)}, bf16[3,1280,64]{2,1,0:T(8,12...) while((s32[]{:T(128)}, f32[3,1280,64]{1,2,0:T(8,128)}, ...), condition=%wide.region_29.29_spmd, body=%wide.region_25.28_spmd.sunk | while | flops 537026560 | bytes 55747860 | solution.py:145
  1011.5 24.9 %while.173 = (s32[]{:T(128)}, f32[1280,64]{0,1:T(8,128)S(1)}, f32[1280,64]{0,1:T(8,128)S(1)}, f32[2,640,64]{1,2,0:T(8,128)}, s32[2]{0:T(128)S(1)}, /*index=5*/s3...) while((s32[]{:T(128)}, f32[1280,64]{0,1:T(8,128)S(1)}, ...), condition=%wide.region_28.27_spmd.clone, body=%wide.region_26.26_spmd.clone.sunk | while | flops 537026560 | bytes 43285332 | solution.py:140
  1044.3 24.9 %while.173 = (s32[]{:T(128)}, f32[1280,64]{0,1:T(8,128)S(1)}, f32[1280,64]{0,1:T(8,128)S(1)}, f32[2,640,64]{1,2,0:T(8,128)}, s32[2]{0:T(128)S(1)}, /*index=5*/s3...) while((s32[]{:T(128)}, f32[1280,64]{0,1:T(8,128)S(1)}, ...), condition=%wide.region_28.27_spmd.clone, body=%wide.region_26.26_spmd.clone.sunk | while | flops 537026560 | bytes 43285332 | solution.py:140
  1077.0 24.9 %while.173 = (s32[]{:T(128)}, f32[1280,64]{0,1:T(8,128)S(1)}, f32[1280,64]{0,1:T(8,128)S(1)}, f32[2,640,64]{1,2,0:T(8,128)}, s32[2]{0:T(128)S(1)}, /*index=5*/s3...) while((s32[]{:T(128)}, f32[1280,64]{0,1:T(8,128)S(1)}, ...), condition=%wide.region_28.27_spmd.clone, body=%wide.region_26.26_spmd.clone.sunk | while | flops 537026560 | bytes 43285332 | solution.py:140
  1133.0 35.1 %reduce-scatter.23.cloned.1.call-done = bf16[320,768]{1,0:T(8,128)(2,1)} async-done(((bf16[1280,768]{1,0:T(8,128)(2,1)}), bf16[320,768]{1,0:T(8,128)(2,1)}) %reduce-scatter.23.cloned.1.call-update) | async-done | bytes 491536 | tf_op jit(solution)/shard_map/while/body/eval_jaxpr/reduce_scatter | solution.py:194
  1176.2 23.2 %reduce-scatter.25.cloned.1.call-done = bf16[192,3,192]{2,0,1:T(8,128)(2,1)} async-done(((bf16[768,3,192]{2,0,1:T(8,128)(2,1)}), bf16[192,3,192]{2,0,1:T(8,128)(2,1)}) %reduce-scatter.25.cloned.1.call-update) | async-done | bytes 221200 | tf_op jit(solution)/shard_map/while/body/eval_jaxpr/reduce_scatter | solution.py:360
  1205.8 23.3 %all_gather.115 = bf16[1,288,768]{1,0,2:T(2,128)(2,1)S(1)} all-gather(bf16[1,288,192]{1,0,2:T(2,128)(2,1)S(1)} %get-tuple-element.3351), channel_id=1, replica_groups=mesh['dp'=4,'pipe'=2,'tensor'=4] {'dp'}, dimensions={2}, use_global_device_ids=true | all-gather | bytes 552960 | tf_op jit(solution)/shard_map/while/body/eval_jaxpr/all_gather | solution.py:163
  1231.7 22.1 %all_gather.116 = bf16[1,768,2,288]{3,2,0,1:T(2,128)(2,1)S(1)} all-gather(bf16[1,192,2,288]{3,2,0,1:T(2,128)(2,1)S(1)} %get-tuple-element.3350), channel_id=1, replica_groups=mesh['dp'=4,'pipe'=2,'tensor'=4] {'dp'}, dimensions={1}, use_global_device_ids=true | all-gather | bytes 1105920 | tf_op jit(solution)/shard_map/while/body/eval_jaxpr/all_gather | solution.py:162
  1274.7 30.1 %reduce-scatter.21.cloned.1.call-done = bf16[320,768]{1,0:T(8,128)(2,1)} async-done(((bf16[1280,768]{1,0:T(8,128)(2,1)}), bf16[320,768]{1,0:T(8,128)(2,1)}) %reduce-scatter.21.cloned.1.call-update) | async-done | bytes 491536 | tf_op jit(solution)/shard_map/while/body/eval_jaxpr/reduce_scatter | solution.py:194
  1334.8 27.3 %all_gather.119 = bf16[1,768,3,192]{3,2,0,1:T(4,128)(2,1)S(1)} all-gather(bf16[1,192,3,192]{3,2,0,1:T(4,128)(2,1)} %get-tuple-element.3361), channel_id=1, replica_groups=mesh['dp'=4,'pipe'=2,'tensor'=4] {'dp'}, dimensions={1}, use_global_device_ids=true | all-gather | bytes 1105920 | tf_op jit(solution)/shard_map/while/body/eval_jaxpr/all_gather | solution.py:160
  1382.7 98.3 %while.172 = (s32[]{:T(128)}, f32[3,1280,64]{1,2,0:T(8,128)}, f32[3,1280,64]{1,2,0:T(8,128)}, bf16[3,1280,64]{1,2,0:T(8,128)(2,1)}, bf16[3,1280,64]{2,1,0:T(8,12...) while((s32[]{:T(128)}, f32[3,1280,64]{1,2,0:T(8,128)}, ...), condition=%wide.region_29.29_spmd, body=%wide.region_25.28_spmd.sunk | while | flops 537026560 | bytes 55747860 | solution.py:145
  1386.8 24.9 %while.173 = (s32[]{:T(128)}, f32[1280,64]{0,1:T(8,128)S(1)}, f32[1280,64]{0,1:T(8,128)S(1)}, f32[2,640,64]{1,2,0:T(8,128)}, s32[2]{0:T(128)S(1)}, /*index=5*/s3...) while((s32[]{:T(128)}, f32[1280,64]{0,1:T(8,128)S(1)}, ...), condition=%wide.region_28.27_spmd.clone, body=%wide.region_26.26_spmd.clone.sunk | while | flops 537026560 | bytes 43285332 | solution.py:140
  1419.6 24.9 %while.173 = (s32[]{:T(128)}, f32[1280,64]{0,1:T(8,128)S(1)}, f32[1280,64]{0,1:T(8,128)S(1)}, f32[2,640,64]{1,2,0:T(8,128)}, s32[2]{0:T(128)S(1)}, /*index=5*/s3...) while((s32[]{:T(128)}, f32[1280,64]{0,1:T(8,128)S(1)}, ...), condition=%wide.region_28.27_spmd.clone, body=%wide.region_26.26_spmd.clone.sunk | while | flops 537026560 | bytes 43285332 | solution.py:140
  1452.3 24.9 %while.173 = (s32[]{:T(128)}, f32[1280,64]{0,1:T(8,128)S(1)}, f32[1280,64]{0,1:T(8,128)S(1)}, f32[2,640,64]{1,2,0:T(8,128)}, s32[2]{0:T(128)S(1)}, /*index=5*/s3...) while((s32[]{:T(128)}, f32[1280,64]{0,1:T(8,128)S(1)}, ...), condition=%wide.region_28.27_spmd.clone, body=%wide.region_26.26_spmd.clone.sunk | while | flops 537026560 | bytes 43285332 | solution.py:140
  1508.3 34.9 %reduce-scatter.23.cloned.1.call-done = bf16[320,768]{1,0:T(8,128)(2,1)} async-done(((bf16[1280,768]{1,0:T(8,128)(2,1)}), bf16[320,768]{1,0:T(8,128)(2,1)}) %reduce-scatter.23.cloned.1.call-update) | async-done | bytes 491536 | tf_op jit(solution)/shard_map/while/body/eval_jaxpr/reduce_scatter | solution.py:194
  1552.3 22.4 %reduce-scatter.25.cloned.1.call-done = bf16[192,3,192]{2,0,1:T(8,128)(2,1)} async-done(((bf16[768,3,192]{2,0,1:T(8,128)(2,1)}), bf16[192,3,192]{2,0,1:T(8,128)(2,1)}) %reduce-scatter.25.cloned.1.call-update) | async-done | bytes 221200 | tf_op jit(solution)/shard_map/while/body/eval_jaxpr/reduce_scatter | solution.py:360
  1581.2 23.3 %all_gather.115 = bf16[1,288,768]{1,0,2:T(2,128)(2,1)S(1)} all-gather(bf16[1,288,192]{1,0,2:T(2,128)(2,1)S(1)} %get-tuple-element.3351), channel_id=1, replica_groups=mesh['dp'=4,'pipe'=2,'tensor'=4] {'dp'}, dimensions={2}, use_global_device_ids=true | all-gather | bytes 552960 | tf_op jit(solution)/shard_map/while/body/eval_jaxpr/all_gather | solution.py:163
  1607.1 22.1 %all_gather.116 = bf16[1,768,2,288]{3,2,0,1:T(2,128)(2,1)S(1)} all-gather(bf16[1,192,2,288]{3,2,0,1:T(2,128)(2,1)S(1)} %get-tuple-element.3350), channel_id=1, replica_groups=mesh['dp'=4,'pipe'=2,'tensor'=4] {'dp'}, dimensions={1}, use_global_device_ids=true | all-gather | bytes 1105920 | tf_op jit(solution)/shard_map/while/body/eval_jaxpr/all_gather | solution.py:162
  1650.1 30.1 %reduce-scatter.21.cloned.1.call-done = bf16[320,768]{1,0:T(8,128)(2,1)} async-done(((bf16[1280,768]{1,0:T(8,128)(2,1)}), bf16[320,768]{1,0:T(8,128)(2,1)}) %reduce-scatter.21.cloned.1.call-update) | async-done | bytes 491536 | tf_op jit(solution)/shard_map/while/body/eval_jaxpr/reduce_scatter | solution.py:194
  1710.3 27.3 %all_gather.119 = bf16[1,768,3,192]{3,2,0,1:T(4,128)(2,1)S(1)} all-gather(bf16[1,192,3,192]{3,2,0,1:T(4,128)(2,1)} %get-tuple-element.3361), channel_id=1, replica_groups=mesh['dp'=4,'pipe'=2,'tensor'=4] {'dp'}, dimensions={1}, use_global_device_ids=true | all-gather | bytes 1105920 | tf_op jit(solution)/shard_map/while/body/eval_jaxpr/all_gather | solution.py:160
  1758.1 98.3 %while.172 = (s32[]{:T(128)}, f32[3,1280,64]{1,2,0:T(8,128)}, f32[3,1280,64]{1,2,0:T(8,128)}, bf16[3,1280,64]{1,2,0:T(8,128)(2,1)}, bf16[3,1280,64]{2,1,0:T(8,12...) while((s32[]{:T(128)}, f32[3,1280,64]{1,2,0:T(8,128)}, ...), condition=%wide.region_29.29_spmd, body=%wide.region_25.28_spmd.sunk | while | flops 537026560 | bytes 55747860 | solution.py:145
  1762.2 24.9 %while.173 = (s32[]{:T(128)}, f32[1280,64]{0,1:T(8,128)S(1)}, f32[1280,64]{0,1:T(8,128)S(1)}, f32[2,640,64]{1,2,0:T(8,128)}, s32[2]{0:T(128)S(1)}, /*index=5*/s3...) while((s32[]{:T(128)}, f32[1280,64]{0,1:T(8,128)S(1)}, ...), condition=%wide.region_28.27_spmd.clone, body=%wide.region_26.26_spmd.clone.sunk | while | flops 537026560 | bytes 43285332 | solution.py:140
  1795.0 24.9 %while.173 = (s32[]{:T(128)}, f32[1280,64]{0,1:T(8,128)S(1)}, f32[1280,64]{0,1:T(8,128)S(1)}, f32[2,640,64]{1,2,0:T(8,128)}, s32[2]{0:T(128)S(1)}, /*index=5*/s3...) while((s32[]{:T(128)}, f32[1280,64]{0,1:T(8,128)S(1)}, ...), condition=%wide.region_28.27_spmd.clone, body=%wide.region_26.26_spmd.clone.sunk | while | flops 537026560 | bytes 43285332 | solution.py:140
  1827.8 24.9 %while.173 = (s32[]{:T(128)}, f32[1280,64]{0,1:T(8,128)S(1)}, f32[1280,64]{0,1:T(8,128)S(1)}, f32[2,640,64]{1,2,0:T(8,128)}, s32[2]{0:T(128)S(1)}, /*index=5*/s3...) while((s32[]{:T(128)}, f32[1280,64]{0,1:T(8,128)S(1)}, ...), condition=%wide.region_28.27_spmd.clone, body=%wide.region_26.26_spmd.clone.sunk | while | flops 537026560 | bytes 43285332 | solution.py:140
  1883.8 35.1 %reduce-scatter.23.cloned.1.call-done = bf16[320,768]{1,0:T(8,128)(2,1)} async-done(((bf16[1280,768]{1,0:T(8,128)(2,1)}), bf16[320,768]{1,0:T(8,128)(2,1)}) %reduce-scatter.23.cloned.1.call-update) | async-done | bytes 491536 | tf_op jit(solution)/shard_map/while/body/eval_jaxpr/reduce_scatter | solution.py:194
  1927.9 22.3 %reduce-scatter.25.cloned.1.call-done = bf16[192,3,192]{2,0,1:T(8,128)(2,1)} async-done(((bf16[768,3,192]{2,0,1:T(8,128)(2,1)}), bf16[192,3,192]{2,0,1:T(8,128)(2,1)}) %reduce-scatter.25.cloned.1.call-update) | async-done | bytes 221200 | tf_op jit(solution)/shard_map/while/body/eval_jaxpr/reduce_scatter | solution.py:360
  1958.1 40.0 %all-reduce.6 = f32[1536]{0:T(1024)S(1)} all-reduce(f32[1536]{0:T(1024)S(1)} %copy-done.63), channel_id=10, replica_groups=mesh['dp'=4,'pipe'=2,'tensor'=4] {'dp','tensor'}, use_global_device_ids=true, to_apply=%region_43.44.clone | all-reduce | flops 1536 | bytes 12288
  (1558 shorter events, 1171.6 us)
Async XLA Ops:
  17.4 66.4 %all-gather.5.cloned.1.call-start = ((), (), s32[]{:S(2)}) async-start(), calls=%async_computation.8 | async-start | bytes 2457600 | tf_op jit(solution)/shard_map/while/body/eval_jaxpr/all_gather | solution.py:169
  23.7 153.2 %reduce-scatter.17.cloned.1.call-start = ((), (), s32[]{:S(2)}) async-start(), calls=%async_computation.9 | async-start | bytes 2457600 | tf_op jit(solution)/shard_map/while/body/eval_jaxpr/reduce_scatter | solution.py:173
  143.3 89.3 %all-gather.7.cloned.1.call-start = ((), (), s32[]{:S(2)}) async-start(), calls=%async_computation.10 | async-start | bytes 2457600 | tf_op jit(solution)/shard_map/while/body/eval_jaxpr/all_gather | solution.py:169
  180.7 95.0 %reduce-scatter.19.cloned.1.call-start = ((), (), s32[]{:S(2)}) async-start(), calls=%async_computation.11 | async-start | bytes 2457600 | tf_op jit(solution)/shard_map/while/body/eval_jaxpr/reduce_scatter | solution.py:173
  277.7 4.0 collective-permute-start.1
  282.3 63.0 %all-gather.5.cloned.1.call-start = ((), (), s32[]{:S(2)}) async-start(), calls=%async_computation.8 | async-start | bytes 2457600 | tf_op jit(solution)/shard_map/while/body/eval_jaxpr/all_gather | solution.py:169
  288.6 148.9 %reduce-scatter.17.cloned.1.call-start = ((), (), s32[]{:S(2)}) async-start(), calls=%async_computation.9 | async-start | bytes 2457600 | tf_op jit(solution)/shard_map/while/body/eval_jaxpr/reduce_scatter | solution.py:173
  404.8 88.5 %all-gather.7.cloned.1.call-start = ((), (), s32[]{:S(2)}) async-start(), calls=%async_computation.10 | async-start | bytes 2457600 | tf_op jit(solution)/shard_map/while/body/eval_jaxpr/all_gather | solution.py:169
  441.3 95.0 %reduce-scatter.19.cloned.1.call-start = ((), (), s32[]{:S(2)}) async-start(), calls=%async_computation.11 | async-start | bytes 2457600 | tf_op jit(solution)/shard_map/while/body/eval_jaxpr/reduce_scatter | solution.py:173
  538.3 4.0 collective-permute-start.1
  543.0 63.0 %all-gather.5.cloned.1.call-start = ((), (), s32[]{:S(2)}) async-start(), calls=%async_computation.8 | async-start | bytes 2457600 | tf_op jit(solution)/shard_map/while/body/eval_jaxpr/all_gather | solution.py:169
  549.3 148.9 %reduce-scatter.17.cloned.1.call-start = ((), (), s32[]{:S(2)}) async-start(), calls=%async_computation.9 | async-start | bytes 2457600 | tf_op jit(solution)/shard_map/while/body/eval_jaxpr/reduce_scatter | solution.py:173
  665.5 88.4 %all-gather.7.cloned.1.call-start = ((), (), s32[]{:S(2)}) async-start(), calls=%async_computation.10 | async-start | bytes 2457600 | tf_op jit(solution)/shard_map/while/body/eval_jaxpr/all_gather | solution.py:169
  702.0 95.1 %reduce-scatter.19.cloned.1.call-start = ((), (), s32[]{:S(2)}) async-start(), calls=%async_computation.11 | async-start | bytes 2457600 | tf_op jit(solution)/shard_map/while/body/eval_jaxpr/reduce_scatter | solution.py:173
  799.0 3.9 collective-permute-start.1
  826.8 106.9 %copy-start.18 = (bf16[320,768]{1,0:T(8,128)(2,1)}, bf16[320,768]{1,0:T(8,128)(2,1)S(1)}, u32[]{:S(2)}) copy-start(bf16[320,768]{1,0:T(8,128)(2,1)S(1)} %get-tuple-element.3298) | copy-start | bytes 1474564 | tf_op jit(solution)/shard_map/while
  826.8 59.5 %all-gather.9.cloned.1.call-start = ((), (), s32[]{:S(2)}) async-start(), calls=%async_computation.12 | async-start | bytes 2457600 | tf_op jit(solution)/shard_map/while/body/eval_jaxpr/all_gather | solution.py:182
  830.7 98.8 %reduce-scatter.21.cloned.1.call-start = ((), (), s32[]{:S(2)}) async-start(), calls=%async_computation.13 | async-start | bytes 2457600 | tf_op jit(solution)/shard_map/while/body/eval_jaxpr/reduce_scatter | solution.py:194
  897.0 106.7 %all-gather.11.cloned.1.call-start = ((), (), s32[]{:S(2)}) async-start(), calls=%async_computation.14 | async-start | bytes 2457600 | tf_op jit(solution)/shard_map/while/body/eval_jaxpr/all_gather | solution.py:182
  935.6 183.2 %reduce-scatter.31.cloned.1.call-start = ((), (), s32[]{:S(2)}) async-start(), calls=%async_computation.19 | async-start | bytes 737280 | tf_op jit(solution)/shard_map/while
  995.4 129.1 %reduce-scatter.29.cloned.1.call-start = ((), (), s32[]{:S(2)}) async-start(), calls=%async_computation.18 | async-start | bytes 1474560 | tf_op jit(solution)/shard_map/while/body/eval_jaxpr/reduce_scatter | solution.py:366
  1003.7 128.3 %reduce-scatter.27.cloned.1.call-start = ((), (), s32[]{:S(2)}) async-start(), calls=%async_computation.17 | async-start | bytes 491520 | tf_op jit(solution)/shard_map/while
  1111.1 56.9 %reduce-scatter.23.cloned.1.call-start = ((), (), s32[]{:S(2)}) async-start(), calls=%async_computation.15 | async-start | bytes 2457600 | tf_op jit(solution)/shard_map/while/body/eval_jaxpr/reduce_scatter | solution.py:194
  1117.3 82.1 %reduce-scatter.25.cloned.1.call-start = ((), (), s32[]{:S(2)}) async-start(), calls=%async_computation.16 | async-start | bytes 1474560 | tf_op jit(solution)/shard_map/while/body/eval_jaxpr/reduce_scatter | solution.py:360
  1126.4 44.9 %copy-start.19 = (bf16[320,768]{1,0:T(8,128)(2,1)S(1)}, bf16[320,768]{1,0:T(8,128)(2,1)}, u32[]{:S(2)}) copy-start(bf16[320,768]{1,0:T(8,128)(2,1)} %copy-done.18) | copy-start | bytes 1474564 | tf_op jit(solution)/shard_map/while
  1126.4 44.9 %copy-start.58 = (f32[320]{0:T(512)S(1)}, f32[320]{0:T(512)}, u32[]{:S(2)}) copy-start(f32[320]{0:T(512)} %copy-done.57) | copy-start | bytes 3844 | tf_op jit(solution)/shard_map/while
  1174.0 27.3 %collective-permute-start = (bf16[320,768]{1,0:T(8,128)(2,1)}, bf16[320,768]{1,0:T(8,128)(2,1)S(1)}, u32[]{:S(2)}, u32[]{:S(2)}) collective-permute-start(bf16[320,768]{1,0:T(8,128)(2,1)} %get-tuple-element.2921), channel_id=1, source_target_pairs={{4,0},{5,1},{6,2},{7,3},{12,8},{13,9},{14,10},{15,11},{20,16},{21,... | collective-permute-start | bytes 1474568 | tf_op jit(solution)/shard_map/while/body/eval_jaxpr/ppermute | solution.py:15
  1201.9 107.1 %copy-start.18 = (bf16[320,768]{1,0:T(8,128)(2,1)}, bf16[320,768]{1,0:T(8,128)(2,1)S(1)}, u32[]{:S(2)}) copy-start(bf16[320,768]{1,0:T(8,128)(2,1)S(1)} %get-tuple-element.3298) | copy-start | bytes 1474564 | tf_op jit(solution)/shard_map/while
  1201.9 57.9 %all-gather.9.cloned.1.call-start = ((), (), s32[]{:S(2)}) async-start(), calls=%async_computation.12 | async-start | bytes 2457600 | tf_op jit(solution)/shard_map/while/body/eval_jaxpr/all_gather | solution.py:182
  1205.7 99.0 %reduce-scatter.21.cloned.1.call-start = ((), (), s32[]{:S(2)}) async-start(), calls=%async_computation.13 | async-start | bytes 2457600 | tf_op jit(solution)/shard_map/while/body/eval_jaxpr/reduce_scatter | solution.py:194
  1270.4 108.6 %all-gather.11.cloned.1.call-start = ((), (), s32[]{:S(2)}) async-start(), calls=%async_computation.14 | async-start | bytes 2457600 | tf_op jit(solution)/shard_map/while/body/eval_jaxpr/all_gather | solution.py:182
  1310.9 183.2 %reduce-scatter.31.cloned.1.call-start = ((), (), s32[]{:S(2)}) async-start(), calls=%async_computation.19 | async-start | bytes 737280 | tf_op jit(solution)/shard_map/while
  1370.7 129.1 %reduce-scatter.29.cloned.1.call-start = ((), (), s32[]{:S(2)}) async-start(), calls=%async_computation.18 | async-start | bytes 1474560 | tf_op jit(solution)/shard_map/while/body/eval_jaxpr/reduce_scatter | solution.py:366
  1379.0 128.3 %reduce-scatter.27.cloned.1.call-start = ((), (), s32[]{:S(2)}) async-start(), calls=%async_computation.17 | async-start | bytes 491520 | tf_op jit(solution)/shard_map/while
  1486.4 56.8 %reduce-scatter.23.cloned.1.call-start = ((), (), s32[]{:S(2)}) async-start(), calls=%async_computation.15 | async-start | bytes 2457600 | tf_op jit(solution)/shard_map/while/body/eval_jaxpr/reduce_scatter | solution.py:194
  1492.6 82.0 %reduce-scatter.25.cloned.1.call-start = ((), (), s32[]{:S(2)}) async-start(), calls=%async_computation.16 | async-start | bytes 1474560 | tf_op jit(solution)/shard_map/while/body/eval_jaxpr/reduce_scatter | solution.py:360
  1549.1 27.6 %collective-permute-start = (bf16[320,768]{1,0:T(8,128)(2,1)}, bf16[320,768]{1,0:T(8,128)(2,1)S(1)}, u32[]{:S(2)}, u32[]{:S(2)}) collective-permute-start(bf16[320,768]{1,0:T(8,128)(2,1)} %get-tuple-element.2921), channel_id=1, source_target_pairs={{4,0},{5,1},{6,2},{7,3},{12,8},{13,9},{14,10},{15,11},{20,16},{21,... | collective-permute-start | bytes 1474568 | tf_op jit(solution)/shard_map/while/body/eval_jaxpr/ppermute | solution.py:15
  1577.3 107.1 %copy-start.18 = (bf16[320,768]{1,0:T(8,128)(2,1)}, bf16[320,768]{1,0:T(8,128)(2,1)S(1)}, u32[]{:S(2)}) copy-start(bf16[320,768]{1,0:T(8,128)(2,1)S(1)} %get-tuple-element.3298) | copy-start | bytes 1474564 | tf_op jit(solution)/shard_map/while
  1577.3 57.9 %all-gather.9.cloned.1.call-start = ((), (), s32[]{:S(2)}) async-start(), calls=%async_computation.12 | async-start | bytes 2457600 | tf_op jit(solution)/shard_map/while/body/eval_jaxpr/all_gather | solution.py:182
  1581.2 99.0 %reduce-scatter.21.cloned.1.call-start = ((), (), s32[]{:S(2)}) async-start(), calls=%async_computation.13 | async-start | bytes 2457600 | tf_op jit(solution)/shard_map/while/body/eval_jaxpr/reduce_scatter | solution.py:194
  1645.8 108.6 %all-gather.11.cloned.1.call-start = ((), (), s32[]{:S(2)}) async-start(), calls=%async_computation.14 | async-start | bytes 2457600 | tf_op jit(solution)/shard_map/while/body/eval_jaxpr/all_gather | solution.py:182
  1686.4 183.2 %reduce-scatter.31.cloned.1.call-start = ((), (), s32[]{:S(2)}) async-start(), calls=%async_computation.19 | async-start | bytes 737280 | tf_op jit(solution)/shard_map/while
  1746.2 129.1 %reduce-scatter.29.cloned.1.call-start = ((), (), s32[]{:S(2)}) async-start(), calls=%async_computation.18 | async-start | bytes 1474560 | tf_op jit(solution)/shard_map/while/body/eval_jaxpr/reduce_scatter | solution.py:366
  1754.4 128.3 %reduce-scatter.27.cloned.1.call-start = ((), (), s32[]{:S(2)}) async-start(), calls=%async_computation.17 | async-start | bytes 491520 | tf_op jit(solution)/shard_map/while
  1861.9 57.0 %reduce-scatter.23.cloned.1.call-start = ((), (), s32[]{:S(2)}) async-start(), calls=%async_computation.15 | async-start | bytes 2457600 | tf_op jit(solution)/shard_map/while/body/eval_jaxpr/reduce_scatter | solution.py:194
  1868.1 82.1 %reduce-scatter.25.cloned.1.call-start = ((), (), s32[]{:S(2)}) async-start(), calls=%async_computation.16 | async-start | bytes 1474560 | tf_op jit(solution)/shard_map/while/body/eval_jaxpr/reduce_scatter | solution.py:360
  1924.8 27.4 %collective-permute-start = (bf16[320,768]{1,0:T(8,128)(2,1)}, bf16[320,768]{1,0:T(8,128)(2,1)S(1)}, u32[]{:S(2)}, u32[]{:S(2)}) collective-permute-start(bf16[320,768]{1,0:T(8,128)(2,1)} %get-tuple-element.2921), channel_id=1, source_target_pairs={{4,0},{5,1},{6,2},{7,3},{12,8},{13,9},{14,10},{15,11},{20,16},{21,... | collective-permute-start | bytes 1474568 | tf_op jit(solution)/shard_map/while/body/eval_jaxpr/ppermute | solution.py:15
  1952.8 45.3 %copy-start.64 = (u32[32]{0:T(128)S(1)}, u32[32]{0:T(128)}, u32[]{:S(2)}) copy-start(u32[32]{0:T(128)} %constant.639) | copy-start | bytes 388
  (248 other events, 1751.3 us)
Sparse Core Ops, SparseCore 0:
  23.8 36.9 all-gather.4
  143.4 33.4 reduce-scatter.16
  180.8 34.1 all-gather.6
  242.6 33.0 reduce-scatter.18
  288.7 34.2 all-gather.4
  404.9 32.5 reduce-scatter.16
  441.4 34.1 all-gather.6
  503.3 33.0 reduce-scatter.18
  549.4 34.1 all-gather.4
  665.6 32.5 reduce-scatter.16
  702.1 34.2 all-gather.6
  763.9 33.0 reduce-scatter.18
  830.8 34.2 all-gather.8
  897.1 32.2 reduce-scatter.20
  935.8 34.1 all-gather.10
  995.5 22.1 reduce-scatter.30
  1020.0 27.4 reduce-scatter.28
  1111.2 20.6 reduce-scatter.26
  1135.6 32.4 reduce-scatter.22
  1170.2 29.1 reduce-scatter.24
  1205.9 32.9 all-gather.8
  1270.5 34.1 reduce-scatter.20
  1311.0 34.1 all-gather.10
  1370.9 22.1 reduce-scatter.30
  1395.4 27.4 reduce-scatter.28
  1486.5 20.6 reduce-scatter.26
  1510.8 32.3 reduce-scatter.22
  1545.5 29.1 reduce-scatter.24
  1581.3 32.9 all-gather.8
  1646.0 34.1 reduce-scatter.20
  1686.5 34.2 all-gather.10
  1746.3 22.0 reduce-scatter.30
  1770.7 27.5 reduce-scatter.28
  1862.0 20.7 reduce-scatter.26
  1886.4 32.3 reduce-scatter.22
  1921.0 29.1 reduce-scatter.24
where the time goes:
time: 2030 us; the launch traced here: 2010 us
  blocking collectives  612 us (30%)
  waiting for transfers between devices  413 us (20%)
  local copies, waits for them, and re-layouts  353 us (17%)
  matrix products  321 us (16%)
  other arithmetic  229 us (11%)
  loops' own time  50.8 us (3%)
    reduce_scatter x6, waiting for transfers between devices, back_rows(): lax.psum_scatter(jnp.einsum('sf,df->sd', grad_flat, weight_flat, preferre...  193 us
    all_gather x6, blocking collectives, fetch_weights(): lax.all_gather(qkv_weight, 'dp', axis=1, tiled=True)  172 us
    all_gather x6, blocking collectives, fetch_weights(): lax.all_gather(down_weight, 'dp', axis=2, tiled=True)  142 us
    all_gather x6, blocking collectives, fetch_weights(): lax.all_gather(gate_up_weight, 'dp', axis=1, tiled=True)  139 us
    reduce_scatter x6, waiting for transfers between devices, reduce_rows(): lax.psum_scatter(jnp.dot(left_rows, weight, preferred_element_type=jnp.fl...  134 us
    all_gather x6, blocking collectives, fetch_weights(): lax.all_gather(out_weight, 'dp', axis=2, tiled=True)  118 us
    dot_general x36, matrix products, per_block(): jnp.einsum('qd,kd->qk', query_rows, key_head, preferred_element_type=jnp....  90.5 us
    while x519, local copies, waits for them, and re-layouts  85.7 us
  transfers between devices with their start and end apart: 42, of which 18 were waited for; matrix products, arithmetic and copies ran while one was open for 26% of the time, Pallas kernels for 0%

commit v1 on v0

v1 whole, which is shorter than its diff:
```python
import functools

import jax
import jax.numpy as jnp
from jax import lax
from jax.experimental import pallas as pl
from jax.experimental.pallas import tpu as pltpu
from jax.sharding import PartitionSpec as P

HEAD_DIM = 64
WINDOW = 128
EPS = 1e-05
BLOCK = 256
BF16 = jnp.bfloat16
F32 = jnp.float32
VMEM_BYTES = 48 * 1024 * 1024


def swap_cores(block):
    return lax.ppermute(block, "pipe", [(0, 1), (1, 0)])


def to_mate(block, bit):
    size = lax.axis_size("tensor")
    return lax.ppermute(block, "tensor", [(i, i ^ bit) for i in range(size)])


def put(buffer, block, index):
    return lax.dynamic_update_slice_in_dim(buffer, block[None], index, 0)


def take(buffer, index):
    return lax.dynamic_index_in_dim(buffer, index, 0, keepdims=False)


def gather_tensor(block):
    me = lax.axis_index("tensor")
    half = block.shape[0] // 2
    one = to_mate(block, 1)
    two = to_mate(block, 2)
    far_head = to_mate(two[:half], 1)
    far_tail = to_mate(one[half:], 2)
    out = jnp.zeros((4,) + block.shape, block.dtype)
    out = put(out, block, me)
    out = put(out, one, me ^ 1)
    out = put(out, two, me ^ 2)
    return put(out, jnp.concatenate([far_head, far_tail], 0), me ^ 3)


def scatter_tensor(blocks):
    me = lax.axis_index("tensor")
    half = blocks.shape[1] // 2
    low = blocks.dtype
    far = take(blocks, me ^ 3)
    head = to_mate(far[:half], 1)
    tail = to_mate(far[half:], 2)
    one = take(blocks, me ^ 1).astype(F32)
    two = take(blocks, me ^ 2).astype(F32)
    one = jnp.concatenate([one[:half], one[half:] + tail.astype(F32)], 0).astype(low)
    two = jnp.concatenate([two[:half] + head.astype(F32), two[half:]], 0).astype(low)
    from_one = to_mate(one, 1)
    from_two = to_mate(two, 2)
    return take(blocks, me).astype(F32) + from_one.astype(F32) + from_two.astype(F32)


def swap_tensor(blocks):
    me = lax.axis_index("tensor")
    out = jnp.zeros_like(blocks)
    out = put(out, take(blocks, me), me)
    for bit in (1, 2, 3):
        out = put(out, to_mate(take(blocks, me ^ bit), bit), me ^ bit)
    return out


def gather_dp(block):
    size = lax.axis_size("dp")
    if size > 4:
        return lax.all_gather(block, "dp", axis=0)
    me = lax.axis_index("dp")
    out = put(jnp.zeros((size,) + block.shape, block.dtype), block, me)
    for step in range(1, size):
        route = [(i, (i + step) % size) for i in range(size)]
        out = put(out, lax.ppermute(block, "dp", route), (me - step) % size)
    return out


def scatter_dp(blocks, low):
    size = lax.axis_size("dp")
    if size > 4:
        return lax.psum_scatter(
            blocks.astype(low), "dp", scatter_dimension=0, tiled=False
        ).astype(F32)
    me = lax.axis_index("dp")
    total = take(blocks, me)
    for step in range(1, size):
        route = [(i, (i + step) % size) for i in range(size)]
        sent = take(blocks, (me + step) % size).astype(low)
        total = total + lax.ppermute(sent, "dp", route).astype(F32)
    return total


def join_halves(mine, other, axis):
    core = lax.axis_index("pipe")
    out = jnp.stack([mine, other], axis)
    return jnp.where(core == 0, out, jnp.stack([other, mine], axis))


def layer_halves(shard):
    core = lax.axis_index("pipe")
    rows = shard.shape[0] // 2
    mine = lax.dynamic_slice_in_dim(shard, core * rows, rows, 0)
    other = lax.dynamic_slice_in_dim(shard, (1 - core) * rows, rows, 0)
    got = swap_cores(other)
    first = jnp.where(core == 0, mine, got)
    second = jnp.where(core == 0, got, mine)
    return first, second


def whole_dp(half):
    gathered = gather_dp(half)
    both = join_halves(gathered, swap_cores(gathered), 1)
    return both.reshape(-1, half.shape[-1])


def whole_all(half):
    gathered = gather_tensor(gather_dp(half))
    both = join_halves(gathered, swap_cores(gathered), 2)
    return both.reshape(4, -1, half.shape[-1])


def half_sums(grad):
    core = lax.axis_index("pipe")
    n = lax.axis_size("dp")
    lead = grad.shape[:-2]
    rows = grad.shape[-2] // (2 * n)
    split = grad.reshape(lead + (n, 2, rows, grad.shape[-1]))
    axis = len(lead) + 1
    mine = lax.dynamic_index_in_dim(split, core, axis, keepdims=False)
    other = lax.dynamic_index_in_dim(split, 1 - core, axis, keepdims=False)
    return mine.astype(F32) + swap_cores(other).astype(F32)


def reduce_dp(grad):
    return scatter_dp(half_sums(grad), BF16)


def reduce_all(grad):
    return scatter_dp(scatter_tensor(half_sums(grad).astype(BF16)), BF16)


def own_layer(first, second):
    core = lax.axis_index("pipe")
    mine = jnp.where(core == 0, first, second)
    other = swap_cores(jnp.where(core == 0, second, first))
    return join_halves(mine, other, 0).reshape(-1, first.shape[-1])


def norm_parts(stream):
    average = jnp.mean(stream, axis=-1, keepdims=True)
    centred = stream - average
    spread = jnp.mean(centred * centred, axis=-1, keepdims=True)
    scale = lax.rsqrt(spread + EPS)
    return centred * scale, scale


def norm_back(grad, unit, scale, gain):
    scaled = grad * gain
    mean_one = jnp.mean(scaled, axis=-1, keepdims=True)
    mean_two = jnp.mean(scaled * unit, axis=-1, keepdims=True)
    return scale * (scaled - mean_one - unit * mean_two)


def dot(left, right, dims):
    return lax.dot_general(left, right, (dims, ((), ())), preferred_element_type=F32)


NN = ((1,), (0,))
NT = ((1,), (1,))
TN = ((0,), (0,))


def window_start(block_id, rows, span):
    if span == rows:
        return 0
    start = jnp.clip(block_id * BLOCK - WINDOW // 2, 0, rows - span)
    return pl.multiple_of(start, WINDOW // 2)


def key_mask(start, span, first, last):
    keys = start + lax.broadcasted_iota(jnp.int32, (span, BLOCK), 0)
    return (keys >= first) & (keys < last)


def attend_kernel(
    span, proj_ref, cos_ref, sin_ref, first_ref, last_ref,
    mixed_ref, queries_ref, keys_ref, values_ref, mass_ref, key_rows, value_rows,
):
    width, rows = queries_ref.shape
    heads = width // HEAD_DIM
    half = HEAD_DIM // 2
    cosines, sines = cos_ref[...], sin_ref[...]
    for head in range(heads):
        low = head * HEAD_DIM
        for part, ref in ((0, queries_ref), (1, keys_ref)):
            upper = proj_ref[part * width + low : part * width + low + half, :]
            lower = proj_ref[part * width + low + half : part * width + low + HEAD_DIM, :]
            turned = jnp.concatenate(
                [upper * cosines - lower * sines, lower * cosines + upper * sines], 0
            )
            ref[low : low + HEAD_DIM, :] = turned.astype(BF16)
            if part == 1:
                key_rows[head] = turned.T.astype(BF16)
        value = proj_ref[2 * width + low : 2 * width + low + HEAD_DIM, :]
        values_ref[low : low + HEAD_DIM, :] = value.astype(BF16)
        value_rows[head] = value.T.astype(BF16)
    mass_ref[...] = jnp.zeros_like(mass_ref)

    def block(block_id, carry):
        start = window_start(block_id, rows, span)
        columns = pl.ds(pl.multiple_of(block_id * BLOCK, BLOCK), BLOCK)
        mask = key_mask(start, span, first_ref[:, columns], last_ref[:, columns])
        outs = []
        for head in range(heads):
            low = head * HEAD_DIM
            query = queries_ref[low : low + HEAD_DIM, columns] * BF16(HEAD_DIM**-0.5)
            scores = dot(key_rows[head, pl.ds(start, span), :], query, NN)
            scores = jnp.where(mask, scores, -1e30)
            top = jnp.max(scores, axis=0, keepdims=True)
            expos = jnp.exp(scores - top)
            total = jnp.sum(expos, axis=0, keepdims=True)
            probs = (expos * (1.0 / total)).astype(BF16)
            if span == rows:
                value = values_ref[low : low + HEAD_DIM, :]
            else:
                value = value_rows[head, pl.ds(start, span), :].T
            outs.append(dot(value, probs, NN))
            mass_ref[head : head + 1, columns] = top + jnp.log(total)
        mixed_ref[columns, :] = jnp.concatenate(outs, 0).T.astype(BF16)
        return carry

    lax.fori_loop(0, rows // BLOCK, block, 0)


def attend(projected, cosines, sines, first, last, is_local):
    width3, rows = projected.shape
    width = width3 // 3
    heads = width // HEAD_DIM
    span = min(rows, BLOCK + WINDOW) if is_local else rows
    shape = jax.ShapeDtypeStruct((width, rows), BF16)
    return pl.pallas_call(
        functools.partial(attend_kernel, span),
        out_shape=(
            jax.ShapeDtypeStruct((rows, width), BF16), shape, shape, shape,
            jax.ShapeDtypeStruct((8, rows), F32),
        ),
        scratch_shapes=[
            pltpu.VMEM((heads, rows, HEAD_DIM), BF16),
            pltpu.VMEM((heads, rows, HEAD_DIM), BF16),
        ],
        compiler_params=pltpu.CompilerParams(vmem_limit_bytes=VMEM_BYTES),
        name="attend_local" if is_local else "attend_global",
    )(projected, cosines, sines, first, last)


def attend_back_kernel(
    span, queries_ref, keys_ref, values_ref, mass_ref, grad_ref,
    cos_ref, sin_ref, first_ref, last_ref, out_ref,
    query_rows, key_rows, value_rows, grad_cols, grad_rows, sum_q, sum_k, sum_v,
):
    width, rows = queries_ref.shape
    heads = width // HEAD_DIM
    half = HEAD_DIM // 2
    scale = HEAD_DIM**-0.5
    grad_cols[...] = grad_ref[...].astype(F32).T.astype(BF16)
    for head in range(heads):
        cut = slice(head * HEAD_DIM, (head + 1) * HEAD_DIM)
        query_rows[head] = (queries_ref[cut, :].astype(F32) * scale).T.astype(BF16)
        key_rows[head] = keys_ref[cut, :].astype(F32).T.astype(BF16)
        value_rows[head] = values_ref[cut, :].astype(F32).T.astype(BF16)
        grad_rows[head] = grad_ref[:, cut]
    sum_k[...] = jnp.zeros_like(sum_k)
    sum_v[...] = jnp.zeros_like(sum_v)

    def block(block_id, carry):
        start = window_start(block_id, rows, span)
        window = pl.ds(start, span)
        columns = pl.ds(pl.multiple_of(block_id * BLOCK, BLOCK), BLOCK)
        mask = key_mask(start, span, first_ref[:, columns], last_ref[:, columns])
        for head in range(heads):
            cut = slice(head * HEAD_DIM, (head + 1) * HEAD_DIM)
            query = queries_ref[cut, columns] * BF16(scale)
            key = key_rows[head, window, :]
            scores = dot(key, query, NN) - mass_ref[head : head + 1, columns]
            probs = jnp.exp(jnp.where(mask, scores, -1e30))
            grad_probs = dot(value_rows[head, window, :], grad_cols[cut, columns], NN)
            weighted = probs * grad_probs
            inner = jnp.sum(weighted, axis=0, keepdims=True)
            grad_scores = (weighted - probs * inner).astype(BF16)
            sum_v[head, window, :] += dot(probs.astype(BF16), grad_rows[head, columns, :], NN)
            sum_k[head, window, :] += dot(grad_scores, query_rows[head, columns, :], NN)
            key_cols = keys_ref[cut, :] if span == rows else key.T
            sum_q[cut, columns] = dot(key_cols, grad_scores, NN)
        return carry

    lax.fori_loop(0, rows // BLOCK, block, 0)
    cosines, sines = cos_ref[...], sin_ref[...]
    for head in range(heads):
        low = head * HEAD_DIM
        turned_q = sum_q[low : low + HEAD_DIM, :] * scale
        for part, turned in ((0, turned_q), (1, sum_k[head].T)):
            upper, lower = turned[:half], turned[half:]
            raw = jnp.concatenate(
                [upper * cosines + lower * sines, lower * cosines - upper * sines], 0
            )
            out_ref[part * width + low : part * width + low + HEAD_DIM, :] = raw.astype(BF16)
        out_ref[2 * width + low : 2 * width + low + HEAD_DIM, :] = sum_v[head].T.astype(BF16)


def attend_back(queries, keys, values, mass, grad, cosines, sines, first, last, is_local):
    width, rows = queries.shape
    heads = width // HEAD_DIM
    span = min(rows, BLOCK + WINDOW) if is_local else rows
    low_rows = pltpu.VMEM((heads, rows, HEAD_DIM), BF16)
    sums = pltpu.VMEM((heads, rows, HEAD_DIM), F32)
    return pl.pallas_call(
        functools.partial(attend_back_kernel, span),
        out_shape=jax.ShapeDtypeStruct((3 * width, rows), BF16),
        scratch_shapes=[
            low_rows, low_rows, low_rows, pltpu.VMEM((width, rows), BF16), low_rows,
            pltpu.VMEM((width, rows), F32), sums, sums,
        ],
        compiler_params=pltpu.CompilerParams(vmem_limit_bytes=VMEM_BYTES),
        name="attend_back_local" if is_local else "attend_back_global",
    )(queries, keys, values, mass, grad, cosines, sines, first, last)


def erf_parts(gate):
    cumulative = 0.5 * (1.0 + lax.erf(gate * 0.7071067811865476))
    density = 0.3989422804014327 * jnp.exp(-0.5 * gate * gate)
    return cumulative, density


def token_kernel(
    pair, mixed_ref, in_ref, mats_ref, down_ref, gain_ref, next_ref,
    mid_ref, out_ref, normed_ref, sums,
):
    parts, _, width = mixed_ref.shape
    units = pair // 2
    sums[...] = in_ref[...].astype(F32)

    def project(part, carry):
        sums[...] += dot(mixed_ref[part], mats_ref[part, :, pair : pair + width], NT)
        return carry

    lax.fori_loop(0, parts, project, 0)
    mid = sums[...]
    mid_ref[...] = mid
    normed = (norm_parts(mid)[0] * gain_ref[...]).astype(BF16)

    def feed(part, carry):
        gate_up = dot(normed, mats_ref[part, :, :pair], NN)
        gate = gate_up[:, :units]
        hidden = (gate * erf_parts(gate)[0] * gate_up[:, units:]).astype(BF16)
        sums[...] += dot(hidden, down_ref[part], NT)
        return carry

    lax.fori_loop(0, parts, feed, 0)
    low = sums[...].astype(BF16)
    out_ref[...] = low
    normed_ref[...] = (norm_parts(low.astype(F32))[0] * next_ref[...]).astype(BF16)


def token_forward(mixed, layer_in, mats, down, gain, next_gain):
    pair = mats.shape[2] - mixed.shape[2]
    shape = layer_in.shape
    return pl.pallas_call(
        functools.partial(token_kernel, pair),
        out_shape=(
            jax.ShapeDtypeStruct(shape, F32),
            jax.ShapeDtypeStruct(shape, BF16),
            jax.ShapeDtypeStruct(shape, BF16),
        ),
        scratch_shapes=[pltpu.VMEM(shape, F32)],
        compiler_params=pltpu.CompilerParams(vmem_limit_bytes=VMEM_BYTES),
        name="token_forward",
    )(mixed, layer_in, mats, down, gain, next_gain)


def token_back_kernel(
    pair, grad_ref, mid_ref, mixed_ref, mats_ref, down_ref, gain_ref,
    mats_grad_ref, down_grad_ref, mixed_grad_ref, grad_mid_ref, gain_grad_ref, sums,
):
    parts, _, width = mixed_ref.shape
    units = pair // 2
    grad = grad_ref[...].astype(F32)
    grad_low = grad.astype(BF16)
    grad_flip = grad.T.astype(BF16)
    unit, scale = norm_parts(mid_ref[...])
    gained = unit * gain_ref[...]
    normed = gained.astype(BF16)
    normed_flip = gained.T.astype(BF16)
    sums[...] = jnp.zeros_like(sums)

    def feed(part, carry):
        gate_up = dot(normed, mats_ref[part, :, :pair], NN)
        gate, up = gate_up[:, :units], gate_up[:, units:]
        cumulative, density = erf_parts(gate)
        gelu = gate * cumulative
        hidden = (gelu * up).astype(BF16)
        grad_hidden = dot(grad_low, down_ref[part], NN)
        grad_gate = grad_hidden * up * (cumulative + gate * density)
        grad_up = grad_hidden * gelu
        grad_pair = jnp.concatenate([grad_gate, grad_up], 1).astype(BF16)
        down_grad_ref[part] = dot(grad_flip, hidden, NN).astype(BF16)
        mats_grad_ref[part, :, :pair] = dot(normed_flip, grad_pair, NN).astype(BF16)
        sums[...] += dot(grad_pair, mats_ref[part, :, :pair], NT)
        return carry

    lax.fori_loop(0, parts, feed, 0)
    grad_normed = sums[...]
    gain_grad_ref[...] = jnp.sum(grad_normed * unit, axis=0, keepdims=True)
    grad_mid = grad + norm_back(grad_normed, unit, scale, gain_ref[...])
    grad_mid_ref[...] = grad_mid
    mid_low = grad_mid.astype(BF16)
    mid_flip = grad_mid.T.astype(BF16)

    def project(part, carry):
        weight = mats_ref[part, :, pair : pair + width]
        mixed_grad_ref[part] = dot(mid_low, weight, NN).astype(BF16)
        mats_grad_ref[part, :, pair : pair + width] = dot(
            mid_flip, mixed_ref[part], NN
        ).astype(BF16)
        return carry

    lax.fori_loop(0, parts, project, 0)


def token_back(grad, mid, mixed, mats, down, gain):
    pair = mats.shape[2] - mixed.shape[2]
    return pl.pallas_call(
        functools.partial(token_back_kernel, pair),
        out_shape=(
            jax.ShapeDtypeStruct(mats.shape, BF16),
            jax.ShapeDtypeStruct(down.shape, BF16),
            jax.ShapeDtypeStruct(mixed.shape, BF16),
            jax.ShapeDtypeStruct(mid.shape, F32),
            jax.ShapeDtypeStruct((1, mid.shape[1]), F32),
        ),
        scratch_shapes=[pltpu.VMEM(mid.shape, F32)],
        compiler_params=pltpu.CompilerParams(vmem_limit_bytes=VMEM_BYTES),
        name="token_back",
    )(grad, mid, mixed, mats, down, gain)


def frequencies(theta_base, half_dim):
    return theta_base ** (-(jnp.arange(half_dim, dtype=F32) * 2.0) / (2.0 * half_dim))


def sequences(seq_lengths, rows):
    seq_ends = jnp.cumsum(seq_lengths)
    positions = jnp.arange(rows, dtype=jnp.int32)
    seq_of = jnp.sum((positions[:, None] >= seq_ends[None, :]).astype(jnp.int32), axis=1)
    matches = jnp.arange(seq_lengths.shape[0], dtype=jnp.int32)[None, :] == seq_of[:, None]
    last = jnp.sum(jnp.where(matches, seq_ends[None, :], 0), axis=1)
    first = jnp.sum(jnp.where(matches, (seq_ends - seq_lengths)[None, :], 0), axis=1)
    return first[None], last[None], positions[None]


def body(
    tokens, lengths, qkv_weight, out_weight, gate_up_weight, down_weight, gains, out_cotangent
):
    core = lax.axis_index("pipe")
    model = tokens.shape[-1]
    local_rows = tokens.shape[2]
    rows = 4 * local_rows
    shard_rows = qkv_weight.shape[1]
    width = qkv_weight.shape[3]
    pair = 2 * gate_up_weight.shape[3]

    stream = take(tokens[0], core)
    cotangent = take(out_cotangent[0], core)
    first, last, positions = sequences(take(lengths[0], core), rows)
    bounds = (
        (jnp.maximum(first, positions - WINDOW // 2), jnp.minimum(last, positions + WINDOW // 2 + 1)),
        (first, last),
    )
    tables = []
    for base in (10000.0, 160000.0):
        turns = frequencies(base, HEAD_DIM // 2)[:, None] * (positions - first).astype(F32)
        tables.append((jnp.cos(turns), jnp.sin(turns)))

    other_gains = swap_cores(gains[0])
    gain_rows = (
        jnp.where(core == 0, gains[0], other_gains)[None],
        jnp.where(core == 0, other_gains, gains[0])[None],
    )

    qkv_halves = layer_halves(qkv_weight[0].reshape(shard_rows, 3 * width))
    mats_halves = layer_halves(
        jnp.concatenate([gate_up_weight[0].reshape(shard_rows, pair), out_weight[0].T], 1)
    )
    down_halves = layer_halves(down_weight[0].T)

    normed = (norm_parts(stream.astype(F32))[0] * gain_rows[0][:, :model]).astype(BF16)
    layer_in = stream
    saved = []
    for layer in (0, 1):
        qkv = whole_dp(qkv_halves[layer])
        normed_full = gather_tensor(normed).reshape(rows, model)
        mats = whole_all(mats_halves[layer])
        down = whole_all(down_halves[layer])
        projected = dot(qkv, normed_full, ((0,), (1,)))
        mixed, queries, keys, values, mass = attend(
            projected, *tables[layer], *bounds[layer], layer == 0
        )
        mixed = swap_tensor(mixed.reshape(4, local_rows, width))
        mid, layer_out, normed = token_forward(
            mixed, layer_in, mats, down, gain_rows[layer][:, model:], gain_rows[1][:, :model]
        )
        saved.append((layer_in, qkv, mats, down, normed_full, queries, keys, values, mass, mixed, mid))
        layer_in = layer_out
        if layer == 0:
            first_out = layer_out
    second_out = layer_in

    grad = cotangent
    reduced = [None, None]
    gain_grads = [None, None]
    input_grads = [None, None]
    for layer in (1, 0):
        stream, qkv, mats, down, normed_full, queries, keys, values, mass, mixed, mid = saved[layer]
        mats_grad, down_grad, mixed_grad, grad_mid, gain_mlp = token_back(
            grad, mid, mixed, mats, down, gain_rows[layer][:, model:]
        )
        grad_full = swap_tensor(mixed_grad).reshape(rows, width)
        grad_projected = attend_back(
            queries, keys, values, mass, grad_full, *tables[layer], *bounds[layer], layer == 0
        )
        qkv_grad = dot(normed_full, grad_projected, ((0,), (1,))).astype(BF16)
        partial_in = dot(grad_projected, qkv, ((0,), (1,))).astype(BF16)
        grad_normed = scatter_tensor(partial_in.reshape(4, local_rows, model))
        unit, scale = norm_parts(stream.astype(F32))
        gain_attn = jnp.sum(grad_normed * unit, axis=0, keepdims=True)
        grad_in = grad_mid + norm_back(grad_normed, unit, scale, gain_rows[layer][:, :model])
        gain_grads[layer] = jnp.concatenate([gain_attn, gain_mlp], 1)
        reduced[layer] = (reduce_all(mats_grad), reduce_all(down_grad), reduce_dp(qkv_grad))
        if layer == 1:
            grad = grad_in.astype(BF16)
            grad_in = grad.astype(F32)
        input_grads[layer] = grad_in

    mats_grad, down_grad, qkv_grad = (own_layer(one, two) for one, two in zip(*reduced))
    n = lax.axis_size("dp")
    gain_mine = jnp.where(core == 0, gain_grads[0], gain_grads[1])
    gain_other = swap_cores(jnp.where(core == 0, gain_grads[1], gain_grads[0]))
    gain_blocks = (gain_mine + gain_other).reshape(n, 4, -1)
    gain_blocks = jnp.moveaxis(gain_blocks, 1, 0)
    gain_part = scatter_dp(jnp.sum(swap_tensor(gain_blocks), axis=0), F32)

    activations = join_halves(
        jnp.where(core == 0, first_out, second_out),
        swap_cores(jnp.where(core == 0, second_out, first_out)),
        0,
    )
    grads_in = join_halves(
        jnp.where(core == 0, input_grads[0], input_grads[1]),
        swap_cores(jnp.where(core == 0, input_grads[1], input_grads[0])),
        0,
    )
    return (
        activations[None, None],
        grads_in[None, None],
        qkv_grad.reshape(qkv_weight.shape),
        mats_grad[:, pair:].T[None],
        mats_grad[:, :pair].reshape(gate_up_weight.shape),
        down_grad.T[None],
        gain_part[None],
    )


def solution(mesh):
    return jax.shard_map(
        body,
        mesh=mesh,
        in_specs=(
            P("dp", None, "tensor", None),
            P("dp", None, None),
            P("pipe", "dp", None, "tensor"),
            P("pipe", "tensor", "dp"),
            P("pipe", "dp", None, "tensor"),
            P("pipe", "tensor", "dp"),
            P("pipe", None),
            P("dp", None, "tensor", None),
        ),
        out_specs=(
            P("pipe", "dp", None, "tensor", None),
            P("pipe", "dp", None, "tensor", None),
            P("pipe", "dp", None, "tensor"),
            P("pipe", "tensor", "dp"),
            P("pipe", "dp", None, "tensor"),
            P("pipe", "tensor", "dp"),
            P("pipe", ("dp", "tensor")),
        ),
        check_vma=False,
    )
```

time: 2030 us -> 596 us (0.29)
  blocking collectives: 612 us -> 0 us
  matrix products: 321 us -> 14.3 us
  local copies, waits for them, and re-layouts: 353 us -> 75.6 us
  waiting for transfers between devices: 413 us -> 212 us
  other arithmetic: 229 us -> 50.1 us
  starting transfers between devices: 13.3 us -> 126 us
  Pallas kernels: 0 us -> 108 us
  loops' own time: 50.8 us -> 0 us
    all_gather x24 -> x0, blocking collectives: 572 us -> none  [the longest x6 172 us: fetch_weights(): lax.all_gather(qkv_weight, 'dp', axis=1, tiled=True)]
    reduce_scatter x18 -> x0, waiting for transfers between devices: 396 us -> none  [the longest x6 193 us: back_rows(): lax.psum_scatter(jnp.einsum('sf,df->sd', grad_flat, weight_flat, preferre...]
    dot_general x162 -> x6, matrix products: 312 us -> 14.3 us  [dot(): lax.dot_general(left, right, (dims, ((), ())), preferred_element_type=F32)]
    ppermute x6 -> x124, waiting for transfers between devices: 0.02 us -> 212 us  [the longest x63 120 us: to_mate(): return lax.ppermute(block, 'tensor', [(i, i ^ bit) for i in range(size)])]
    ppermute x6 -> x124, starting transfers between devices: 11.9 us -> 126 us  [the longest x63 64.6 us: to_mate(): return lax.ppermute(block, 'tensor', [(i, i ^ bit) for i in range(size)])]
    pallas_call x0 -> x8, Pallas kernels: none -> 108 us  [the longest x2 36.9 us: token_back(): pl.pallas_call(functools.partial(token_back_kernel, pair), out_shape=(jax...]
    while x538 -> x0, local copies, waits for them, and re-layouts: 101 us -> none
    squeeze x69 -> x10, local copies, waits for them, and re-layouts: 78.5 us -> 7.75 us  [the longest x4 6.03 us: half_sums(): other = lax.dynamic_index_in_dim(split, 1 - core, axis, keepdims=False)]
  transfers between devices with their start and end apart: 42 -> 124, of which waited for: 18 -> 60; matrix products, arithmetic and copies ran while one was open for 26% -> 21% of each run, Pallas kernels for 0% -> 11%
where the time goes in v1:
time: 596 us; the launch traced here: 589 us
  waiting for transfers between devices  212 us (36%)
  starting transfers between devices  126 us (21%)
  Pallas kernels  108 us (18%)
  local copies, waits for them, and re-layouts  75.6 us (13%)
  other arithmetic  50.1 us (8%)
  matrix products  14.3 us (2%)
    ppermute x63, waiting for transfers between devices, to_mate(): return lax.ppermute(block, 'tensor', [(i, i ^ bit) for i in range(size)])  120 us
    ppermute x18, waiting for transfers between devices, gather_dp(): out = put(out, lax.ppermute(block, 'dp', route), (me - step) % size)  67.1 us
    ppermute x63, starting transfers between devices, to_mate(): return lax.ppermute(block, 'tensor', [(i, i ^ bit) for i in range(size)])  64.6 us
    pallas_call x2, Pallas kernels, token_back(): pl.pallas_call(functools.partial(token_back_kernel, pair), out_shape=(jax...  36.9 us
    ppermute x21, starting transfers between devices, scatter_dp(): total = total + lax.ppermute(sent, 'dp', route).astype(F32)  35.6 us
    pallas_call x2, Pallas kernels, attend_back(): pl.pallas_call(functools.partial(attend_back_kernel, span), out_shape=jax...  27.2 us
    pallas_call x2, Pallas kernels, attend(): pl.pallas_call(functools.partial(attend_kernel, span), out_shape=(jax.Sha...  24.9 us
    ppermute x21, waiting for transfers between devices, scatter_dp(): total = total + lax.ppermute(sent, 'dp', route).astype(F32)  24.4 us
  transfers between devices with their start and end apart: 124, of which 60 were waited for; matrix products, arithmetic and copies ran while one was open for 21% of the time, Pallas kernels for 11%

profile of v1, /device:TPU:0, one launch (start us, length us, event | category | flops | bytes accessed | tf_op | source)
XLA Modules:
  0.0 589.1 jit_solution(8890007909878710895)
XLA Ops:
  16.4 3.1 collective-permute-start.23
  28.2 3.1 collective-permute-start.52
  42.2 6.7 %collective-permute-done.1 = bf16[96,576]{1,0:T(8,128)(2,1)S(1)} collective-permute-done((bf16[96,576]{1,0:T(8,128)(2,1)S(1)}, bf16[96,576]{1,0:T(8,128)(2,1)S(1)}, u32[]{:S(2)}, u32[]{:S(2)}) %collective-permute-start.1) | collective-permute-done | bytes 110624 | tf_op jit(solution)/shard_map/ppermute | solution.py:83
  48.9 5.9 collective-permute-done.2
  54.8 4.9 collective-permute-done.3
  59.7 6.7 %collective-permute-done.31 = bf16[96,576]{1,0:T(8,128)(2,1)S(1)} collective-permute-done((bf16[96,576]{1,0:T(8,128)(2,1)S(1)}, bf16[96,576]{1,0:T(8,128)(2,1)S(1)}, u32[]{:S(2)}, u32[]{:S(2)}) %collective-permute-start.31) | collective-permute-done | bytes 110624 | tf_op jit(solution)/shard_map/ppermute | solution.py:83
  66.5 6.5 %collective-permute-done.32 = bf16[96,576]{1,0:T(8,128)(2,1)S(1)} collective-permute-done((bf16[96,576]{1,0:T(8,128)(2,1)S(1)}, bf16[96,576]{1,0:T(8,128)(2,1)S(1)}, u32[]{:S(2)}, u32[]{:S(2)}) %collective-permute-start.32) | collective-permute-done | bytes 110624 | tf_op jit(solution)/shard_map/ppermute | solution.py:83
  79.6 6.7 %collective-permute-done.42 = bf16[96,768]{1,0:T(8,128)(2,1)S(1)} collective-permute-done((bf16[96,768]{1,0:T(8,128)(2,1)S(1)}, bf16[96,768]{1,0:T(8,128)(2,1)S(1)}, u32[]{:S(2)}, u32[]{:S(2)}) %collective-permute-start.42) | collective-permute-done | bytes 147488 | tf_op jit(solution)/shard_map/ppermute | solution.py:83
  86.7 6.6 %collective-permute-done.43 = bf16[96,768]{1,0:T(8,128)(2,1)S(1)} collective-permute-done((bf16[96,768]{1,0:T(8,128)(2,1)S(1)}, bf16[96,768]{1,0:T(8,128)(2,1)S(1)}, u32[]{:S(2)}, u32[]{:S(2)}) %collective-permute-start.43) | collective-permute-done | bytes 147488 | tf_op jit(solution)/shard_map/ppermute | solution.py:83
  93.3 4.5 collective-permute-start.44
  103.1 5.6 collective-permute-done.14
  108.8 6.0 %collective-permute-done.15 = bf16[96,768]{1,0:T(8,128)(2,1)S(1)} collective-permute-done((bf16[96,768]{1,0:T(8,128)(2,1)S(1)}, bf16[96,768]{1,0:T(8,128)(2,1)S(1)}, u32[]{:S(2)}, u32[]{:S(2)}) %collective-permute-start.15) | collective-permute-done | bytes 147488 | tf_op jit(solution)/shard_map/ppermute | solution.py:83
  122.7 3.8 collective-permute-start.54
  134.3 3.7 collective-permute-done.29
  140.5 4.3 collective-permute-done.56
  153.2 17.9 %collective-permute-done.8 = bf16[160,768]{1,0:T(8,128)(2,1)S(1)} collective-permute-done((bf16[160,768]{1,0:T(8,128)(2,1)S(1)}, bf16[160,768]{1,0:T(8,128)(2,1)S(1)}, u32[]{:S(2)}, u32[]{:S(2)}) %collective-permute-start.8) | collective-permute-done | bytes 245792 | tf_op jit(solution)/shard_map/ppermute | solution.py:25
  173.3 4.0 collective-permute-done.9
  182.4 5.6 collective-permute-done.19
  197.1 3.2 fusion.104.proj_ref
  200.3 7.9 %attend_local.1 = (bf16[1280,192]{1,0:T(8,128)(2,1)S(1)}, bf16[192,1280]{1,0:T(8,128)(2,1)S(1)}, bf16[192,1280]{1,0:T(8,128)(2,1)S(1)}, bf16[192,1280]{1,0:T(8,128)(2,1)S(1)}, f32[8,1280]{1,0:T(8,128)S(1)}) custom-call(f32[576,1280]{1,0:T(8,128)S(1)} %fusion.104.proj_ref, f32[32,1280]{1,0:T(8,128)S(1)} %get-tuple-element.208.cos_ref, ...), custom_call_target="tpu_custom_call" | custom-call | tf_op jit(solution)/shard_map/attend_local/pallas_call | solution.py:250
  210.6 4.5 collective-permute-done.10
  215.4 5.5 collective-permute-done.11
  221.5 5.6 collective-permute-done.12
  231.0 6.5 %maximum_select_fusion = bf16[4,4,2,96,768]{4,3,2,1,0:T(8,128)(2,1)} fusion(bf16[4,4,1,96,768]{4,3,2,1,0:T(8,128)(2,1)S(1)} %bitcast.585, bf16[4,4,1,96,768]{4,3,2,1,0:T(8,128)(2,1)} %bitcast.34, pred[]{:T(512)S(6)} %eq.86), kind=kLoop, calls=%fused_computation | loop fusion | flops 7077888 | bytes 9437185 | tf_op jit(solution)/shard_map/jit(_where)/select_n | solution.py:105
  237.4 9.1 %token_forward.2 = (f32[320,768]{1,0:T(8,128)S(1)}, bf16[320,768]{1,0:T(8,128)(2,1)S(1)}, bf16[320,768]{1,0:T(8,128)(2,1)S(1)}) custom-call(bf16[4,320,192]{2,1,0:T(8,128)(2,1)S(1)} %bitcast_dynamic-update-slice_fusion.26.mixed_ref, bf16[320,768]{1,0:T(8,128)(2,1)S(1)} %get-tuple-element.107.in_ref, bf16[4,768,768]{2,1,0:T(8,128)(2,1)} %bitcast.555, ...), custom_call_target="tpu_custom_call" | custom-call | tf_op jit(solution)/shard_map/token_forward/pallas_call | solution.py:376
  248.0 3.1 maximum_select_fusion.1
  254.2 3.9 collective-permute-done.36
  259.9 4.4 collective-permute-done.37
  267.4 17.1 %attend_global.1 = (bf16[1280,192]{1,0:T(8,128)(2,1)S(1)}, bf16[192,1280]{1,0:T(8,128)(2,1)S(1)}, bf16[192,1280]{1,0:T(8,128)(2,1)S(1)}, bf16[192,1280]{1,0:T(8,128)(2,1)S(1)}, f32[8,1280]{1,0:T(8,128)S(1)}) custom-call(f32[576,1280]{1,0:T(8,128)S(1)} %fusion.105.proj_ref, f32[32,1280]{1,0:T(8,128)S(1)} %copy-done.12, f32[32,1280]{1,0:T(8,128)S(1)} %copy-done.11, ...), custom_call_target="tpu_custom_call" | custom-call | tf_op jit(solution)/shard_map/attend_global/pallas_call | solution.py:250
  292.6 10.0 %token_forward.3 = (f32[320,768]{1,0:T(8,128)S(1)}, bf16[320,768]{1,0:T(8,128)(2,1)S(1)}, bf16[320,768]{1,0:T(8,128)(2,1)}) custom-call(bf16[4,320,192]{2,1,0:T(8,128)(2,1)S(1)} %bitcast_dynamic-update-slice_fusion.23.mixed_ref, bf16[320,768]{1,0:T(8,128)(2,1)S(1)} %get-tuple-element.33.in_ref, bf16[4,768,768]{2,1,0:T(8,128)(2,1)} %bitcast.557, ...), custom_call_target="tpu_custom_call" | custom-call | tf_op jit(solution)/shard_map/token_forward/pallas_call | solution.py:376
  302.6 18.3 %token_back.2 = (bf16[4,768,768]{2,1,0:T(8,128)(2,1)}, bf16[4,768,288]{2,1,0:T(8,128)(2,1)S(1)}, bf16[4,320,192]{2,1,0:T(8,128)(2,1)S(1)}, f32[320,768]{1,0:T(8,128)S(1)}, f32[1,768]{1,0:T(1,128)S(1)}) custom-call(bf16[320,768]{1,0:T(8,128)(2,1)S(1)} %copy-done.8, f32[320,768]{1,0:T(8,128)S(1)} %get-tuple-element.37.mid_ref, ...), custom_call_target="tpu_custom_call" | custom-call | tf_op jit(solution)/shard_map/token_back/pallas_call | solution.py:440
  326.9 3.3 dynamic-slice_bitcast_fusion
  331.2 18.4 %attend_back_global.1 = bf16[576,1280]{1,0:T(8,128)(2,1)S(1)} custom-call(bf16[192,1280]{1,0:T(8,128)(2,1)S(1)} %get-tuple-element.39.queries_ref, bf16[192,1280]{1,0:T(8,128)(2,1)S(1)} %get-tuple-element.40.keys_ref, bf16[192,1280]{1,0:T(8,128)(2,1)S(1)} %get-tuple-element.41.values_ref, f32[8,1280]{1,0:T(8,128)S(1)} %get-tuple-element.42.mass_ref, ...), custom_call_target="tpu_custom_call" | custom-call | tf_op jit(solution)/shard_map/attend_back_global/pallas_call | solution.py:325
  370.2 4.3 collective-permute-start.80
  379.8 18.6 %token_back.3 = (bf16[4,768,768]{2,1,0:T(8,128)(2,1)}, bf16[4,768,288]{2,1,0:T(8,128)(2,1)S(1)}, bf16[4,320,192]{2,1,0:T(8,128)(2,1)S(1)}, f32[320,768]{1,0:T(8,128)S(1)}, f32[1,768]{1,0:T(1,128)S(1)}) custom-call(bf16[320,768]{1,0:T(8,128)(2,1)S(1)} %fusion.21.grad_ref, f32[320,768]{1,0:T(8,128)S(1)} %copy-done.14, bf16[4,320,192]{2,1,0:T(8,128)(2,1)S(1)} %copy-done.5, ...), custom_call_target="tpu_custom_call" | custom-call | tf_op jit(solution)/shard_map/token_back/pallas_call | solution.py:440
  425.8 8.8 %attend_back_local.1 = bf16[576,1280]{1,0:T(8,128)(2,1)S(1)} custom-call(bf16[192,1280]{1,0:T(8,128)(2,1)S(1)} %copy-done.16, bf16[192,1280]{1,0:T(8,128)(2,1)S(1)} %copy-done.18, bf16[192,1280]{1,0:T(8,128)(2,1)S(1)} %copy-done.20, f32[8,1280]{1,0:T(8,128)S(1)} %copy-done.22, bf16[1280,192]{1,0:T(8,128)(2,1)S(1)} %bitcast.549, ...), custom_call_target="tpu_custom_call" | custom-call | tf_op jit(solution)/shard_map/attend_back_local/pallas_call | solution.py:325
  439.6 3.8 convolution_convert_fusion.3
  449.8 4.6 collective-permute-start.76
  454.3 3.8 collective-permute-done.75
  458.1 3.8 collective-permute-done.76
  496.8 4.9 collective-permute-done.110
  503.8 4.7 collective-permute-done.102
  515.5 5.0 collective-permute-done.92
  530.3 10.0 %collective-permute-done.93 = bf16[4,96,768]{2,1,0:T(8,128)(2,1)S(1)} collective-permute-done((bf16[4,96,768]{2,1,0:T(8,128)(2,1)S(1)}, bf16[4,96,768]{2,1,0:T(8,128)(2,1)S(1)}, u32[]{:S(2)}, u32[]{:S(2)}) %collective-permute-start.93) | collective-permute-done | bytes 589856 | tf_op jit(solution)/shard_map/ppermute | solution.py:25
  557.9 6.4 %collective-permute-done.106 = bf16[96,288]{0,1:T(8,128)(2,1)S(1)} collective-permute-done((bf16[96,288]{0,1:T(8,128)(2,1)S(1)}, bf16[96,288]{0,1:T(8,128)(2,1)S(1)}, u32[]{:S(2)}, u32[]{:S(2)}) %collective-permute-start.106) | collective-permute-done | bytes 55328 | tf_op jit(solution)/shard_map/ppermute | solution.py:98
  567.6 3.3 collective-permute-start.90
  571.7 4.0 collective-permute-done.98
  576.2 3.3 collective-permute-done.89
  (562 shorter events, 270.5 us)
Async XLA Ops:
  3.8 37.4 %collective-permute-start.13 = (bf16[96,768]{1,0:T(8,128)(2,1)}, bf16[96,768]{1,0:T(8,128)(2,1)S(1)}, u32[]{:S(2)}, u32[]{:S(2)}) collective-permute-start(bf16[96,768]{1,0:T(8,128)(2,1)} %fusion.66), channel_id=1, source_target_pairs={{0,4},{4,0},{1,5},{5,1},{2,6},{6,2},{3,7},{7,3},{8,12},{12,8},{9,1... | collective-permute-start | bytes 442376 | tf_op jit(solution)/shard_map/ppermute | solution.py:20
  5.2 11.0 %collective-permute-start.22 = (bf16[96,288]{0,1:T(8,128)(2,1)S(1)}, bf16[96,288]{0,1:T(8,128)(2,1)S(1)}, u32[]{:S(2)}, u32[]{:S(2)}) collective-permute-start(bf16[96,288]{0,1:T(8,128)(2,1)S(1)} %dynamic-slice_bitcast_fusion.54), channel_id=1, source_target_pairs={{0,4},{4,0},{1,5},{5,1},{2,6},{6,2},{3,7},{7,3},{8,12},{12,8},{9,1... | collective-permute-start | bytes 165896 | tf_op jit(solution)/shard_map/ppermute | solution.py:20
  8.7 30.8 %collective-permute-start = (bf16[96,576]{1,0:T(8,128)(2,1)}, bf16[96,576]{1,0:T(8,128)(2,1)}, u32[]{:S(2)}, u32[]{:S(2)}) collective-permute-start(bf16[96,576]{1,0:T(8,128)(2,1)} %copy.237), channel_id=1, source_target_pairs={{0,4},{4,0},{1,5},{5,1},{2,6},{6,2},{3,7},{7,3},{8,12},{12,8},{9,1... | collective-permute-start | bytes 331784 | tf_op jit(solution)/shard_map/ppermute | solution.py:20
  31.7 116.5 %collective-permute-start.6 = (bf16[320,768]{1,0:T(8,128)(2,1)}, bf16[320,768]{1,0:T(8,128)(2,1)}, u32[]{:S(2)}, u32[]{:S(2)}) collective-permute-start(bf16[320,768]{1,0:T(8,128)(2,1)} %fusion.24), channel_id=1, source_target_pairs={{0,1},{1,0},{2,3},{3,2},{4,5},{5,4},{6,7},{7,6},{8,9},{9,8},{10,11... | collective-permute-start | bytes 1474568 | tf_op jit(solution)/shard_map/ppermute | solution.py:25
  34.3 110.6 %collective-permute-start.7 = (bf16[320,768]{1,0:T(8,128)(2,1)}, bf16[320,768]{1,0:T(8,128)(2,1)}, u32[]{:S(2)}, u32[]{:S(2)}) collective-permute-start(bf16[320,768]{1,0:T(8,128)(2,1)} %fusion.24), channel_id=1, source_target_pairs={{0,2},{1,3},{2,0},{3,1},{4,6},{5,7},{6,4},{7,5},{8,10},{9,11},{10,... | collective-permute-start | bytes 1474568 | tf_op jit(solution)/shard_map/ppermute | solution.py:25
  36.8 89.7 %collective-permute-start.26 = (bf16[4,96,288]{2,1,0:T(8,128)(2,1)S(1)}, bf16[4,96,288]{2,1,0:T(8,128)(2,1)}, u32[]{:S(2)}, u32[]{:S(2)}) collective-permute-start(bf16[4,96,288]{2,1,0:T(8,128)(2,1)S(1)} %constant_dynamic-update-slice_fusion.8), channel_id=1, source_target_pairs={{0,1},{1,0},{2,3},{3,2},{4,5},{5,4},{6,7},{7,6},{8,9},{9,8},{10,11... | collective-permute-start | bytes 663560 | tf_op jit(solution)/shard_map/ppermute | solution.py:25
  39.5 83.2 %collective-permute-start.27 = (bf16[4,96,288]{2,1,0:T(8,128)(2,1)S(1)}, bf16[4,96,288]{2,1,0:T(8,128)(2,1)S(1)}, u32[]{:S(2)}, u32[]{:S(2)}) collective-permute-start(bf16[4,96,288]{2,1,0:T(8,128)(2,1)S(1)} %constant_dynamic-update-slice_fusion.8), channel_id=1, source_target_pairs={{0,2},{1,3},{2,0},{3,1},{4,6},{5,7},{6,4},{7,5},{8,10},{9,11},{10,... | collective-permute-start | bytes 663560 | tf_op jit(solution)/shard_map/ppermute | solution.py:25
  126.5 26.6 %collective-permute-start.4 = (bf16[4,96,576]{2,1,0:T(8,128)(2,1)S(1)}, bf16[4,96,576]{2,1,0:T(8,128)(2,1)S(1)}, u32[]{:S(2)}, u32[]{:S(2)}) collective-permute-start(bf16[4,96,576]{2,1,0:T(8,128)(2,1)S(1)} %bitcast_dynamic-update-slice_fusion.41), channel_id=1, source_target_pairs={{0,4},{4,0},{1,5},{5,1},{2,6},{6,2},{3,7},{7,3},{8,12},{12,8},{9,1... | collective-permute-start | bytes 1327112 | tf_op jit(solution)/shard_map/ppermute | solution.py:20
  140.4 39.9 %collective-permute-start.45 = (bf16[4,96,768]{2,1,0:T(8,128)(2,1)S(1)}, bf16[4,96,768]{2,1,0:T(8,128)(2,1)S(1)}, u32[]{:S(2)}, u32[]{:S(2)}) collective-permute-start(bf16[4,96,768]{2,1,0:T(8,128)(2,1)S(1)} %bitcast_dynamic-update-slice_fusion.29), channel_id=1, source_target_pairs={{0,1},{1,0},{2,3},{3,2},{4,5},{5,4},{6,7},{7,6},{8,9},{9,8},{10,11... | collective-permute-start | bytes 1769480 | tf_op jit(solution)/shard_map/ppermute | solution.py:25
  144.7 34.4 %collective-permute-start.17 = (bf16[4,96,768]{2,1,0:T(8,128)(2,1)S(1)}, bf16[4,96,768]{2,1,0:T(8,128)(2,1)S(1)}, u32[]{:S(2)}, u32[]{:S(2)}) collective-permute-start(bf16[4,96,768]{2,1,0:T(8,128)(2,1)S(1)} %bitcast_dynamic-update-slice_fusion.33), channel_id=1, source_target_pairs={{0,1},{1,0},{2,3},{3,2},{4,5},{5,4},{6,7},{7,6},{8,9},{9,8},{10,11... | collective-permute-start | bytes 1769480 | tf_op jit(solution)/shard_map/ppermute | solution.py:25
  144.8 33.3 %collective-permute-start.18 = (bf16[4,96,768]{2,1,0:T(8,128)(2,1)S(1)}, bf16[4,96,768]{2,1,0:T(8,128)(2,1)S(1)}, u32[]{:S(2)}, u32[]{:S(2)}) collective-permute-start(bf16[4,96,768]{2,1,0:T(8,128)(2,1)S(1)} %bitcast_dynamic-update-slice_fusion.33), channel_id=1, source_target_pairs={{0,2},{1,3},{2,0},{3,1},{4,6},{5,7},{6,4},{7,5},{8,10},{9,11},{10,... | collective-permute-start | bytes 1769480 | tf_op jit(solution)/shard_map/ppermute | solution.py:25
  148.2 22.9 %collective-permute-start.8 = (bf16[160,768]{1,0:T(8,128)(2,1)S(1)}, bf16[160,768]{1,0:T(8,128)(2,1)S(1)}, u32[]{:S(2)}, u32[]{:S(2)}) collective-permute-start(bf16[160,768]{1,0:T(8,128)(2,1)S(1)} %slice.438), channel_id=1, source_target_pairs={{0,1},{1,0},{2,3},{3,2},{4,5},{5,4},{6,7},{7,6},{8,9},{9,8},{10,11... | collective-permute-start | bytes 737288 | tf_op jit(solution)/shard_map/ppermute | solution.py:25
  153.1 27.0 %collective-permute-start.46 = (bf16[4,96,768]{2,1,0:T(8,128)(2,1)S(1)}, bf16[4,96,768]{2,1,0:T(8,128)(2,1)S(1)}, u32[]{:S(2)}, u32[]{:S(2)}) collective-permute-start(bf16[4,96,768]{2,1,0:T(8,128)(2,1)S(1)} %bitcast_dynamic-update-slice_fusion.29), channel_id=1, source_target_pairs={{0,2},{1,3},{2,0},{3,1},{4,6},{5,7},{6,4},{7,5},{8,10},{9,11},{10,... | collective-permute-start | bytes 1769480 | tf_op jit(solution)/shard_map/ppermute | solution.py:25
  177.3 31.1 %collective-permute-start.34 = (bf16[4,96,576]{2,1,0:T(8,128)(2,1)S(1)}, bf16[4,96,576]{2,1,0:T(8,128)(2,1)S(1)}, u32[]{:S(2)}, u32[]{:S(2)}) collective-permute-start(bf16[4,96,576]{2,1,0:T(8,128)(2,1)S(1)} %bitcast_dynamic-update-slice_fusion.37), channel_id=1, source_target_pairs={{0,4},{4,0},{1,5},{5,1},{2,6},{6,2},{3,7},{7,3},{8,12},{12,8},{9,1... | collective-permute-start | bytes 1327112 | tf_op jit(solution)/shard_map/ppermute | solution.py:20
  180.1 50.2 %collective-permute-start.30 = (bf16[4,4,96,288]{3,2,1,0:T(8,128)(2,1)S(1)}, bf16[4,4,96,288]{3,2,1,0:T(8,128)(2,1)S(1)}, u32[]{:S(2)}, u32[]{:S(2)}) collective-permute-start(bf16[4,4,96,288]{3,2,1,0:T(8,128)(2,1)S(1)} %fusion.52), channel_id=1, source_target_pairs={{0,4},{4,0},{1,5},{5,1},{2,6},{6,2},{3,7},{7,3},{8,12},{12,8},{9,1... | collective-permute-start | bytes 2654216 | tf_op jit(solution)/shard_map/ppermute | solution.py:20
  180.3 13.6 %collective-permute-start.47 = (bf16[2,96,768]{2,1,0:T(8,128)(2,1)S(1)}, bf16[2,96,768]{2,1,0:T(8,128)(2,1)S(1)}, u32[]{:S(2)}, u32[]{:S(2)}) collective-permute-start(bf16[2,96,768]{2,1,0:T(8,128)(2,1)S(1)} %slice.448), channel_id=1, source_target_pairs={{0,1},{1,0},{2,3},{3,2},{4,5},{5,4},{6,7},{7,6},{8,9},{9,8},{10,11... | collective-permute-start | bytes 884744 | tf_op jit(solution)/shard_map/ppermute | solution.py:25
  189.2 41.7 %collective-permute-start.21 = (bf16[4,4,96,768]{3,2,1,0:T(8,128)(2,1)}, bf16[4,4,96,768]{3,2,1,0:T(8,128)(2,1)S(1)}, u32[]{:S(2)}, u32[]{:S(2)}) collective-permute-start(bf16[4,4,96,768]{3,2,1,0:T(8,128)(2,1)} %fusion.37), channel_id=1, source_target_pairs={{0,4},{4,0},{1,5},{5,1},{2,6},{6,2},{3,7},{7,3},{8,12},{12,8},{9,1... | collective-permute-start | bytes 7077896 | tf_op jit(solution)/shard_map/ppermute | solution.py:20
  194.0 33.2 %collective-permute-start.57 = (bf16[4,4,96,288]{3,2,1,0:T(8,128)(2,1)S(1)}, bf16[4,4,96,288]{3,2,1,0:T(8,128)(2,1)}, u32[]{:S(2)}, u32[]{:S(2)}) collective-permute-start(bf16[4,4,96,288]{3,2,1,0:T(8,128)(2,1)S(1)} %fusion.53), channel_id=1, source_target_pairs={{0,4},{4,0},{1,5},{5,1},{2,6},{6,2},{3,7},{7,3},{8,12},{12,8},{9,1... | collective-permute-start | bytes 2654216 | tf_op jit(solution)/shard_map/ppermute | solution.py:20
  197.1 50.9 %collective-permute-start.49 = (bf16[4,4,96,768]{3,2,1,0:T(8,128)(2,1)}, bf16[4,4,96,768]{3,2,1,0:T(8,128)(2,1)S(1)}, u32[]{:S(2)}, u32[]{:S(2)}) collective-permute-start(bf16[4,4,96,768]{3,2,1,0:T(8,128)(2,1)} %fusion.38), channel_id=1, source_target_pairs={{0,4},{4,0},{1,5},{5,1},{2,6},{6,2},{3,7},{7,3},{8,12},{12,8},{9,1... | collective-permute-start | bytes 7077896 | tf_op jit(solution)/shard_map/ppermute | solution.py:20
  246.6 12.8 %collective-permute-start.35 = (bf16[320,768]{1,0:T(8,128)(2,1)S(1)}, bf16[320,768]{1,0:T(8,128)(2,1)S(1)}, u32[]{:S(2)}, u32[]{:S(2)}) collective-permute-start(bf16[320,768]{1,0:T(8,128)(2,1)S(1)} %get-tuple-element.34), channel_id=1, source_target_pairs={{0,1},{1,0},{2,3},{3,2},{4,5},{5,4},{6,7},{7,6},{8,9},{9,8},{10,11... | collective-permute-start | bytes 1474568 | tf_op jit(solution)/shard_map/ppermute | solution.py:25
  326.8 39.1 %collective-permute-start.58 = (bf16[320,768]{1,0:T(8,128)(2,1)}, bf16[320,768]{1,0:T(8,128)(2,1)}, u32[]{:S(2)}, u32[]{:S(2)}) collective-permute-start(bf16[320,768]{1,0:T(8,128)(2,1)} %get-tuple-element.171), channel_id=1, source_target_pairs={{0,4},{4,0},{1,5},{5,1},{2,6},{6,2},{3,7},{7,3},{8,12},{12,8},{9,1... | collective-permute-start | bytes 1474568 | tf_op jit(solution)/shard_map/ppermute | solution.py:20
  363.4 13.3 %collective-permute-start.63 = (bf16[320,768]{1,0:T(8,128)(2,1)S(1)}, bf16[320,768]{1,0:T(8,128)(2,1)S(1)}, u32[]{:S(2)}, u32[]{:S(2)}) collective-permute-start(bf16[320,768]{1,0:T(8,128)(2,1)S(1)} %pad_maximum_fusion.4), channel_id=1, source_target_pairs={{0,1},{1,0},{2,3},{3,2},{4,5},{5,4},{6,7},{7,6},{8,9},{9,8},{10,11... | collective-permute-start | bytes 1474568 | tf_op jit(solution)/shard_map/ppermute | solution.py:25
  364.8 13.0 %collective-permute-start.65 = (bf16[320,768]{1,0:T(8,128)(2,1)S(1)}, bf16[320,768]{1,0:T(8,128)(2,1)S(1)}, u32[]{:S(2)}, u32[]{:S(2)}) collective-permute-start(bf16[320,768]{1,0:T(8,128)(2,1)S(1)} %pad_maximum_fusion.5), channel_id=1, source_target_pairs={{0,2},{1,3},{2,0},{3,1},{4,6},{5,7},{6,4},{7,5},{8,10},{9,11},{10,... | collective-permute-start | bytes 1474568 | tf_op jit(solution)/shard_map/ppermute | solution.py:25
  370.2 79.5 %collective-permute-start.79 = (bf16[96,576]{1,0:T(8,128)(2,1)}, bf16[96,576]{1,0:T(8,128)(2,1)}, u32[]{:S(2)}, u32[]{:S(2)}) collective-permute-start(bf16[96,576]{1,0:T(8,128)(2,1)} %get-tuple-element.164), channel_id=1, source_target_pairs={{0,8},{8,16},{16,24},{24,0},{1,9},{9,17},{17,25},{25,1},{2,10},{10... | collective-permute-start | bytes 331784 | tf_op jit(solution)/shard_map/ppermute | solution.py:98
  370.2 79.6 %collective-permute-start.80 = (bf16[96,576]{1,0:T(8,128)(2,1)}, bf16[96,576]{1,0:T(8,128)(2,1)}, u32[]{:S(2)}, u32[]{:S(2)}) collective-permute-start(bf16[96,576]{1,0:T(8,128)(2,1)} %get-tuple-element.166), channel_id=1, source_target_pairs={{0,16},{8,24},{16,0},{24,8},{1,17},{9,25},{17,1},{25,9},{2,18},{10... | collective-permute-start | bytes 331784 | tf_op jit(solution)/shard_map/ppermute | solution.py:98
  374.5 79.8 %collective-permute-start.81 = (bf16[96,576]{1,0:T(8,128)(2,1)}, bf16[96,576]{1,0:T(8,128)(2,1)}, u32[]{:S(2)}, u32[]{:S(2)}) collective-permute-start(bf16[96,576]{1,0:T(8,128)(2,1)} %get-tuple-element.165), channel_id=1, source_target_pairs={{0,24},{8,0},{16,8},{24,16},{1,25},{9,1},{17,9},{25,17},{2,26},{10... | collective-permute-start | bytes 331784 | tf_op jit(solution)/shard_map/ppermute | solution.py:98
  399.2 17.2 %collective-permute-start.66 = (bf16[320,192]{1,0:T(8,128)(2,1)}, bf16[320,192]{1,0:T(8,128)(2,1)}, u32[]{:S(2)}, u32[]{:S(2)}) collective-permute-start(bf16[320,192]{1,0:T(8,128)(2,1)} %get-tuple-element.174), channel_id=1, source_target_pairs={{0,1},{1,0},{2,3},{3,2},{4,5},{5,4},{6,7},{7,6},{8,9},{9,8},{10,11... | collective-permute-start | bytes 368648 | tf_op jit(solution)/shard_map/ppermute | solution.py:25
  400.0 19.0 %collective-permute-start.67 = (bf16[320,192]{1,0:T(8,128)(2,1)S(1)}, bf16[320,192]{1,0:T(8,128)(2,1)}, u32[]{:S(2)}, u32[]{:S(2)}) collective-permute-start(bf16[320,192]{1,0:T(8,128)(2,1)S(1)} %get-tuple-element.173), channel_id=1, source_target_pairs={{0,2},{1,3},{2,0},{3,1},{4,6},{5,7},{6,4},{7,5},{8,10},{9,11},{10,... | collective-permute-start | bytes 368648 | tf_op jit(solution)/shard_map/ppermute | solution.py:25
  447.4 16.6 %collective-permute-start.70 = (bf16[320,768]{1,0:T(8,128)(2,1)S(1)}, bf16[320,768]{1,0:T(8,128)(2,1)S(1)}, u32[]{:S(2)}, u32[]{:S(2)}) collective-permute-start(bf16[320,768]{1,0:T(8,128)(2,1)S(1)} %pad_maximum_fusion.6), channel_id=1, source_target_pairs={{0,1},{1,0},{2,3},{3,2},{4,5},{5,4},{6,7},{7,6},{8,9},{9,8},{10,11... | collective-permute-start | bytes 1474568 | tf_op jit(solution)/shard_map/ppermute | solution.py:25
  448.3 15.8 %collective-permute-start.72 = (bf16[320,768]{1,0:T(8,128)(2,1)S(1)}, bf16[320,768]{1,0:T(8,128)(2,1)S(1)}, u32[]{:S(2)}, u32[]{:S(2)}) collective-permute-start(bf16[320,768]{1,0:T(8,128)(2,1)S(1)} %pad_maximum_fusion.7), channel_id=1, source_target_pairs={{0,2},{1,3},{2,0},{3,1},{4,6},{5,7},{6,4},{7,5},{8,10},{9,11},{10,... | collective-permute-start | bytes 1474568 | tf_op jit(solution)/shard_map/ppermute | solution.py:25
  449.8 12.2 %collective-permute-start.76 = (bf16[96,576]{1,0:T(8,128)(2,1)S(1)}, bf16[96,576]{1,0:T(8,128)(2,1)S(1)}, u32[]{:S(2)}, u32[]{:S(2)}) collective-permute-start(bf16[96,576]{1,0:T(8,128)(2,1)S(1)} %get-tuple-element.169), channel_id=1, source_target_pairs={{0,16},{8,24},{16,0},{24,8},{1,17},{9,25},{17,1},{25,9},{2,18},{10... | collective-permute-start | bytes 331784 | tf_op jit(solution)/shard_map/ppermute | solution.py:98
  458.1 23.4 %collective-permute-start.108 = (bf16[4,4,96,288]{2,3,1,0:T(8,128)(2,1)}, bf16[4,4,96,288]{2,3,1,0:T(8,128)(2,1)}, u32[]{:S(2)}, u32[]{:S(2)}) collective-permute-start(bf16[4,4,96,288]{2,3,1,0:T(8,128)(2,1)} %bitcast.194), channel_id=1, source_target_pairs={{0,4},{4,0},{1,5},{5,1},{2,6},{6,2},{3,7},{7,3},{8,12},{12,8},{9,1... | collective-permute-start | bytes 2654216 | tf_op jit(solution)/shard_map/ppermute | solution.py:20
  461.9 22.6 %collective-permute-start.100 = (bf16[4,4,96,288]{2,3,1,0:T(8,128)(2,1)}, bf16[4,4,96,288]{2,3,1,0:T(8,128)(2,1)}, u32[]{:S(2)}, u32[]{:S(2)}) collective-permute-start(bf16[4,4,96,288]{2,3,1,0:T(8,128)(2,1)} %bitcast.180), channel_id=1, source_target_pairs={{0,4},{4,0},{1,5},{5,1},{2,6},{6,2},{3,7},{7,3},{8,12},{12,8},{9,1... | collective-permute-start | bytes 2654216 | tf_op jit(solution)/shard_map/ppermute | solution.py:20
  479.5 30.1 %collective-permute-start.91 = (bf16[4,4,96,768]{3,2,1,0:T(8,128)(2,1)}, bf16[4,4,96,768]{3,2,1,0:T(8,128)(2,1)S(1)}, u32[]{:S(2)}, u32[]{:S(2)}) collective-permute-start(bf16[4,4,96,768]{3,2,1,0:T(8,128)(2,1)} %dynamic-slice_bitcast_fusion), channel_id=1, source_target_pairs={{0,4},{4,0},{1,5},{5,1},{2,6},{6,2},{3,7},{7,3},{8,12},{12,8},{9,1... | collective-permute-start | bytes 7077896 | tf_op jit(solution)/shard_map/ppermute | solution.py:20
  480.5 32.0 %collective-permute-start.83 = (bf16[4,4,96,768]{3,2,1,0:T(8,128)(2,1)}, bf16[4,4,96,768]{3,2,1,0:T(8,128)(2,1)S(1)}, u32[]{:S(2)}, u32[]{:S(2)}) collective-permute-start(bf16[4,4,96,768]{3,2,1,0:T(8,128)(2,1)} %dynamic-slice_bitcast_fusion.1), channel_id=1, source_target_pairs={{0,4},{4,0},{1,5},{5,1},{2,6},{6,2},{3,7},{7,3},{8,12},{12,8},{9,1... | collective-permute-start | bytes 7077896 | tf_op jit(solution)/shard_map/ppermute | solution.py:20
  480.5 103.4 %collective-permute-start.73 = (f32[320,768]{1,0:T(8,128)}, f32[320,768]{1,0:T(8,128)S(1)}, u32[]{:S(2)}, u32[]{:S(2)}) collective-permute-start(f32[320,768]{1,0:T(8,128)} %convert_select_fusion), channel_id=1, source_target_pairs={{0,4},{4,0},{1,5},{5,1},{2,6},{6,2},{3,7},{7,3},{8,12},{12,8},{9,1... | collective-permute-start | bytes 2949128 | tf_op jit(solution)/shard_map/ppermute | solution.py:20
  513.3 13.5 %collective-permute-start.84 = (bf16[2,96,768]{2,1,0:T(8,128)(2,1)S(1)}, bf16[2,96,768]{2,1,0:T(8,128)(2,1)S(1)}, u32[]{:S(2)}, u32[]{:S(2)}) collective-permute-start(bf16[2,96,768]{2,1,0:T(8,128)(2,1)S(1)} %get-tuple-element.127), channel_id=1, source_target_pairs={{0,2},{1,3},{2,0},{3,1},{4,6},{5,7},{6,4},{7,5},{8,10},{9,11},{10,... | collective-permute-start | bytes 884744 | tf_op jit(solution)/shard_map/ppermute | solution.py:25
  514.5 13.3 %collective-permute-start.86 = (bf16[2,96,768]{2,1,0:T(8,128)(2,1)S(1)}, bf16[2,96,768]{2,1,0:T(8,128)(2,1)S(1)}, u32[]{:S(2)}, u32[]{:S(2)}) collective-permute-start(bf16[2,96,768]{2,1,0:T(8,128)(2,1)S(1)} %get-tuple-element.129), channel_id=1, source_target_pairs={{0,1},{1,0},{2,3},{3,2},{4,5},{5,4},{6,7},{7,6},{8,9},{9,8},{10,11... | collective-permute-start | bytes 884744 | tf_op jit(solution)/shard_map/ppermute | solution.py:25
  521.6 18.7 %collective-permute-start.93 = (bf16[4,96,768]{2,1,0:T(8,128)(2,1)S(1)}, bf16[4,96,768]{2,1,0:T(8,128)(2,1)S(1)}, u32[]{:S(2)}, u32[]{:S(2)}) collective-permute-start(bf16[4,96,768]{2,1,0:T(8,128)(2,1)S(1)} %pad_maximum_fusion.2), channel_id=1, source_target_pairs={{0,1},{1,0},{2,3},{3,2},{4,5},{5,4},{6,7},{7,6},{8,9},{9,8},{10,11... | collective-permute-start | bytes 1769480 | tf_op jit(solution)/shard_map/ppermute | solution.py:25
  522.8 19.3 %collective-permute-start.95 = (bf16[4,96,768]{2,1,0:T(8,128)(2,1)S(1)}, bf16[4,96,768]{2,1,0:T(8,128)(2,1)S(1)}, u32[]{:S(2)}, u32[]{:S(2)}) collective-permute-start(bf16[4,96,768]{2,1,0:T(8,128)(2,1)S(1)} %pad_maximum_fusion.3), channel_id=1, source_target_pairs={{0,2},{1,3},{2,0},{3,1},{4,6},{5,7},{6,4},{7,5},{8,10},{9,11},{10,... | collective-permute-start | bytes 1769480 | tf_op jit(solution)/shard_map/ppermute | solution.py:25
  527.9 21.1 %collective-permute-start.85 = (bf16[4,96,768]{2,1,0:T(8,128)(2,1)S(1)}, bf16[4,96,768]{2,1,0:T(8,128)(2,1)S(1)}, u32[]{:S(2)}, u32[]{:S(2)}) collective-permute-start(bf16[4,96,768]{2,1,0:T(8,128)(2,1)S(1)} %pad_maximum_fusion), channel_id=1, source_target_pairs={{0,1},{1,0},{2,3},{3,2},{4,5},{5,4},{6,7},{7,6},{8,9},{9,8},{10,11... | collective-permute-start | bytes 1769480 | tf_op jit(solution)/shard_map/ppermute | solution.py:25
  529.1 22.6 %collective-permute-start.87 = (bf16[4,96,768]{2,1,0:T(8,128)(2,1)S(1)}, bf16[4,96,768]{2,1,0:T(8,128)(2,1)S(1)}, u32[]{:S(2)}, u32[]{:S(2)}) collective-permute-start(bf16[4,96,768]{2,1,0:T(8,128)(2,1)S(1)} %pad_maximum_fusion.1), channel_id=1, source_target_pairs={{0,2},{1,3},{2,0},{3,1},{4,6},{5,7},{6,4},{7,5},{8,10},{9,11},{10,... | collective-permute-start | bytes 1769480 | tf_op jit(solution)/shard_map/ppermute | solution.py:25
  549.0 18.0 %collective-permute-start.96 = (bf16[96,768]{1,0:T(8,128)(2,1)S(1)}, bf16[96,768]{1,0:T(8,128)(2,1)S(1)}, u32[]{:S(2)}, u32[]{:S(2)}) collective-permute-start(bf16[96,768]{1,0:T(8,128)(2,1)S(1)} %get-tuple-element.158), channel_id=1, source_target_pairs={{0,8},{8,16},{16,24},{24,0},{1,9},{9,17},{17,25},{25,1},{2,10},{10... | collective-permute-start | bytes 442376 | tf_op jit(solution)/shard_map/ppermute | solution.py:98
  551.7 15.9 %collective-permute-start.97 = (bf16[96,768]{1,0:T(8,128)(2,1)S(1)}, bf16[96,768]{1,0:T(8,128)(2,1)S(1)}, u32[]{:S(2)}, u32[]{:S(2)}) collective-permute-start(bf16[96,768]{1,0:T(8,128)(2,1)S(1)} %get-tuple-element.160), channel_id=1, source_target_pairs={{0,16},{8,24},{16,0},{24,8},{1,17},{9,25},{17,1},{25,9},{2,18},{10... | collective-permute-start | bytes 442376 | tf_op jit(solution)/shard_map/ppermute | solution.py:98
  555.5 11.5 %collective-permute-start.107 = (bf16[96,288]{0,1:T(8,128)(2,1)S(1)}, bf16[96,288]{0,1:T(8,128)(2,1)S(1)}, u32[]{:S(2)}, u32[]{:S(2)}) collective-permute-start(bf16[96,288]{0,1:T(8,128)(2,1)S(1)} %get-tuple-element.192), channel_id=1, source_target_pairs={{0,24},{8,0},{16,8},{24,16},{1,25},{9,1},{17,9},{25,17},{2,26},{10... | collective-permute-start | bytes 165896 | tf_op jit(solution)/shard_map/ppermute | solution.py:98
  564.2 11.4 %collective-permute-start.98 = (bf16[96,768]{1,0:T(8,128)(2,1)S(1)}, bf16[96,768]{1,0:T(8,128)(2,1)S(1)}, u32[]{:S(2)}, u32[]{:S(2)}) collective-permute-start(bf16[96,768]{1,0:T(8,128)(2,1)S(1)} %get-tuple-element.159), channel_id=1, source_target_pairs={{0,24},{8,0},{16,8},{24,16},{1,25},{9,1},{17,9},{25,17},{2,26},{10... | collective-permute-start | bytes 442376 | tf_op jit(solution)/shard_map/ppermute | solution.py:98
  567.0 12.4 %collective-permute-start.89 = (bf16[96,768]{1,0:T(8,128)(2,1)S(1)}, bf16[96,768]{1,0:T(8,128)(2,1)S(1)}, u32[]{:S(2)}, u32[]{:S(2)}) collective-permute-start(bf16[96,768]{1,0:T(8,128)(2,1)S(1)} %get-tuple-element.163), channel_id=1, source_target_pairs={{0,16},{8,24},{16,0},{24,8},{1,17},{9,25},{17,1},{25,9},{2,18},{10... | collective-permute-start | bytes 442376 | tf_op jit(solution)/shard_map/ppermute | solution.py:98
  567.6 11.9 %collective-permute-start.90 = (bf16[96,768]{1,0:T(8,128)(2,1)S(1)}, bf16[96,768]{1,0:T(8,128)(2,1)S(1)}, u32[]{:S(2)}, u32[]{:S(2)}) collective-permute-start(bf16[96,768]{1,0:T(8,128)(2,1)S(1)} %get-tuple-element.162), channel_id=1, source_target_pairs={{0,24},{8,0},{16,8},{24,16},{1,25},{9,1},{17,9},{25,17},{2,26},{10... | collective-permute-start | bytes 442376 | tf_op jit(solution)/shard_map/ppermute | solution.py:98
  (129 other events, 1135.1 us)

commit v2 on v1

v2 whole, which is shorter than its diff:
```python
import functools

import jax
import jax.numpy as jnp
from jax import lax
from jax.experimental import pallas as pl
from jax.experimental.pallas import tpu as pltpu
from jax.sharding import PartitionSpec as P

HEAD_DIM = 64
WINDOW = 128
EPS = 1e-05
BLOCK = 256
BF16 = jnp.bfloat16
F32 = jnp.float32
VMEM_BYTES = 48 * 1024 * 1024


def swap_cores(block):
    return lax.ppermute(block, "pipe", [(0, 1), (1, 0)])


def to_mate(block, bit):
    size = lax.axis_size("tensor")
    return lax.ppermute(block, "tensor", [(i, i ^ bit) for i in range(size)])


def put(buffer, block, index):
    return lax.dynamic_update_slice_in_dim(buffer, block[None], index, 0)


def take(buffer, index):
    return lax.dynamic_index_in_dim(buffer, index, 0, keepdims=False)


def spread_tensor(block):
    half = block.shape[0] // 2
    one = to_mate(block, 1)
    two = to_mate(block, 2)
    return block, one, two, to_mate(two[:half], 1), to_mate(one[half:], 2)


def scatter_tensor(own, one, two, far):
    half = far.shape[0] // 2
    low = far.dtype
    head = to_mate(far[:half], 1)
    tail = to_mate(far[half:], 2)
    one = jnp.concatenate([one[:half], (one[half:].astype(F32) + tail.astype(F32)).astype(low)], 0)
    two = jnp.concatenate([(two[:half].astype(F32) + head.astype(F32)).astype(low), two[half:]], 0)
    from_one = to_mate(one, 1)
    from_two = to_mate(two, 2)
    return own.astype(F32) + from_one.astype(F32) + from_two.astype(F32)


def swap_tensor(blocks):
    return (blocks[0],) + tuple(to_mate(blocks[bit], bit) for bit in (1, 2, 3))


def after(block, *earlier):
    return lax.optimization_barrier((block,) + earlier)[0]


def few_dp():
    return lax.axis_size("dp") <= 4


def ring(step):
    size = lax.axis_size("dp")
    return [(i, (i + step) % size) for i in range(size)]


def gather_dp(block):
    if not few_dp():
        return lax.all_gather(block, "dp", axis=0)
    moved = [lax.ppermute(block, "dp", ring(step)) for step in range(1, lax.axis_size("dp"))]
    return jnp.stack([block] + moved)


def scatter_dp(blocks, low):
    if not few_dp():
        return lax.psum_scatter(
            blocks.astype(low), "dp", scatter_dimension=0, tiled=False
        ).astype(F32)
    total = blocks[0]
    for step in range(1, lax.axis_size("dp")):
        total = total + lax.ppermute(blocks[step].astype(low), "dp", ring(-step)).astype(F32)
    return total


def join_halves(mine, other, axis):
    core = lax.axis_index("pipe")
    out = jnp.stack([mine, other], axis)
    return jnp.where(core == 0, out, jnp.stack([other, mine], axis))


def layer_halves(shard):
    core = lax.axis_index("pipe")
    rows = shard.shape[0] // 2
    mine = lax.dynamic_slice_in_dim(shard, core * rows, rows, 0)
    other = lax.dynamic_slice_in_dim(shard, (1 - core) * rows, rows, 0)
    got = swap_cores(other)
    first = jnp.where(core == 0, mine, got)
    second = jnp.where(core == 0, got, mine)
    return first, second


def placement():
    me = lax.axis_index("tensor")
    if not few_dp():
        return jnp.stack([me, 0, 0]).astype(jnp.int32)
    n = lax.axis_size("dp")
    slots = [(lax.axis_index("dp") - step) % n for step in range(n)]
    return jnp.stack([me, lax.axis_index("pipe")] + slots).astype(jnp.int32)


def halves(gathered):
    other = swap_cores(gathered)
    if few_dp():
        return gathered, other
    both = join_halves(gathered, other, gathered.ndim - 2)
    both = both.reshape(gathered.shape[:-3] + (2, -1, gathered.shape[-1]))
    return both[..., :1, :, :], both[..., 1:, :, :]


def half_sums(mine, other):
    if few_dp():
        return mine, swap_cores(other)
    core = lax.axis_index("pipe")
    n = lax.axis_size("dp")
    full = jnp.concatenate([mine, other], -3)
    full = full.reshape(full.shape[:-3] + (n, 2, -1, full.shape[-1]))
    axis = full.ndim - 3
    kept = lax.dynamic_index_in_dim(full, core, axis, keepdims=False)
    return kept, swap_cores(lax.dynamic_index_in_dim(full, 1 - core, axis, keepdims=False))


def add_low(left, right):
    return (left.astype(F32) + right.astype(F32)).astype(BF16)


def own_layer(first, second):
    core = lax.axis_index("pipe")
    mine = jnp.where(core == 0, first, second)
    other = swap_cores(jnp.where(core == 0, second, first))
    return join_halves(mine, other, 0).reshape(-1, first.shape[-1])


def norm_parts(stream):
    average = jnp.mean(stream, axis=-1, keepdims=True)
    centred = stream - average
    spread = jnp.mean(centred * centred, axis=-1, keepdims=True)
    scale = lax.rsqrt(spread + EPS)
    return centred * scale, scale


def norm_back(grad, unit, scale, gain):
    scaled = grad * gain
    mean_one = jnp.mean(scaled, axis=-1, keepdims=True)
    mean_two = jnp.mean(scaled * unit, axis=-1, keepdims=True)
    return scale * (scaled - mean_one - unit * mean_two)


def dot(left, right, dims):
    return lax.dot_general(left, right, (dims, ((), ())), preferred_element_type=F32)


NN = ((1,), (0,))
NT = ((1,), (1,))
TN = ((0,), (0,))


def cost(micros):
    return pl.CostEstimate(
        flops=int(micros * 1.15e9), bytes_accessed=int(micros * 3.6e6), transcendentals=0
    )


def run_all(copies):
    for copy in copies:
        copy.start()
    for copy in copies:
        copy.wait()


def slot_rows(place_ref, slot, half, rows):
    return pl.ds(pl.multiple_of((place_ref[2 + slot] * 2 + half) * rows, rows), rows)


def half_copies(place_ref, mine_ref, other_ref, whole_ref, sems, outward):
    core = place_ref[1]
    slots, rows = mine_ref.shape[0], mine_ref.shape[1]
    copies = []
    for slot in range(slots):
        for part, (ref, half) in enumerate(((mine_ref, core), (other_ref, 1 - core))):
            inside = whole_ref.at[slot_rows(place_ref, slot, half, rows), :]
            pair = (inside, ref.at[slot]) if outward else (ref.at[slot], inside)
            copies.append(pltpu.make_async_copy(*pair, sems.at[slot, part]))
    return copies


def pack(block):
    half = block.shape[0] // 2
    return jnp.concatenate([block[:half], block[half:]], 1)


def unpack(block):
    half = block.shape[1] // 2
    return jnp.concatenate([block[:, :half], block[:, half:]], 0)


ANYWHERE = pl.BlockSpec(memory_space=pl.ANY)
SCALARS = pl.BlockSpec(memory_space=pltpu.SMEM)
WHOLE = pl.BlockSpec(memory_space=pltpu.VMEM)


def window_start(block_id, rows, span):
    if span == rows:
        return 0
    start = jnp.clip(block_id * BLOCK - WINDOW // 2, 0, rows - span)
    return pl.multiple_of(start, WINDOW // 2)


def key_mask(start, span, first, last):
    keys = start + lax.broadcasted_iota(jnp.int32, (span, BLOCK), 0)
    return (keys >= first) & (keys < last)


def attend_kernel(
    span, place_ref, own_ref, one_ref, two_ref, head_ref, tail_ref, mine_ref, other_ref,
    cos_ref, sin_ref, first_ref, last_ref,
    mixed0_ref, mixed1_ref, mixed2_ref, mixed3_ref, queries_ref, keys_ref, values_ref, mass_ref,
    normed_ref, qkv_ref, key_rows, value_rows, proj, mixed_rows, sems, weight_sems,
):
    width, rows = queries_ref.shape
    heads = width // HEAD_DIM
    half = HEAD_DIM // 2
    local = rows // 4
    me = place_ref[0]
    copies = half_copies(place_ref, mine_ref, other_ref, qkv_ref, weight_sems, False)
    pieces = (
        (own_ref, 0, 0), (one_ref, 1, 0), (two_ref, 2, 0), (head_ref, 3, 0), (tail_ref, 3, local // 2)
    )
    for index, (ref, bit, shift) in enumerate(pieces):
        low = pl.multiple_of((me ^ bit) * local + shift, local // 2)
        target = normed_ref.at[pl.ds(low, ref.shape[0]), :]
        copies.append(pltpu.make_async_copy(ref, target, sems.at[index]))
    run_all(copies)
    proj[...] = dot(qkv_ref[...].T, normed_ref[...], NT)
    cosines, sines = cos_ref[...], sin_ref[...]
    for head in range(heads):
        low = head * HEAD_DIM
        for part, ref in ((0, queries_ref), (1, keys_ref)):
            upper = proj[part * width + low : part * width + low + half, :]
            lower = proj[part * width + low + half : part * width + low + HEAD_DIM, :]
            turned = jnp.concatenate(
                [upper * cosines - lower * sines, lower * cosines + upper * sines], 0
            )
            ref[low : low + HEAD_DIM, :] = turned.astype(BF16)
            if part == 1:
                key_rows[head] = turned.T.astype(BF16)
        value = proj[2 * width + low : 2 * width + low + HEAD_DIM, :]
        values_ref[low : low + HEAD_DIM, :] = value.astype(BF16)
        value_rows[head] = value.T.astype(BF16)
    mass_ref[...] = jnp.zeros_like(mass_ref)

    def block(block_id, carry):
        start = window_start(block_id, rows, span)
        columns = pl.ds(pl.multiple_of(block_id * BLOCK, BLOCK), BLOCK)
        mask = key_mask(start, span, first_ref[:, columns], last_ref[:, columns])
        outs = []
        for head in range(heads):
            low = head * HEAD_DIM
            query = queries_ref[low : low + HEAD_DIM, columns] * BF16(HEAD_DIM**-0.5)
            scores = dot(key_rows[head, pl.ds(start, span), :], query, NN)
            scores = jnp.where(mask, scores, -1e30)
            top = jnp.max(scores, axis=0, keepdims=True)
            expos = jnp.exp(scores - top)
            total = jnp.sum(expos, axis=0, keepdims=True)
            probs = (expos * (1.0 / total)).astype(BF16)
            if span == rows:
                value = values_ref[low : low + HEAD_DIM, :]
            else:
                value = value_rows[head, pl.ds(start, span), :].T
            outs.append(dot(value, probs, NN))
            mass_ref[head : head + 1, columns] = top + jnp.log(total)
        mixed_rows[columns, :] = jnp.concatenate(outs, 0).T.astype(BF16)
        return carry

    lax.fori_loop(0, rows // BLOCK, block, 0)
    for bit, ref in enumerate((mixed0_ref, mixed1_ref, mixed2_ref, mixed3_ref)):
        low = pl.multiple_of((me ^ bit) * local, local)
        ref[...] = pack(mixed_rows[pl.ds(low, local), :])


def attend(place, pieces, mine, other, cosines, sines, first, last, is_local):
    local, model = pieces[0].shape
    rows = 4 * local
    width = mine.shape[2] // 3
    heads = width // HEAD_DIM
    span = min(rows, BLOCK + WINDOW) if is_local else rows
    shape = jax.ShapeDtypeStruct((width, rows), BF16)
    mixed = jax.ShapeDtypeStruct((local // 2, 2 * width), BF16)
    return pl.pallas_call(
        functools.partial(attend_kernel, span),
        out_shape=(
            mixed, mixed, mixed, mixed, shape, shape, shape, jax.ShapeDtypeStruct((8, rows), F32),
            jax.ShapeDtypeStruct((rows, model), BF16),
            jax.ShapeDtypeStruct((model, 3 * width), BF16),
        ),
        in_specs=[SCALARS] + [ANYWHERE] * 7 + [WHOLE] * 4,
        scratch_shapes=[
            pltpu.VMEM((heads, rows, HEAD_DIM), BF16),
            pltpu.VMEM((heads, rows, HEAD_DIM), BF16),
            pltpu.VMEM((3 * width, rows), F32),
            pltpu.VMEM((rows, width), BF16),
            pltpu.SemaphoreType.DMA((5,)),
            pltpu.SemaphoreType.DMA((mine.shape[0], 2)),
        ],
        compiler_params=pltpu.CompilerParams(vmem_limit_bytes=VMEM_BYTES),
        cost_estimate=cost(11 if is_local else 20),
        name="attend_local" if is_local else "attend_global",
    )(place, *pieces, mine, other, cosines, sines, first, last)


def attend_back_kernel(
    span, place_ref, queries_ref, keys_ref, values_ref, mass_ref,
    grad0_ref, grad1_ref, grad2_ref, grad3_ref,
    cos_ref, sin_ref, first_ref, last_ref, qkv_ref,
    part0_ref, part1_ref, part2_ref, part3_ref, out_ref,
    query_rows, key_rows, value_rows, grad_cols, grad_all, grad_rows, sum_q, sum_k, sum_v, flat,
):
    width, rows = queries_ref.shape
    heads = width // HEAD_DIM
    half = HEAD_DIM // 2
    local = rows // 4
    scale = HEAD_DIM**-0.5
    me = place_ref[0]
    for bit, ref in enumerate((grad0_ref, grad1_ref, grad2_ref, grad3_ref)):
        low = pl.multiple_of((me ^ bit) * local, local)
        grad_all[pl.ds(low, local), :] = unpack(ref[...])
    grad_cols[...] = grad_all[...].T
    for head in range(heads):
        cut = slice(head * HEAD_DIM, (head + 1) * HEAD_DIM)
        query_rows[head] = (queries_ref[cut, :] * BF16(scale)).T
        key_rows[head] = keys_ref[cut, :].T
        value_rows[head] = values_ref[cut, :].T
        grad_rows[head] = grad_all[:, cut]
    sum_k[...] = jnp.zeros_like(sum_k)
    sum_v[...] = jnp.zeros_like(sum_v)

    def block(block_id, carry):
        start = window_start(block_id, rows, span)
        window = pl.ds(start, span)
        columns = pl.ds(pl.multiple_of(block_id * BLOCK, BLOCK), BLOCK)
        mask = key_mask(start, span, first_ref[:, columns], last_ref[:, columns])
        for head in range(heads):
            cut = slice(head * HEAD_DIM, (head + 1) * HEAD_DIM)
            query = queries_ref[cut, columns] * BF16(scale)
            key = key_rows[head, window, :]
            scores = dot(key, query, NN) - mass_ref[head : head + 1, columns]
            probs = jnp.exp(jnp.where(mask, scores, -1e30))
            grad_probs = dot(value_rows[head, window, :], grad_cols[cut, columns], NN)
            weighted = probs * grad_probs
            inner = jnp.sum(weighted, axis=0, keepdims=True)
            grad_scores = (weighted - probs * inner).astype(BF16)
            sum_v[head, window, :] += dot(probs.astype(BF16), grad_rows[head, columns, :], NN)
            sum_k[head, window, :] += dot(grad_scores, query_rows[head, columns, :], NN)
            key_cols = keys_ref[cut, :] if span == rows else key.T
            sum_q[cut, columns] = dot(key_cols, grad_scores, NN)
        return carry

    lax.fori_loop(0, rows // BLOCK, block, 0)
    cosines, sines = cos_ref[...], sin_ref[...]
    for head in range(heads):
        low = head * HEAD_DIM
        turned_q = sum_q[low : low + HEAD_DIM, :] * scale
        for part, turned in ((0, turned_q), (1, sum_k[head].T)):
            upper, lower = turned[:half], turned[half:]
            raw = jnp.concatenate(
                [upper * cosines + lower * sines, lower * cosines - upper * sines], 0
            )
            flat[part * width + low : part * width + low + HEAD_DIM, :] = raw.astype(BF16)
        flat[2 * width + low : 2 * width + low + HEAD_DIM, :] = sum_v[head].T.astype(BF16)
    out_ref[...] = flat[...].T
    for bit, ref in enumerate((part0_ref, part1_ref, part2_ref, part3_ref)):
        low = pl.multiple_of((me ^ bit) * local, local)
        ref[...] = dot(out_ref[pl.ds(low, local), :], qkv_ref[...], NT).astype(BF16)


def attend_back(place, queries, keys, values, mass, grads, cosines, sines, first, last, qkv, is_local):
    width, rows = queries.shape
    model = qkv.shape[0]
    heads = width // HEAD_DIM
    span = min(rows, BLOCK + WINDOW) if is_local else rows
    low_rows = pltpu.VMEM((heads, rows, HEAD_DIM), BF16)
    sums = pltpu.VMEM((heads, rows, HEAD_DIM), F32)
    part = jax.ShapeDtypeStruct((rows // 4, model), BF16)
    return pl.pallas_call(
        functools.partial(attend_back_kernel, span),
        out_shape=(part, part, part, part, jax.ShapeDtypeStruct((rows, 3 * width), BF16)),
        in_specs=[SCALARS] + [WHOLE] * 13,
        scratch_shapes=[
            low_rows, low_rows, low_rows, pltpu.VMEM((width, rows), BF16),
            pltpu.VMEM((rows, width), BF16), low_rows,
            pltpu.VMEM((width, rows), F32), sums, sums, pltpu.VMEM((3 * width, rows), BF16),
        ],
        compiler_params=pltpu.CompilerParams(vmem_limit_bytes=VMEM_BYTES),
        cost_estimate=cost(11 if is_local else 21),
        name="attend_back_local" if is_local else "attend_back_global",
    )(place, queries, keys, values, mass, *grads, cosines, sines, first, last, qkv)


def qkv_grad_kernel(place_ref, normed_ref, grad_ref, mine_ref, other_ref, whole, sems):
    whole[...] = dot(normed_ref[...].T, grad_ref[...], NN).astype(BF16)
    run_all(half_copies(place_ref, mine_ref, other_ref, whole, sems, True))


def qkv_grad(place, normed, grad, shape):
    part = jax.ShapeDtypeStruct(shape, BF16)
    return pl.pallas_call(
        qkv_grad_kernel,
        out_shape=(part, part),
        in_specs=[SCALARS, WHOLE, WHOLE],
        out_specs=(ANYWHERE, ANYWHERE),
        scratch_shapes=[
            pltpu.VMEM((normed.shape[1], grad.shape[1]), BF16),
            pltpu.SemaphoreType.DMA((shape[0], 2)),
        ],
        compiler_params=pltpu.CompilerParams(vmem_limit_bytes=VMEM_BYTES),
        cost_estimate=cost(4),
        name="qkv_grad",
    )(place, normed, grad)


def erf_parts(gate):
    cumulative = 0.5 * (1.0 + lax.erf(gate * 0.7071067811865476))
    density = 0.3989422804014327 * jnp.exp(-0.5 * gate * gate)
    return cumulative, density


def token_kernel(
    pair, place_ref, mixed0_ref, mixed1_ref, mixed2_ref, mixed3_ref, in_ref, mine_ref, other_ref,
    gain_ref, next_ref, mid_ref, out_ref, normed_ref, sums, mats, sems,
):
    parts = mats.shape[0]
    width = mixed0_ref.shape[1] // 2
    units = pair // 2
    copies = []
    for part in range(parts):
        copies += half_copies(
            place_ref, mine_ref.at[part], other_ref.at[part], mats.at[part], sems.at[part], False
        )
    run_all(copies)
    mid = in_ref[...].astype(F32)
    for part, ref in enumerate((mixed0_ref, mixed1_ref, mixed2_ref, mixed3_ref)):
        mid += dot(unpack(ref[...]), mats[part, :, pair : pair + width], NT)
    mid_ref[...] = mid
    sums[...] = mid
    normed = (norm_parts(mid)[0] * gain_ref[...]).astype(BF16)

    def feed(part, carry):
        gate_up = dot(normed, mats[part, :, :pair], NN)
        gate = gate_up[:, :units]
        hidden = (gate * erf_parts(gate)[0] * gate_up[:, units:]).astype(BF16)
        sums[...] += dot(hidden, mats[part, :, pair + width :], NT)
        return carry

    lax.fori_loop(0, parts, feed, 0)
    low = sums[...].astype(BF16)
    out_ref[...] = low
    normed_ref[...] = (norm_parts(low.astype(F32))[0] * next_ref[...]).astype(BF16)


def token_forward(place, mixed, layer_in, mine, other, gain, next_gain, pair):
    shape = layer_in.shape
    parts, slots = mine.shape[:2]
    return pl.pallas_call(
        functools.partial(token_kernel, pair),
        out_shape=(
            jax.ShapeDtypeStruct(shape, F32),
            jax.ShapeDtypeStruct(shape, BF16),
            jax.ShapeDtypeStruct(shape, BF16),
        ),
        in_specs=[SCALARS] + [WHOLE] * 5 + [ANYWHERE] * 2 + [WHOLE] * 2,
        scratch_shapes=[
            pltpu.VMEM(shape, F32),
            pltpu.VMEM((parts, shape[1], mine.shape[3]), BF16),
            pltpu.SemaphoreType.DMA((parts, slots, 2)),
        ],
        compiler_params=pltpu.CompilerParams(vmem_limit_bytes=VMEM_BYTES),
        cost_estimate=cost(10),
        name="token_forward",
    )(place, *mixed, layer_in, mine, other, gain, next_gain)


def token_back_kernel(
    pair, place_ref, grad_ref, mid_ref, mixed0_ref, mixed1_ref, mixed2_ref, mixed3_ref,
    mine_ref, other_ref, gain_ref,
    mine_grad_ref, other_grad_ref, mixed_grad0_ref, mixed_grad1_ref, mixed_grad2_ref, mixed_grad3_ref,
    grad_mid_ref, gain_grad_ref, sums, mats, grads, sems,
):
    parts = mats.shape[0]
    width = mixed0_ref.shape[1] // 2
    units = pair // 2
    copies = []
    for part in range(parts):
        copies += half_copies(
            place_ref, mine_ref.at[part], other_ref.at[part], mats.at[part], sems.at[part], False
        )
    run_all(copies)
    grad = grad_ref[...].astype(F32)
    grad_low = grad.astype(BF16)
    grad_flip = grad.T.astype(BF16)
    unit, scale = norm_parts(mid_ref[...])
    gained = unit * gain_ref[...]
    normed = gained.astype(BF16)
    normed_flip = gained.T.astype(BF16)
    sums[...] = jnp.zeros_like(sums)

    def feed(part, carry):
        gate_up = dot(normed, mats[part, :, :pair], NN)
        gate, up = gate_up[:, :units], gate_up[:, units:]
        cumulative, density = erf_parts(gate)
        gelu = gate * cumulative
        hidden = (gelu * up).astype(BF16)
        grad_hidden = dot(grad_low, mats[part, :, pair + width :], NN)
        grad_gate = grad_hidden * up * (cumulative + gate * density)
        grad_up = grad_hidden * gelu
        grad_pair = jnp.concatenate([grad_gate, grad_up], 1).astype(BF16)
        grads[part, :, pair + width :] = dot(grad_flip, hidden, NN).astype(BF16)
        grads[part, :, :pair] = dot(normed_flip, grad_pair, NN).astype(BF16)
        sums[...] += dot(grad_pair, mats[part, :, :pair], NT)
        return carry

    lax.fori_loop(0, parts, feed, 0)
    grad_normed = sums[...]
    gain_grad_ref[...] = jnp.sum(grad_normed * unit, axis=0, keepdims=True)
    grad_mid = grad + norm_back(grad_normed, unit, scale, gain_ref[...])
    grad_mid_ref[...] = grad_mid
    mid_low = grad_mid.astype(BF16)
    mid_flip = grad_mid.T.astype(BF16)
    mixed_refs = (mixed0_ref, mixed1_ref, mixed2_ref, mixed3_ref)
    mixed_grad_refs = (mixed_grad0_ref, mixed_grad1_ref, mixed_grad2_ref, mixed_grad3_ref)
    copies = []
    for part in range(parts):
        weight = mats[part, :, pair : pair + width]
        mixed_grad_refs[part][...] = pack(dot(mid_low, weight, NN).astype(BF16))
        grads[part, :, pair : pair + width] = dot(
            mid_flip, unpack(mixed_refs[part][...]), NN
        ).astype(BF16)
        batch = half_copies(
            place_ref, mine_grad_ref.at[part], other_grad_ref.at[part], grads.at[part],
            sems.at[part], True,
        )
        for copy in batch:
            copy.start()
        copies += batch
    for copy in copies:
        copy.wait()


def token_back(place, grad, mid, mixed, mine, other, gain, pair):
    parts, slots = mine.shape[:2]
    mats = pltpu.VMEM((parts, mid.shape[1], mine.shape[3]), BF16)
    half = jax.ShapeDtypeStruct(mine.shape, BF16)
    mixed_grad = jax.ShapeDtypeStruct(mixed[0].shape, BF16)
    return pl.pallas_call(
        functools.partial(token_back_kernel, pair),
        out_shape=(
            half, half, mixed_grad, mixed_grad, mixed_grad, mixed_grad,
            jax.ShapeDtypeStruct(mid.shape, F32),
            jax.ShapeDtypeStruct((1, mid.shape[1]), F32),
        ),
        in_specs=[SCALARS] + [WHOLE] * 6 + [ANYWHERE] * 2 + [WHOLE],
        out_specs=(ANYWHERE, ANYWHERE) + (WHOLE,) * 6,
        scratch_shapes=[
            pltpu.VMEM(mid.shape, F32), mats, mats, pltpu.SemaphoreType.DMA((parts, slots, 2)),
        ],
        compiler_params=pltpu.CompilerParams(vmem_limit_bytes=VMEM_BYTES),
        cost_estimate=cost(20),
        name="token_back",
    )(place, grad, mid, *mixed, mine, other, gain)


def frequencies(theta_base, half_dim):
    return theta_base ** (-(jnp.arange(half_dim, dtype=F32) * 2.0) / (2.0 * half_dim))


def sequences(seq_lengths, rows):
    seq_ends = jnp.cumsum(seq_lengths)
    positions = jnp.arange(rows, dtype=jnp.int32)
    seq_of = jnp.sum((positions[:, None] >= seq_ends[None, :]).astype(jnp.int32), axis=1)
    matches = jnp.arange(seq_lengths.shape[0], dtype=jnp.int32)[None, :] == seq_of[:, None]
    last = jnp.sum(jnp.where(matches, seq_ends[None, :], 0), axis=1)
    first = jnp.sum(jnp.where(matches, (seq_ends - seq_lengths)[None, :], 0), axis=1)
    return first[None], last[None], positions[None]


def body(
    tokens, lengths, qkv_weight, out_weight, gate_up_weight, down_weight, gains, out_cotangent
):
    core = lax.axis_index("pipe")
    model = tokens.shape[-1]
    local_rows = tokens.shape[2]
    rows = 4 * local_rows
    shard_rows = qkv_weight.shape[1]
    width = qkv_weight.shape[3]
    pair = 2 * gate_up_weight.shape[3]

    stream = take(tokens[0], core)
    cotangent = take(out_cotangent[0], core)
    first, last, positions = sequences(take(lengths[0], core), rows)
    bounds = (
        (jnp.maximum(first, positions - WINDOW // 2), jnp.minimum(last, positions + WINDOW // 2 + 1)),
        (first, last),
    )
    tables = []
    for base in (10000.0, 160000.0):
        turns = frequencies(base, HEAD_DIM // 2)[:, None] * (positions - first).astype(F32)
        tables.append((jnp.cos(turns), jnp.sin(turns)))

    other_gains = swap_cores(gains[0])
    gain_rows = (
        jnp.where(core == 0, gains[0], other_gains)[None],
        jnp.where(core == 0, other_gains, gains[0])[None],
    )
    place = placement()

    normed = (norm_parts(stream.astype(F32))[0] * gain_rows[0][:, :model]).astype(BF16)
    qkv_halves = layer_halves(qkv_weight[0].reshape(shard_rows, 3 * width))
    mats_halves = layer_halves(
        jnp.concatenate(
            [gate_up_weight[0].reshape(shard_rows, pair), out_weight[0].T, down_weight[0].T], 1
        )
    )
    qkv_first = gather_dp(qkv_halves[0])
    mats_first = gather_dp(mats_halves[0])
    qkv_second, mats_second = lax.optimization_barrier(
        (qkv_halves[1], mats_halves[1], qkv_first, mats_first)
    )[:2]
    qkv_gathered = (qkv_first, gather_dp(qkv_second))
    mats_gathered = (mats_first, gather_dp(mats_second))

    layer_in = stream
    saved = []
    for layer in (0, 1):
        pieces = spread_tensor(normed)
        qkv_mine, qkv_other = halves(qkv_gathered[layer])
        own, one, two, head, tail = spread_tensor(mats_gathered[layer])
        mats_mine, mats_other = halves(
            jnp.stack([own, one, two, jnp.concatenate([head, tail], 0)])
        )
        *mixed, queries, keys, values, mass, normed_full, qkv = attend(
            place, pieces, qkv_mine, qkv_other, *tables[layer], *bounds[layer], layer == 0
        )
        mixed = swap_tensor(mixed)
        mid, layer_out, normed = token_forward(
            place, mixed, layer_in, mats_mine, mats_other,
            gain_rows[layer][:, model:], gain_rows[1][:, :model], pair,
        )
        saved.append(
            (layer_in, qkv, qkv_mine.shape, mats_mine, mats_other, normed_full,
             queries, keys, values, mass, mixed, mid)
        )
        layer_in = layer_out
        if layer == 0:
            first_out = layer_out
    second_out = layer_in

    grad = cotangent
    reduced = [None, None]
    gain_grads = [None, None]
    input_grads = [None, None]
    for layer in (1, 0):
        (stream, qkv, qkv_shape, mats_mine, mats_other, normed_full,
         queries, keys, values, mass, mixed, mid) = saved[layer]
        mine_grad, other_grad, *mixed_grad, grad_mid, gain_mlp = token_back(
            place, grad, mid, mixed, mats_mine, mats_other, gain_rows[layer][:, model:], pair
        )
        mixed_grad = swap_tensor(mixed_grad)
        *partial_in, grad_projected = attend_back(
            place, queries, keys, values, mass, mixed_grad, *tables[layer], *bounds[layer], qkv,
            layer == 0,
        )
        grad_normed = scatter_tensor(*partial_in)
        unit, scale = norm_parts(stream.astype(F32))
        gain_attn = jnp.sum(grad_normed * unit, axis=0, keepdims=True)
        grad_in = grad_mid + norm_back(grad_normed, unit, scale, gain_rows[layer][:, :model])
        gain_grads[layer] = jnp.concatenate([gain_attn, gain_mlp], 1)

        mats_kept, mats_came = half_sums(mine_grad, other_grad)
        mats_sum = scatter_tensor(*(add_low(mats_kept[i], mats_came[i]) for i in range(4)))
        qkv_kept, qkv_came = half_sums(
            *qkv_grad(place, normed_full, grad_projected, qkv_shape)
        )
        qkv_sum = qkv_kept.astype(F32) + qkv_came.astype(F32)
        reduced[layer] = scatter_dp(jnp.concatenate([mats_sum, qkv_sum], -1), BF16)
        if layer == 1:
            grad = grad_in.astype(BF16)
            grad_in = grad.astype(F32)
        input_grads[layer] = grad_in

    weight_grad = own_layer(*reduced)
    out_low, down_low = pair + width, pair + width + down_weight.shape[1]
    n = lax.axis_size("dp")
    gain_mine = jnp.where(core == 0, gain_grads[0], gain_grads[1])
    gain_other = swap_cores(jnp.where(core == 0, gain_grads[1], gain_grads[0]))
    gain_blocks = jnp.moveaxis((gain_mine + gain_other).reshape(n, 4, -1), 1, 0)
    me = lax.axis_index("tensor")
    gain_blocks = sum(swap_tensor([take(gain_blocks, me ^ bit) for bit in range(4)]))
    if few_dp():
        rank = lax.axis_index("dp")
        gain_blocks = jnp.stack([take(gain_blocks, (rank - step) % n) for step in range(n)])
    gain_part = scatter_dp(gain_blocks, F32)

    activations = join_halves(
        jnp.where(core == 0, first_out, second_out),
        swap_cores(jnp.where(core == 0, second_out, first_out)),
        0,
    )
    grads_in = join_halves(
        jnp.where(core == 0, input_grads[0], input_grads[1]),
        swap_cores(jnp.where(core == 0, input_grads[1], input_grads[0])),
        0,
    )
    return (
        activations[None, None],
        grads_in[None, None],
        weight_grad[:, down_low:].reshape(qkv_weight.shape),
        weight_grad[:, pair:out_low].T[None],
        weight_grad[:, :pair].reshape(gate_up_weight.shape),
        weight_grad[:, out_low:down_low].T[None],
        gain_part[None],
    )


def solution(mesh):
    return jax.shard_map(
        body,
        mesh=mesh,
        in_specs=(
            P("dp", None, "tensor", None),
            P("dp", None, None),
            P("pipe", "dp", None, "tensor"),
            P("pipe", "tensor", "dp"),
            P("pipe", "dp", None, "tensor"),
            P("pipe", "tensor", "dp"),
            P("pipe", None),
            P("dp", None, "tensor", None),
        ),
        out_specs=(
            P("pipe", "dp", None, "tensor", None),
            P("pipe", "dp", None, "tensor", None),
            P("pipe", "dp", None, "tensor"),
            P("pipe", "tensor", "dp"),
            P("pipe", "dp", None, "tensor"),
            P("pipe", "tensor", "dp"),
            P("pipe", ("dp", "tensor")),
        ),
        check_vma=False,
    )
```

time: 596 us -> 507 us (0.85)
  local copies, waits for them, and re-layouts: 75.6 us -> 23.8 us
  Pallas kernels: 108 us -> 134 us
  waiting for transfers between devices: 212 us -> 193 us
  matrix products: 14.3 us -> 0 us
  starting transfers between devices: 126 us -> 112 us
  other arithmetic: 50.1 us -> 36.4 us
    ppermute x39 -> x21, waiting for transfers between devices: 91.5 us -> 65.1 us  [the longest x12 33.6 us: gather_dp(): lax.ppermute(block, 'dp', ring(step))]
    pallas_call x6 -> x8, Pallas kernels: 89.1 us -> 113 us  [the longest x2 36.7 us: token_back(): pl.pallas_call(functools.partial(token_back_kernel, pair), out_shape=(hal...]
    select_n x11 -> x3, other arithmetic: 20.5 us -> 2.58 us  [join_halves(): return jnp.where(core == 0, out, jnp.stack([other, mine], axis))]
    dot_general x6 -> x0, matrix products: 14.3 us -> none  [dot(): lax.dot_general(left, right, (dims, ((), ())), preferred_element_type=F32)]
    ppermute x63 -> x47, starting transfers between devices: 64.6 us -> 50.6 us  [to_mate(): return lax.ppermute(block, 'tensor', [(i, i ^ bit) for i in range(size)])]
    dynamic_update_slice x53 -> x0, local copies, waits for them, and re-layouts: 12.6 us -> none  [put(): return lax.dynamic_update_slice_in_dim(buffer, block[None], index, 0)]
    ppermute x63 -> x47, waiting for transfers between devices: 120 us -> 128 us  [to_mate(): return lax.ppermute(block, 'tensor', [(i, i ^ bit) for i in range(size)])]
    dynamic_slice x4 -> x0, local copies, waits for them, and re-layouts: 7.55 us -> none  [the longest x2 4.85 us: half_sums(): other = lax.dynamic_index_in_dim(split, 1 - core, axis, keepdims=False)]
  transfers between devices with their start and end apart: 124 -> 83, of which waited for: 60 -> 35; matrix products, arithmetic and copies ran while one was open for 21% -> 9% of each run, Pallas kernels for 11% -> 17%
where the time goes in v2:
time: 507 us; the launch traced here: 501 us
  waiting for transfers between devices  193 us (38%)
  Pallas kernels  134 us (26%)
  starting transfers between devices  112 us (22%)
  other arithmetic  36.4 us (7%)
  local copies, waits for them, and re-layouts  23.8 us (5%)
    ppermute x47, waiting for transfers between devices, to_mate(): return lax.ppermute(block, 'tensor', [(i, i ^ bit) for i in range(size)])  128 us
    ppermute x47, starting transfers between devices, to_mate(): return lax.ppermute(block, 'tensor', [(i, i ^ bit) for i in range(size)])  50.6 us
    pallas_call x2, Pallas kernels, token_back(): pl.pallas_call(functools.partial(token_back_kernel, pair), out_shape=(hal...  36.7 us
    pallas_call x2, Pallas kernels, attend(): pl.pallas_call(functools.partial(attend_kernel, span), out_shape=(mixed,...  36.2 us
    ppermute x12, waiting for transfers between devices, gather_dp(): lax.ppermute(block, 'dp', ring(step))  33.6 us
    pallas_call x2, Pallas kernels, attend_back(): pl.pallas_call(functools.partial(attend_back_kernel, span), out_shape=(pa...  32.8 us
    ppermute x9, waiting for transfers between devices, scatter_dp(): lax.ppermute(blocks[step].astype(low), 'dp', ring(-step)).astype(F32)  31.5 us
    ppermute x12, starting transfers between devices, gather_dp(): lax.ppermute(block, 'dp', ring(step))  30.4 us
  transfers between devices with their start and end apart: 83, of which 35 were waited for; matrix products, arithmetic and copies ran while one was open for 9% of the time, Pallas kernels for 17%

profile of v2, /device:TPU:0, one launch (start us, length us, event | category | flops | bytes accessed | tf_op | source)
XLA Modules:
  0.0 501.0 jit_solution(7763143894943030088)
XLA Ops:
  7.2 2.6 collective-permute-start.14
  9.8 2.6 collective-permute-start.15
  13.8 4.5 collective-permute-done.14
  18.3 9.2 %collective-permute-done.15 = bf16[96,1056]{1,0:T(8,128)(2,1)S(1)} collective-permute-done((bf16[96,1056]{1,0:T(8,128)(2,1)S(1)}, bf16[96,1056]{1,0:T(8,128)(2,1)S(1)}, u32[]{:S(2)}, u32[]{:S(2)}) %collective-permute-start.15) | collective-permute-done | bytes 202784 | tf_op jit(solution)/shard_map/ppermute | solution.py:75
  33.7 4.2 collective-permute-start.7
  37.9 3.4 collective-permute-start.8
  44.5 4.7 collective-permute-done.6
  51.7 2.8 collective-permute-start.35
  56.8 2.5 collective-permute-done.33
  59.3 7.0 %collective-permute-done.34 = bf16[96,1056]{1,0:T(8,128)(2,1)S(1)} collective-permute-done((bf16[96,1056]{1,0:T(8,128)(2,1)S(1)}, bf16[96,1056]{1,0:T(8,128)(2,1)S(1)}, u32[]{:S(2)}, u32[]{:S(2)}) %collective-permute-start.34) | collective-permute-done | bytes 202784 | tf_op jit(solution)/shard_map/ppermute | solution.py:75
  68.4 3.1 pad_maximum_fusion.mine_ref
  76.7 23.3 %collective-permute-done.2.two_ref = bf16[320,768]{1,0:T(8,128)(2,1)S(1)} collective-permute-done((bf16[320,768]{1,0:T(8,128)(2,1)S(1)}, bf16[320,768]{1,0:T(8,128)(2,1)S(1)}, u32[]{:S(2)}, u32[]{:S(2)}) %collective-permute-start.2) | collective-permute-done | bytes 491552 | tf_op jit(solution)/shard_map/ppermute | solution.py:25
  106.5 5.4 %collective-permute-start.26 = (bf16[96,576]{1,0:T(8,128)(2,1)}, bf16[96,576]{1,0:T(8,128)(2,1)S(1)}, u32[]{:S(2)}, u32[]{:S(2)}) collective-permute-start(bf16[96,576]{1,0:T(8,128)(2,1)} %get-tuple-element.70), channel_id=1, source_target_pairs={{0,8},{8,16},{16,24},{24,0},{1,9},{9,17},{17,25},{25,1},{2,10},{10... | collective-permute-start | bytes 331784 | tf_op jit(solution)/shard_map/ppermute | solution.py:75
  114.4 13.7 %attend_local.1 = (bf16[160,384]{1,0:T(8,128)(2,1)S(1)}, bf16[160,384]{1,0:T(8,128)(2,1)S(1)}, bf16[160,384]{1,0:T(8,128)(2,1)S(1)}, bf16[160,384]{1,0:T(8,128)(...) custom-call(s32[6]{0:T(128)S(1)} %stack.159.place_ref, ...), custom_call_target="tpu_custom_call" | custom-call | flops 12650000384 | bytes 39600000 | tf_op jit(solution)/shard_map/attend_local/pallas_call | solution.py:303
  131.8 3.2 pad_maximum_fusion.1.mine_ref
  136.6 9.8 %token_forward.2 = (f32[320,768]{1,0:T(8,128)S(1)}, bf16[320,768]{1,0:T(8,128)(2,1)S(1)}, bf16[320,768]{1,0:T(8,128)(2,1)S(1)}) custom-call(s32[6]{0:T(128)S(1)} %stack.159.place_ref, bf16[160,384]{1,0:T(8,128)(2,1)S(1)} %get-tuple-element.64.mixed0_ref, bf16[160,384]{1,0:T(8,128)(2,1)S(1)} %collective-permute-done.10.mixed1_ref, ...), custom_call_target="tpu_custom_call" | custom-call | flops 11500000256 | bytes 36000000 | tf_op jit(solution)/shard_map/token_forward/pallas_call | solution.py:477
  148.4 2.4 collective-permute-start.27
  150.8 3.3 collective-permute-start.28
  154.1 2.5 collective-permute-done.27
  164.5 4.5 collective-permute-done.24.head_ref
  174.0 22.6 %attend_global.1 = (bf16[160,384]{1,0:T(8,128)(2,1)S(1)}, bf16[160,384]{1,0:T(8,128)(2,1)S(1)}, bf16[160,384]{1,0:T(8,128)(2,1)S(1)}, bf16[160,384]{1,0:T(8,128)...) custom-call(s32[6]{0:T(128)S(1)} %stack.159.place_ref, ...), custom_call_target="tpu_custom_call" | custom-call | flops 23000000512 | bytes 72000000 | tf_op jit(solution)/shard_map/attend_global/pallas_call | solution.py:303
  202.2 3.3 collective-permute-done.31.mixed2_ref
  205.5 10.6 %token_forward.3 = (f32[320,768]{1,0:T(8,128)S(1)}, bf16[320,768]{1,0:T(8,128)(2,1)S(1)}, bf16[320,768]{1,0:T(8,128)(2,1)}) custom-call(s32[6]{0:T(128)S(1)} %stack.159.place_ref, bf16[160,384]{1,0:T(8,128)(2,1)S(1)} %get-tuple-element.71.mixed0_ref, bf16[160,384]{1,0:T(8,128)(2,1)S(1)} %collective-permute-done.30.mixed1_ref, ...), custom_call_target="tpu_custom_call" | custom-call | flops 11500000256 | bytes 36000000 | tf_op jit(solution)/shard_map/token_forward/pallas_call | solution.py:477
  216.2 18.5 %token_back.2 = (bf16[4,4,96,1056]{3,2,1,0:T(8,128)(2,1)}, bf16[4,4,96,1056]{3,2,1,0:T(8,128)(2,1)}, bf16[160,384]{1,0:T(8,128)(2,1)S(1)}, bf16[160,384]{1,0:T(8...) custom-call(s32[6]{0:T(128)S(1)} %stack.159.place_ref, ...), custom_call_target="tpu_custom_call" | custom-call | flops 23000000512 | bytes 72000000 | tf_op jit(solution)/shard_map/token_back/pallas_call | solution.py:567
  242.4 21.0 %attend_back_global.1 = (bf16[320,768]{1,0:T(8,128)(2,1)S(1)}, bf16[320,768]{1,0:T(8,128)(2,1)S(1)}, bf16[320,768]{1,0:T(8,128)(2,1)S(1)}, bf16[320,768]{1,0:T(8,128)(2,1)S(1)}, bf16[1280,576]{1,0:T(8,128)(2,1)}) custom-call(s32[6]{0:T(128)S(1)} %stack.159.place_ref, bf16[192,1280]{1,0:T(8,128)(2,1)S(1)} %get-tuple-element.79.queries_ref, ...), custom_call_target="tpu_custom_call" | custom-call | flops 24149999616 | bytes 75600000 | tf_op jit(solution)/shard_map/attend_back_global/pallas_call | solution.py:398
  266.5 3.2 collective-permute-done.45
  271.1 2.7 collective-permute-done.47
  275.9 3.8 qkv_grad.3
  279.8 4.1 collective-permute-done.46
  284.0 2.5 collective-permute-done.48
  288.4 18.2 %token_back.3 = (bf16[4,4,96,1056]{3,2,1,0:T(8,128)(2,1)}, bf16[4,4,96,1056]{3,2,1,0:T(8,128)(2,1)}, bf16[160,384]{1,0:T(8,128)(2,1)S(1)}, bf16[160,384]{1,0:T(8...) custom-call(s32[6]{0:T(128)S(1)} %stack.159.place_ref, ...), custom_call_target="tpu_custom_call" | custom-call | flops 23000000512 | bytes 72000000 | tf_op jit(solution)/shard_map/token_back/pallas_call | solution.py:567
  314.6 11.7 %attend_back_local.1 = (bf16[320,768]{1,0:T(8,128)(2,1)S(1)}, bf16[320,768]{1,0:T(8,128)(2,1)S(1)}, bf16[320,768]{1,0:T(8,128)(2,1)S(1)}, bf16[320,768]{1,0:T(8,128)(2,1)S(1)}, bf16[1280,576]{1,0:T(8,128)(2,1)}) custom-call(s32[6]{0:T(128)S(1)} %stack.159.place_ref, bf16[192,1280]{1,0:T(8,128)(2,1)S(1)} %copy-done.24, bf16[192,1280]{1,0:T(8,128)(2,1)S(1)} %copy-done.26, ...), custom_call_target="tpu_custom_call" | custom-call | flops 12650000384 | bytes 39600000 | tf_op jit(solution)/shard_map/attend_back_local/pallas_call | solution.py:398
  329.8 3.6 qkv_grad.2
  336.2 11.2 %collective-permute-done.53 = bf16[320,768]{1,0:T(8,128)(2,1)S(1)} collective-permute-done((bf16[320,768]{1,0:T(8,128)(2,1)S(1)}, bf16[320,768]{1,0:T(8,128)(2,1)S(1)}, u32[]{:S(2)}, u32[]{:S(2)}) %collective-permute-start.53) | collective-permute-done | bytes 491552 | tf_op jit(solution)/shard_map/ppermute | solution.py:25
  352.7 3.1 add_convert_fusion.2
  358.5 9.4 %collective-permute-done.67 = bf16[2,96,1056]{2,1,0:T(8,128)(2,1)S(1)} collective-permute-done((bf16[2,96,1056]{2,1,0:T(8,128)(2,1)S(1)}, bf16[2,96,1056]{2,1,0:T(8,128)(2,1)S(1)}, u32[]{:S(2)}, u32[]{:S(2)}) %collective-permute-start.67) | collective-permute-done | bytes 405536 | tf_op jit(solution)/shard_map/ppermute | solution.py:25
  371.0 2.3 add_convert_fusion.6
  374.3 25.2 %collective-permute-done.58 = bf16[2,96,1056]{2,1,0:T(8,128)(2,1)S(1)} collective-permute-done((bf16[2,96,1056]{2,1,0:T(8,128)(2,1)S(1)}, bf16[2,96,1056]{2,1,0:T(8,128)(2,1)S(1)}, u32[]{:S(2)}, u32[]{:S(2)}) %collective-permute-start.58) | collective-permute-done | bytes 405536 | tf_op jit(solution)/shard_map/ppermute | solution.py:25
  400.6 8.9 %collective-permute-done.60 = bf16[2,96,1056]{2,1,0:T(8,128)(2,1)S(1)} collective-permute-done((bf16[2,96,1056]{2,1,0:T(8,128)(2,1)S(1)}, bf16[2,96,1056]{2,1,0:T(8,128)(2,1)S(1)}, u32[]{:S(2)}, u32[]{:S(2)}) %collective-permute-start.60) | collective-permute-done | bytes 405536 | tf_op jit(solution)/shard_map/ppermute | solution.py:25
  415.5 13.9 %collective-permute-done.59 = bf16[4,96,1056]{2,1,0:T(8,128)(2,1)S(1)} collective-permute-done((bf16[4,96,1056]{2,1,0:T(8,128)(2,1)S(1)}, bf16[4,96,1056]{2,1,0:T(8,128)(2,1)S(1)}, u32[]{:S(2)}, u32[]{:S(2)}) %collective-permute-start.59) | collective-permute-done | bytes 811040 | tf_op jit(solution)/shard_map/ppermute | solution.py:25
  429.4 5.2 %collective-permute-start.72 = (bf16[96,1632]{1,0:T(8,128)(2,1)S(1)}, bf16[96,1632]{1,0:T(8,128)(2,1)S(1)}, u32[]{:S(2)}, u32[]{:S(2)}) collective-permute-start(bf16[96,1632]{1,0:T(8,128)(2,1)S(1)} %get-tuple-element.158), channel_id=1, source_target_pairs={{0,24},{8,0},{16,8},{24,16},{1,25},{9,1},{17,9},{25,17},{2,26},{10... | collective-permute-start | bytes 940040 | tf_op jit(solution)/shard_map/ppermute | solution.py:86
  437.7 2.6 collective-permute-start.63
  441.5 2.7 collective-permute-done.72
  444.2 13.5 %collective-permute-start.65 = (bf16[96,1632]{1,0:T(8,128)(2,1)S(1)}, bf16[96,1632]{1,0:T(8,128)(2,1)S(1)}, u32[]{:S(2)}, u32[]{:S(2)}) collective-permute-start(bf16[96,1632]{1,0:T(8,128)(2,1)S(1)} %get-tuple-element.162), channel_id=1, source_target_pairs={{0,8},{8,16},{16,24},{24,0},{1,9},{9,17},{17,25},{25,1},{2,10},{10... | collective-permute-start | bytes 940040 | tf_op jit(solution)/shard_map/ppermute | solution.py:86
  457.8 18.0 %collective-permute-done.73 = bf16[96,1632]{1,0:T(8,128)(2,1)S(1)} collective-permute-done((bf16[96,1632]{1,0:T(8,128)(2,1)S(1)}, bf16[96,1632]{1,0:T(8,128)(2,1)S(1)}, u32[]{:S(2)}, u32[]{:S(2)}) %collective-permute-start.73) | collective-permute-done | bytes 313376 | tf_op jit(solution)/shard_map/ppermute | solution.py:86
  476.3 8.5 %collective-permute-done.64 = bf16[96,1632]{1,0:T(8,128)(2,1)S(1)} collective-permute-done((bf16[96,1632]{1,0:T(8,128)(2,1)S(1)}, bf16[96,1632]{1,0:T(8,128)(2,1)S(1)}, u32[]{:S(2)}, u32[]{:S(2)}) %collective-permute-start.64) | collective-permute-done | bytes 313376 | tf_op jit(solution)/shard_map/ppermute | solution.py:86
  485.6 3.3 collective-permute-start.81
  491.9 2.3 collective-permute-done.82
  (365 shorter events, 128.0 us)
Async XLA Ops:
  2.9 29.2 %collective-permute-start.5 = (bf16[96,576]{1,0:T(8,128)(2,1)}, bf16[96,576]{1,0:T(8,128)(2,1)}, u32[]{:S(2)}, u32[]{:S(2)}) collective-permute-start(bf16[96,576]{1,0:T(8,128)(2,1)} %copy.39), channel_id=1, source_target_pairs={{0,4},{4,0},{1,5},{5,1},{2,6},{6,2},{3,7},{7,3},{8,12},{12,8},{9,1... | collective-permute-start | bytes 331784 | tf_op jit(solution)/shard_map/ppermute | solution.py:20
  5.8 35.5 %collective-permute-start = (f32[1536]{0:T(1024)}, f32[1536]{0:T(1024)}, u32[]{:S(2)}, u32[]{:S(2)}) collective-permute-start(f32[1536]{0:T(1024)} %reduce), channel_id=1, source_target_pairs={{0,4},{4,0},{1,5},{5,1},{2,6},{6,2},{3,7},{7,3},{8,12},{12,8},{9,1... | collective-permute-start | bytes 18440 | tf_op jit(solution)/shard_map/ppermute | solution.py:20
  9.8 17.7 %collective-permute-start.15 = (bf16[96,1056]{1,0:T(8,128)(2,1)S(1)}, bf16[96,1056]{1,0:T(8,128)(2,1)S(1)}, u32[]{:S(2)}, u32[]{:S(2)}) collective-permute-start(bf16[96,1056]{1,0:T(8,128)(2,1)S(1)} %get-tuple-element.175), channel_id=1, source_target_pairs={{0,16},{8,24},{16,0},{24,8},{1,17},{9,25},{17,1},{25,9},{2,18},{10... | collective-permute-start | bytes 608264 | tf_op jit(solution)/shard_map/ppermute | solution.py:75
  12.4 15.1 %collective-permute-start.16 = (bf16[96,1056]{1,0:T(8,128)(2,1)S(1)}, bf16[96,1056]{1,0:T(8,128)(2,1)S(1)}, u32[]{:S(2)}, u32[]{:S(2)}) collective-permute-start(bf16[96,1056]{1,0:T(8,128)(2,1)S(1)} %get-tuple-element.175), channel_id=1, source_target_pairs={{0,24},{8,0},{16,8},{24,16},{1,25},{9,1},{17,9},{25,17},{2,26},{10... | collective-permute-start | bytes 608264 | tf_op jit(solution)/shard_map/ppermute | solution.py:75
  28.9 25.6 %collective-permute-start.18 = (bf16[4,96,1056]{2,1,0:T(8,128)(2,1)}, bf16[4,96,1056]{2,1,0:T(8,128)(2,1)S(1)}, u32[]{:S(2)}, u32[]{:S(2)}) collective-permute-start(bf16[4,96,1056]{2,1,0:T(8,128)(2,1)} %get-tuple-element.173), channel_id=1, source_target_pairs={{0,2},{1,3},{2,0},{3,1},{4,6},{5,7},{6,4},{7,5},{8,10},{9,11},{10,... | collective-permute-start | bytes 2433032 | tf_op jit(solution)/shard_map/ppermute | solution.py:25
  30.4 24.7 %collective-permute-start.17 = (bf16[4,96,1056]{2,1,0:T(8,128)(2,1)}, bf16[4,96,1056]{2,1,0:T(8,128)(2,1)}, u32[]{:S(2)}, u32[]{:S(2)}) collective-permute-start(bf16[4,96,1056]{2,1,0:T(8,128)(2,1)} %get-tuple-element.173), channel_id=1, source_target_pairs={{0,1},{1,0},{2,3},{3,2},{4,5},{5,4},{6,7},{7,6},{8,9},{9,8},{10,11... | collective-permute-start | bytes 2433032 | tf_op jit(solution)/shard_map/ppermute | solution.py:25
  49.7 16.7 %collective-permute-start.34 = (bf16[96,1056]{1,0:T(8,128)(2,1)S(1)}, bf16[96,1056]{1,0:T(8,128)(2,1)S(1)}, u32[]{:S(2)}, u32[]{:S(2)}) collective-permute-start(bf16[96,1056]{1,0:T(8,128)(2,1)S(1)} %get-tuple-element.75), channel_id=1, source_target_pairs={{0,16},{8,24},{16,0},{24,8},{1,17},{9,25},{17,1},{25,9},{2,18},{10... | collective-permute-start | bytes 608264 | tf_op jit(solution)/shard_map/ppermute | solution.py:75
  51.7 14.6 %collective-permute-start.35 = (bf16[96,1056]{1,0:T(8,128)(2,1)S(1)}, bf16[96,1056]{1,0:T(8,128)(2,1)S(1)}, u32[]{:S(2)}, u32[]{:S(2)}) collective-permute-start(bf16[96,1056]{1,0:T(8,128)(2,1)S(1)} %get-tuple-element.75), channel_id=1, source_target_pairs={{0,24},{8,0},{16,8},{24,16},{1,25},{9,1},{17,9},{25,17},{2,26},{10... | collective-permute-start | bytes 608264 | tf_op jit(solution)/shard_map/ppermute | solution.py:75
  54.6 13.7 %collective-permute-start.19 = (bf16[2,96,1056]{2,1,0:T(8,128)(2,1)S(1)}, bf16[2,96,1056]{2,1,0:T(8,128)(2,1)S(1)}, u32[]{:S(2)}, u32[]{:S(2)}) collective-permute-start(bf16[2,96,1056]{2,1,0:T(8,128)(2,1)S(1)} %slice.306), channel_id=1, source_target_pairs={{0,1},{1,0},{2,3},{3,2},{4,5},{5,4},{6,7},{7,6},{8,9},{9,8},{10,11... | collective-permute-start | bytes 1216520 | tf_op jit(solution)/shard_map/ppermute | solution.py:25
  56.2 12.0 %collective-permute-start.20 = (bf16[2,96,1056]{2,1,0:T(8,128)(2,1)S(1)}, bf16[2,96,1056]{2,1,0:T(8,128)(2,1)S(1)}, u32[]{:S(2)}, u32[]{:S(2)}) collective-permute-start(bf16[2,96,1056]{2,1,0:T(8,128)(2,1)S(1)} %slice.307), channel_id=1, source_target_pairs={{0,2},{1,3},{2,0},{3,1},{4,6},{5,7},{6,4},{7,5},{8,10},{9,11},{10,... | collective-permute-start | bytes 1216520 | tf_op jit(solution)/shard_map/ppermute | solution.py:25
  67.8 35.1 %collective-permute-start.37 = (bf16[4,96,1056]{2,1,0:T(8,128)(2,1)}, bf16[4,96,1056]{2,1,0:T(8,128)(2,1)S(1)}, u32[]{:S(2)}, u32[]{:S(2)}) collective-permute-start(bf16[4,96,1056]{2,1,0:T(8,128)(2,1)} %get-tuple-element.171), channel_id=1, source_target_pairs={{0,2},{1,3},{2,0},{3,1},{4,6},{5,7},{6,4},{7,5},{8,10},{9,11},{10,... | collective-permute-start | bytes 2433032 | tf_op jit(solution)/shard_map/ppermute | solution.py:25
  71.5 65.1 %collective-permute-start.21 = (bf16[4,4,96,1056]{3,2,1,0:T(8,128)(2,1)}, bf16[4,4,96,1056]{3,2,1,0:T(8,128)(2,1)}, u32[]{:S(2)}, u32[]{:S(2)}) collective-permute-start(bf16[4,4,96,1056]{3,2,1,0:T(8,128)(2,1)} %pad_maximum_fusion.mine_ref), channel_id=1, source_target_pairs={{0,4},{4,0},{1,5},{5,1},{2,6},{6,2},{3,7},{7,3},{8,12},{12,8},{9,1... | collective-permute-start | bytes 9732104 | tf_op jit(solution)/shard_map/ppermute | solution.py:20
  71.8 28.2 %collective-permute-start.2 = (bf16[320,768]{1,0:T(8,128)(2,1)S(1)}, bf16[320,768]{1,0:T(8,128)(2,1)S(1)}, u32[]{:S(2)}, u32[]{:S(2)}) collective-permute-start(bf16[320,768]{1,0:T(8,128)(2,1)S(1)} %fusion.22.own_ref), channel_id=1, source_target_pairs={{0,2},{1,3},{2,0},{3,1},{4,6},{5,7},{6,4},{7,5},{8,10},{9,11},{10,... | collective-permute-start | bytes 1474568 | tf_op jit(solution)/shard_map/ppermute | solution.py:25
  73.3 27.4 %collective-permute-start.1 = (bf16[320,768]{1,0:T(8,128)(2,1)S(1)}, bf16[320,768]{1,0:T(8,128)(2,1)S(1)}, u32[]{:S(2)}, u32[]{:S(2)}) collective-permute-start(bf16[320,768]{1,0:T(8,128)(2,1)S(1)} %fusion.22.own_ref), channel_id=1, source_target_pairs={{0,1},{1,0},{2,3},{3,2},{4,5},{5,4},{6,7},{7,6},{8,9},{9,8},{10,11... | collective-permute-start | bytes 1474568 | tf_op jit(solution)/shard_map/ppermute | solution.py:25
  73.9 32.6 %collective-permute-start.36 = (bf16[4,96,1056]{2,1,0:T(8,128)(2,1)}, bf16[4,96,1056]{2,1,0:T(8,128)(2,1)}, u32[]{:S(2)}, u32[]{:S(2)}) collective-permute-start(bf16[4,96,1056]{2,1,0:T(8,128)(2,1)} %get-tuple-element.171), channel_id=1, source_target_pairs={{0,1},{1,0},{2,3},{3,2},{4,5},{5,4},{6,7},{7,6},{8,9},{9,8},{10,11... | collective-permute-start | bytes 2433032 | tf_op jit(solution)/shard_map/ppermute | solution.py:25
  100.0 12.9 %collective-permute-start.9 = (bf16[4,96,576]{2,1,0:T(8,128)(2,1)S(1)}, bf16[4,96,576]{2,1,0:T(8,128)(2,1)}, u32[]{:S(2)}, u32[]{:S(2)}) collective-permute-start(bf16[4,96,576]{2,1,0:T(8,128)(2,1)S(1)} %pad_maximum_fusion.10.mine_ref), channel_id=1, source_target_pairs={{0,4},{4,0},{1,5},{5,1},{2,6},{6,2},{3,7},{7,3},{8,12},{12,8},{9,1... | collective-permute-start | bytes 1327112 | tf_op jit(solution)/shard_map/ppermute | solution.py:20
  100.8 12.6 %collective-permute-start.3 = (bf16[160,768]{1,0:T(8,128)(2,1)}, bf16[160,768]{1,0:T(8,128)(2,1)S(1)}, u32[]{:S(2)}, u32[]{:S(2)}) collective-permute-start(bf16[160,768]{1,0:T(8,128)(2,1)} %slice.304), channel_id=1, source_target_pairs={{0,1},{1,0},{2,3},{3,2},{4,5},{5,4},{6,7},{7,6},{8,9},{9,8},{10,11... | collective-permute-start | bytes 737288 | tf_op jit(solution)/shard_map/ppermute | solution.py:25
  106.5 44.4 %collective-permute-start.26 = (bf16[96,576]{1,0:T(8,128)(2,1)}, bf16[96,576]{1,0:T(8,128)(2,1)S(1)}, u32[]{:S(2)}, u32[]{:S(2)}) collective-permute-start(bf16[96,576]{1,0:T(8,128)(2,1)} %get-tuple-element.70), channel_id=1, source_target_pairs={{0,8},{8,16},{16,24},{24,0},{1,9},{9,17},{17,25},{25,1},{2,10},{10... | collective-permute-start | bytes 331784 | tf_op jit(solution)/shard_map/ppermute | solution.py:75
  112.9 16.4 %collective-permute-start.38 = (bf16[2,96,1056]{2,1,0:T(8,128)(2,1)S(1)}, bf16[2,96,1056]{2,1,0:T(8,128)(2,1)S(1)}, u32[]{:S(2)}, u32[]{:S(2)}) collective-permute-start(bf16[2,96,1056]{2,1,0:T(8,128)(2,1)S(1)} %slice.312), channel_id=1, source_target_pairs={{0,1},{1,0},{2,3},{3,2},{4,5},{5,4},{6,7},{7,6},{8,9},{9,8},{10,11... | collective-permute-start | bytes 1216520 | tf_op jit(solution)/shard_map/ppermute | solution.py:25
  113.5 17.3 %collective-permute-start.39 = (bf16[2,96,1056]{2,1,0:T(8,128)(2,1)S(1)}, bf16[2,96,1056]{2,1,0:T(8,128)(2,1)S(1)}, u32[]{:S(2)}, u32[]{:S(2)}) collective-permute-start(bf16[2,96,1056]{2,1,0:T(8,128)(2,1)S(1)} %slice.313), channel_id=1, source_target_pairs={{0,2},{1,3},{2,0},{3,1},{4,6},{5,7},{6,4},{7,5},{8,10},{9,11},{10,... | collective-permute-start | bytes 1216520 | tf_op jit(solution)/shard_map/ppermute | solution.py:25
  135.0 65.3 %collective-permute-start.40 = (bf16[4,4,96,1056]{3,2,1,0:T(8,128)(2,1)}, bf16[4,4,96,1056]{3,2,1,0:T(8,128)(2,1)}, u32[]{:S(2)}, u32[]{:S(2)}) collective-permute-start(bf16[4,4,96,1056]{3,2,1,0:T(8,128)(2,1)} %pad_maximum_fusion.1.mine_ref), channel_id=1, source_target_pairs={{0,4},{4,0},{1,5},{5,1},{2,6},{6,2},{3,7},{7,3},{8,12},{12,8},{9,1... | collective-permute-start | bytes 9732104 | tf_op jit(solution)/shard_map/ppermute | solution.py:20
  146.5 12.4 %collective-permute-start.23 = (bf16[320,768]{1,0:T(8,128)(2,1)S(1)}, bf16[320,768]{1,0:T(8,128)(2,1)S(1)}, u32[]{:S(2)}, u32[]{:S(2)}) collective-permute-start(bf16[320,768]{1,0:T(8,128)(2,1)S(1)} %get-tuple-element.69.own_ref), channel_id=1, source_target_pairs={{0,2},{1,3},{2,0},{3,1},{4,6},{5,7},{6,4},{7,5},{8,10},{9,11},{10,... | collective-permute-start | bytes 1474568 | tf_op jit(solution)/shard_map/ppermute | solution.py:25
  147.2 14.1 %collective-permute-start.22 = (bf16[320,768]{1,0:T(8,128)(2,1)S(1)}, bf16[320,768]{1,0:T(8,128)(2,1)S(1)}, u32[]{:S(2)}, u32[]{:S(2)}) collective-permute-start(bf16[320,768]{1,0:T(8,128)(2,1)S(1)} %get-tuple-element.69.own_ref), channel_id=1, source_target_pairs={{0,1},{1,0},{2,3},{3,2},{4,5},{5,4},{6,7},{7,6},{8,9},{9,8},{10,11... | collective-permute-start | bytes 1474568 | tf_op jit(solution)/shard_map/ppermute | solution.py:25
  264.9 87.8 %collective-permute-start.66 = (bf16[4,4,96,1056]{3,2,1,0:T(8,128)(2,1)}, bf16[4,4,96,1056]{3,2,1,0:T(8,128)(2,1)}, u32[]{:S(2)}, u32[]{:S(2)}) collective-permute-start(bf16[4,4,96,1056]{3,2,1,0:T(8,128)(2,1)} %get-tuple-element.114), channel_id=1, source_target_pairs={{0,4},{4,0},{1,5},{5,1},{2,6},{6,2},{3,7},{7,3},{8,12},{12,8},{9,1... | collective-permute-start | bytes 9732104 | tf_op jit(solution)/shard_map/ppermute | solution.py:20
  269.8 14.1 %collective-permute-start.46 = (bf16[320,768]{1,0:T(8,128)(2,1)S(1)}, bf16[320,768]{1,0:T(8,128)(2,1)S(1)}, u32[]{:S(2)}, u32[]{:S(2)}) collective-permute-start(bf16[320,768]{1,0:T(8,128)(2,1)S(1)} %pad_maximum_fusion.12), channel_id=1, source_target_pairs={{0,1},{1,0},{2,3},{3,2},{4,5},{5,4},{6,7},{7,6},{8,9},{9,8},{10,11... | collective-permute-start | bytes 1474568 | tf_op jit(solution)/shard_map/ppermute | solution.py:25
  273.9 12.5 %collective-permute-start.48 = (bf16[320,768]{1,0:T(8,128)(2,1)S(1)}, bf16[320,768]{1,0:T(8,128)(2,1)S(1)}, u32[]{:S(2)}, u32[]{:S(2)}) collective-permute-start(bf16[320,768]{1,0:T(8,128)(2,1)S(1)} %pad_maximum_fusion.13), channel_id=1, source_target_pairs={{0,2},{1,3},{2,0},{3,1},{4,6},{5,7},{6,4},{7,5},{8,10},{9,11},{10,... | collective-permute-start | bytes 1474568 | tf_op jit(solution)/shard_map/ppermute | solution.py:25
  279.7 30.4 %collective-permute-start.71 = (bf16[4,96,576]{2,1,0:T(8,128)(2,1)S(1)}, bf16[4,96,576]{2,1,0:T(8,128)(2,1)S(1)}, u32[]{:S(2)}, u32[]{:S(2)}) collective-permute-start(bf16[4,96,576]{2,1,0:T(8,128)(2,1)S(1)} %get-tuple-element.118), channel_id=1, source_target_pairs={{0,4},{4,0},{1,5},{5,1},{2,6},{6,2},{3,7},{7,3},{8,12},{12,8},{9,1... | collective-permute-start | bytes 1327112 | tf_op jit(solution)/shard_map/ppermute | solution.py:20
  311.2 59.8 %collective-permute-start.57 = (bf16[4,4,96,1056]{3,2,1,0:T(8,128)(2,1)}, bf16[4,4,96,1056]{3,2,1,0:T(8,128)(2,1)}, u32[]{:S(2)}, u32[]{:S(2)}) collective-permute-start(bf16[4,4,96,1056]{3,2,1,0:T(8,128)(2,1)} %get-tuple-element.108), channel_id=1, source_target_pairs={{0,4},{4,0},{1,5},{5,1},{2,6},{6,2},{3,7},{7,3},{8,12},{12,8},{9,1... | collective-permute-start | bytes 9732104 | tf_op jit(solution)/shard_map/ppermute | solution.py:20
  333.7 13.7 %collective-permute-start.53 = (bf16[320,768]{1,0:T(8,128)(2,1)S(1)}, bf16[320,768]{1,0:T(8,128)(2,1)S(1)}, u32[]{:S(2)}, u32[]{:S(2)}) collective-permute-start(bf16[320,768]{1,0:T(8,128)(2,1)S(1)} %pad_maximum_fusion.14), channel_id=1, source_target_pairs={{0,1},{1,0},{2,3},{3,2},{4,5},{5,4},{6,7},{7,6},{8,9},{9,8},{10,11... | collective-permute-start | bytes 1474568 | tf_op jit(solution)/shard_map/ppermute | solution.py:25
  335.3 13.4 %collective-permute-start.55 = (bf16[320,768]{1,0:T(8,128)(2,1)S(1)}, bf16[320,768]{1,0:T(8,128)(2,1)S(1)}, u32[]{:S(2)}, u32[]{:S(2)}) collective-permute-start(bf16[320,768]{1,0:T(8,128)(2,1)S(1)} %pad_maximum_fusion.15), channel_id=1, source_target_pairs={{0,2},{1,3},{2,0},{3,1},{4,6},{5,7},{6,4},{7,5},{8,10},{9,11},{10,... | collective-permute-start | bytes 1474568 | tf_op jit(solution)/shard_map/ppermute | solution.py:25
  351.1 85.4 %collective-permute-start.77 = (f32[4,96]{1,0:T(4,128)S(1)}, f32[4,96]{1,0:T(4,128)S(1)}, u32[]{:S(2)}, u32[]{:S(2)}) collective-permute-start(f32[4,96]{1,0:T(4,128)S(1)} %bitcast.201), channel_id=1, source_target_pairs={{0,1},{1,0},{2,3},{3,2},{4,5},{5,4},{6,7},{7,6},{8,9},{9,8},{10,11... | collective-permute-start | bytes 4616 | tf_op jit(solution)/shard_map/ppermute | solution.py:25
  351.8 86.0 %collective-permute-start.78 = (f32[4,96]{1,0:T(4,128)S(1)}, f32[4,96]{1,0:T(4,128)S(1)}, u32[]{:S(2)}, u32[]{:S(2)}) collective-permute-start(f32[4,96]{1,0:T(4,128)S(1)} %bitcast.200), channel_id=1, source_target_pairs={{0,2},{1,3},{2,0},{3,1},{4,6},{5,7},{6,4},{7,5},{8,10},{9,11},{10,... | collective-permute-start | bytes 4616 | tf_op jit(solution)/shard_map/ppermute | solution.py:25
  355.9 12.1 %collective-permute-start.67 = (bf16[2,96,1056]{2,1,0:T(8,128)(2,1)S(1)}, bf16[2,96,1056]{2,1,0:T(8,128)(2,1)S(1)}, u32[]{:S(2)}, u32[]{:S(2)}) collective-permute-start(bf16[2,96,1056]{2,1,0:T(8,128)(2,1)S(1)} %get-tuple-element.166), channel_id=1, source_target_pairs={{0,2},{1,3},{2,0},{3,1},{4,6},{5,7},{6,4},{7,5},{8,10},{9,11},{10,... | collective-permute-start | bytes 1216520 | tf_op jit(solution)/shard_map/ppermute | solution.py:25
  357.1 12.4 %collective-permute-start.69 = (bf16[2,96,1056]{2,1,0:T(8,128)(2,1)S(1)}, bf16[2,96,1056]{2,1,0:T(8,128)(2,1)S(1)}, u32[]{:S(2)}, u32[]{:S(2)}) collective-permute-start(bf16[2,96,1056]{2,1,0:T(8,128)(2,1)S(1)} %get-tuple-element.167), channel_id=1, source_target_pairs={{0,1},{1,0},{2,3},{3,2},{4,5},{5,4},{6,7},{7,6},{8,9},{9,8},{10,11... | collective-permute-start | bytes 1216520 | tf_op jit(solution)/shard_map/ppermute | solution.py:25
  368.2 42.9 %collective-permute-start.68 = (bf16[4,96,1056]{2,1,0:T(8,128)(2,1)S(1)}, bf16[4,96,1056]{2,1,0:T(8,128)(2,1)S(1)}, u32[]{:S(2)}, u32[]{:S(2)}) collective-permute-start(bf16[4,96,1056]{2,1,0:T(8,128)(2,1)S(1)} %pad_maximum_fusion.8), channel_id=1, source_target_pairs={{0,1},{1,0},{2,3},{3,2},{4,5},{5,4},{6,7},{7,6},{8,9},{9,8},{10,11... | collective-permute-start | bytes 2433032 | tf_op jit(solution)/shard_map/ppermute | solution.py:25
  369.7 42.9 %collective-permute-start.70 = (bf16[4,96,1056]{2,1,0:T(8,128)(2,1)S(1)}, bf16[4,96,1056]{2,1,0:T(8,128)(2,1)S(1)}, u32[]{:S(2)}, u32[]{:S(2)}) collective-permute-start(bf16[4,96,1056]{2,1,0:T(8,128)(2,1)S(1)} %pad_maximum_fusion.9), channel_id=1, source_target_pairs={{0,2},{1,3},{2,0},{3,1},{4,6},{5,7},{6,4},{7,5},{8,10},{9,11},{10,... | collective-permute-start | bytes 2433032 | tf_op jit(solution)/shard_map/ppermute | solution.py:25
  373.4 26.1 %collective-permute-start.58 = (bf16[2,96,1056]{2,1,0:T(8,128)(2,1)S(1)}, bf16[2,96,1056]{2,1,0:T(8,128)(2,1)S(1)}, u32[]{:S(2)}, u32[]{:S(2)}) collective-permute-start(bf16[2,96,1056]{2,1,0:T(8,128)(2,1)S(1)} %get-tuple-element.168), channel_id=1, source_target_pairs={{0,2},{1,3},{2,0},{3,1},{4,6},{5,7},{6,4},{7,5},{8,10},{9,11},{10,... | collective-permute-start | bytes 1216520 | tf_op jit(solution)/shard_map/ppermute | solution.py:25
  409.5 30.9 %collective-permute-start.79 = (f32[4,96]{1,0:T(4,128)S(1)}, f32[4,96]{1,0:T(4,128)S(1)}, u32[]{:S(2)}, u32[]{:S(2)}) collective-permute-start(f32[4,96]{1,0:T(4,128)S(1)} %bitcast.199), channel_id=1, source_target_pairs={{0,3},{1,2},{2,1},{3,0},{4,7},{5,6},{6,5},{7,4},{8,11},{9,10},{10,... | collective-permute-start | bytes 4616 | tf_op jit(solution)/shard_map/ppermute | solution.py:25
  411.1 18.3 %collective-permute-start.59 = (bf16[4,96,1056]{2,1,0:T(8,128)(2,1)S(1)}, bf16[4,96,1056]{2,1,0:T(8,128)(2,1)S(1)}, u32[]{:S(2)}, u32[]{:S(2)}) collective-permute-start(bf16[4,96,1056]{2,1,0:T(8,128)(2,1)S(1)} %pad_maximum_fusion.6), channel_id=1, source_target_pairs={{0,1},{1,0},{2,3},{3,2},{4,5},{5,4},{6,7},{7,6},{8,9},{9,8},{10,11... | collective-permute-start | bytes 2433032 | tf_op jit(solution)/shard_map/ppermute | solution.py:25
  412.6 22.0 %collective-permute-start.61 = (bf16[4,96,1056]{2,1,0:T(8,128)(2,1)S(1)}, bf16[4,96,1056]{2,1,0:T(8,128)(2,1)S(1)}, u32[]{:S(2)}, u32[]{:S(2)}) collective-permute-start(bf16[4,96,1056]{2,1,0:T(8,128)(2,1)S(1)} %pad_maximum_fusion.7), channel_id=1, source_target_pairs={{0,2},{1,3},{2,0},{3,1},{4,6},{5,7},{6,4},{7,5},{8,10},{9,11},{10,... | collective-permute-start | bytes 2433032 | tf_op jit(solution)/shard_map/ppermute | solution.py:25
  429.4 14.8 %collective-permute-start.72 = (bf16[96,1632]{1,0:T(8,128)(2,1)S(1)}, bf16[96,1632]{1,0:T(8,128)(2,1)S(1)}, u32[]{:S(2)}, u32[]{:S(2)}) collective-permute-start(bf16[96,1632]{1,0:T(8,128)(2,1)S(1)} %get-tuple-element.158), channel_id=1, source_target_pairs={{0,24},{8,0},{16,8},{24,16},{1,25},{9,1},{17,9},{25,17},{2,26},{10... | collective-permute-start | bytes 940040 | tf_op jit(solution)/shard_map/ppermute | solution.py:86
  434.6 41.2 %collective-permute-start.73 = (bf16[96,1632]{1,0:T(8,128)(2,1)S(1)}, bf16[96,1632]{1,0:T(8,128)(2,1)S(1)}, u32[]{:S(2)}, u32[]{:S(2)}) collective-permute-start(bf16[96,1632]{1,0:T(8,128)(2,1)S(1)} %get-tuple-element.160), channel_id=1, source_target_pairs={{0,16},{8,24},{16,0},{24,8},{1,17},{9,25},{17,1},{25,9},{2,18},{10... | collective-permute-start | bytes 940040 | tf_op jit(solution)/shard_map/ppermute | solution.py:86
  436.5 39.3 %collective-permute-start.74 = (bf16[96,1632]{1,0:T(8,128)(2,1)S(1)}, bf16[96,1632]{1,0:T(8,128)(2,1)S(1)}, u32[]{:S(2)}, u32[]{:S(2)}) collective-permute-start(bf16[96,1632]{1,0:T(8,128)(2,1)S(1)} %get-tuple-element.159), channel_id=1, source_target_pairs={{0,8},{8,16},{16,24},{24,0},{1,9},{9,17},{17,25},{25,1},{2,10},{10... | collective-permute-start | bytes 940040 | tf_op jit(solution)/shard_map/ppermute | solution.py:86
  437.7 38.6 %collective-permute-start.63 = (bf16[96,1632]{1,0:T(8,128)(2,1)S(1)}, bf16[96,1632]{1,0:T(8,128)(2,1)S(1)}, u32[]{:S(2)}, u32[]{:S(2)}) collective-permute-start(bf16[96,1632]{1,0:T(8,128)(2,1)S(1)} %get-tuple-element.161), channel_id=1, source_target_pairs={{0,24},{8,0},{16,8},{24,16},{1,25},{9,1},{17,9},{25,17},{2,26},{10... | collective-permute-start | bytes 940040 | tf_op jit(solution)/shard_map/ppermute | solution.py:86
  440.4 44.5 %collective-permute-start.64 = (bf16[96,1632]{1,0:T(8,128)(2,1)S(1)}, bf16[96,1632]{1,0:T(8,128)(2,1)S(1)}, u32[]{:S(2)}, u32[]{:S(2)}) collective-permute-start(bf16[96,1632]{1,0:T(8,128)(2,1)S(1)} %get-tuple-element.163), channel_id=1, source_target_pairs={{0,16},{8,24},{16,0},{24,8},{1,17},{9,25},{17,1},{25,9},{2,18},{10... | collective-permute-start | bytes 940040 | tf_op jit(solution)/shard_map/ppermute | solution.py:86
  444.2 40.7 %collective-permute-start.65 = (bf16[96,1632]{1,0:T(8,128)(2,1)S(1)}, bf16[96,1632]{1,0:T(8,128)(2,1)S(1)}, u32[]{:S(2)}, u32[]{:S(2)}) collective-permute-start(bf16[96,1632]{1,0:T(8,128)(2,1)S(1)} %get-tuple-element.162), channel_id=1, source_target_pairs={{0,8},{8,16},{16,24},{24,0},{1,9},{9,17},{17,25},{25,1},{2,10},{10... | collective-permute-start | bytes 940040 | tf_op jit(solution)/shard_map/ppermute | solution.py:86
  475.8 13.1 %collective-permute-start.41 = (bf16[320,768]{1,0:T(8,128)(2,1)S(1)}, bf16[320,768]{1,0:T(8,128)(2,1)S(1)}, u32[]{:S(2)}, u32[]{:S(2)}) collective-permute-start(bf16[320,768]{1,0:T(8,128)(2,1)S(1)} %copy-done.42), channel_id=1, source_target_pairs={{0,4},{4,0},{1,5},{5,1},{2,6},{6,2},{3,7},{7,3},{8,12},{12,8},{9,1... | collective-permute-start | bytes 1474568 | tf_op jit(solution)/shard_map/ppermute | solution.py:20
  475.8 18.9 %collective-permute-start.56 = (f32[320,768]{1,0:T(8,128)S(1)}, f32[320,768]{1,0:T(8,128)S(1)}, u32[]{:S(2)}, u32[]{:S(2)}) collective-permute-start(f32[320,768]{1,0:T(8,128)S(1)} %convert_select_fusion), channel_id=1, source_target_pairs={{0,4},{4,0},{1,5},{5,1},{2,6},{6,2},{3,7},{7,3},{8,12},{12,8},{9,1... | collective-permute-start | bytes 2949128 | tf_op jit(solution)/shard_map/ppermute | solution.py:20
  (90 other events, 951.0 us)

commit v3 on v2

--- a/solution.py
+++ b/solution.py
@@ -13,7 +13,7 @@
 BLOCK = 256
 BF16 = jnp.bfloat16
 F32 = jnp.float32
-VMEM_BYTES = 48 * 1024 * 1024
+VMEM_BYTES = 36 * 1024 * 1024
 
 
 def swap_cores(block):
@@ -33,58 +33,84 @@
     return lax.dynamic_index_in_dim(buffer, index, 0, keepdims=False)
 
 
-def spread_tensor(block):
-    half = block.shape[0] // 2
-    one = to_mate(block, 1)
-    two = to_mate(block, 2)
-    return block, one, two, to_mate(two[:half], 1), to_mate(one[half:], 2)
-
-
-def scatter_tensor(own, one, two, far):
+def to_neighbours(block):
+    return to_mate(block, 1), to_mate(block, 2)
+
+
+def to_far(one, two):
+    half = one.shape[0] // 2
+    return to_mate(two[:half], 1), to_mate(one[half:], 2)
+
+
+def after(blocks, *earlier):
+    return lax.optimization_barrier((blocks, earlier))[0]
+
+
+def far_terms(far):
     half = far.shape[0] // 2
-    low = far.dtype
-    head = to_mate(far[:half], 1)
-    tail = to_mate(far[half:], 2)
-    one = jnp.concatenate([one[:half], (one[half:].astype(F32) + tail.astype(F32)).astype(low)], 0)
-    two = jnp.concatenate([(two[:half].astype(F32) + head.astype(F32)).astype(low), two[half:]], 0)
-    from_one = to_mate(one, 1)
-    from_two = to_mate(two, 2)
-    return own.astype(F32) + from_one.astype(F32) + from_two.astype(F32)
+    return to_mate(far[:half], 1), to_mate(far[half:], 2)
+
+
+def near_terms(one, two, head, tail):
+    half = head.shape[0]
+    one = jnp.concatenate([one[:half], add_low(one[half:], tail)], 0)
+    two = jnp.concatenate([add_low(two[:half], head), two[half:]], 0)
+    return one, two
+
+
+def to_near(pair):
+    return to_mate(pair[0], 1), to_mate(pair[1], 2)
+
+
+def slot_sums(kept, came, near):
+    return [
+        add_up(kept[0][slot], came[0][slot], near[0][slot], near[1][slot]).astype(BF16)
+        for slot in range(kept.shape[1])
+    ]
+
+
+def add_low(left, right):
+    return (left.astype(F32) + right.astype(F32)).astype(BF16)
+
+
+def add_up(*terms):
+    return sum(term.astype(F32) for term in terms)
 
 
 def swap_tensor(blocks):
     return (blocks[0],) + tuple(to_mate(blocks[bit], bit) for bit in (1, 2, 3))
 
 
-def after(block, *earlier):
-    return lax.optimization_barrier((block,) + earlier)[0]
-
-
-def few_dp():
-    return lax.axis_size("dp") <= 4
-
-
-def ring(step):
-    size = lax.axis_size("dp")
-    return [(i, (i + step) % size) for i in range(size)]
+def four_dp():
+    return lax.axis_size("dp") == 4
+
+
+def to_peer(block, bit):
+    return lax.ppermute(block, "dp", [(i, i ^ bit) for i in range(4)])
 
 
 def gather_dp(block):
-    if not few_dp():
-        return lax.all_gather(block, "dp", axis=0)
-    moved = [lax.ppermute(block, "dp", ring(step)) for step in range(1, lax.axis_size("dp"))]
-    return jnp.stack([block] + moved)
-
-
-def scatter_dp(blocks, low):
-    if not few_dp():
-        return lax.psum_scatter(
-            blocks.astype(low), "dp", scatter_dimension=0, tiled=False
-        ).astype(F32)
-    total = blocks[0]
-    for step in range(1, lax.axis_size("dp")):
-        total = total + lax.ppermute(blocks[step].astype(low), "dp", ring(-step)).astype(F32)
-    return total
+    if four_dp():
+        return [block] + [to_peer(block, bit) for bit in (1, 2, 3)]
+    return [lax.all_gather(block, "dp", axis=0)]
+
+
+def stacked(blocks, low, high):
+    if four_dp():
+        return jnp.stack([block[low:high] for block in blocks])
+    return blocks[0][:, low:high]
+
+
+def scatter_dp(blocks):
+    return tuple(to_peer(blocks[bit], bit) for bit in (1, 2, 3)) if four_dp() else ()
+
+
+def scatter_sum(blocks, came):
+    if four_dp():
+        return add_up(blocks[0], *came)
+    return lax.psum_scatter(
+        jnp.stack(blocks), "dp", scatter_dimension=0, tiled=False
+    ).astype(F32)
 
 
 def join_halves(mine, other, axis):
@@ -106,24 +132,30 @@
 
 def placement():
     me = lax.axis_index("tensor")
-    if not few_dp():
+    if not four_dp():
         return jnp.stack([me, 0, 0]).astype(jnp.int32)
-    n = lax.axis_size("dp")
-    slots = [(lax.axis_index("dp") - step) % n for step in range(n)]
+    slots = [lax.axis_index("dp") ^ bit for bit in range(4)]
     return jnp.stack([me, lax.axis_index("pipe")] + slots).astype(jnp.int32)
 
 
-def halves(gathered):
-    other = swap_cores(gathered)
-    if few_dp():
-        return gathered, other
-    both = join_halves(gathered, other, gathered.ndim - 2)
-    both = both.reshape(gathered.shape[:-3] + (2, -1, gathered.shape[-1]))
+def halves(block):
+    other = swap_cores(block)
+    if four_dp():
+        return block, other
+    both = join_halves(block, other, block.ndim - 2)
+    both = both.reshape(block.shape[:-3] + (2, -1, block.shape[-1]))
     return both[..., :1, :, :], both[..., 1:, :, :]
 
 
+def piece_halves(pieces):
+    if four_dp():
+        return pieces, tuple(swap_cores(piece) for piece in pieces)
+    whole = pieces[:3] + (jnp.concatenate(pieces[3:], 0),)
+    return tuple(zip(*(halves(piece) for piece in whole)))
+
+
 def half_sums(mine, other):
-    if few_dp():
+    if four_dp():
         return mine, swap_cores(other)
     core = lax.axis_index("pipe")
     n = lax.axis_size("dp")
@@ -134,10 +166,6 @@
     return kept, swap_cores(lax.dynamic_index_in_dim(full, 1 - core, axis, keepdims=False))
 
 
-def add_low(left, right):
-    return (left.astype(F32) + right.astype(F32)).astype(BF16)
-
-
 def own_layer(first, second):
     core = lax.axis_index("pipe")
     mine = jnp.where(core == 0, first, second)
@@ -175,27 +203,32 @@
     )
 
 
-def run_all(copies):
-    for copy in copies:
-        copy.start()
-    for copy in copies:
-        copy.wait()
-
-
 def slot_rows(place_ref, slot, half, rows):
     return pl.ds(pl.multiple_of((place_ref[2 + slot] * 2 + half) * rows, rows), rows)
 
 
-def half_copies(place_ref, mine_ref, other_ref, whole_ref, sems, outward):
+def load_halves(place_ref, mine_ref, other_ref, whole_ref, low=0):
     core = place_ref[1]
     slots, rows = mine_ref.shape[0], mine_ref.shape[1]
-    copies = []
+    packed = mine_ref.shape[2] == 2 * whole_ref.shape[1]
     for slot in range(slots):
-        for part, (ref, half) in enumerate(((mine_ref, core), (other_ref, 1 - core))):
-            inside = whole_ref.at[slot_rows(place_ref, slot, half, rows), :]
-            pair = (inside, ref.at[slot]) if outward else (ref.at[slot], inside)
-            copies.append(pltpu.make_async_copy(*pair, sems.at[slot, part]))
-    return copies
+        for ref, half in ((mine_ref, core), (other_ref, 1 - core)):
+            target = slot_rows(place_ref, low + slot, half, 2 * rows if packed else rows)
+            whole_ref[target, :] = unpack(ref[slot]) if packed else ref[slot]
+
+
+def store_halves(place_ref, whole_ref, mine_ref, other_ref, columns):
+    core = place_ref[1]
+    slots, rows = mine_ref.shape[0], mine_ref.shape[1]
+    for slot in range(slots):
+        for ref, half in ((mine_ref, core), (other_ref, 1 - core)):
+            ref[slot, :, columns] = whole_ref[slot_rows(place_ref, slot, half, rows), columns]
+
+
+def load_pieces(place_ref, mine_refs, other_refs, whole_ref):
+    for index, (mine_ref, other_ref) in enumerate(zip(mine_refs, other_refs)):
+        low = mine_refs[3].shape[0] if index == 4 else 0
+        load_halves(place_ref, mine_ref, other_ref, whole_ref.at[min(index, 3)], low)
 
 
 def pack(block):
@@ -208,7 +241,6 @@
     return jnp.concatenate([block[:, :half], block[:, half:]], 0)
 
 
-ANYWHERE = pl.BlockSpec(memory_space=pl.ANY)
 SCALARS = pl.BlockSpec(memory_space=pltpu.SMEM)
 WHOLE = pl.BlockSpec(memory_space=pltpu.VMEM)
 
@@ -229,22 +261,20 @@
     span, place_ref, own_ref, one_ref, two_ref, head_ref, tail_ref, mine_ref, other_ref,
     cos_ref, sin_ref, first_ref, last_ref,
     mixed0_ref, mixed1_ref, mixed2_ref, mixed3_ref, queries_ref, keys_ref, values_ref, mass_ref,
-    normed_ref, qkv_ref, key_rows, value_rows, proj, mixed_rows, sems, weight_sems,
+    normed_ref, qkv_ref, key_rows, value_rows, proj, mixed_rows,
 ):
     width, rows = queries_ref.shape
     heads = width // HEAD_DIM
     half = HEAD_DIM // 2
     local = rows // 4
     me = place_ref[0]
-    copies = half_copies(place_ref, mine_ref, other_ref, qkv_ref, weight_sems, False)
+    load_halves(place_ref, mine_ref, other_ref, qkv_ref)
     pieces = (
         (own_ref, 0, 0), (one_ref, 1, 0), (two_ref, 2, 0), (head_ref, 3, 0), (tail_ref, 3, local // 2)
     )
-    for index, (ref, bit, shift) in enumerate(pieces):
+    for ref, bit, shift in pieces:
         low = pl.multiple_of((me ^ bit) * local + shift, local // 2)
-        target = normed_ref.at[pl.ds(low, ref.shape[0]), :]
-        copies.append(pltpu.make_async_copy(ref, target, sems.at[index]))
-    run_all(copies)
+        normed_ref[pl.ds(low, ref.shape[0]), :] = ref[...]
     proj[...] = dot(qkv_ref[...].T, normed_ref[...], NT)
     cosines, sines = cos_ref[...], sin_ref[...]
     for head in range(heads):
@@ -292,10 +322,9 @@
         ref[...] = pack(mixed_rows[pl.ds(low, local), :])
 
 
-def attend(place, pieces, mine, other, cosines, sines, first, last, is_local):
+def attend(place, pieces, mine, other, width, cosines, sines, first, last, is_local):
     local, model = pieces[0].shape
     rows = 4 * local
-    width = mine.shape[2] // 3
     heads = width // HEAD_DIM
     span = min(rows, BLOCK + WINDOW) if is_local else rows
     shape = jax.ShapeDtypeStruct((width, rows), BF16)
@@ -307,14 +336,12 @@
             jax.ShapeDtypeStruct((rows, model), BF16),
             jax.ShapeDtypeStruct((model, 3 * width), BF16),
         ),
-        in_specs=[SCALARS] + [ANYWHERE] * 7 + [WHOLE] * 4,
+        in_specs=[SCALARS] + [WHOLE] * 11,
         scratch_shapes=[
             pltpu.VMEM((heads, rows, HEAD_DIM), BF16),
             pltpu.VMEM((heads, rows, HEAD_DIM), BF16),
             pltpu.VMEM((3 * width, rows), F32),
             pltpu.VMEM((rows, width), BF16),
-            pltpu.SemaphoreType.DMA((5,)),
-            pltpu.SemaphoreType.DMA((mine.shape[0], 2)),
         ],
         compiler_params=pltpu.CompilerParams(vmem_limit_bytes=VMEM_BYTES),
         cost_estimate=cost(11 if is_local else 20),
@@ -410,26 +437,24 @@
     )(place, queries, keys, values, mass, *grads, cosines, sines, first, last, qkv)
 
 
-def qkv_grad_kernel(place_ref, normed_ref, grad_ref, mine_ref, other_ref, whole, sems):
-    whole[...] = dot(normed_ref[...].T, grad_ref[...], NN).astype(BF16)
-    run_all(half_copies(place_ref, mine_ref, other_ref, whole, sems, True))
-
-
-def qkv_grad(place, normed, grad, shape):
+def qkv_grad_kernel(place_ref, normed_ref, grad_ref, qkv_ref, mine_ref, other_ref, gain_ref, whole):
+    grad = dot(normed_ref[...].T, grad_ref[...], NN)
+    gain_ref[...] = jnp.sum(grad * qkv_ref[...].astype(F32), axis=1, keepdims=True)
+    whole[...] = grad.astype(BF16)
+    store_halves(place_ref, whole, mine_ref, other_ref, slice(None))
+
+
+def qkv_grad(place, normed, grad, qkv, shape):
     part = jax.ShapeDtypeStruct(shape, BF16)
     return pl.pallas_call(
         qkv_grad_kernel,
-        out_shape=(part, part),
-        in_specs=[SCALARS, WHOLE, WHOLE],
-        out_specs=(ANYWHERE, ANYWHERE),
-        scratch_shapes=[
-            pltpu.VMEM((normed.shape[1], grad.shape[1]), BF16),
-            pltpu.SemaphoreType.DMA((shape[0], 2)),
-        ],
+        out_shape=(part, part, jax.ShapeDtypeStruct((qkv.shape[0], 1), F32)),
+        in_specs=[SCALARS, WHOLE, WHOLE, WHOLE],
+        scratch_shapes=[pltpu.VMEM((normed.shape[1], grad.shape[1]), BF16)],
         compiler_params=pltpu.CompilerParams(vmem_limit_bytes=VMEM_BYTES),
         cost_estimate=cost(4),
         name="qkv_grad",
-    )(place, normed, grad)
+    )(place, normed, grad, qkv)
 
 
 def erf_parts(gate):
@@ -438,19 +463,14 @@
     return cumulative, density
 
 
-def token_kernel(
-    pair, place_ref, mixed0_ref, mixed1_ref, mixed2_ref, mixed3_ref, in_ref, mine_ref, other_ref,
-    gain_ref, next_ref, mid_ref, out_ref, normed_ref, sums, mats, sems,
-):
+def token_kernel(pair, place_ref, mixed0_ref, mixed1_ref, mixed2_ref, mixed3_ref, in_ref, *refs):
+    pieces = (len(refs) - 7) // 2
+    mine_refs, other_refs = refs[:pieces], refs[pieces : 2 * pieces]
+    gain_ref, next_ref, mid_ref, out_ref, normed_ref, sums, mats = refs[2 * pieces :]
     parts = mats.shape[0]
     width = mixed0_ref.shape[1] // 2
     units = pair // 2
-    copies = []
-    for part in range(parts):
-        copies += half_copies(
-            place_ref, mine_ref.at[part], other_ref.at[part], mats.at[part], sems.at[part], False
-        )
-    run_all(copies)
+    load_pieces(place_ref, mine_refs, other_refs, mats)
     mid = in_ref[...].astype(F32)
     for part, ref in enumerate((mixed0_ref, mixed1_ref, mixed2_ref, mixed3_ref)):
         mid += dot(unpack(ref[...]), mats[part, :, pair : pair + width], NT)
@@ -462,7 +482,7 @@
         gate_up = dot(normed, mats[part, :, :pair], NN)
         gate = gate_up[:, :units]
         hidden = (gate * erf_parts(gate)[0] * gate_up[:, units:]).astype(BF16)
-        sums[...] += dot(hidden, mats[part, :, pair + width :], NT)
+        sums[...] += dot(hidden, mats[part, :, pair + width : pair + width + units], NT)
         return carry
 
     lax.fori_loop(0, parts, feed, 0)
@@ -473,7 +493,6 @@
 
 def token_forward(place, mixed, layer_in, mine, other, gain, next_gain, pair):
     shape = layer_in.shape
-    parts, slots = mine.shape[:2]
     return pl.pallas_call(
         functools.partial(token_kernel, pair),
         out_shape=(
@@ -481,33 +500,28 @@
             jax.ShapeDtypeStruct(shape, BF16),
             jax.ShapeDtypeStruct(shape, BF16),
         ),
-        in_specs=[SCALARS] + [WHOLE] * 5 + [ANYWHERE] * 2 + [WHOLE] * 2,
+        in_specs=[SCALARS] + [WHOLE] * (7 + 2 * len(mine)),
         scratch_shapes=[
             pltpu.VMEM(shape, F32),
-            pltpu.VMEM((parts, shape[1], mine.shape[3]), BF16),
-            pltpu.SemaphoreType.DMA((parts, slots, 2)),
+            pltpu.VMEM((4, shape[1], mine[0].shape[2]), BF16),
         ],
         compiler_params=pltpu.CompilerParams(vmem_limit_bytes=VMEM_BYTES),
         cost_estimate=cost(10),
         name="token_forward",
-    )(place, *mixed, layer_in, mine, other, gain, next_gain)
+    )(place, *mixed, layer_in, *mine, *other, gain, next_gain)
 
 
 def token_back_kernel(
-    pair, place_ref, grad_ref, mid_ref, mixed0_ref, mixed1_ref, mixed2_ref, mixed3_ref,
-    mine_ref, other_ref, gain_ref,
-    mine_grad_ref, other_grad_ref, mixed_grad0_ref, mixed_grad1_ref, mixed_grad2_ref, mixed_grad3_ref,
-    grad_mid_ref, gain_grad_ref, sums, mats, grads, sems,
+    pair, place_ref, grad_ref, mid_ref, mixed0_ref, mixed1_ref, mixed2_ref, mixed3_ref, *refs
 ):
+    pieces = (len(refs) - 12) // 2
+    mine_refs, other_refs = refs[:pieces], refs[pieces : 2 * pieces]
+    (gain_ref, mine_grad_ref, other_grad_ref, mixed_grad0_ref, mixed_grad1_ref, mixed_grad2_ref,
+     mixed_grad3_ref, grad_mid_ref, gain_grad_ref, sums, mats, grads) = refs[2 * pieces :]
     parts = mats.shape[0]
     width = mixed0_ref.shape[1] // 2
     units = pair // 2
-    copies = []
-    for part in range(parts):
-        copies += half_copies(
-            place_ref, mine_ref.at[part], other_ref.at[part], mats.at[part], sems.at[part], False
-        )
-    run_all(copies)
+    load_pieces(place_ref, mine_refs, other_refs, mats)
     grad = grad_ref[...].astype(F32)
     grad_low = grad.astype(BF16)
     grad_flip = grad.T.astype(BF16)
@@ -523,12 +537,16 @@
         cumulative, density = erf_parts(gate)
         gelu = gate * cumulative
         hidden = (gelu * up).astype(BF16)
-        grad_hidden = dot(grad_low, mats[part, :, pair + width :], NN)
+        grad_hidden = dot(grad_low, mats[part, :, pair + width : pair + width + units], NN)
         grad_gate = grad_hidden * up * (cumulative + gate * density)
         grad_up = grad_hidden * gelu
         grad_pair = jnp.concatenate([grad_gate, grad_up], 1).astype(BF16)
-        grads[part, :, pair + width :] = dot(grad_flip, hidden, NN).astype(BF16)
-        grads[part, :, :pair] = dot(normed_flip, grad_pair, NN).astype(BF16)
+        grads[:, pair + width :] = dot(grad_flip, hidden, NN).astype(BF16)
+        grads[:, :pair] = dot(normed_flip, grad_pair, NN).astype(BF16)
+        for columns in (slice(0, pair), slice(pair + width, None)):
+            store_halves(
+                place_ref, grads, mine_grad_ref.at[part], other_grad_ref.at[part], columns
+            )
         sums[...] += dot(grad_pair, mats[part, :, :pair], NT)
         return carry
 
@@ -541,28 +559,20 @@
     mid_flip = grad_mid.T.astype(BF16)
     mixed_refs = (mixed0_ref, mixed1_ref, mixed2_ref, mixed3_ref)
     mixed_grad_refs = (mixed_grad0_ref, mixed_grad1_ref, mixed_grad2_ref, mixed_grad3_ref)
-    copies = []
     for part in range(parts):
         weight = mats[part, :, pair : pair + width]
         mixed_grad_refs[part][...] = pack(dot(mid_low, weight, NN).astype(BF16))
-        grads[part, :, pair : pair + width] = dot(
-            mid_flip, unpack(mixed_refs[part][...]), NN
-        ).astype(BF16)
-        batch = half_copies(
-            place_ref, mine_grad_ref.at[part], other_grad_ref.at[part], grads.at[part],
-            sems.at[part], True,
+        grads[:, pair : pair + width] = dot(mid_flip, unpack(mixed_refs[part][...]), NN).astype(BF16)
+        store_halves(
+            place_ref, grads, mine_grad_ref.at[part], other_grad_ref.at[part],
+            slice(pair, pair + width),
         )
-        for copy in batch:
-            copy.start()
-        copies += batch
-    for copy in copies:
-        copy.wait()
 
 
 def token_back(place, grad, mid, mixed, mine, other, gain, pair):
-    parts, slots = mine.shape[:2]
-    mats = pltpu.VMEM((parts, mid.shape[1], mine.shape[3]), BF16)
-    half = jax.ShapeDtypeStruct(mine.shape, BF16)
+    shape = mine[0].shape
+    total = pair + mixed[0].shape[1] // 2 + pair // 2
+    half = jax.ShapeDtypeStruct((4,) + shape[:2] + (total,), BF16)
     mixed_grad = jax.ShapeDtypeStruct(mixed[0].shape, BF16)
     return pl.pallas_call(
         functools.partial(token_back_kernel, pair),
@@ -571,15 +581,16 @@
             jax.ShapeDtypeStruct(mid.shape, F32),
             jax.ShapeDtypeStruct((1, mid.shape[1]), F32),
         ),
-        in_specs=[SCALARS] + [WHOLE] * 6 + [ANYWHERE] * 2 + [WHOLE],
-        out_specs=(ANYWHERE, ANYWHERE) + (WHOLE,) * 6,
+        in_specs=[SCALARS] + [WHOLE] * (7 + 2 * len(mine)),
         scratch_shapes=[
-            pltpu.VMEM(mid.shape, F32), mats, mats, pltpu.SemaphoreType.DMA((parts, slots, 2)),
+            pltpu.VMEM(mid.shape, F32),
+            pltpu.VMEM((4, mid.shape[1], shape[2]), BF16),
+            pltpu.VMEM((mid.shape[1], total), BF16),
         ],
         compiler_params=pltpu.CompilerParams(vmem_limit_bytes=VMEM_BYTES),
         cost_estimate=cost(20),
         name="token_back",
-    )(place, grad, mid, *mixed, mine, other, gain)
+    )(place, grad, mid, *mixed, *mine, *other, gain)
 
 
 def frequencies(theta_base, half_dim):
@@ -627,92 +638,174 @@
     place = placement()
 
     normed = (norm_parts(stream.astype(F32))[0] * gain_rows[0][:, :model]).astype(BF16)
-    qkv_halves = layer_halves(qkv_weight[0].reshape(shard_rows, 3 * width))
-    mats_halves = layer_halves(
-        jnp.concatenate(
-            [gate_up_weight[0].reshape(shard_rows, pair), out_weight[0].T, down_weight[0].T], 1
+    mats = jnp.concatenate(
+        [gate_up_weight[0].reshape(shard_rows, pair), out_weight[0].T, down_weight[0].T], 1
+    )
+    spare = 6 * width - mats.shape[1]
+    mats = jnp.pad(mats, ((0, 0), (0, spare))).reshape(2, shard_rows // 2, 6 * width)
+    qkv = qkv_weight[0].reshape(2, 2, shard_rows // 4, 3 * width)
+    qkv = jnp.concatenate([qkv[:, 0], qkv[:, 1]], -1)
+    first_half, second_half = layer_halves(
+        jnp.concatenate([mats, qkv], 1).reshape(-1, 6 * width)
+    )
+    split = shard_rows // 2
+    total = first_half.shape[0]
+    qkv_shape = (4, split, 3 * width) if four_dp() else (1, model // 2, 3 * width)
+
+    def qkv_halves(blocks):
+        block = stacked(blocks, split, total)
+        if not four_dp():
+            block = jnp.concatenate([block[..., : 3 * width], block[..., 3 * width :]], 1)
+        return halves(block)
+
+    normed, first_half, second_half = after((normed, first_half, second_half))
+    near, blocks = to_neighbours(normed), gather_dp(first_half)
+    far = to_far(*after(near))
+    far, blocks = after((far, blocks))
+    mats_first = stacked(blocks, 0, split)
+    qkv_parts = [qkv_halves(blocks), None]
+    mats_first, second_half = after((mats_first, second_half), qkv_parts[0])
+    pieces = (normed,) + near + far
+    saved_attend = [None, None]
+    saved_token = [None, None]
+
+    mats_near = to_neighbours(mats_first)
+    second_blocks = gather_dp(second_half)
+    second_blocks, second_late = second_blocks[:3], second_blocks[3:]
+    *mixed, queries, keys, values, mass, normed_full, qkv = attend(
+        place, pieces, *qkv_parts[0], width, *tables[0], *bounds[0], True
+    )
+    saved_attend[0] = (queries, keys, values, mass, normed_full, qkv)
+    mixed, mats_first, mats_near, second_blocks = after(
+        (mixed, mats_first, mats_near, second_blocks)
+    )
+    mixed, mats_far = after((swap_tensor(mixed), to_far(*mats_near)))
+    mats = piece_halves((mats_first,) + mats_near + mats_far)
+    mid, first_out, normed = token_forward(
+        place, mixed, stream, *mats, gain_rows[0][:, model:], gain_rows[1][:, :model], pair
+    )
+    saved_token[0] = (mid, mixed) + mats
+
+    normed, second_late = after((normed, second_late))
+    near = after(to_neighbours(normed))
+    blocks = second_blocks + second_late
+    qkv_parts[1] = qkv_halves(blocks)
+    far, qkv_parts[1] = after((to_far(*near), qkv_parts[1]))
+    pieces = (normed,) + near + far
+    mats_second = after(stacked(blocks, 0, split), far)
+    second_near = to_neighbours(mats_second)
+    *mixed, queries, keys, values, mass, normed_full, qkv = attend(
+        place, pieces, *qkv_parts[1], width, *tables[1], *bounds[1], False
+    )
+    saved_attend[1] = (queries, keys, values, mass, normed_full, qkv)
+    mixed, second_near = after((mixed, second_near))
+    mixed, second_far = after((swap_tensor(mixed), to_far(*second_near)))
+    mats = piece_halves((mats_second,) + second_near + second_far)
+    mid, second_out, _ = token_forward(
+        place, mixed, first_out, *mats, gain_rows[1][:, model:], gain_rows[1][:, :model], pair
+    )
+    saved_token[1] = (mid, mixed) + mats
+
+    def token_step(layer, grad):
+        mid, mixed, mine, other = saved_token[layer]
+        return token_back(
+            place, grad, mid, mixed, mine, other, gain_rows[layer][:, model:], pair
         )
-    )
-    qkv_first = gather_dp(qkv_halves[0])
-    mats_first = gather_dp(mats_halves[0])
-    qkv_second, mats_second = lax.optimization_barrier(
-        (qkv_halves[1], mats_halves[1], qkv_first, mats_first)
-    )[:2]
-    qkv_gathered = (qkv_first, gather_dp(qkv_second))
-    mats_gathered = (mats_first, gather_dp(mats_second))
-
-    layer_in = stream
-    saved = []
-    for layer in (0, 1):
-        pieces = spread_tensor(normed)
-        qkv_mine, qkv_other = halves(qkv_gathered[layer])
-        own, one, two, head, tail = spread_tensor(mats_gathered[layer])
-        mats_mine, mats_other = halves(
-            jnp.stack([own, one, two, jnp.concatenate([head, tail], 0)])
+
+    def attend_step(layer, mixed_grad):
+        queries, keys, values, mass, _, qkv = saved_attend[layer]
+        return attend_back(
+            place, queries, keys, values, mass, mixed_grad, *tables[layer], *bounds[layer],
+            qkv, layer == 0,
         )
-        *mixed, queries, keys, values, mass, normed_full, qkv = attend(
-            place, pieces, qkv_mine, qkv_other, *tables[layer], *bounds[layer], layer == 0
+
+    def weight_step(layer, grad_projected):
+        normed_full, qkv = saved_attend[layer][4:]
+        mine, other, gain_sum = qkv_grad(
+            place, normed_full, grad_projected, qkv, qkv_shape
         )
-        mixed = swap_tensor(mixed)
-        mid, layer_out, normed = token_forward(
-            place, mixed, layer_in, mats_mine, mats_other,
-            gain_rows[layer][:, model:], gain_rows[1][:, :model], pair,
-        )
-        saved.append(
-            (layer_in, qkv, qkv_mine.shape, mats_mine, mats_other, normed_full,
-             queries, keys, values, mass, mixed, mid)
-        )
-        layer_in = layer_out
-        if layer == 0:
-            first_out = layer_out
-    second_out = layer_in
-
-    grad = cotangent
-    reduced = [None, None]
-    gain_grads = [None, None]
-    input_grads = [None, None]
-    for layer in (1, 0):
-        (stream, qkv, qkv_shape, mats_mine, mats_other, normed_full,
-         queries, keys, values, mass, mixed, mid) = saved[layer]
-        mine_grad, other_grad, *mixed_grad, grad_mid, gain_mlp = token_back(
-            place, grad, mid, mixed, mats_mine, mats_other, gain_rows[layer][:, model:], pair
-        )
-        mixed_grad = swap_tensor(mixed_grad)
-        *partial_in, grad_projected = attend_back(
-            place, queries, keys, values, mass, mixed_grad, *tables[layer], *bounds[layer], qkv,
-            layer == 0,
-        )
-        grad_normed = scatter_tensor(*partial_in)
-        unit, scale = norm_parts(stream.astype(F32))
-        gain_attn = jnp.sum(grad_normed * unit, axis=0, keepdims=True)
-        grad_in = grad_mid + norm_back(grad_normed, unit, scale, gain_rows[layer][:, :model])
-        gain_grads[layer] = jnp.concatenate([gain_attn, gain_mlp], 1)
-
-        mats_kept, mats_came = half_sums(mine_grad, other_grad)
-        mats_sum = scatter_tensor(*(add_low(mats_kept[i], mats_came[i]) for i in range(4)))
-        qkv_kept, qkv_came = half_sums(
-            *qkv_grad(place, normed_full, grad_projected, qkv_shape)
-        )
-        qkv_sum = qkv_kept.astype(F32) + qkv_came.astype(F32)
-        reduced[layer] = scatter_dp(jnp.concatenate([mats_sum, qkv_sum], -1), BF16)
-        if layer == 1:
-            grad = grad_in.astype(BF16)
-            grad_in = grad.astype(F32)
-        input_grads[layer] = grad_in
-
-    weight_grad = own_layer(*reduced)
-    out_low, down_low = pair + width, pair + width + down_weight.shape[1]
-    n = lax.axis_size("dp")
-    gain_mine = jnp.where(core == 0, gain_grads[0], gain_grads[1])
-    gain_other = swap_cores(jnp.where(core == 0, gain_grads[1], gain_grads[0]))
-    gain_blocks = jnp.moveaxis((gain_mine + gain_other).reshape(n, 4, -1), 1, 0)
-    me = lax.axis_index("tensor")
-    gain_blocks = sum(swap_tensor([take(gain_blocks, me ^ bit) for bit in range(4)]))
-    if few_dp():
-        rank = lax.axis_index("dp")
-        gain_blocks = jnp.stack([take(gain_blocks, (rank - step) % n) for step in range(n)])
-    gain_part = scatter_dp(gain_blocks, F32)
-
+        return half_sums(mine, other) + (gain_sum.reshape(1, model) / gain_rows[layer][:, :model],)
+
+    def norm_step(layer, partial_in, near, grad_mid):
+        grad_normed = add_up(partial_in[0], *near)
+        unit, scale = norm_parts((stream, first_out)[layer].astype(F32))
+        return grad_mid + norm_back(grad_normed, unit, scale, gain_rows[layer][:, :model])
+
+    def qkv_blocks(kept, came):
+        return [add_low(kept[slot], came[slot]) for slot in range(kept.shape[0])]
+
+    mine_grad, other_grad, *mixed_grad, grad_mid, gain_mlp = token_step(1, cotangent)
+    mixed_grad = swap_tensor(mixed_grad)
+    kept, came = half_sums(mine_grad, other_grad)
+    mixed_grad, kept, came = after((mixed_grad, kept, came))
+    far = far_terms(add_low(kept[3], came[3]))
+    *partial_in, grad_projected = attend_step(1, mixed_grad)
+    partial_in, grad_projected, far = after((partial_in, grad_projected, far))
+    in_far = far_terms(partial_in[3])
+    pair_terms = near_terms(add_low(kept[1], came[1]), add_low(kept[2], came[2]), *far)
+    qkv_kept, qkv_came, gain_attn = weight_step(1, grad_projected)
+    second_gain = jnp.concatenate([gain_attn, gain_mlp], 1)
+    in_far, qkv_kept, qkv_came = after((in_far, qkv_kept, qkv_came))
+    second_qkv = qkv_blocks(qkv_kept, qkv_came)
+    in_near = to_near(near_terms(partial_in[1], partial_in[2], *in_far))
+    in_near, pair_terms, second_qkv = after((in_near, pair_terms, second_qkv))
+    near, second_qkv_came = to_near(pair_terms), scatter_dp(second_qkv)
+    grad = norm_step(1, partial_in, in_near, grad_mid).astype(BF16)
+    second_grad = grad.astype(F32)
+
+    second_kept, second_came = kept, came
+    mine_grad, other_grad, *mixed_grad, grad_mid, gain_mlp = token_step(0, grad)
+    mixed_grad, other_grad, near, second_qkv_came = after(
+        (mixed_grad, other_grad, near, second_qkv_came)
+    )
+    mixed_grad = swap_tensor(mixed_grad)
+    kept, came = half_sums(mine_grad, other_grad)
+    second_mats = slot_sums(second_kept, second_came, near)
+    mixed_grad, kept, came, second_mats = after((mixed_grad, kept, came, second_mats))
+    far = far_terms(add_low(kept[3], came[3]))
+    second_mats_came = scatter_dp(second_mats)
+    second_early, second_late = second_mats_came[1:], second_mats_came[:1]
+    *partial_in, grad_projected = attend_step(0, mixed_grad)
+    partial_in, grad_projected, far, kept, came, second_early = after(
+        (partial_in, grad_projected, far, kept, came, second_early)
+    )
+    second_mats_came = second_late + second_early
+
+    near = to_near(near_terms(add_low(kept[1], came[1]), add_low(kept[2], came[2]), *far))
+    qkv_kept, qkv_came, gain_attn = weight_step(0, grad_projected)
+    first_gain = jnp.concatenate([gain_attn, gain_mlp], 1)
+    first_qkv = qkv_blocks(qkv_kept, qkv_came)
+    first_qkv_came = scatter_dp(first_qkv)
+    gain_sum = jnp.where(core == 0, first_gain, second_gain)
+    gain_sum += swap_cores(jnp.where(core == 0, second_gain, first_gain))
+    near, first_qkv_came, second_mats_came, partial_in, gain_sum = after(
+        (near, first_qkv_came, second_mats_came, partial_in, gain_sum)
+    )
+    first_mats = slot_sums(kept, came, near)
+    first_mats_came, in_far = scatter_dp(first_mats), far_terms(partial_in[3])
+    gain_sum += to_mate(gain_sum, 1)
+    first_mats_came, in_far, partial_in, gain_sum = after(
+        (first_mats_came, in_far, partial_in, gain_sum)
+    )
+    in_near = to_near(near_terms(partial_in[1], partial_in[2], *in_far))
+    gain_sum += to_mate(gain_sum, 2)
+    chunk = model * 2 // (4 * lax.axis_size("dp"))
+    me = lax.axis_index("dp") * 4 + lax.axis_index("tensor")
+    if four_dp():
+        gain_sum += to_peer(gain_sum, 1)
+        gain_sum += to_peer(gain_sum, 2)
+    else:
+        gain_sum = lax.psum(gain_sum, "dp")
+    gain_part = lax.dynamic_slice_in_dim(gain_sum[0], me * chunk, chunk, 0)
+    first_grad = norm_step(0, partial_in, in_near, grad_mid)
+    input_grads = (first_grad, second_grad)
+
+    qkv_total = own_layer(
+        scatter_sum(first_qkv, first_qkv_came), scatter_sum(second_qkv, second_qkv_came)
+    )
+    mats_total = own_layer(
+        scatter_sum(first_mats, first_mats_came), scatter_sum(second_mats, second_mats_came)
+    )
     activations = join_halves(
         jnp.where(core == 0, first_out, second_out),
         swap_cores(jnp.where(core == 0, second_out, first_out)),
@@ -726,10 +819,10 @@
     return (
         activations[None, None],
         grads_in[None, None],
-        weight_grad[:, down_low:].reshape(qkv_weight.shape),
-        weight_grad[:, pair:out_low].T[None],
-        weight_grad[:, :pair].reshape(gate_up_weight.shape),
-        weight_grad[:, out_low:down_low].T[None],
+        qkv_total.reshape(qkv_weight.shape),
+        mats_total[:, pair : pair + width].T[None],
+        mats_total[:, :pair].reshape(gate_up_weight.shape),
+        mats_total[:, pair + width :].T[None],
         gain_part[None],
     )
 

time: 507 us -> 411 us (0.81)
  waiting for transfers between devices: 193 us -> 121 us
  Pallas kernels: 134 us -> 110 us
  starting transfers between devices: 112 us -> 102 us
    ppermute x47 -> x46, waiting for transfers between devices: 128 us -> 76.2 us  [to_mate(): return lax.ppermute(block, 'tensor', [(i, i ^ bit) for i in range(size)])]
    ppermute x21 -> x20, waiting for transfers between devices: 65.1 us -> 41.5 us  [to_peer(): return lax.ppermute(block, 'dp', [(i, i ^ bit) for i in range(4)])]
    ppermute x21 -> x20, starting transfers between devices: 59.4 us -> 45.9 us  [to_peer(): return lax.ppermute(block, 'dp', [(i, i ^ bit) for i in range(4)])]
    another operation x11 -> x5, other arithmetic: 11 us -> 0.59 us  [the longest x4 0.41 us: stacked(): return jnp.stack([block[low:high] for block in blocks])]
    pallas_call x2, Pallas kernels: 36.7 us -> 27.9 us  [token_back(): pl.pallas_call(functools.partial(token_back_kernel, pair), out_shape=(hal...]
    pallas_call x2, Pallas kernels: 36.2 us -> 29.3 us  [attend(): pl.pallas_call(functools.partial(attend_kernel, span), out_shape=(mixed,...]
    pallas_call x2, Pallas kernels: 20.5 us -> 14.7 us  [token_forward(): pl.pallas_call(functools.partial(token_kernel, pair), out_shape=(jax.Shap...]
    ppermute x47 -> x46, starting transfers between devices: 50.6 us -> 52.7 us  [to_mate(): return lax.ppermute(block, 'tensor', [(i, i ^ bit) for i in range(size)])]
  transfers between devices with their start and end apart: 83 -> 89, of which waited for: 35 -> 42; matrix products, arithmetic and copies ran while one was open for 9% -> 12% of each run, Pallas kernels for 17% -> 21%
where the time goes in v3:
time: 411 us; the launch traced here: 406 us
  waiting for transfers between devices  121 us (29%)
  Pallas kernels  110 us (27%)
  starting transfers between devices  102 us (25%)
  other arithmetic  40.5 us (10%)
  local copies, waits for them, and re-layouts  28.6 us (7%)
    ppermute x46, waiting for transfers between devices, to_mate(): return lax.ppermute(block, 'tensor', [(i, i ^ bit) for i in range(size)])  76.2 us
    ppermute x46, starting transfers between devices, to_mate(): return lax.ppermute(block, 'tensor', [(i, i ^ bit) for i in range(size)])  52.7 us
    ppermute x20, starting transfers between devices, to_peer(): return lax.ppermute(block, 'dp', [(i, i ^ bit) for i in range(4)])  45.9 us
    ppermute x20, waiting for transfers between devices, to_peer(): return lax.ppermute(block, 'dp', [(i, i ^ bit) for i in range(4)])  41.5 us
    pallas_call x2, Pallas kernels, attend_back(): pl.pallas_call(functools.partial(attend_back_kernel, span), out_shape=(pa...  32.9 us
    pallas_call x2, Pallas kernels, attend(): pl.pallas_call(functools.partial(attend_kernel, span), out_shape=(mixed,...  29.3 us
    pallas_call x2, Pallas kernels, token_back(): pl.pallas_call(functools.partial(token_back_kernel, pair), out_shape=(hal...  27.9 us
    unnamed x210, local copies, waits for them, and re-layouts  15.5 us
  transfers between devices with their start and end apart: 89, of which 42 were waited for; matrix products, arithmetic and copies ran while one was open for 12% of the time, Pallas kernels for 21%

profile of v3, /device:TPU:0, one launch (start us, length us, event | category | flops | bytes accessed | tf_op | source)
XLA Modules:
  0.0 405.6 jit_solution(7884501357338112766)
XLA Ops:
  7.8 2.9 collective-permute-start.2
  15.1 2.6 collective-permute-start.7
  18.0 4.2 %collective-permute-done.2.one_ref = bf16[320,768]{1,0:T(8,128)(2,1)S(1)} collective-permute-done((bf16[320,768]{1,0:T(8,128)(2,1)S(1)}, bf16[320,768]{1,0:T(8,128)(2,1)S(1)}, u32[]{:S(2)}, u32[]{:S(2)}) %collective-permute-start.2) | collective-permute-done | bytes 491552 | tf_op jit(solution)/shard_map/ppermute | solution.py:25
  29.2 12.1 %collective-permute-done.7 = bf16[144,1152]{1,0:T(8,128)(2,1)} collective-permute-done((bf16[144,1152]{1,0:T(8,128)(2,1)}, bf16[144,1152]{1,0:T(8,128)(2,1)}, u32[]{:S(2)}, u32[]{:S(2)}) %collective-permute-start.7) | collective-permute-done | bytes 331808 | tf_op jit(solution)/shard_map/ppermute | solution.py:89
  47.4 5.9 %collective-permute-start.12 = (bf16[144,1152]{1,0:T(8,128)(2,1)S(1)}, bf16[144,1152]{1,0:T(8,128)(2,1)S(1)}, u32[]{:S(2)}, u32[]{:S(2)}) collective-permute-start(bf16[144,1152]{1,0:T(8,128)(2,1)S(1)} %copy-done.73), channel_id=1, source_target_pairs={{0,8},{8,0},{16,24},{24,16},{1,9},{9,1},{17,25},{25,17},{2,10},{10... | collective-permute-start | bytes 995336 | tf_op jit(solution)/shard_map/ppermute | solution.py:89
  54.3 10.6 %attend_local.1 = (bf16[160,384]{1,0:T(8,128)(2,1)S(1)}, bf16[160,384]{1,0:T(8,128)(2,1)S(1)}, bf16[160,384]{1,0:T(8,128)(2,1)S(1)}, bf16[160,384]{1,0:T(8,128)(...) custom-call(s32[6]{0:T(128)S(1)} %stack.143.place_ref, ...), custom_call_target="tpu_custom_call" | custom-call | flops 12650000384 | bytes 39600000 | tf_op jit(solution)/shard_map/attend_local/pallas_call | solution.py:332
  67.8 2.5 collective-permute-done.13
  80.2 7.6 %collective-permute-done.17.refs_3_ = bf16[2,96,1152]{2,1,0:T(8,128)(2,1)S(1)} collective-permute-done((bf16[2,96,1152]{2,1,0:T(8,128)(2,1)S(1)}, bf16[2,96,1152]{2,1,0:T(8,128)(2,1)S(1)}, u32[]{:S(2)}, u32[]{:S(2)}) %collective-permute-start.17) | collective-permute-done | bytes 442400 | tf_op jit(solution)/shard_map/ppermute | solution.py:25
  90.7 2.5 collective-permute-start.24
  93.2 7.0 %token_forward.2 = (f32[320,768]{1,0:T(8,128)S(1)}, bf16[320,768]{1,0:T(8,128)(2,1)S(1)}, bf16[320,768]{1,0:T(8,128)(2,1)S(1)}) custom-call(s32[6]{0:T(128)S(1)} %stack.143.place_ref, bf16[160,384]{1,0:T(8,128)(2,1)S(1)} %get-tuple-element.215.mixed0_ref, bf16[160,384]{1,0:T(8,128)(2,1)S(1)} %collective-permute-done.14.mixed1_ref, ...), custom_call_target="tpu_custom_call" | custom-call | flops 11500000256 | bytes 36000000 | tf_op jit(solution)/shard_map/token_forward/pallas_call | solution.py:496
  103.9 10.9 %collective-permute-done.25.one_ref = bf16[320,768]{1,0:T(8,128)(2,1)S(1)} collective-permute-done((bf16[320,768]{1,0:T(8,128)(2,1)S(1)}, bf16[320,768]{1,0:T(8,128)(2,1)S(1)}, u32[]{:S(2)}, u32[]{:S(2)}) %collective-permute-start.25) | collective-permute-done | bytes 491552 | tf_op jit(solution)/shard_map/ppermute | solution.py:25
  117.9 3.3 collective-permute-done.27.head_ref
  121.2 1.9 collective-permute-done.28.tail_ref
  124.2 18.7 %attend_global.1 = (bf16[160,384]{1,0:T(8,128)(2,1)S(1)}, bf16[160,384]{1,0:T(8,128)(2,1)S(1)}, bf16[160,384]{1,0:T(8,128)(2,1)S(1)}, bf16[160,384]{1,0:T(8,128)...) custom-call(s32[6]{0:T(128)S(1)} %stack.143.place_ref, ...), custom_call_target="tpu_custom_call" | custom-call | flops 23000000512 | bytes 72000000 | tf_op jit(solution)/shard_map/attend_global/pallas_call | solution.py:332
  142.9 2.0 collective-permute-start.32
  146.5 2.0 collective-permute-start.35
  149.6 2.3 collective-permute-done.33.mixed2_ref
  153.1 5.0 %collective-permute-done.35.refs_3_ = bf16[2,96,1152]{2,1,0:T(8,128)(2,1)S(1)} collective-permute-done((bf16[2,96,1152]{2,1,0:T(8,128)(2,1)S(1)}, bf16[2,96,1152]{2,1,0:T(8,128)(2,1)S(1)}, u32[]{:S(2)}, u32[]{:S(2)}) %collective-permute-start.35) | collective-permute-done | bytes 442400 | tf_op jit(solution)/shard_map/ppermute | solution.py:25
  160.9 7.7 %token_forward.3 = (f32[320,768]{1,0:T(8,128)S(1)}, bf16[320,768]{1,0:T(8,128)(2,1)S(1)}, bf16[320,768]{1,0:T(8,128)(2,1)}) custom-call(s32[6]{0:T(128)S(1)} %stack.143.place_ref, bf16[160,384]{1,0:T(8,128)(2,1)S(1)} %get-tuple-element.246.mixed0_ref, bf16[160,384]{1,0:T(8,128)(2,1)S(1)} %collective-permute-done.32.mixed1_ref, ...), custom_call_target="tpu_custom_call" | custom-call | flops 11500000256 | bytes 36000000 | tf_op jit(solution)/shard_map/token_forward/pallas_call | solution.py:496
  169.4 13.8 %token_back.2 = (bf16[4,4,96,1056]{3,2,1,0:T(8,128)(2,1)S(1)}, bf16[4,4,96,1056]{3,2,1,0:T(8,128)(2,1)S(1)}, bf16[160,384]{1,0:T(8,128)(2,1)S(1)}, bf16[160,384]...) custom-call(s32[6]{0:T(128)S(1)} %stack.143.place_ref, ...), custom_call_target="tpu_custom_call" | custom-call | flops 23000000512 | bytes 72000000 | tf_op jit(solution)/shard_map/token_back/pallas_call | solution.py:577
  185.6 1.9 collective-permute-start.45
  187.5 2.6 collective-permute-done.43.grad1_ref
  190.3 2.4 collective-permute-done.45.grad3_ref
  197.8 21.2 %attend_back_global.1 = (bf16[320,768]{1,0:T(8,128)(2,1)S(1)}, bf16[320,768]{1,0:T(8,128)(2,1)S(1)}, bf16[320,768]{1,0:T(8,128)(2,1)S(1)}, bf16[320,768]{1,0:T(8,128)(2,1)S(1)}, bf16[1280,576]{1,0:T(8,128)(2,1)S(1)}) custom-call(s32[6]{0:T(128)S(1)} %stack.143.place_ref, bf16[192,1280]{1,0:T(8,128)(2,1)S(1)} %get-tuple-element.255.queries_ref, ...), custom_call_target="tpu_custom_call" | custom-call | flops 24149999616 | bytes 75600000 | tf_op jit(solution)/shard_map/attend_back_global/pallas_call | solution.py:425
  219.9 3.1 qkv_grad.2
  237.8 2.0 fusion.42
  239.8 6.8 %collective-permute-done.53 = bf16[320,768]{1,0:T(8,128)(2,1)S(1)} collective-permute-done((bf16[320,768]{1,0:T(8,128)(2,1)S(1)}, bf16[320,768]{1,0:T(8,128)(2,1)S(1)}, u32[]{:S(2)}, u32[]{:S(2)}) %collective-permute-start.53) | collective-permute-done | bytes 491552 | tf_op jit(solution)/shard_map/ppermute | solution.py:25
  246.6 1.9 collective-permute-done.52
  251.4 9.4 %collective-permute-start.56 = (bf16[96,576]{1,0:T(8,128)(2,1)S(1)}, bf16[96,576]{1,0:T(8,128)(2,1)S(1)}, u32[]{:S(2)}, u32[]{:S(2)}) collective-permute-start(bf16[96,576]{1,0:T(8,128)(2,1)S(1)} %get-tuple-element.306), channel_id=1, source_target_pairs={{0,8},{8,0},{16,24},{24,16},{1,9},{9,1},{17,25},{25,17},{2,10},{10... | collective-permute-start | bytes 331784 | tf_op jit(solution)/shard_map/ppermute | solution.py:89
  263.9 14.1 %token_back.3 = (bf16[4,4,96,1056]{3,2,1,0:T(8,128)(2,1)S(1)}, bf16[4,4,96,1056]{3,2,1,0:T(8,128)(2,1)S(1)}, bf16[160,384]{1,0:T(8,128)(2,1)S(1)}, bf16[160,384]...) custom-call(s32[6]{0:T(128)S(1)} %stack.143.place_ref, ...), custom_call_target="tpu_custom_call" | custom-call | flops 23000000512 | bytes 72000000 | tf_op jit(solution)/shard_map/token_back/pallas_call | solution.py:577
  282.9 2.7 fusion.31
  285.7 2.5 collective-permute-done.60.grad2_ref
  292.1 2.0 collective-permute-start.65
  295.6 11.7 %attend_back_local.1 = (bf16[320,768]{1,0:T(8,128)(2,1)S(1)}, bf16[320,768]{1,0:T(8,128)(2,1)S(1)}, bf16[320,768]{1,0:T(8,128)(2,1)S(1)}, bf16[320,768]{1,0:T(8,128)(2,1)S(1)}, bf16[1280,576]{1,0:T(8,128)(2,1)S(1)}) custom-call(s32[6]{0:T(128)S(1)} %stack.143.place_ref, bf16[192,1280]{1,0:T(8,128)(2,1)S(1)} %copy-done.59, bf16[192,1280]{1,0:T(8,128)(2,1)S(1)} %copy-done.61, ...), custom_call_target="tpu_custom_call" | custom-call | flops 12650000384 | bytes 39600000 | tf_op jit(solution)/shard_map/attend_back_local/pallas_call | solution.py:425
  309.7 2.4 qkv_grad.3
  315.1 2.4 add_convert_fusion
  320.6 4.7 %collective-permute-start.70 = (bf16[96,576]{1,0:T(8,128)(2,1)S(1)}, bf16[96,576]{1,0:T(8,128)(2,1)S(1)}, u32[]{:S(2)}, u32[]{:S(2)}) collective-permute-start(bf16[96,576]{1,0:T(8,128)(2,1)S(1)} %get-tuple-element.428), channel_id=1, source_target_pairs={{0,8},{8,0},{16,24},{24,16},{1,9},{9,1},{17,25},{25,17},{2,10},{10... | collective-permute-start | bytes 331784 | tf_op jit(solution)/shard_map/ppermute | solution.py:89
  327.8 3.4 collective-permute-done.70
  331.2 6.5 %collective-permute-done.71 = bf16[96,576]{1,0:T(8,128)(2,1)S(1)} collective-permute-done((bf16[96,576]{1,0:T(8,128)(2,1)S(1)}, bf16[96,576]{1,0:T(8,128)(2,1)S(1)}, u32[]{:S(2)}, u32[]{:S(2)}) %collective-permute-start.71) | collective-permute-done | bytes 110624 | tf_op jit(solution)/shard_map/ppermute | solution.py:89
  337.7 2.2 collective-permute-done.68
  343.9 4.7 %collective-permute-start.75 = (bf16[96,1056]{1,0:T(8,128)(2,1)S(1)}, bf16[96,1056]{1,0:T(8,128)(2,1)S(1)}, u32[]{:S(2)}, u32[]{:S(2)}) collective-permute-start(bf16[96,1056]{1,0:T(8,128)(2,1)S(1)} %get-tuple-element.412), channel_id=1, source_target_pairs={{0,8},{8,0},{16,24},{24,16},{1,9},{9,1},{17,25},{25,17},{2,10},{10... | collective-permute-start | bytes 608264 | tf_op jit(solution)/shard_map/ppermute | solution.py:89
  354.0 2.4 collective-permute-done.75
  356.4 10.8 %collective-permute-done.76 = bf16[96,1056]{1,0:T(8,128)(2,1)S(1)} collective-permute-done((bf16[96,1056]{1,0:T(8,128)(2,1)S(1)}, bf16[96,1056]{1,0:T(8,128)(2,1)S(1)}, u32[]{:S(2)}, u32[]{:S(2)}) %collective-permute-start.76) | collective-permute-done | bytes 202784 | tf_op jit(solution)/shard_map/ppermute | solution.py:89
  371.1 10.1 %collective-permute-done.81 = bf16[320,768]{1,0:T(8,128)(2,1)S(1)} collective-permute-done((bf16[320,768]{1,0:T(8,128)(2,1)S(1)}, bf16[320,768]{1,0:T(8,128)(2,1)S(1)}, u32[]{:S(2)}, u32[]{:S(2)}) %collective-permute-start.81) | collective-permute-done | bytes 491552 | tf_op jit(solution)/shard_map/ppermute | solution.py:25
  387.7 2.5 collective-permute-done.86
  391.0 2.3 maximum_select_fusion.1
  394.0 1.9 collective-permute-start.88
  402.3 3.0 maximum_select_fusion
  (479 shorter events, 134.0 us)
Async XLA Ops:
  7.8 14.3 %collective-permute-start.2 = (bf16[320,768]{1,0:T(8,128)(2,1)S(1)}, bf16[320,768]{1,0:T(8,128)(2,1)S(1)}, u32[]{:S(2)}, u32[]{:S(2)}) collective-permute-start(bf16[320,768]{1,0:T(8,128)(2,1)S(1)} %fusion.15.own_ref), channel_id=1, source_target_pairs={{0,1},{1,0},{2,3},{3,2},{4,5},{5,4},{6,7},{7,6},{8,9},{9,8},{10,11... | collective-permute-start | bytes 1474568 | tf_op jit(solution)/shard_map/ppermute | solution.py:25
  10.7 12.9 %collective-permute-start.3 = (bf16[320,768]{1,0:T(8,128)(2,1)S(1)}, bf16[320,768]{1,0:T(8,128)(2,1)S(1)}, u32[]{:S(2)}, u32[]{:S(2)}) collective-permute-start(bf16[320,768]{1,0:T(8,128)(2,1)S(1)} %fusion.15.own_ref), channel_id=1, source_target_pairs={{0,2},{1,3},{2,0},{3,1},{4,6},{5,7},{6,4},{7,5},{8,10},{9,11},{10,... | collective-permute-start | bytes 1474568 | tf_op jit(solution)/shard_map/ppermute | solution.py:25
  13.5 15.7 %collective-permute-start.6 = (bf16[144,1152]{1,0:T(8,128)(2,1)}, bf16[144,1152]{1,0:T(8,128)(2,1)}, u32[]{:S(2)}, u32[]{:S(2)}) collective-permute-start(bf16[144,1152]{1,0:T(8,128)(2,1)} %get-tuple-element.198), channel_id=1, source_target_pairs={{0,8},{8,0},{16,24},{24,16},{1,9},{9,1},{17,25},{25,17},{2,10},{10... | collective-permute-start | bytes 995336 | tf_op jit(solution)/shard_map/ppermute | solution.py:89
  15.1 26.2 %collective-permute-start.7 = (bf16[144,1152]{1,0:T(8,128)(2,1)}, bf16[144,1152]{1,0:T(8,128)(2,1)}, u32[]{:S(2)}, u32[]{:S(2)}) collective-permute-start(bf16[144,1152]{1,0:T(8,128)(2,1)} %get-tuple-element.198), channel_id=1, source_target_pairs={{0,16},{8,24},{16,0},{24,8},{1,17},{9,25},{17,1},{25,9},{2,18},{10... | collective-permute-start | bytes 995336 | tf_op jit(solution)/shard_map/ppermute | solution.py:89
  17.7 23.6 %collective-permute-start.8 = (bf16[144,1152]{1,0:T(8,128)(2,1)}, bf16[144,1152]{1,0:T(8,128)(2,1)}, u32[]{:S(2)}, u32[]{:S(2)}) collective-permute-start(bf16[144,1152]{1,0:T(8,128)(2,1)} %get-tuple-element.198), channel_id=1, source_target_pairs={{0,24},{8,16},{16,8},{24,0},{1,25},{9,17},{17,9},{25,1},{2,26},{10... | collective-permute-start | bytes 995336 | tf_op jit(solution)/shard_map/ppermute | solution.py:89
  25.1 16.2 %collective-permute-start.4 = (bf16[160,768]{1,0:T(8,128)(2,1)}, bf16[160,768]{1,0:T(8,128)(2,1)}, u32[]{:S(2)}, u32[]{:S(2)}) collective-permute-start(bf16[160,768]{1,0:T(8,128)(2,1)} %slice.437), channel_id=1, source_target_pairs={{0,1},{1,0},{2,3},{3,2},{4,5},{5,4},{6,7},{7,6},{8,9},{9,8},{10,11... | collective-permute-start | bytes 737288 | tf_op jit(solution)/shard_map/ppermute | solution.py:25
  26.1 15.2 %collective-permute-start.5 = (bf16[160,768]{1,0:T(8,128)(2,1)}, bf16[160,768]{1,0:T(8,128)(2,1)}, u32[]{:S(2)}, u32[]{:S(2)}) collective-permute-start(bf16[160,768]{1,0:T(8,128)(2,1)} %slice.438), channel_id=1, source_target_pairs={{0,2},{1,3},{2,0},{3,1},{4,6},{5,7},{6,4},{7,5},{8,10},{9,11},{10,... | collective-permute-start | bytes 737288 | tf_op jit(solution)/shard_map/ppermute | solution.py:25
  46.4 24.0 %collective-permute-start.10 = (bf16[4,96,1152]{2,1,0:T(8,128)(2,1)S(1)}, bf16[4,96,1152]{2,1,0:T(8,128)(2,1)S(1)}, u32[]{:S(2)}, u32[]{:S(2)}) collective-permute-start(bf16[4,96,1152]{2,1,0:T(8,128)(2,1)S(1)} %pad_maximum_fusion.refs_0_), channel_id=1, source_target_pairs={{0,1},{1,0},{2,3},{3,2},{4,5},{5,4},{6,7},{7,6},{8,9},{9,8},{10,11... | collective-permute-start | bytes 2654216 | tf_op jit(solution)/shard_map/ppermute | solution.py:25
  46.9 23.5 %collective-permute-start.11 = (bf16[4,96,1152]{2,1,0:T(8,128)(2,1)S(1)}, bf16[4,96,1152]{2,1,0:T(8,128)(2,1)S(1)}, u32[]{:S(2)}, u32[]{:S(2)}) collective-permute-start(bf16[4,96,1152]{2,1,0:T(8,128)(2,1)S(1)} %pad_maximum_fusion.refs_0_), channel_id=1, source_target_pairs={{0,2},{1,3},{2,0},{3,1},{4,6},{5,7},{6,4},{7,5},{8,10},{9,11},{10,... | collective-permute-start | bytes 2654216 | tf_op jit(solution)/shard_map/ppermute | solution.py:25
  47.4 20.4 %collective-permute-start.12 = (bf16[144,1152]{1,0:T(8,128)(2,1)S(1)}, bf16[144,1152]{1,0:T(8,128)(2,1)S(1)}, u32[]{:S(2)}, u32[]{:S(2)}) collective-permute-start(bf16[144,1152]{1,0:T(8,128)(2,1)S(1)} %copy-done.73), channel_id=1, source_target_pairs={{0,8},{8,0},{16,24},{24,16},{1,9},{9,1},{17,25},{25,17},{2,10},{10... | collective-permute-start | bytes 995336 | tf_op jit(solution)/shard_map/ppermute | solution.py:89
  53.3 17.1 %collective-permute-start.13 = (bf16[144,1152]{1,0:T(8,128)(2,1)S(1)}, bf16[144,1152]{1,0:T(8,128)(2,1)S(1)}, u32[]{:S(2)}, u32[]{:S(2)}) collective-permute-start(bf16[144,1152]{1,0:T(8,128)(2,1)S(1)} %copy-done.73), channel_id=1, source_target_pairs={{0,16},{8,24},{16,0},{24,8},{1,17},{9,25},{17,1},{25,9},{2,18},{10... | collective-permute-start | bytes 995336 | tf_op jit(solution)/shard_map/ppermute | solution.py:89
  74.1 19.1 %collective-permute-start.21 = (bf16[4,96,1152]{2,1,0:T(8,128)(2,1)S(1)}, bf16[4,96,1152]{2,1,0:T(8,128)(2,1)S(1)}, u32[]{:S(2)}, u32[]{:S(2)}) collective-permute-start(bf16[4,96,1152]{2,1,0:T(8,128)(2,1)S(1)} %collective-permute-done.11.refs_2_), channel_id=1, source_target_pairs={{0,4},{4,0},{1,5},{5,1},{2,6},{6,2},{3,7},{7,3},{8,12},{12,8},{9,1... | collective-permute-start | bytes 2654216 | tf_op jit(solution)/shard_map/ppermute | solution.py:20
  74.2 19.0 %collective-permute-start.20 = (bf16[4,96,1152]{2,1,0:T(8,128)(2,1)S(1)}, bf16[4,96,1152]{2,1,0:T(8,128)(2,1)S(1)}, u32[]{:S(2)}, u32[]{:S(2)}) collective-permute-start(bf16[4,96,1152]{2,1,0:T(8,128)(2,1)S(1)} %collective-permute-done.10.refs_1_), channel_id=1, source_target_pairs={{0,4},{4,0},{1,5},{5,1},{2,6},{6,2},{3,7},{7,3},{8,12},{12,8},{9,1... | collective-permute-start | bytes 2654216 | tf_op jit(solution)/shard_map/ppermute | solution.py:20
  75.3 12.4 %collective-permute-start.17 = (bf16[2,96,1152]{2,1,0:T(8,128)(2,1)S(1)}, bf16[2,96,1152]{2,1,0:T(8,128)(2,1)S(1)}, u32[]{:S(2)}, u32[]{:S(2)}) collective-permute-start(bf16[2,96,1152]{2,1,0:T(8,128)(2,1)S(1)} %slice.447), channel_id=1, source_target_pairs={{0,1},{1,0},{2,3},{3,2},{4,5},{5,4},{6,7},{7,6},{8,9},{9,8},{10,11... | collective-permute-start | bytes 1327112 | tf_op jit(solution)/shard_map/ppermute | solution.py:25
  80.2 13.0 %collective-permute-start.19 = (bf16[4,96,1152]{2,1,0:T(8,128)(2,1)S(1)}, bf16[4,96,1152]{2,1,0:T(8,128)(2,1)S(1)}, u32[]{:S(2)}, u32[]{:S(2)}) collective-permute-start(bf16[4,96,1152]{2,1,0:T(8,128)(2,1)S(1)} %pad_maximum_fusion.refs_0_), channel_id=1, source_target_pairs={{0,4},{4,0},{1,5},{5,1},{2,6},{6,2},{3,7},{7,3},{8,12},{12,8},{9,1... | collective-permute-start | bytes 2654216 | tf_op jit(solution)/shard_map/ppermute | solution.py:20
  102.4 12.4 %collective-permute-start.25 = (bf16[320,768]{1,0:T(8,128)(2,1)S(1)}, bf16[320,768]{1,0:T(8,128)(2,1)S(1)}, u32[]{:S(2)}, u32[]{:S(2)}) collective-permute-start(bf16[320,768]{1,0:T(8,128)(2,1)S(1)} %get-tuple-element.224.own_ref), channel_id=1, source_target_pairs={{0,1},{1,0},{2,3},{3,2},{4,5},{5,4},{6,7},{7,6},{8,9},{9,8},{10,11... | collective-permute-start | bytes 1474568 | tf_op jit(solution)/shard_map/ppermute | solution.py:25
  102.8 12.1 %collective-permute-start.26 = (bf16[320,768]{1,0:T(8,128)(2,1)S(1)}, bf16[320,768]{1,0:T(8,128)(2,1)S(1)}, u32[]{:S(2)}, u32[]{:S(2)}) collective-permute-start(bf16[320,768]{1,0:T(8,128)(2,1)S(1)} %get-tuple-element.224.own_ref), channel_id=1, source_target_pairs={{0,2},{1,3},{2,0},{3,1},{4,6},{5,7},{6,4},{7,5},{8,10},{9,11},{10,... | collective-permute-start | bytes 1474568 | tf_op jit(solution)/shard_map/ppermute | solution.py:25
  103.8 14.0 %collective-permute-start.29 = (bf16[4,48,1152]{2,1,0:T(8,128)(2,1)S(1)}, bf16[4,48,1152]{2,1,0:T(8,128)(2,1)S(1)}, u32[]{:S(2)}, u32[]{:S(2)}) collective-permute-start(bf16[4,48,1152]{2,1,0:T(8,128)(2,1)S(1)} %pad_maximum_fusion.12.mine_ref), channel_id=1, source_target_pairs={{0,4},{4,0},{1,5},{5,1},{2,6},{6,2},{3,7},{7,3},{8,12},{12,8},{9,1... | collective-permute-start | bytes 1327112 | tf_op jit(solution)/shard_map/ppermute | solution.py:20
  123.1 19.9 %collective-permute-start.30 = (bf16[4,96,1152]{2,1,0:T(8,128)(2,1)S(1)}, bf16[4,96,1152]{2,1,0:T(8,128)(2,1)S(1)}, u32[]{:S(2)}, u32[]{:S(2)}) collective-permute-start(bf16[4,96,1152]{2,1,0:T(8,128)(2,1)S(1)} %pad_maximum_fusion.1.refs_0_), channel_id=1, source_target_pairs={{0,1},{1,0},{2,3},{3,2},{4,5},{5,4},{6,7},{7,6},{8,9},{9,8},{10,11... | collective-permute-start | bytes 2654216 | tf_op jit(solution)/shard_map/ppermute | solution.py:25
  123.3 19.6 %collective-permute-start.31 = (bf16[4,96,1152]{2,1,0:T(8,128)(2,1)S(1)}, bf16[4,96,1152]{2,1,0:T(8,128)(2,1)S(1)}, u32[]{:S(2)}, u32[]{:S(2)}) collective-permute-start(bf16[4,96,1152]{2,1,0:T(8,128)(2,1)S(1)} %pad_maximum_fusion.1.refs_0_), channel_id=1, source_target_pairs={{0,2},{1,3},{2,0},{3,1},{4,6},{5,7},{6,4},{7,5},{8,10},{9,11},{10,... | collective-permute-start | bytes 2654216 | tf_op jit(solution)/shard_map/ppermute | solution.py:25
  194.6 25.3 %collective-permute-start.47 = (bf16[2,96,1056]{2,1,0:T(8,128)(2,1)S(1)}, bf16[2,96,1056]{2,1,0:T(8,128)(2,1)S(1)}, u32[]{:S(2)}, u32[]{:S(2)}) collective-permute-start(bf16[2,96,1056]{2,1,0:T(8,128)(2,1)S(1)} %get-tuple-element.438), channel_id=1, source_target_pairs={{0,1},{1,0},{2,3},{3,2},{4,5},{5,4},{6,7},{7,6},{8,9},{9,8},{10,11... | collective-permute-start | bytes 1216520 | tf_op jit(solution)/shard_map/ppermute | solution.py:25
  195.9 23.9 %collective-permute-start.48 = (bf16[2,96,1056]{2,1,0:T(8,128)(2,1)S(1)}, bf16[2,96,1056]{2,1,0:T(8,128)(2,1)S(1)}, u32[]{:S(2)}, u32[]{:S(2)}) collective-permute-start(bf16[2,96,1056]{2,1,0:T(8,128)(2,1)S(1)} %get-tuple-element.437), channel_id=1, source_target_pairs={{0,2},{1,3},{2,0},{3,1},{4,6},{5,7},{6,4},{7,5},{8,10},{9,11},{10,... | collective-permute-start | bytes 1216520 | tf_op jit(solution)/shard_map/ppermute | solution.py:25
  234.1 12.5 %collective-permute-start.53 = (bf16[320,768]{1,0:T(8,128)(2,1)S(1)}, bf16[320,768]{1,0:T(8,128)(2,1)S(1)}, u32[]{:S(2)}, u32[]{:S(2)}) collective-permute-start(bf16[320,768]{1,0:T(8,128)(2,1)S(1)} %pad_maximum_fusion.8), channel_id=1, source_target_pairs={{0,2},{1,3},{2,0},{3,1},{4,6},{5,7},{6,4},{7,5},{8,10},{9,11},{10,... | collective-permute-start | bytes 1474568 | tf_op jit(solution)/shard_map/ppermute | solution.py:25
  236.2 12.2 %collective-permute-start.52 = (bf16[320,768]{1,0:T(8,128)(2,1)S(1)}, bf16[320,768]{1,0:T(8,128)(2,1)S(1)}, u32[]{:S(2)}, u32[]{:S(2)}) collective-permute-start(bf16[320,768]{1,0:T(8,128)(2,1)S(1)} %pad_maximum_fusion.7), channel_id=1, source_target_pairs={{0,1},{1,0},{2,3},{3,2},{4,5},{5,4},{6,7},{7,6},{8,9},{9,8},{10,11... | collective-permute-start | bytes 1474568 | tf_op jit(solution)/shard_map/ppermute | solution.py:25
  249.0 29.0 %collective-permute-start.54 = (bf16[4,96,1056]{2,1,0:T(8,128)(2,1)S(1)}, bf16[4,96,1056]{2,1,0:T(8,128)(2,1)S(1)}, u32[]{:S(2)}, u32[]{:S(2)}) collective-permute-start(bf16[4,96,1056]{2,1,0:T(8,128)(2,1)S(1)} %pad_maximum_fusion.2), channel_id=1, source_target_pairs={{0,1},{1,0},{2,3},{3,2},{4,5},{5,4},{6,7},{7,6},{8,9},{9,8},{10,11... | collective-permute-start | bytes 2433032 | tf_op jit(solution)/shard_map/ppermute | solution.py:25
  250.4 27.7 %collective-permute-start.55 = (bf16[4,96,1056]{2,1,0:T(8,128)(2,1)S(1)}, bf16[4,96,1056]{2,1,0:T(8,128)(2,1)S(1)}, u32[]{:S(2)}, u32[]{:S(2)}) collective-permute-start(bf16[4,96,1056]{2,1,0:T(8,128)(2,1)S(1)} %pad_maximum_fusion.3), channel_id=1, source_target_pairs={{0,2},{1,3},{2,0},{3,1},{4,6},{5,7},{6,4},{7,5},{8,10},{9,11},{10,... | collective-permute-start | bytes 2433032 | tf_op jit(solution)/shard_map/ppermute | solution.py:25
  251.4 26.6 %collective-permute-start.56 = (bf16[96,576]{1,0:T(8,128)(2,1)S(1)}, bf16[96,576]{1,0:T(8,128)(2,1)S(1)}, u32[]{:S(2)}, u32[]{:S(2)}) collective-permute-start(bf16[96,576]{1,0:T(8,128)(2,1)S(1)} %get-tuple-element.306), channel_id=1, source_target_pairs={{0,8},{8,0},{16,24},{24,16},{1,9},{9,1},{17,25},{25,17},{2,10},{10... | collective-permute-start | bytes 331784 | tf_op jit(solution)/shard_map/ppermute | solution.py:89
  260.8 17.2 %collective-permute-start.57 = (bf16[96,576]{1,0:T(8,128)(2,1)S(1)}, bf16[96,576]{1,0:T(8,128)(2,1)S(1)}, u32[]{:S(2)}, u32[]{:S(2)}) collective-permute-start(bf16[96,576]{1,0:T(8,128)(2,1)S(1)} %get-tuple-element.307), channel_id=1, source_target_pairs={{0,16},{8,24},{16,0},{24,8},{1,17},{9,25},{17,1},{25,9},{2,18},{10... | collective-permute-start | bytes 331784 | tf_op jit(solution)/shard_map/ppermute | solution.py:89
  261.7 16.3 %collective-permute-start.58 = (bf16[96,576]{1,0:T(8,128)(2,1)S(1)}, bf16[96,576]{1,0:T(8,128)(2,1)S(1)}, u32[]{:S(2)}, u32[]{:S(2)}) collective-permute-start(bf16[96,576]{1,0:T(8,128)(2,1)S(1)} %get-tuple-element.308), channel_id=1, source_target_pairs={{0,24},{8,16},{16,8},{24,0},{1,25},{9,17},{17,9},{25,1},{2,26},{10... | collective-permute-start | bytes 331784 | tf_op jit(solution)/shard_map/ppermute | solution.py:89
  290.0 18.9 %collective-permute-start.63 = (bf16[2,96,1056]{2,1,0:T(8,128)(2,1)S(1)}, bf16[2,96,1056]{2,1,0:T(8,128)(2,1)S(1)}, u32[]{:S(2)}, u32[]{:S(2)}) collective-permute-start(bf16[2,96,1056]{2,1,0:T(8,128)(2,1)S(1)} %get-tuple-element.436), channel_id=1, source_target_pairs={{0,1},{1,0},{2,3},{3,2},{4,5},{5,4},{6,7},{7,6},{8,9},{9,8},{10,11... | collective-permute-start | bytes 1216520 | tf_op jit(solution)/shard_map/ppermute | solution.py:25
  291.1 17.9 %collective-permute-start.64 = (bf16[2,96,1056]{2,1,0:T(8,128)(2,1)S(1)}, bf16[2,96,1056]{2,1,0:T(8,128)(2,1)S(1)}, u32[]{:S(2)}, u32[]{:S(2)}) collective-permute-start(bf16[2,96,1056]{2,1,0:T(8,128)(2,1)S(1)} %get-tuple-element.435), channel_id=1, source_target_pairs={{0,2},{1,3},{2,0},{3,1},{4,6},{5,7},{6,4},{7,5},{8,10},{9,11},{10,... | collective-permute-start | bytes 1216520 | tf_op jit(solution)/shard_map/ppermute | solution.py:25
  292.1 16.8 %collective-permute-start.65 = (bf16[96,1056]{1,0:T(8,128)(2,1)S(1)}, bf16[96,1056]{1,0:T(8,128)(2,1)S(1)}, u32[]{:S(2)}, u32[]{:S(2)}) collective-permute-start(bf16[96,1056]{1,0:T(8,128)(2,1)S(1)} %get-tuple-element.329), channel_id=1, source_target_pairs={{0,16},{8,24},{16,0},{24,8},{1,17},{9,25},{17,1},{25,9},{2,18},{10... | collective-permute-start | bytes 608264 | tf_op jit(solution)/shard_map/ppermute | solution.py:89
  294.1 14.8 %collective-permute-start.66 = (bf16[96,1056]{1,0:T(8,128)(2,1)S(1)}, bf16[96,1056]{1,0:T(8,128)(2,1)S(1)}, u32[]{:S(2)}, u32[]{:S(2)}) collective-permute-start(bf16[96,1056]{1,0:T(8,128)(2,1)S(1)} %get-tuple-element.330), channel_id=1, source_target_pairs={{0,24},{8,16},{16,8},{24,0},{1,25},{9,17},{17,9},{25,1},{2,26},{10... | collective-permute-start | bytes 608264 | tf_op jit(solution)/shard_map/ppermute | solution.py:89
  295.5 29.8 %collective-permute-start.73 = (bf16[96,1056]{1,0:T(8,128)(2,1)}, bf16[96,1056]{1,0:T(8,128)(2,1)}, u32[]{:S(2)}, u32[]{:S(2)}) collective-permute-start(bf16[96,1056]{1,0:T(8,128)(2,1)} %get-tuple-element.339), channel_id=1, source_target_pairs={{0,8},{8,0},{16,24},{24,16},{1,9},{9,1},{17,25},{25,17},{2,10},{10... | collective-permute-start | bytes 608264 | tf_op jit(solution)/shard_map/ppermute | solution.py:89
  317.8 22.1 %collective-permute-start.68 = (bf16[4,96,1056]{2,1,0:T(8,128)(2,1)S(1)}, bf16[4,96,1056]{2,1,0:T(8,128)(2,1)S(1)}, u32[]{:S(2)}, u32[]{:S(2)}) collective-permute-start(bf16[4,96,1056]{2,1,0:T(8,128)(2,1)S(1)} %pad_maximum_fusion.5), channel_id=1, source_target_pairs={{0,2},{1,3},{2,0},{3,1},{4,6},{5,7},{6,4},{7,5},{8,10},{9,11},{10,... | collective-permute-start | bytes 2433032 | tf_op jit(solution)/shard_map/ppermute | solution.py:25
  319.1 21.8 %collective-permute-start.67 = (bf16[4,96,1056]{2,1,0:T(8,128)(2,1)S(1)}, bf16[4,96,1056]{2,1,0:T(8,128)(2,1)S(1)}, u32[]{:S(2)}, u32[]{:S(2)}) collective-permute-start(bf16[4,96,1056]{2,1,0:T(8,128)(2,1)S(1)} %pad_maximum_fusion.4), channel_id=1, source_target_pairs={{0,1},{1,0},{2,3},{3,2},{4,5},{5,4},{6,7},{7,6},{8,9},{9,8},{10,11... | collective-permute-start | bytes 2433032 | tf_op jit(solution)/shard_map/ppermute | solution.py:25
  325.3 12.4 %collective-permute-start.71 = (bf16[96,576]{1,0:T(8,128)(2,1)S(1)}, bf16[96,576]{1,0:T(8,128)(2,1)S(1)}, u32[]{:S(2)}, u32[]{:S(2)}) collective-permute-start(bf16[96,576]{1,0:T(8,128)(2,1)S(1)} %get-tuple-element.427), channel_id=1, source_target_pairs={{0,16},{8,24},{16,0},{24,8},{1,17},{9,25},{17,1},{25,9},{2,18},{10... | collective-permute-start | bytes 331784 | tf_op jit(solution)/shard_map/ppermute | solution.py:89
  343.9 12.6 %collective-permute-start.75 = (bf16[96,1056]{1,0:T(8,128)(2,1)S(1)}, bf16[96,1056]{1,0:T(8,128)(2,1)S(1)}, u32[]{:S(2)}, u32[]{:S(2)}) collective-permute-start(bf16[96,1056]{1,0:T(8,128)(2,1)S(1)} %get-tuple-element.412), channel_id=1, source_target_pairs={{0,8},{8,0},{16,24},{24,16},{1,9},{9,1},{17,25},{25,17},{2,10},{10... | collective-permute-start | bytes 608264 | tf_op jit(solution)/shard_map/ppermute | solution.py:89
  348.5 18.7 %collective-permute-start.76 = (bf16[96,1056]{1,0:T(8,128)(2,1)S(1)}, bf16[96,1056]{1,0:T(8,128)(2,1)S(1)}, u32[]{:S(2)}, u32[]{:S(2)}) collective-permute-start(bf16[96,1056]{1,0:T(8,128)(2,1)S(1)} %get-tuple-element.411), channel_id=1, source_target_pairs={{0,16},{8,24},{16,0},{24,8},{1,17},{9,25},{17,1},{25,9},{2,18},{10... | collective-permute-start | bytes 608264 | tf_op jit(solution)/shard_map/ppermute | solution.py:89
  349.5 17.8 %collective-permute-start.77 = (bf16[96,1056]{1,0:T(8,128)(2,1)S(1)}, bf16[96,1056]{1,0:T(8,128)(2,1)S(1)}, u32[]{:S(2)}, u32[]{:S(2)}) collective-permute-start(bf16[96,1056]{1,0:T(8,128)(2,1)S(1)} %get-tuple-element.410), channel_id=1, source_target_pairs={{0,24},{8,16},{16,8},{24,0},{1,25},{9,17},{17,9},{25,1},{2,26},{10... | collective-permute-start | bytes 608264 | tf_op jit(solution)/shard_map/ppermute | solution.py:89
  351.0 16.3 %collective-permute-start.78 = (bf16[160,768]{1,0:T(8,128)(2,1)S(1)}, bf16[160,768]{1,0:T(8,128)(2,1)S(1)}, u32[]{:S(2)}, u32[]{:S(2)}) collective-permute-start(bf16[160,768]{1,0:T(8,128)(2,1)S(1)} %get-tuple-element.440), channel_id=1, source_target_pairs={{0,1},{1,0},{2,3},{3,2},{4,5},{5,4},{6,7},{7,6},{8,9},{9,8},{10,11... | collective-permute-start | bytes 737288 | tf_op jit(solution)/shard_map/ppermute | solution.py:25
  351.9 15.4 %collective-permute-start.79 = (bf16[160,768]{1,0:T(8,128)(2,1)S(1)}, bf16[160,768]{1,0:T(8,128)(2,1)S(1)}, u32[]{:S(2)}, u32[]{:S(2)}) collective-permute-start(bf16[160,768]{1,0:T(8,128)(2,1)S(1)} %get-tuple-element.439), channel_id=1, source_target_pairs={{0,2},{1,3},{2,0},{3,1},{4,6},{5,7},{6,4},{7,5},{8,10},{9,11},{10,... | collective-permute-start | bytes 737288 | tf_op jit(solution)/shard_map/ppermute | solution.py:25
  356.4 34.6 %collective-permute-start.42 = (bf16[320,768]{1,0:T(8,128)(2,1)}, bf16[320,768]{1,0:T(8,128)(2,1)}, u32[]{:S(2)}, u32[]{:S(2)}) collective-permute-start(bf16[320,768]{1,0:T(8,128)(2,1)} %get-tuple-element.434), channel_id=1, source_target_pairs={{0,4},{4,0},{1,5},{5,1},{2,6},{6,2},{3,7},{7,3},{8,12},{12,8},{9,1... | collective-permute-start | bytes 1474568 | tf_op jit(solution)/shard_map/ppermute | solution.py:20
  367.3 28.6 %collective-permute-start.84 = (f32[96,576]{1,0:T(8,128)S(1)}, f32[96,576]{1,0:T(8,128)}, u32[]{:S(2)}, u32[]{:S(2)}) collective-permute-start(f32[96,576]{1,0:T(8,128)S(1)} %get-tuple-element.423), channel_id=1, source_target_pairs={{0,4},{4,0},{1,5},{5,1},{2,6},{6,2},{3,7},{7,3},{8,12},{12,8},{9,1... | collective-permute-start | bytes 663560 | tf_op jit(solution)/shard_map/ppermute | solution.py:20
  367.5 13.7 %collective-permute-start.81 = (bf16[320,768]{1,0:T(8,128)(2,1)S(1)}, bf16[320,768]{1,0:T(8,128)(2,1)S(1)}, u32[]{:S(2)}, u32[]{:S(2)}) collective-permute-start(bf16[320,768]{1,0:T(8,128)(2,1)S(1)} %pad_maximum_fusion.9), channel_id=1, source_target_pairs={{0,1},{1,0},{2,3},{3,2},{4,5},{5,4},{6,7},{7,6},{8,9},{9,8},{10,11... | collective-permute-start | bytes 1474568 | tf_op jit(solution)/shard_map/ppermute | solution.py:25
  368.5 13.4 %collective-permute-start.82 = (bf16[320,768]{1,0:T(8,128)(2,1)S(1)}, bf16[320,768]{1,0:T(8,128)(2,1)S(1)}, u32[]{:S(2)}, u32[]{:S(2)}) collective-permute-start(bf16[320,768]{1,0:T(8,128)(2,1)S(1)} %pad_maximum_fusion.10), channel_id=1, source_target_pairs={{0,2},{1,3},{2,0},{3,1},{4,6},{5,7},{6,4},{7,5},{8,10},{9,11},{10,... | collective-permute-start | bytes 1474568 | tf_op jit(solution)/shard_map/ppermute | solution.py:25
  385.0 17.3 %collective-permute-start.83 = (f32[320,768]{1,0:T(8,128)}, f32[320,768]{1,0:T(8,128)}, u32[]{:S(2)}, u32[]{:S(2)}) collective-permute-start(f32[320,768]{1,0:T(8,128)} %convert_select_fusion), channel_id=1, source_target_pairs={{0,4},{4,0},{1,5},{5,1},{2,6},{6,2},{3,7},{7,3},{8,12},{12,8},{9,1... | collective-permute-start | bytes 2949128 | tf_op jit(solution)/shard_map/ppermute | solution.py:20
  386.0 13.1 %collective-permute-start.85 = (f32[96,1056]{1,0:T(8,128)S(1)}, f32[96,1056]{1,0:T(8,128)S(1)}, u32[]{:S(2)}, u32[]{:S(2)}) collective-permute-start(f32[96,1056]{1,0:T(8,128)S(1)} %broadcast_select_fusion.3), channel_id=1, source_target_pairs={{0,4},{4,0},{1,5},{5,1},{2,6},{6,2},{3,7},{7,3},{8,12},{12,8},{9,1... | collective-permute-start | bytes 1216520 | tf_op jit(solution)/shard_map/ppermute | solution.py:20
  (144 other events, 1697.4 us)

commit v4 on v3

--- a/solution.py
+++ b/solution.py
@@ -11,6 +11,7 @@
 WINDOW = 128
 EPS = 1e-05
 BLOCK = 256
+CHUNK = 128
 BF16 = jnp.bfloat16
 F32 = jnp.float32
 VMEM_BYTES = 36 * 1024 * 1024
@@ -58,6 +59,23 @@
     return one, two
 
 
+def rows_early(parts):
+    _, one0, _, _, two1, far0, far1 = parts
+    return to_mate(far0, 1), to_mate(far1, 2), to_mate(one0, 1), to_mate(two1, 2)
+
+
+def rows_late(parts, early):
+    _, _, one1, two0, _, _, _ = parts
+    return to_mate(add_low(one1, early[1]), 1), to_mate(add_low(two0, early[0]), 2)
+
+
+def rows_sum(parts, early, late):
+    half = early[2].shape[0]
+    upper = add_up(parts[0][:half], early[2], late[1])
+    lower = add_up(parts[0][half:], late[0], early[3])
+    return jnp.concatenate([upper, lower], 0)
+
+
 def to_near(pair):
     return to_mate(pair[0], 1), to_mate(pair[1], 2)
 
@@ -93,12 +111,6 @@
     if four_dp():
         return [block] + [to_peer(block, bit) for bit in (1, 2, 3)]
     return [lax.all_gather(block, "dp", axis=0)]
-
-
-def stacked(blocks, low, high):
-    if four_dp():
-        return jnp.stack([block[low:high] for block in blocks])
-    return blocks[0][:, low:high]
 
 
 def scatter_dp(blocks):
@@ -220,9 +232,13 @@
 def store_halves(place_ref, whole_ref, mine_ref, other_ref, columns):
     core = place_ref[1]
     slots, rows = mine_ref.shape[0], mine_ref.shape[1]
+    packed = mine_ref.shape[2] == 2 * whole_ref.shape[1]
     for slot in range(slots):
         for ref, half in ((mine_ref, core), (other_ref, 1 - core)):
-            ref[slot, :, columns] = whole_ref[slot_rows(place_ref, slot, half, rows), columns]
+            if packed:
+                ref[slot] = pack(whole_ref[slot_rows(place_ref, slot, half, 2 * rows), :])
+            else:
+                ref[slot, :, columns] = whole_ref[slot_rows(place_ref, slot, half, rows), columns]
 
 
 def load_pieces(place_ref, mine_refs, other_refs, whole_ref):
@@ -257,11 +273,32 @@
     return (keys >= first) & (keys < last)
 
 
+def stack_kernel(split, block0_ref, block1_ref, block2_ref, block3_ref, upper_ref, lower_ref):
+    for slot, ref in enumerate((block0_ref, block1_ref, block2_ref, block3_ref)):
+        upper_ref[slot] = ref[:split]
+        lower_ref[slot] = ref[split:]
+
+
+def stack_blocks(blocks, split):
+    rows, columns = blocks[0].shape
+    return pl.pallas_call(
+        functools.partial(stack_kernel, split),
+        out_shape=(
+            jax.ShapeDtypeStruct((4, split, columns), BF16),
+            jax.ShapeDtypeStruct((4, rows - split, columns), BF16),
+        ),
+        in_specs=[WHOLE] * 4,
+        compiler_params=pltpu.CompilerParams(vmem_limit_bytes=VMEM_BYTES),
+        cost_estimate=cost(2),
+        name="stack_blocks",
+    )(*blocks)
+
+
 def attend_kernel(
     span, place_ref, own_ref, one_ref, two_ref, head_ref, tail_ref, mine_ref, other_ref,
     cos_ref, sin_ref, first_ref, last_ref,
     mixed0_ref, mixed1_ref, mixed2_ref, mixed3_ref, queries_ref, keys_ref, values_ref, mass_ref,
-    normed_ref, qkv_ref, key_rows, value_rows, proj, mixed_rows,
+    normed_ref, qkv_ref, outs_ref, key_rows, value_rows, proj, mixed_rows, bias, scores,
 ):
     width, rows = queries_ref.shape
     heads = width // HEAD_DIM
@@ -297,22 +334,30 @@
         start = window_start(block_id, rows, span)
         columns = pl.ds(pl.multiple_of(block_id * BLOCK, BLOCK), BLOCK)
         mask = key_mask(start, span, first_ref[:, columns], last_ref[:, columns])
+        bias[...] = jnp.where(mask, 0.0, -1e30)
         outs = []
         for head in range(heads):
             low = head * HEAD_DIM
             query = queries_ref[low : low + HEAD_DIM, columns] * BF16(HEAD_DIM**-0.5)
-            scores = dot(key_rows[head, pl.ds(start, span), :], query, NN)
-            scores = jnp.where(mask, scores, -1e30)
-            top = jnp.max(scores, axis=0, keepdims=True)
-            expos = jnp.exp(scores - top)
-            total = jnp.sum(expos, axis=0, keepdims=True)
-            probs = (expos * (1.0 / total)).astype(BF16)
-            if span == rows:
-                value = values_ref[low : low + HEAD_DIM, :]
-            else:
-                value = value_rows[head, pl.ds(start, span), :].T
-            outs.append(dot(value, probs, NN))
+            top = jnp.full((1, BLOCK), -2e30, F32)
+            for part in range(0, span, CHUNK):
+                key = key_rows[head, pl.ds(start + part, CHUNK), :]
+                score = dot(key, query, NN) + bias[part : part + CHUNK]
+                scores[part : part + CHUNK] = score
+                top = jnp.maximum(top, jnp.max(score, axis=0, keepdims=True))
+            total = jnp.zeros((1, BLOCK), F32)
+            out = jnp.zeros((HEAD_DIM, BLOCK), F32)
+            for part in range(0, span, CHUNK):
+                expos = jnp.exp(scores[part : part + CHUNK] - top)
+                total += jnp.sum(expos, axis=0, keepdims=True)
+                if span == rows:
+                    value = values_ref[low : low + HEAD_DIM, part : part + CHUNK]
+                else:
+                    value = value_rows[head, pl.ds(start + part, CHUNK), :].T
+                out += dot(value, expos.astype(BF16), NN)
+            outs.append(out * (1.0 / total))
             mass_ref[head : head + 1, columns] = top + jnp.log(total)
+        outs_ref[:, columns] = jnp.concatenate(outs, 0)
         mixed_rows[columns, :] = jnp.concatenate(outs, 0).T.astype(BF16)
         return carry
 
@@ -335,6 +380,7 @@
             mixed, mixed, mixed, mixed, shape, shape, shape, jax.ShapeDtypeStruct((8, rows), F32),
             jax.ShapeDtypeStruct((rows, model), BF16),
             jax.ShapeDtypeStruct((model, 3 * width), BF16),
+            jax.ShapeDtypeStruct((width, rows), F32),
         ),
         in_specs=[SCALARS] + [WHOLE] * 11,
         scratch_shapes=[
@@ -342,6 +388,8 @@
             pltpu.VMEM((heads, rows, HEAD_DIM), BF16),
             pltpu.VMEM((3 * width, rows), F32),
             pltpu.VMEM((rows, width), BF16),
+            pltpu.VMEM((span, BLOCK), F32),
+            pltpu.VMEM((span, BLOCK), F32),
         ],
         compiler_params=pltpu.CompilerParams(vmem_limit_bytes=VMEM_BYTES),
         cost_estimate=cost(11 if is_local else 20),
@@ -352,9 +400,10 @@
 def attend_back_kernel(
     span, place_ref, queries_ref, keys_ref, values_ref, mass_ref,
     grad0_ref, grad1_ref, grad2_ref, grad3_ref,
-    cos_ref, sin_ref, first_ref, last_ref, qkv_ref,
-    part0_ref, part1_ref, part2_ref, part3_ref, out_ref,
-    query_rows, key_rows, value_rows, grad_cols, grad_all, grad_rows, sum_q, sum_k, sum_v, flat,
+    cos_ref, sin_ref, first_ref, last_ref, qkv_ref, outs_ref,
+    own_ref, one0_ref, one1_ref, two0_ref, two1_ref, far0_ref, far1_ref, out_ref,
+    query_rows, key_rows, value_rows, grad_cols, grad_all, grad_rows, sum_q, sum_k, sum_v, flat, bias,
+    probs_low, scores_low,
 ):
     width, rows = queries_ref.shape
     heads = width // HEAD_DIM
@@ -377,23 +426,27 @@
 
     def block(block_id, carry):
         start = window_start(block_id, rows, span)
-        window = pl.ds(start, span)
         columns = pl.ds(pl.multiple_of(block_id * BLOCK, BLOCK), BLOCK)
         mask = key_mask(start, span, first_ref[:, columns], last_ref[:, columns])
+        bias[...] = jnp.where(mask, 0.0, -1e30)
         for head in range(heads):
             cut = slice(head * HEAD_DIM, (head + 1) * HEAD_DIM)
             query = queries_ref[cut, columns] * BF16(scale)
-            key = key_rows[head, window, :]
-            scores = dot(key, query, NN) - mass_ref[head : head + 1, columns]
-            probs = jnp.exp(jnp.where(mask, scores, -1e30))
-            grad_probs = dot(value_rows[head, window, :], grad_cols[cut, columns], NN)
-            weighted = probs * grad_probs
-            inner = jnp.sum(weighted, axis=0, keepdims=True)
-            grad_scores = (weighted - probs * inner).astype(BF16)
-            sum_v[head, window, :] += dot(probs.astype(BF16), grad_rows[head, columns, :], NN)
-            sum_k[head, window, :] += dot(grad_scores, query_rows[head, columns, :], NN)
-            key_cols = keys_ref[cut, :] if span == rows else key.T
-            sum_q[cut, columns] = dot(key_cols, grad_scores, NN)
+            grad = grad_cols[cut, columns]
+            mass = mass_ref[head : head + 1, columns]
+            inner = jnp.sum(grad.astype(F32) * outs_ref[cut, columns], axis=0, keepdims=True)
+            for part in range(0, span, CHUNK):
+                window = pl.ds(start + part, CHUNK)
+                scores = dot(key_rows[head, window, :], query, NN)
+                probs = jnp.exp(scores - mass + bias[part : part + CHUNK])
+                grad_probs = dot(value_rows[head, window, :], grad, NN)
+                probs_low[part : part + CHUNK] = probs.astype(BF16)
+                scores_low[part : part + CHUNK] = (probs * (grad_probs - inner)).astype(BF16)
+            window = pl.ds(start, span)
+            key_cols = keys_ref[cut, :] if span == rows else key_rows[head, window, :].T
+            sum_v[head, window, :] += dot(probs_low[...], grad_rows[head, columns, :], NN)
+            sum_k[head, window, :] += dot(scores_low[...], query_rows[head, columns, :], NN)
+            sum_q[cut, columns] = dot(key_cols, scores_low[...], NN)
         return carry
 
     lax.fori_loop(0, rows // BLOCK, block, 0)
@@ -409,12 +462,18 @@
             flat[part * width + low : part * width + low + HEAD_DIM, :] = raw.astype(BF16)
         flat[2 * width + low : 2 * width + low + HEAD_DIM, :] = sum_v[head].T.astype(BF16)
     out_ref[...] = flat[...].T
-    for bit, ref in enumerate((part0_ref, part1_ref, part2_ref, part3_ref)):
+    targets = ((own_ref,), (one0_ref, one1_ref), (two0_ref, two1_ref), (far0_ref, far1_ref))
+    for bit, refs in enumerate(targets):
         low = pl.multiple_of((me ^ bit) * local, local)
-        ref[...] = dot(out_ref[pl.ds(low, local), :], qkv_ref[...], NT).astype(BF16)
-
-
-def attend_back(place, queries, keys, values, mass, grads, cosines, sines, first, last, qkv, is_local):
+        part = dot(out_ref[pl.ds(low, local), :], qkv_ref[...], NT).astype(BF16)
+        size = local // len(refs)
+        for index, ref in enumerate(refs):
+            ref[...] = part[index * size : (index + 1) * size]
+
+
+def attend_back(
+    place, queries, keys, values, mass, grads, cosines, sines, first, last, qkv, outs, is_local
+):
     width, rows = queries.shape
     model = qkv.shape[0]
     heads = width // HEAD_DIM
@@ -422,19 +481,22 @@
     low_rows = pltpu.VMEM((heads, rows, HEAD_DIM), BF16)
     sums = pltpu.VMEM((heads, rows, HEAD_DIM), F32)
     part = jax.ShapeDtypeStruct((rows // 4, model), BF16)
+    half = jax.ShapeDtypeStruct((rows // 8, model), BF16)
     return pl.pallas_call(
         functools.partial(attend_back_kernel, span),
-        out_shape=(part, part, part, part, jax.ShapeDtypeStruct((rows, 3 * width), BF16)),
-        in_specs=[SCALARS] + [WHOLE] * 13,
+        out_shape=(part,) + (half,) * 6 + (jax.ShapeDtypeStruct((rows, 3 * width), BF16),),
+        in_specs=[SCALARS] + [WHOLE] * 14,
         scratch_shapes=[
             low_rows, low_rows, low_rows, pltpu.VMEM((width, rows), BF16),
             pltpu.VMEM((rows, width), BF16), low_rows,
             pltpu.VMEM((width, rows), F32), sums, sums, pltpu.VMEM((3 * width, rows), BF16),
+            pltpu.VMEM((span, BLOCK), F32), pltpu.VMEM((span, BLOCK), BF16),
+            pltpu.VMEM((span, BLOCK), BF16),
         ],
         compiler_params=pltpu.CompilerParams(vmem_limit_bytes=VMEM_BYTES),
         cost_estimate=cost(11 if is_local else 21),
         name="attend_back_local" if is_local else "attend_back_global",
-    )(place, queries, keys, values, mass, *grads, cosines, sines, first, last, qkv)
+    )(place, queries, keys, values, mass, *grads, cosines, sines, first, last, qkv, outs)
 
 
 def qkv_grad_kernel(place_ref, normed_ref, grad_ref, qkv_ref, mine_ref, other_ref, gain_ref, whole):
@@ -530,6 +592,8 @@
     normed = gained.astype(BF16)
     normed_flip = gained.T.astype(BF16)
     sums[...] = jnp.zeros_like(sums)
+    used = pair + width + units
+    grads[:, used:] = jnp.zeros((grads.shape[0], grads.shape[1] - used), BF16)
 
     def feed(part, carry):
         gate_up = dot(normed, mats[part, :, :pair], NN)
@@ -541,7 +605,7 @@
         grad_gate = grad_hidden * up * (cumulative + gate * density)
         grad_up = grad_hidden * gelu
         grad_pair = jnp.concatenate([grad_gate, grad_up], 1).astype(BF16)
-        grads[:, pair + width :] = dot(grad_flip, hidden, NN).astype(BF16)
+        grads[:, pair + width : used] = dot(grad_flip, hidden, NN).astype(BF16)
         grads[:, :pair] = dot(normed_flip, grad_pair, NN).astype(BF16)
         for columns in (slice(0, pair), slice(pair + width, None)):
             store_halves(
@@ -571,8 +635,7 @@
 
 def token_back(place, grad, mid, mixed, mine, other, gain, pair):
     shape = mine[0].shape
-    total = pair + mixed[0].shape[1] // 2 + pair // 2
-    half = jax.ShapeDtypeStruct((4,) + shape[:2] + (total,), BF16)
+    half = jax.ShapeDtypeStruct((4,) + shape, BF16)
     mixed_grad = jax.ShapeDtypeStruct(mixed[0].shape, BF16)
     return pl.pallas_call(
         functools.partial(token_back_kernel, pair),
@@ -585,7 +648,7 @@
         scratch_shapes=[
             pltpu.VMEM(mid.shape, F32),
             pltpu.VMEM((4, mid.shape[1], shape[2]), BF16),
-            pltpu.VMEM((mid.shape[1], total), BF16),
+            pltpu.VMEM((mid.shape[1], shape[2]), BF16),
         ],
         compiler_params=pltpu.CompilerParams(vmem_limit_bytes=VMEM_BYTES),
         cost_estimate=cost(20),
@@ -650,21 +713,22 @@
     )
     split = shard_rows // 2
     total = first_half.shape[0]
-    qkv_shape = (4, split, 3 * width) if four_dp() else (1, model // 2, 3 * width)
-
-    def qkv_halves(blocks):
-        block = stacked(blocks, split, total)
-        if not four_dp():
-            block = jnp.concatenate([block[..., : 3 * width], block[..., 3 * width :]], 1)
-        return halves(block)
+    qkv_shape = (4, split // 2, 6 * width) if four_dp() else (1, model // 2, 3 * width)
+
+    def split_blocks(blocks):
+        if four_dp():
+            upper, lower = stack_blocks(blocks, split)
+            return upper, halves(lower)
+        upper, lower = blocks[0][:, :split], blocks[0][:, split:]
+        lower = jnp.concatenate([lower[..., : 3 * width], lower[..., 3 * width :]], 1)
+        return upper, halves(lower)
 
     normed, first_half, second_half = after((normed, first_half, second_half))
     near, blocks = to_neighbours(normed), gather_dp(first_half)
     far = to_far(*after(near))
     far, blocks = after((far, blocks))
-    mats_first = stacked(blocks, 0, split)
-    qkv_parts = [qkv_halves(blocks), None]
-    mats_first, second_half = after((mats_first, second_half), qkv_parts[0])
+    mats_first, qkv_first = split_blocks(blocks)
+    mats_first, second_half = after((mats_first, second_half), qkv_first)
     pieces = (normed,) + near + far
     saved_attend = [None, None]
     saved_token = [None, None]
@@ -672,10 +736,10 @@
     mats_near = to_neighbours(mats_first)
     second_blocks = gather_dp(second_half)
     second_blocks, second_late = second_blocks[:3], second_blocks[3:]
-    *mixed, queries, keys, values, mass, normed_full, qkv = attend(
-        place, pieces, *qkv_parts[0], width, *tables[0], *bounds[0], True
-    )
-    saved_attend[0] = (queries, keys, values, mass, normed_full, qkv)
+    *mixed, queries, keys, values, mass, normed_full, qkv, outs = attend(
+        place, pieces, *qkv_first, width, *tables[0], *bounds[0], True
+    )
+    saved_attend[0] = (queries, keys, values, mass, normed_full, qkv, outs)
     mixed, mats_first, mats_near, second_blocks = after(
         (mixed, mats_first, mats_near, second_blocks)
     )
@@ -686,18 +750,17 @@
     )
     saved_token[0] = (mid, mixed) + mats
 
-    normed, second_late = after((normed, second_late))
-    near = after(to_neighbours(normed))
+    near, second_late = after((to_neighbours(normed), second_late))
     blocks = second_blocks + second_late
-    qkv_parts[1] = qkv_halves(blocks)
-    far, qkv_parts[1] = after((to_far(*near), qkv_parts[1]))
+    mats_second, qkv_second = split_blocks(blocks)
+    far, qkv_second = after((to_far(*near), qkv_second))
     pieces = (normed,) + near + far
-    mats_second = after(stacked(blocks, 0, split), far)
+    mats_second = after(mats_second, far)
     second_near = to_neighbours(mats_second)
-    *mixed, queries, keys, values, mass, normed_full, qkv = attend(
-        place, pieces, *qkv_parts[1], width, *tables[1], *bounds[1], False
-    )
-    saved_attend[1] = (queries, keys, values, mass, normed_full, qkv)
+    *mixed, queries, keys, values, mass, normed_full, qkv, outs = attend(
+        place, pieces, *qkv_second, width, *tables[1], *bounds[1], False
+    )
+    saved_attend[1] = (queries, keys, values, mass, normed_full, qkv, outs)
     mixed, second_near = after((mixed, second_near))
     mixed, second_far = after((swap_tensor(mixed), to_far(*second_near)))
     mats = piece_halves((mats_second,) + second_near + second_far)
@@ -713,21 +776,20 @@
         )
 
     def attend_step(layer, mixed_grad):
-        queries, keys, values, mass, _, qkv = saved_attend[layer]
+        queries, keys, values, mass, _, qkv, outs = saved_attend[layer]
         return attend_back(
             place, queries, keys, values, mass, mixed_grad, *tables[layer], *bounds[layer],
-            qkv, layer == 0,
+            qkv, outs, layer == 0,
         )
 
     def weight_step(layer, grad_projected):
-        normed_full, qkv = saved_attend[layer][4:]
+        normed_full, qkv = saved_attend[layer][4:6]
         mine, other, gain_sum = qkv_grad(
             place, normed_full, grad_projected, qkv, qkv_shape
         )
         return half_sums(mine, other) + (gain_sum.reshape(1, model) / gain_rows[layer][:, :model],)
 
-    def norm_step(layer, partial_in, near, grad_mid):
-        grad_normed = add_up(partial_in[0], *near)
+    def norm_step(layer, grad_normed, grad_mid):
         unit, scale = norm_parts((stream, first_out)[layer].astype(F32))
         return grad_mid + norm_back(grad_normed, unit, scale, gain_rows[layer][:, :model])
 
@@ -739,56 +801,57 @@
     kept, came = half_sums(mine_grad, other_grad)
     mixed_grad, kept, came = after((mixed_grad, kept, came))
     far = far_terms(add_low(kept[3], came[3]))
-    *partial_in, grad_projected = attend_step(1, mixed_grad)
-    partial_in, grad_projected, far = after((partial_in, grad_projected, far))
-    in_far = far_terms(partial_in[3])
+    *parts, grad_projected = attend_step(1, mixed_grad)
+    parts, grad_projected, far = after((parts, grad_projected, far))
+    early = rows_early(parts)
     pair_terms = near_terms(add_low(kept[1], came[1]), add_low(kept[2], came[2]), *far)
     qkv_kept, qkv_came, gain_attn = weight_step(1, grad_projected)
     second_gain = jnp.concatenate([gain_attn, gain_mlp], 1)
-    in_far, qkv_kept, qkv_came = after((in_far, qkv_kept, qkv_came))
-    second_qkv = qkv_blocks(qkv_kept, qkv_came)
-    in_near = to_near(near_terms(partial_in[1], partial_in[2], *in_far))
-    in_near, pair_terms, second_qkv = after((in_near, pair_terms, second_qkv))
-    near, second_qkv_came = to_near(pair_terms), scatter_dp(second_qkv)
-    grad = norm_step(1, partial_in, in_near, grad_mid).astype(BF16)
+    late = rows_late(parts, early)
+    late, pair_terms, qkv_kept, qkv_came = after((late, pair_terms, qkv_kept, qkv_came), early)
+    near = to_near(pair_terms)
+    grad = norm_step(1, rows_sum(parts, early, late), grad_mid).astype(BF16)
     second_grad = grad.astype(F32)
 
-    second_kept, second_came = kept, came
+    second_kept, second_came, second_qkv = kept, came, qkv_blocks(qkv_kept, qkv_came)
     mine_grad, other_grad, *mixed_grad, grad_mid, gain_mlp = token_step(0, grad)
-    mixed_grad, other_grad, near, second_qkv_came = after(
-        (mixed_grad, other_grad, near, second_qkv_came)
-    )
+    mixed_grad, other_grad, near = after((mixed_grad, other_grad, near))
     mixed_grad = swap_tensor(mixed_grad)
     kept, came = half_sums(mine_grad, other_grad)
-    second_mats = slot_sums(second_kept, second_came, near)
-    mixed_grad, kept, came, second_mats = after((mixed_grad, kept, came, second_mats))
+    second = slot_sums(second_kept, second_came, near)
+    if four_dp():
+        second = [jnp.concatenate(block, 0) for block in zip(second, second_qkv)]
+    mixed_grad, kept, came, second = after((mixed_grad, kept, came, second))
     far = far_terms(add_low(kept[3], came[3]))
-    second_mats_came = scatter_dp(second_mats)
-    second_early, second_late = second_mats_came[1:], second_mats_came[:1]
-    *partial_in, grad_projected = attend_step(0, mixed_grad)
-    partial_in, grad_projected, far, kept, came, second_early = after(
-        (partial_in, grad_projected, far, kept, came, second_early)
-    )
-    second_mats_came = second_late + second_early
-
-    near = to_near(near_terms(add_low(kept[1], came[1]), add_low(kept[2], came[2]), *far))
+    *parts, grad_projected = attend_step(0, mixed_grad)
+    parts, grad_projected, far, kept, came = after((parts, grad_projected, far, kept, came))
+
+    pair_terms = near_terms(add_low(kept[1], came[1]), add_low(kept[2], came[2]), *far)
+    pair_terms, grad_projected = after((pair_terms, grad_projected))
+    near, second_came = to_near(pair_terms), scatter_dp(second)
     qkv_kept, qkv_came, gain_attn = weight_step(0, grad_projected)
     first_gain = jnp.concatenate([gain_attn, gain_mlp], 1)
-    first_qkv = qkv_blocks(qkv_kept, qkv_came)
-    first_qkv_came = scatter_dp(first_qkv)
     gain_sum = jnp.where(core == 0, first_gain, second_gain)
     gain_sum += swap_cores(jnp.where(core == 0, second_gain, first_gain))
-    near, first_qkv_came, second_mats_came, partial_in, gain_sum = after(
-        (near, first_qkv_came, second_mats_came, partial_in, gain_sum)
-    )
-    first_mats = slot_sums(kept, came, near)
-    first_mats_came, in_far = scatter_dp(first_mats), far_terms(partial_in[3])
+    first_qkv = qkv_blocks(qkv_kept, qkv_came)
+    near, second_came, parts, gain_sum, first_qkv = after(
+        (near, second_came, parts, gain_sum, first_qkv)
+    )
+    first = slot_sums(kept, came, near)
+    if four_dp():
+        first = [jnp.concatenate(block, 0) for block in zip(first, first_qkv)]
+    first_came = scatter_dp(first)
     gain_sum += to_mate(gain_sum, 1)
-    first_mats_came, in_far, partial_in, gain_sum = after(
-        (first_mats_came, in_far, partial_in, gain_sum)
-    )
-    in_near = to_near(near_terms(partial_in[1], partial_in[2], *in_far))
+    rows_far = (to_mate(parts[5], 1), to_mate(parts[6], 2))
+    rows_far, parts, gain_sum = after((rows_far, parts, gain_sum))
+    rows_near = to_near(
+        (
+            jnp.concatenate([parts[1], add_low(parts[2], rows_far[1])], 0),
+            jnp.concatenate([add_low(parts[3], rows_far[0]), parts[4]], 0),
+        )
+    )
     gain_sum += to_mate(gain_sum, 2)
+    gain_sum, first_came = after((gain_sum, first_came))
     chunk = model * 2 // (4 * lax.axis_size("dp"))
     me = lax.axis_index("dp") * 4 + lax.axis_index("tensor")
     if four_dp():
@@ -797,15 +860,21 @@
     else:
         gain_sum = lax.psum(gain_sum, "dp")
     gain_part = lax.dynamic_slice_in_dim(gain_sum[0], me * chunk, chunk, 0)
-    first_grad = norm_step(0, partial_in, in_near, grad_mid)
+    first_grad = norm_step(0, add_up(parts[0], *rows_near), grad_mid)
     input_grads = (first_grad, second_grad)
 
-    qkv_total = own_layer(
-        scatter_sum(first_qkv, first_qkv_came), scatter_sum(second_qkv, second_qkv_came)
-    )
-    mats_total = own_layer(
-        scatter_sum(first_mats, first_mats_came), scatter_sum(second_mats, second_mats_came)
-    )
+    if four_dp():
+        total_grad = own_layer(scatter_sum(first, first_came), scatter_sum(second, second_came))
+        total_grad = total_grad.reshape(2, total, 6 * width)
+        mats_total = total_grad[:, :split].reshape(shard_rows, 6 * width)
+        qkv_total = total_grad[:, split:].reshape(-1, 6 * width)
+    else:
+        mats_total = own_layer(scatter_sum(first, ()), scatter_sum(second, ()))
+        qkv_total = own_layer(scatter_sum(first_qkv, ()), scatter_sum(second_qkv, ()))
+    if four_dp():
+        qkv_total = qkv_total.reshape(2, shard_rows // 4, 2, 3 * width)
+        qkv_total = jnp.moveaxis(qkv_total, 2, 1).reshape(shard_rows, 3 * width)
+
     activations = join_halves(
         jnp.where(core == 0, first_out, second_out),
         swap_cores(jnp.where(core == 0, second_out, first_out)),
@@ -822,7 +891,7 @@
         qkv_total.reshape(qkv_weight.shape),
         mats_total[:, pair : pair + width].T[None],
         mats_total[:, :pair].reshape(gate_up_weight.shape),
-        mats_total[:, pair + width :].T[None],
+        mats_total[:, pair + width : pair + width + pair // 2].T[None],
         gain_part[None],
     )
 

time: 411 us -> 389 us (0.946)
  starting transfers between devices: 102 us -> 93.5 us
  Pallas kernels: 110 us -> 102 us
  waiting for transfers between devices: 121 us -> 129 us
  local copies, waits for them, and re-layouts: 28.6 us -> 21 us
  other arithmetic: 40.5 us -> 36 us
    ppermute x20 -> x14, waiting for transfers between devices: 41.5 us -> 64.5 us  [to_peer(): return lax.ppermute(block, 'dp', [(i, i ^ bit) for i in range(4)])]
    ppermute x46 -> x48, waiting for transfers between devices: 76.2 us -> 60 us  [to_mate(): return lax.ppermute(block, 'tensor', [(i, i ^ bit) for i in range(size)])]
    ppermute x20 -> x14, starting transfers between devices: 45.9 us -> 35.3 us  [to_peer(): return lax.ppermute(block, 'dp', [(i, i ^ bit) for i in range(4)])]
    pallas_call x2, Pallas kernels: 29.3 us -> 22.4 us  [attend(): pl.pallas_call(functools.partial(attend_kernel, span), out_shape=(mixed,...]
    ppermute x46 -> x48, starting transfers between devices: 52.7 us -> 55.3 us  [to_mate(): return lax.ppermute(block, 'tensor', [(i, i ^ bit) for i in range(size)])]
    unnamed x210 -> x178, local copies, waits for them, and re-layouts: 15.5 us -> 15 us
  transfers between devices with their start and end apart: 89 -> 84, of which waited for: 42 -> 39; matrix products, arithmetic and copies ran while one was open for 12% -> 9% of each run, Pallas kernels for 21% -> 17%
where the time goes in v4:
time: 389 us; the launch traced here: 384 us
  waiting for transfers between devices  129 us (33%)
  Pallas kernels  102 us (26%)
  starting transfers between devices  93.5 us (24%)
  other arithmetic  36 us (9%)
  local copies, waits for them, and re-layouts  21 us (5%)
    ppermute x14, waiting for transfers between devices, to_peer(): return lax.ppermute(block, 'dp', [(i, i ^ bit) for i in range(4)])  64.5 us
    ppermute x48, waiting for transfers between devices, to_mate(): return lax.ppermute(block, 'tensor', [(i, i ^ bit) for i in range(size)])  60 us
    ppermute x48, starting transfers between devices, to_mate(): return lax.ppermute(block, 'tensor', [(i, i ^ bit) for i in range(size)])  55.3 us
    ppermute x14, starting transfers between devices, to_peer(): return lax.ppermute(block, 'dp', [(i, i ^ bit) for i in range(4)])  35.3 us
    pallas_call x2, Pallas kernels, attend_back(): pl.pallas_call(functools.partial(attend_back_kernel, span), out_shape=(pa...  29.5 us
    pallas_call x2, Pallas kernels, token_back(): pl.pallas_call(functools.partial(token_back_kernel, pair), out_shape=(hal...  27.5 us
    pallas_call x2, Pallas kernels, attend(): pl.pallas_call(functools.partial(attend_kernel, span), out_shape=(mixed,...  22.4 us
    pallas_call x2, Pallas kernels, token_forward(): pl.pallas_call(functools.partial(token_kernel, pair), out_shape=(jax.Shap...  15.1 us
  transfers between devices with their start and end apart: 84, of which 39 were waited for; matrix products, arithmetic and copies ran while one was open for 9% of the time, Pallas kernels for 17%

profile of v4, /device:TPU:0, one launch (start us, length us, event | category | flops | bytes accessed | tf_op | source)
XLA Modules:
  0.0 383.5 jit_solution(2247853652961729426)
XLA Ops:
  7.7 3.0 collective-permute-start.2
  12.4 1.6 collective-permute-start.6
  14.1 2.6 collective-permute-start.7
  16.9 5.2 %collective-permute-done.2.one_ref = bf16[320,768]{1,0:T(8,128)(2,1)S(1)} collective-permute-done((bf16[320,768]{1,0:T(8,128)(2,1)S(1)}, bf16[320,768]{1,0:T(8,128)(2,1)S(1)}, u32[]{:S(2)}, u32[]{:S(2)}) %collective-permute-start.2) | collective-permute-done | bytes 491552 | tf_op jit(solution)/shard_map/ppermute | solution.py:26
  26.1 1.7 collective-permute-start.5
  28.0 12.0 %collective-permute-done.7.block2_ref = bf16[144,1152]{1,0:T(8,128)(2,1)} collective-permute-done((bf16[144,1152]{1,0:T(8,128)(2,1)S(1)}, bf16[144,1152]{1,0:T(8,128)(2,1)}, u32[]{:S(2)}, u32[]{:S(2)}) %collective-permute-start.7) | collective-permute-done | bytes 331808 | tf_op jit(solution)/shard_map/ppermute | solution.py:107
  44.2 5.9 %collective-permute-start.12 = (bf16[144,1152]{1,0:T(8,128)(2,1)S(1)}, bf16[144,1152]{1,0:T(8,128)(2,1)S(1)}, u32[]{:S(2)}, u32[]{:S(2)}) collective-permute-start(bf16[144,1152]{1,0:T(8,128)(2,1)S(1)} %get-tuple-element.244.block0_ref), channel_id=1, source_target_pairs={{0,8},{8,0},{16,24},{24,16},{1,9},{9,1},{17,25},{25,17},{2,10},{10... | collective-permute-start | bytes 995336 | tf_op jit(solution)/shard_map/ppermute | solution.py:107
  51.1 8.7 %attend_local.1 = (bf16[160,384]{1,0:T(8,128)(2,1)S(1)}, bf16[160,384]{1,0:T(8,128)(2,1)S(1)}, bf16[160,384]{1,0:T(8,128)(2,1)S(1)}, bf16[160,384]{1,0:T(8,128)(...) custom-call(s32[6]{0:T(128)S(1)} %stack.69.place_ref, ...), custom_call_target="tpu_custom_call" | custom-call | flops 12650000384 | bytes 39600000 | tf_op jit(solution)/shard_map/attend_local/pallas_call | solution.py:377
  64.6 2.5 collective-permute-done.13.block2_ref
  70.8 1.6 collective-permute-start.17
  72.4 1.6 collective-permute-start.18
  75.2 2.2 collective-permute-done.16.mixed3_ref
  77.4 5.1 %collective-permute-done.17.refs_3_ = bf16[2,96,1152]{2,1,0:T(8,128)(2,1)S(1)} collective-permute-done((bf16[2,96,1152]{2,1,0:T(8,128)(2,1)S(1)}, bf16[2,96,1152]{2,1,0:T(8,128)(2,1)S(1)}, u32[]{:S(2)}, u32[]{:S(2)}) %collective-permute-start.17) | collective-permute-done | bytes 442400 | tf_op jit(solution)/shard_map/ppermute | solution.py:26
  85.6 7.0 %token_forward.2 = (f32[320,768]{1,0:T(8,128)S(1)}, bf16[320,768]{1,0:T(8,128)(2,1)S(1)}, bf16[320,768]{1,0:T(8,128)(2,1)S(1)}) custom-call(s32[6]{0:T(128)S(1)} %stack.69.place_ref, bf16[160,384]{1,0:T(8,128)(2,1)S(1)} %get-tuple-element.233.mixed0_ref, bf16[160,384]{1,0:T(8,128)(2,1)S(1)} %collective-permute-done.14.mixed1_ref, ...), custom_call_target="tpu_custom_call" | custom-call | flops 11500000256 | bytes 36000000 | tf_op jit(solution)/shard_map/token_forward/pallas_call | solution.py:558
  94.4 2.5 collective-permute-start.26
  96.8 8.7 %collective-permute-done.26.block3_ref = bf16[144,1152]{1,0:T(8,128)(2,1)S(1)} collective-permute-done((bf16[144,1152]{1,0:T(8,128)(2,1)S(1)}, bf16[144,1152]{1,0:T(8,128)(2,1)S(1)}, u32[]{:S(2)}, u32[]{:S(2)}) %collective-permute-start.26) | collective-permute-done | bytes 331808 | tf_op jit(solution)/shard_map/ppermute | solution.py:107
  109.1 5.8 %collective-permute-done.27.head_ref = bf16[160,768]{1,0:T(8,128)(2,1)S(1)} collective-permute-done((bf16[160,768]{1,0:T(8,128)(2,1)S(1)}, bf16[160,768]{1,0:T(8,128)(2,1)S(1)}, u32[]{:S(2)}, u32[]{:S(2)}) %collective-permute-start.27) | collective-permute-done | bytes 245792 | tf_op jit(solution)/shard_map/ppermute | solution.py:26
  117.8 13.7 %attend_global.1 = (bf16[160,384]{1,0:T(8,128)(2,1)S(1)}, bf16[160,384]{1,0:T(8,128)(2,1)S(1)}, bf16[160,384]{1,0:T(8,128)(2,1)S(1)}, bf16[160,384]{1,0:T(8,128)...) custom-call(s32[6]{0:T(128)S(1)} %stack.69.place_ref, ...), custom_call_target="tpu_custom_call" | custom-call | flops 23000000512 | bytes 72000000 | tf_op jit(solution)/shard_map/attend_global/pallas_call | solution.py:377
  131.5 5.6 %collective-permute-done.30.refs_1_ = bf16[4,96,1152]{2,1,0:T(8,128)(2,1)S(1)} collective-permute-done((bf16[4,96,1152]{2,1,0:T(8,128)(2,1)S(1)}, bf16[4,96,1152]{2,1,0:T(8,128)(2,1)S(1)}, u32[]{:S(2)}, u32[]{:S(2)}) %collective-permute-start.30) | collective-permute-done | bytes 884768 | tf_op jit(solution)/shard_map/ppermute | solution.py:26
  143.5 3.0 collective-permute-done.33.mixed2_ref
  147.0 7.0 %collective-permute-done.35.refs_3_ = bf16[2,96,1152]{2,1,0:T(8,128)(2,1)S(1)} collective-permute-done((bf16[2,96,1152]{2,1,0:T(8,128)(2,1)S(1)}, bf16[2,96,1152]{2,1,0:T(8,128)(2,1)S(1)}, u32[]{:S(2)}, u32[]{:S(2)}) %collective-permute-start.35) | collective-permute-done | bytes 442400 | tf_op jit(solution)/shard_map/ppermute | solution.py:26
  157.3 8.1 %token_forward.3 = (f32[320,768]{1,0:T(8,128)S(1)}, bf16[320,768]{1,0:T(8,128)(2,1)S(1)}, bf16[320,768]{1,0:T(8,128)(2,1)}) custom-call(s32[6]{0:T(128)S(1)} %stack.69.place_ref, bf16[160,384]{1,0:T(8,128)(2,1)S(1)} %get-tuple-element.265.mixed0_ref, bf16[160,384]{1,0:T(8,128)(2,1)S(1)} %collective-permute-done.32.mixed1_ref, ...), custom_call_target="tpu_custom_call" | custom-call | flops 11500000256 | bytes 36000000 | tf_op jit(solution)/shard_map/token_forward/pallas_call | solution.py:558
  166.2 13.6 %token_back.2 = (bf16[4,4,96,1152]{3,2,1,0:T(8,128)(2,1)S(1)}, bf16[4,4,96,1152]{3,2,1,0:T(8,128)(2,1)S(1)}, bf16[160,384]{1,0:T(8,128)(2,1)S(1)}, bf16[160,384]...) custom-call(s32[6]{0:T(128)S(1)} %stack.69.place_ref, ...), custom_call_target="tpu_custom_call" | custom-call | flops 23000000512 | bytes 72000000 | tf_op jit(solution)/shard_map/token_back/pallas_call | solution.py:640
  181.8 2.2 collective-permute-start.45
  184.1 2.6 collective-permute-done.43.grad1_ref
  186.7 2.6 collective-permute-done.45.grad3_ref
  193.6 19.5 %attend_back_global.1 = (bf16[320,768]{1,0:T(8,128)(2,1)S(1)}, bf16[160,768]{1,0:T(8,128)(2,1)}, bf16[160,768]{1,0:T(8,128)(2,1)S(1)}, bf16[160,768]{1,0:T(8,128...) custom-call(s32[6]{0:T(128)S(1)} %stack.69.place_ref, ...), custom_call_target="tpu_custom_call" | custom-call | flops 24149999616 | bytes 75600000 | tf_op jit(solution)/shard_map/attend_back_global/pallas_call | solution.py:485
  213.9 3.3 qkv_grad.2
  223.5 3.8 collective-permute-done.52
  233.2 4.5 %collective-permute-done.53 = bf16[160,768]{1,0:T(8,128)(2,1)S(1)} collective-permute-done((bf16[160,768]{1,0:T(8,128)(2,1)S(1)}, bf16[160,768]{1,0:T(8,128)(2,1)S(1)}, u32[]{:S(2)}, u32[]{:S(2)}) %collective-permute-start.53) | collective-permute-done | bytes 245792 | tf_op jit(solution)/shard_map/ppermute | solution.py:26
  244.2 13.8 %token_back.3 = (bf16[4,4,96,1152]{3,2,1,0:T(8,128)(2,1)S(1)}, bf16[4,4,96,1152]{3,2,1,0:T(8,128)(2,1)S(1)}, bf16[160,384]{1,0:T(8,128)(2,1)S(1)}, bf16[160,384]...) custom-call(s32[6]{0:T(128)S(1)} %stack.69.place_ref, ...), custom_call_target="tpu_custom_call" | custom-call | flops 23000000512 | bytes 72000000 | tf_op jit(solution)/shard_map/token_back/pallas_call | solution.py:640
  258.1 2.5 collective-permute-done.56
  264.6 1.8 collective-permute-start.60
  266.4 2.0 fusion.32
  275.0 10.0 %attend_back_local.1 = (bf16[320,768]{1,0:T(8,128)(2,1)S(1)}, bf16[160,768]{1,0:T(8,128)(2,1)S(1)}, bf16[160,768]{1,0:T(8,128)(2,1)S(1)}, bf16[160,768]{1,0:T(8,...) custom-call(s32[6]{0:T(128)S(1)} %stack.69.place_ref, ...), custom_call_target="tpu_custom_call" | custom-call | flops 12650000384 | bytes 39600000 | tf_op jit(solution)/shard_map/attend_back_local/pallas_call | solution.py:485
  288.5 2.5 qkv_grad.3
  293.8 6.9 %collective-permute-start.66 = (bf16[144,1152]{1,0:T(8,128)(2,1)}, bf16[144,1152]{1,0:T(8,128)(2,1)S(1)}, u32[]{:S(2)}, u32[]{:S(2)}) collective-permute-start(bf16[144,1152]{1,0:T(8,128)(2,1)} %pad_maximum_fusion.8), channel_id=1, source_target_pairs={{0,8},{8,0},{16,24},{24,16},{1,9},{9,1},{17,25},{25,17},{2,10},{10... | collective-permute-start | bytes 995336 | tf_op jit(solution)/shard_map/ppermute | solution.py:107
  304.1 1.6 collective-permute-start.68
  305.8 10.1 %collective-permute-done.66 = bf16[144,1152]{1,0:T(8,128)(2,1)S(1)} collective-permute-done((bf16[144,1152]{1,0:T(8,128)(2,1)}, bf16[144,1152]{1,0:T(8,128)(2,1)S(1)}, u32[]{:S(2)}, u32[]{:S(2)}) %collective-permute-start.66) | collective-permute-done | bytes 331808 | tf_op jit(solution)/shard_map/ppermute | solution.py:107
  315.9 10.8 %collective-permute-done.67 = bf16[144,1152]{1,0:T(8,128)(2,1)S(1)} collective-permute-done((bf16[144,1152]{1,0:T(8,128)(2,1)}, bf16[144,1152]{1,0:T(8,128)(2,1)S(1)}, u32[]{:S(2)}, u32[]{:S(2)}) %collective-permute-start.67) | collective-permute-done | bytes 331808 | tf_op jit(solution)/shard_map/ppermute | solution.py:107
  329.2 2.0 fusion.31
  331.2 2.4 collective-permute-start.80
  334.4 6.0 %collective-permute-start.79 = (bf16[144,1152]{1,0:T(8,128)(2,1)S(1)}, bf16[144,1152]{1,0:T(8,128)(2,1)S(1)}, u32[]{:S(2)}, u32[]{:S(2)}) collective-permute-start(bf16[144,1152]{1,0:T(8,128)(2,1)S(1)} %pad_maximum_fusion.12), channel_id=1, source_target_pairs={{0,16},{8,24},{16,0},{24,8},{1,17},{9,25},{17,1},{25,9},{2,18},{10... | collective-permute-start | bytes 995336 | tf_op jit(solution)/shard_map/ppermute | solution.py:107
  344.3 2.7 collective-permute-start.78
  348.0 14.1 %collective-permute-done.79 = bf16[144,1152]{1,0:T(8,128)(2,1)S(1)} collective-permute-done((bf16[144,1152]{1,0:T(8,128)(2,1)S(1)}, bf16[144,1152]{1,0:T(8,128)(2,1)S(1)}, u32[]{:S(2)}, u32[]{:S(2)}) %collective-permute-start.79) | collective-permute-done | bytes 331808 | tf_op jit(solution)/shard_map/ppermute | solution.py:107
  366.2 3.6 collective-permute-done.82
  370.8 2.3 maximum_select_fusion.2
  380.1 3.0 maximum_select_fusion
  (424 shorter events, 115.5 us)
Async XLA Ops:
  7.7 14.4 %collective-permute-start.2 = (bf16[320,768]{1,0:T(8,128)(2,1)S(1)}, bf16[320,768]{1,0:T(8,128)(2,1)S(1)}, u32[]{:S(2)}, u32[]{:S(2)}) collective-permute-start(bf16[320,768]{1,0:T(8,128)(2,1)S(1)} %fusion.15.own_ref), channel_id=1, source_target_pairs={{0,1},{1,0},{2,3},{3,2},{4,5},{5,4},{6,7},{7,6},{8,9},{9,8},{10,11... | collective-permute-start | bytes 1474568 | tf_op jit(solution)/shard_map/ppermute | solution.py:26
  10.7 12.9 %collective-permute-start.3 = (bf16[320,768]{1,0:T(8,128)(2,1)S(1)}, bf16[320,768]{1,0:T(8,128)(2,1)S(1)}, u32[]{:S(2)}, u32[]{:S(2)}) collective-permute-start(bf16[320,768]{1,0:T(8,128)(2,1)S(1)} %fusion.15.own_ref), channel_id=1, source_target_pairs={{0,2},{1,3},{2,0},{3,1},{4,6},{5,7},{6,4},{7,5},{8,10},{9,11},{10,... | collective-permute-start | bytes 1474568 | tf_op jit(solution)/shard_map/ppermute | solution.py:26
  12.4 15.6 %collective-permute-start.6 = (bf16[144,1152]{1,0:T(8,128)(2,1)S(1)}, bf16[144,1152]{1,0:T(8,128)(2,1)}, u32[]{:S(2)}, u32[]{:S(2)}) collective-permute-start(bf16[144,1152]{1,0:T(8,128)(2,1)S(1)} %get-tuple-element.214.block0_ref), channel_id=1, source_target_pairs={{0,8},{8,0},{16,24},{24,16},{1,9},{9,1},{17,25},{25,17},{2,10},{10... | collective-permute-start | bytes 995336 | tf_op jit(solution)/shard_map/ppermute | solution.py:107
  14.1 26.0 %collective-permute-start.7 = (bf16[144,1152]{1,0:T(8,128)(2,1)S(1)}, bf16[144,1152]{1,0:T(8,128)(2,1)}, u32[]{:S(2)}, u32[]{:S(2)}) collective-permute-start(bf16[144,1152]{1,0:T(8,128)(2,1)S(1)} %get-tuple-element.214.block0_ref), channel_id=1, source_target_pairs={{0,16},{8,24},{16,0},{24,8},{1,17},{9,25},{17,1},{25,9},{2,18},{10... | collective-permute-start | bytes 995336 | tf_op jit(solution)/shard_map/ppermute | solution.py:107
  16.7 23.4 %collective-permute-start.8 = (bf16[144,1152]{1,0:T(8,128)(2,1)S(1)}, bf16[144,1152]{1,0:T(8,128)(2,1)}, u32[]{:S(2)}, u32[]{:S(2)}) collective-permute-start(bf16[144,1152]{1,0:T(8,128)(2,1)S(1)} %get-tuple-element.214.block0_ref), channel_id=1, source_target_pairs={{0,24},{8,16},{16,8},{24,0},{1,25},{9,17},{17,9},{25,1},{2,26},{10... | collective-permute-start | bytes 995336 | tf_op jit(solution)/shard_map/ppermute | solution.py:107
  25.1 15.0 %collective-permute-start.4 = (bf16[160,768]{1,0:T(8,128)(2,1)}, bf16[160,768]{1,0:T(8,128)(2,1)S(1)}, u32[]{:S(2)}, u32[]{:S(2)}) collective-permute-start(bf16[160,768]{1,0:T(8,128)(2,1)} %slice.365), channel_id=1, source_target_pairs={{0,1},{1,0},{2,3},{3,2},{4,5},{5,4},{6,7},{7,6},{8,9},{9,8},{10,11... | collective-permute-start | bytes 737288 | tf_op jit(solution)/shard_map/ppermute | solution.py:26
  26.1 13.9 %collective-permute-start.5 = (bf16[160,768]{1,0:T(8,128)(2,1)}, bf16[160,768]{1,0:T(8,128)(2,1)}, u32[]{:S(2)}, u32[]{:S(2)}) collective-permute-start(bf16[160,768]{1,0:T(8,128)(2,1)} %slice.366), channel_id=1, source_target_pairs={{0,2},{1,3},{2,0},{3,1},{4,6},{5,7},{6,4},{7,5},{8,10},{9,11},{10,... | collective-permute-start | bytes 737288 | tf_op jit(solution)/shard_map/ppermute | solution.py:26
  43.2 24.0 %collective-permute-start.10 = (bf16[4,96,1152]{2,1,0:T(8,128)(2,1)S(1)}, bf16[4,96,1152]{2,1,0:T(8,128)(2,1)S(1)}, u32[]{:S(2)}, u32[]{:S(2)}) collective-permute-start(bf16[4,96,1152]{2,1,0:T(8,128)(2,1)S(1)} %get-tuple-element.237.refs_0_), channel_id=1, source_target_pairs={{0,1},{1,0},{2,3},{3,2},{4,5},{5,4},{6,7},{7,6},{8,9},{9,8},{10,11... | collective-permute-start | bytes 2654216 | tf_op jit(solution)/shard_map/ppermute | solution.py:26
  43.7 23.4 %collective-permute-start.11 = (bf16[4,96,1152]{2,1,0:T(8,128)(2,1)S(1)}, bf16[4,96,1152]{2,1,0:T(8,128)(2,1)S(1)}, u32[]{:S(2)}, u32[]{:S(2)}) collective-permute-start(bf16[4,96,1152]{2,1,0:T(8,128)(2,1)S(1)} %get-tuple-element.237.refs_0_), channel_id=1, source_target_pairs={{0,2},{1,3},{2,0},{3,1},{4,6},{5,7},{6,4},{7,5},{8,10},{9,11},{10,... | collective-permute-start | bytes 2654216 | tf_op jit(solution)/shard_map/ppermute | solution.py:26
  44.2 20.4 %collective-permute-start.12 = (bf16[144,1152]{1,0:T(8,128)(2,1)S(1)}, bf16[144,1152]{1,0:T(8,128)(2,1)S(1)}, u32[]{:S(2)}, u32[]{:S(2)}) collective-permute-start(bf16[144,1152]{1,0:T(8,128)(2,1)S(1)} %get-tuple-element.244.block0_ref), channel_id=1, source_target_pairs={{0,8},{8,0},{16,24},{24,16},{1,9},{9,1},{17,25},{25,17},{2,10},{10... | collective-permute-start | bytes 995336 | tf_op jit(solution)/shard_map/ppermute | solution.py:107
  50.1 17.1 %collective-permute-start.13 = (bf16[144,1152]{1,0:T(8,128)(2,1)S(1)}, bf16[144,1152]{1,0:T(8,128)(2,1)S(1)}, u32[]{:S(2)}, u32[]{:S(2)}) collective-permute-start(bf16[144,1152]{1,0:T(8,128)(2,1)S(1)} %get-tuple-element.244.block0_ref), channel_id=1, source_target_pairs={{0,16},{8,24},{16,0},{24,8},{1,17},{9,25},{17,1},{25,9},{2,18},{10... | collective-permute-start | bytes 995336 | tf_op jit(solution)/shard_map/ppermute | solution.py:107
  70.8 11.8 %collective-permute-start.17 = (bf16[2,96,1152]{2,1,0:T(8,128)(2,1)S(1)}, bf16[2,96,1152]{2,1,0:T(8,128)(2,1)S(1)}, u32[]{:S(2)}, u32[]{:S(2)}) collective-permute-start(bf16[2,96,1152]{2,1,0:T(8,128)(2,1)S(1)} %slice.367), channel_id=1, source_target_pairs={{0,1},{1,0},{2,3},{3,2},{4,5},{5,4},{6,7},{7,6},{8,9},{9,8},{10,11... | collective-permute-start | bytes 1327112 | tf_op jit(solution)/shard_map/ppermute | solution.py:26
  72.4 10.7 %collective-permute-start.18 = (bf16[2,96,1152]{2,1,0:T(8,128)(2,1)S(1)}, bf16[2,96,1152]{2,1,0:T(8,128)(2,1)S(1)}, u32[]{:S(2)}, u32[]{:S(2)}) collective-permute-start(bf16[2,96,1152]{2,1,0:T(8,128)(2,1)S(1)} %slice.368), channel_id=1, source_target_pairs={{0,2},{1,3},{2,0},{3,1},{4,6},{5,7},{6,4},{7,5},{8,10},{9,11},{10,... | collective-permute-start | bytes 1327112 | tf_op jit(solution)/shard_map/ppermute | solution.py:26
  73.9 11.6 %collective-permute-start.20 = (bf16[4,96,1152]{2,1,0:T(8,128)(2,1)S(1)}, bf16[4,96,1152]{2,1,0:T(8,128)(2,1)S(1)}, u32[]{:S(2)}, u32[]{:S(2)}) collective-permute-start(bf16[4,96,1152]{2,1,0:T(8,128)(2,1)S(1)} %collective-permute-done.10.refs_1_), channel_id=1, source_target_pairs={{0,4},{4,0},{1,5},{5,1},{2,6},{6,2},{3,7},{7,3},{8,12},{12,8},{9,1... | collective-permute-start | bytes 2654216 | tf_op jit(solution)/shard_map/ppermute | solution.py:21
  75.2 10.3 %collective-permute-start.19 = (bf16[4,96,1152]{2,1,0:T(8,128)(2,1)S(1)}, bf16[4,96,1152]{2,1,0:T(8,128)(2,1)S(1)}, u32[]{:S(2)}, u32[]{:S(2)}) collective-permute-start(bf16[4,96,1152]{2,1,0:T(8,128)(2,1)S(1)} %get-tuple-element.237.refs_0_), channel_id=1, source_target_pairs={{0,4},{4,0},{1,5},{5,1},{2,6},{6,2},{3,7},{7,3},{8,12},{12,8},{9,1... | collective-permute-start | bytes 2654216 | tf_op jit(solution)/shard_map/ppermute | solution.py:21
  92.7 13.3 %collective-permute-start.24 = (bf16[320,768]{1,0:T(8,128)(2,1)S(1)}, bf16[320,768]{1,0:T(8,128)(2,1)S(1)}, u32[]{:S(2)}, u32[]{:S(2)}) collective-permute-start(bf16[320,768]{1,0:T(8,128)(2,1)S(1)} %get-tuple-element.241.own_ref), channel_id=1, source_target_pairs={{0,1},{1,0},{2,3},{3,2},{4,5},{5,4},{6,7},{7,6},{8,9},{9,8},{10,11... | collective-permute-start | bytes 1474568 | tf_op jit(solution)/shard_map/ppermute | solution.py:26
  93.3 13.0 %collective-permute-start.25 = (bf16[320,768]{1,0:T(8,128)(2,1)S(1)}, bf16[320,768]{1,0:T(8,128)(2,1)S(1)}, u32[]{:S(2)}, u32[]{:S(2)}) collective-permute-start(bf16[320,768]{1,0:T(8,128)(2,1)S(1)} %get-tuple-element.241.own_ref), channel_id=1, source_target_pairs={{0,2},{1,3},{2,0},{3,1},{4,6},{5,7},{6,4},{7,5},{8,10},{9,11},{10,... | collective-permute-start | bytes 1474568 | tf_op jit(solution)/shard_map/ppermute | solution.py:26
  94.4 11.2 %collective-permute-start.26 = (bf16[144,1152]{1,0:T(8,128)(2,1)S(1)}, bf16[144,1152]{1,0:T(8,128)(2,1)S(1)}, u32[]{:S(2)}, u32[]{:S(2)}) collective-permute-start(bf16[144,1152]{1,0:T(8,128)(2,1)S(1)} %get-tuple-element.244.block0_ref), channel_id=1, source_target_pairs={{0,24},{8,16},{16,8},{24,0},{1,25},{9,17},{17,9},{25,1},{2,26},{10... | collective-permute-start | bytes 995336 | tf_op jit(solution)/shard_map/ppermute | solution.py:107
  116.2 20.9 %collective-permute-start.30 = (bf16[4,96,1152]{2,1,0:T(8,128)(2,1)S(1)}, bf16[4,96,1152]{2,1,0:T(8,128)(2,1)S(1)}, u32[]{:S(2)}, u32[]{:S(2)}) collective-permute-start(bf16[4,96,1152]{2,1,0:T(8,128)(2,1)S(1)} %get-tuple-element.258.refs_0_), channel_id=1, source_target_pairs={{0,1},{1,0},{2,3},{3,2},{4,5},{5,4},{6,7},{7,6},{8,9},{9,8},{10,11... | collective-permute-start | bytes 2654216 | tf_op jit(solution)/shard_map/ppermute | solution.py:26
  116.8 20.7 %collective-permute-start.31 = (bf16[4,96,1152]{2,1,0:T(8,128)(2,1)S(1)}, bf16[4,96,1152]{2,1,0:T(8,128)(2,1)S(1)}, u32[]{:S(2)}, u32[]{:S(2)}) collective-permute-start(bf16[4,96,1152]{2,1,0:T(8,128)(2,1)S(1)} %get-tuple-element.258.refs_0_), channel_id=1, source_target_pairs={{0,2},{1,3},{2,0},{3,1},{4,6},{5,7},{6,4},{7,5},{8,10},{9,11},{10,... | collective-permute-start | bytes 2654216 | tf_op jit(solution)/shard_map/ppermute | solution.py:26
  141.0 13.1 %collective-permute-start.35 = (bf16[2,96,1152]{2,1,0:T(8,128)(2,1)S(1)}, bf16[2,96,1152]{2,1,0:T(8,128)(2,1)S(1)}, u32[]{:S(2)}, u32[]{:S(2)}) collective-permute-start(bf16[2,96,1152]{2,1,0:T(8,128)(2,1)S(1)} %slice.373), channel_id=1, source_target_pairs={{0,1},{1,0},{2,3},{3,2},{4,5},{5,4},{6,7},{7,6},{8,9},{9,8},{10,11... | collective-permute-start | bytes 1327112 | tf_op jit(solution)/shard_map/ppermute | solution.py:26
  142.5 12.3 %collective-permute-start.36 = (bf16[2,96,1152]{2,1,0:T(8,128)(2,1)S(1)}, bf16[2,96,1152]{2,1,0:T(8,128)(2,1)S(1)}, u32[]{:S(2)}, u32[]{:S(2)}) collective-permute-start(bf16[2,96,1152]{2,1,0:T(8,128)(2,1)S(1)} %slice.374), channel_id=1, source_target_pairs={{0,2},{1,3},{2,0},{3,1},{4,6},{5,7},{6,4},{7,5},{8,10},{9,11},{10,... | collective-permute-start | bytes 1327112 | tf_op jit(solution)/shard_map/ppermute | solution.py:26
  143.5 11.8 %collective-permute-start.37 = (bf16[4,96,1152]{2,1,0:T(8,128)(2,1)S(1)}, bf16[4,96,1152]{2,1,0:T(8,128)(2,1)S(1)}, u32[]{:S(2)}, u32[]{:S(2)}) collective-permute-start(bf16[4,96,1152]{2,1,0:T(8,128)(2,1)S(1)} %get-tuple-element.258.refs_0_), channel_id=1, source_target_pairs={{0,4},{4,0},{1,5},{5,1},{2,6},{6,2},{3,7},{7,3},{8,12},{12,8},{9,1... | collective-permute-start | bytes 2654216 | tf_op jit(solution)/shard_map/ppermute | solution.py:21
  146.5 10.7 %collective-permute-start.38 = (bf16[4,96,1152]{2,1,0:T(8,128)(2,1)S(1)}, bf16[4,96,1152]{2,1,0:T(8,128)(2,1)S(1)}, u32[]{:S(2)}, u32[]{:S(2)}) collective-permute-start(bf16[4,96,1152]{2,1,0:T(8,128)(2,1)S(1)} %collective-permute-done.30.refs_1_), channel_id=1, source_target_pairs={{0,4},{4,0},{1,5},{5,1},{2,6},{6,2},{3,7},{7,3},{8,12},{12,8},{9,1... | collective-permute-start | bytes 2654216 | tf_op jit(solution)/shard_map/ppermute | solution.py:21
  191.2 22.7 %collective-permute-start.47 = (bf16[2,96,1152]{2,1,0:T(8,128)(2,1)S(1)}, bf16[2,96,1152]{2,1,0:T(8,128)(2,1)S(1)}, u32[]{:S(2)}, u32[]{:S(2)}) collective-permute-start(bf16[2,96,1152]{2,1,0:T(8,128)(2,1)S(1)} %get-tuple-element.463), channel_id=1, source_target_pairs={{0,1},{1,0},{2,3},{3,2},{4,5},{5,4},{6,7},{7,6},{8,9},{9,8},{10,11... | collective-permute-start | bytes 1327112 | tf_op jit(solution)/shard_map/ppermute | solution.py:26
  192.5 21.4 %collective-permute-start.48 = (bf16[2,96,1152]{2,1,0:T(8,128)(2,1)S(1)}, bf16[2,96,1152]{2,1,0:T(8,128)(2,1)S(1)}, u32[]{:S(2)}, u32[]{:S(2)}) collective-permute-start(bf16[2,96,1152]{2,1,0:T(8,128)(2,1)S(1)} %get-tuple-element.462), channel_id=1, source_target_pairs={{0,2},{1,3},{2,0},{3,1},{4,6},{5,7},{6,4},{7,5},{8,10},{9,11},{10,... | collective-permute-start | bytes 1327112 | tf_op jit(solution)/shard_map/ppermute | solution.py:26
  217.2 16.0 %collective-permute-start.54 = (bf16[4,48,1152]{2,1,0:T(8,128)(2,1)}, bf16[4,48,1152]{2,1,0:T(8,128)(2,1)}, u32[]{:S(2)}, u32[]{:S(2)}) collective-permute-start(bf16[4,48,1152]{2,1,0:T(8,128)(2,1)} %get-tuple-element.311), channel_id=1, source_target_pairs={{0,4},{4,0},{1,5},{5,1},{2,6},{6,2},{3,7},{7,3},{8,12},{12,8},{9,1... | collective-permute-start | bytes 1327112 | tf_op jit(solution)/shard_map/ppermute | solution.py:21
  218.8 10.4 %collective-permute-start.50 = (bf16[160,768]{1,0:T(8,128)(2,1)}, bf16[160,768]{1,0:T(8,128)(2,1)}, u32[]{:S(2)}, u32[]{:S(2)}) collective-permute-start(bf16[160,768]{1,0:T(8,128)(2,1)} %get-tuple-element.303), channel_id=1, source_target_pairs={{0,2},{1,3},{2,0},{3,1},{4,6},{5,7},{6,4},{7,5},{8,10},{9,11},{10,... | collective-permute-start | bytes 737288 | tf_op jit(solution)/shard_map/ppermute | solution.py:26
  219.9 12.2 %collective-permute-start.49 = (bf16[160,768]{1,0:T(8,128)(2,1)}, bf16[160,768]{1,0:T(8,128)(2,1)}, u32[]{:S(2)}, u32[]{:S(2)}) collective-permute-start(bf16[160,768]{1,0:T(8,128)(2,1)} %get-tuple-element.301), channel_id=1, source_target_pairs={{0,1},{1,0},{2,3},{3,2},{4,5},{5,4},{6,7},{7,6},{8,9},{9,8},{10,11... | collective-permute-start | bytes 737288 | tf_op jit(solution)/shard_map/ppermute | solution.py:26
  221.1 12.1 %collective-permute-start.55 = (bf16[160,768]{1,0:T(8,128)(2,1)}, bf16[160,768]{1,0:T(8,128)(2,1)}, u32[]{:S(2)}, u32[]{:S(2)}) collective-permute-start(bf16[160,768]{1,0:T(8,128)(2,1)} %get-tuple-element.312), channel_id=1, source_target_pairs={{0,2},{1,3},{2,0},{3,1},{4,6},{5,7},{6,4},{7,5},{8,10},{9,11},{10,... | collective-permute-start | bytes 737288 | tf_op jit(solution)/shard_map/ppermute | solution.py:26
  239.5 21.0 %collective-permute-start.56 = (bf16[4,96,1152]{2,1,0:T(8,128)(2,1)S(1)}, bf16[4,96,1152]{2,1,0:T(8,128)(2,1)S(1)}, u32[]{:S(2)}, u32[]{:S(2)}) collective-permute-start(bf16[4,96,1152]{2,1,0:T(8,128)(2,1)S(1)} %pad_maximum_fusion), channel_id=1, source_target_pairs={{0,1},{1,0},{2,3},{3,2},{4,5},{5,4},{6,7},{7,6},{8,9},{9,8},{10,11... | collective-permute-start | bytes 2654216 | tf_op jit(solution)/shard_map/ppermute | solution.py:26
  241.0 20.7 %collective-permute-start.57 = (bf16[4,96,1152]{2,1,0:T(8,128)(2,1)S(1)}, bf16[4,96,1152]{2,1,0:T(8,128)(2,1)S(1)}, u32[]{:S(2)}, u32[]{:S(2)}) collective-permute-start(bf16[4,96,1152]{2,1,0:T(8,128)(2,1)S(1)} %copy-done.74), channel_id=1, source_target_pairs={{0,2},{1,3},{2,0},{3,1},{4,6},{5,7},{6,4},{7,5},{8,10},{9,11},{10,... | collective-permute-start | bytes 2654216 | tf_op jit(solution)/shard_map/ppermute | solution.py:26
  272.0 13.1 %collective-permute-start.62 = (bf16[2,96,1152]{2,1,0:T(8,128)(2,1)S(1)}, bf16[2,96,1152]{2,1,0:T(8,128)(2,1)S(1)}, u32[]{:S(2)}, u32[]{:S(2)}) collective-permute-start(bf16[2,96,1152]{2,1,0:T(8,128)(2,1)S(1)} %get-tuple-element.457), channel_id=1, source_target_pairs={{0,1},{1,0},{2,3},{3,2},{4,5},{5,4},{6,7},{7,6},{8,9},{9,8},{10,11... | collective-permute-start | bytes 1327112 | tf_op jit(solution)/shard_map/ppermute | solution.py:26
  273.5 11.6 %collective-permute-start.63 = (bf16[2,96,1152]{2,1,0:T(8,128)(2,1)S(1)}, bf16[2,96,1152]{2,1,0:T(8,128)(2,1)S(1)}, u32[]{:S(2)}, u32[]{:S(2)}) collective-permute-start(bf16[2,96,1152]{2,1,0:T(8,128)(2,1)S(1)} %get-tuple-element.456), channel_id=1, source_target_pairs={{0,2},{1,3},{2,0},{3,1},{4,6},{5,7},{6,4},{7,5},{8,10},{9,11},{10,... | collective-permute-start | bytes 1327112 | tf_op jit(solution)/shard_map/ppermute | solution.py:26
  293.8 22.1 %collective-permute-start.66 = (bf16[144,1152]{1,0:T(8,128)(2,1)}, bf16[144,1152]{1,0:T(8,128)(2,1)S(1)}, u32[]{:S(2)}, u32[]{:S(2)}) collective-permute-start(bf16[144,1152]{1,0:T(8,128)(2,1)} %pad_maximum_fusion.8), channel_id=1, source_target_pairs={{0,8},{8,0},{16,24},{24,16},{1,9},{9,1},{17,25},{25,17},{2,10},{10... | collective-permute-start | bytes 995336 | tf_op jit(solution)/shard_map/ppermute | solution.py:107
  300.7 26.0 %collective-permute-start.67 = (bf16[144,1152]{1,0:T(8,128)(2,1)}, bf16[144,1152]{1,0:T(8,128)(2,1)S(1)}, u32[]{:S(2)}, u32[]{:S(2)}) collective-permute-start(bf16[144,1152]{1,0:T(8,128)(2,1)} %pad_maximum_fusion.9), channel_id=1, source_target_pairs={{0,16},{8,24},{16,0},{24,8},{1,17},{9,25},{17,1},{25,9},{2,18},{10... | collective-permute-start | bytes 995336 | tf_op jit(solution)/shard_map/ppermute | solution.py:107
  301.8 25.0 %collective-permute-start.64 = (bf16[4,96,1152]{2,1,0:T(8,128)(2,1)}, bf16[4,96,1152]{2,1,0:T(8,128)(2,1)S(1)}, u32[]{:S(2)}, u32[]{:S(2)}) collective-permute-start(bf16[4,96,1152]{2,1,0:T(8,128)(2,1)} %pad_maximum_fusion.2), channel_id=1, source_target_pairs={{0,1},{1,0},{2,3},{3,2},{4,5},{5,4},{6,7},{7,6},{8,9},{9,8},{10,11... | collective-permute-start | bytes 2654216 | tf_op jit(solution)/shard_map/ppermute | solution.py:26
  303.1 23.7 %collective-permute-start.65 = (bf16[4,96,1152]{2,1,0:T(8,128)(2,1)}, bf16[4,96,1152]{2,1,0:T(8,128)(2,1)S(1)}, u32[]{:S(2)}, u32[]{:S(2)}) collective-permute-start(bf16[4,96,1152]{2,1,0:T(8,128)(2,1)} %pad_maximum_fusion.3), channel_id=1, source_target_pairs={{0,2},{1,3},{2,0},{3,1},{4,6},{5,7},{6,4},{7,5},{8,10},{9,11},{10,... | collective-permute-start | bytes 2654216 | tf_op jit(solution)/shard_map/ppermute | solution.py:26
  304.1 22.7 %collective-permute-start.68 = (bf16[144,1152]{1,0:T(8,128)(2,1)}, bf16[144,1152]{1,0:T(8,128)(2,1)S(1)}, u32[]{:S(2)}, u32[]{:S(2)}) collective-permute-start(bf16[144,1152]{1,0:T(8,128)(2,1)} %pad_maximum_fusion.10), channel_id=1, source_target_pairs={{0,24},{8,16},{16,8},{24,0},{1,25},{9,17},{17,9},{25,1},{2,26},{10... | collective-permute-start | bytes 995336 | tf_op jit(solution)/shard_map/ppermute | solution.py:107
  326.8 13.6 %collective-permute-start.71 = (bf16[160,768]{1,0:T(8,128)(2,1)}, bf16[160,768]{1,0:T(8,128)(2,1)S(1)}, u32[]{:S(2)}, u32[]{:S(2)}) collective-permute-start(bf16[160,768]{1,0:T(8,128)(2,1)} %copy-done.45), channel_id=1, source_target_pairs={{0,1},{1,0},{2,3},{3,2},{4,5},{5,4},{6,7},{7,6},{8,9},{9,8},{10,11... | collective-permute-start | bytes 737288 | tf_op jit(solution)/shard_map/ppermute | solution.py:26
  328.1 12.3 %collective-permute-start.72 = (bf16[160,768]{1,0:T(8,128)(2,1)}, bf16[160,768]{1,0:T(8,128)(2,1)S(1)}, u32[]{:S(2)}, u32[]{:S(2)}) collective-permute-start(bf16[160,768]{1,0:T(8,128)(2,1)} %copy-done.44), channel_id=1, source_target_pairs={{0,2},{1,3},{2,0},{3,1},{4,6},{5,7},{6,4},{7,5},{8,10},{9,11},{10,... | collective-permute-start | bytes 737288 | tf_op jit(solution)/shard_map/ppermute | solution.py:26
  331.2 16.7 %collective-permute-start.80 = (bf16[144,1152]{1,0:T(8,128)(2,1)S(1)}, bf16[144,1152]{1,0:T(8,128)(2,1)S(1)}, u32[]{:S(2)}, u32[]{:S(2)}) collective-permute-start(bf16[144,1152]{1,0:T(8,128)(2,1)S(1)} %pad_maximum_fusion.13), channel_id=1, source_target_pairs={{0,24},{8,16},{16,8},{24,0},{1,25},{9,17},{17,9},{25,1},{2,26},{10... | collective-permute-start | bytes 995336 | tf_op jit(solution)/shard_map/ppermute | solution.py:107
  334.4 27.7 %collective-permute-start.79 = (bf16[144,1152]{1,0:T(8,128)(2,1)S(1)}, bf16[144,1152]{1,0:T(8,128)(2,1)S(1)}, u32[]{:S(2)}, u32[]{:S(2)}) collective-permute-start(bf16[144,1152]{1,0:T(8,128)(2,1)S(1)} %pad_maximum_fusion.12), channel_id=1, source_target_pairs={{0,16},{8,24},{16,0},{24,8},{1,17},{9,25},{17,1},{25,9},{2,18},{10... | collective-permute-start | bytes 995336 | tf_op jit(solution)/shard_map/ppermute | solution.py:107
  341.7 20.4 %collective-permute-start.74 = (bf16[320,768]{1,0:T(8,128)(2,1)S(1)}, bf16[320,768]{1,0:T(8,128)(2,1)S(1)}, u32[]{:S(2)}, u32[]{:S(2)}) collective-permute-start(bf16[320,768]{1,0:T(8,128)(2,1)S(1)} %pad_maximum_fusion.5), channel_id=1, source_target_pairs={{0,1},{1,0},{2,3},{3,2},{4,5},{5,4},{6,7},{7,6},{8,9},{9,8},{10,11... | collective-permute-start | bytes 1474568 | tf_op jit(solution)/shard_map/ppermute | solution.py:26
  343.2 19.0 %collective-permute-start.75 = (bf16[320,768]{1,0:T(8,128)(2,1)S(1)}, bf16[320,768]{1,0:T(8,128)(2,1)S(1)}, u32[]{:S(2)}, u32[]{:S(2)}) collective-permute-start(bf16[320,768]{1,0:T(8,128)(2,1)S(1)} %pad_maximum_fusion.6), channel_id=1, source_target_pairs={{0,2},{1,3},{2,0},{3,1},{4,6},{5,7},{6,4},{7,5},{8,10},{9,11},{10,... | collective-permute-start | bytes 1474568 | tf_op jit(solution)/shard_map/ppermute | solution.py:26
  344.3 17.8 %collective-permute-start.78 = (bf16[144,1152]{1,0:T(8,128)(2,1)S(1)}, bf16[144,1152]{1,0:T(8,128)(2,1)S(1)}, u32[]{:S(2)}, u32[]{:S(2)}) collective-permute-start(bf16[144,1152]{1,0:T(8,128)(2,1)S(1)} %pad_maximum_fusion.11), channel_id=1, source_target_pairs={{0,8},{8,0},{16,24},{24,16},{1,9},{9,1},{17,25},{25,17},{2,10},{10... | collective-permute-start | bytes 995336 | tf_op jit(solution)/shard_map/ppermute | solution.py:107
  348.0 22.9 %collective-permute-start.42 = (bf16[320,768]{1,0:T(8,128)(2,1)}, bf16[320,768]{1,0:T(8,128)(2,1)}, u32[]{:S(2)}, u32[]{:S(2)}) collective-permute-start(bf16[320,768]{1,0:T(8,128)(2,1)} %get-tuple-element.451), channel_id=1, source_target_pairs={{0,4},{4,0},{1,5},{5,1},{2,6},{6,2},{3,7},{7,3},{8,12},{12,8},{9,1... | collective-permute-start | bytes 1474568 | tf_op jit(solution)/shard_map/ppermute | solution.py:21
  365.3 14.8 %collective-permute-start.76 = (f32[320,768]{1,0:T(8,128)}, f32[320,768]{1,0:T(8,128)}, u32[]{:S(2)}, u32[]{:S(2)}) collective-permute-start(f32[320,768]{1,0:T(8,128)} %convert_select_fusion), channel_id=1, source_target_pairs={{0,4},{4,0},{1,5},{5,1},{2,6},{6,2},{3,7},{7,3},{8,12},{12,8},{9,1... | collective-permute-start | bytes 2949128 | tf_op jit(solution)/shard_map/ppermute | solution.py:21
  (123 other events, 1158.1 us)

commit v5 on v4

--- a/solution.py
+++ b/solution.py
@@ -113,8 +113,8 @@
     return [lax.all_gather(block, "dp", axis=0)]
 
 
-def scatter_dp(blocks):
-    return tuple(to_peer(blocks[bit], bit) for bit in (1, 2, 3)) if four_dp() else ()
+def scatter_dp(blocks, bits=(1, 2, 3)):
+    return tuple(to_peer(blocks[bit], bit) for bit in bits) if four_dp() else ()
 
 
 def scatter_sum(blocks, came):
@@ -525,16 +525,12 @@
     return cumulative, density
 
 
-def token_kernel(pair, place_ref, mixed0_ref, mixed1_ref, mixed2_ref, mixed3_ref, in_ref, *refs):
-    pieces = (len(refs) - 7) // 2
-    mine_refs, other_refs = refs[:pieces], refs[pieces : 2 * pieces]
-    gain_ref, next_ref, mid_ref, out_ref, normed_ref, sums, mats = refs[2 * pieces :]
+def forward_step(pair, mixed_refs, in_ref, gain_ref, mid_ref, sums, mats):
     parts = mats.shape[0]
-    width = mixed0_ref.shape[1] // 2
+    width = mixed_refs[0].shape[1] // 2
     units = pair // 2
-    load_pieces(place_ref, mine_refs, other_refs, mats)
     mid = in_ref[...].astype(F32)
-    for part, ref in enumerate((mixed0_ref, mixed1_ref, mixed2_ref, mixed3_ref)):
+    for part, ref in enumerate(mixed_refs):
         mid += dot(unpack(ref[...]), mats[part, :, pair : pair + width], NT)
     mid_ref[...] = mid
     sums[...] = mid
@@ -548,6 +544,15 @@
         return carry
 
     lax.fori_loop(0, parts, feed, 0)
+
+
+def token_kernel(pair, place_ref, mixed0_ref, mixed1_ref, mixed2_ref, mixed3_ref, in_ref, *refs):
+    pieces = (len(refs) - 7) // 2
+    mine_refs, other_refs = refs[:pieces], refs[pieces : 2 * pieces]
+    gain_ref, next_ref, mid_ref, out_ref, normed_ref, sums, mats = refs[2 * pieces :]
+    load_pieces(place_ref, mine_refs, other_refs, mats)
+    mixed_refs = (mixed0_ref, mixed1_ref, mixed2_ref, mixed3_ref)
+    forward_step(pair, mixed_refs, in_ref, gain_ref, mid_ref, sums, mats)
     low = sums[...].astype(BF16)
     out_ref[...] = low
     normed_ref[...] = (norm_parts(low.astype(F32))[0] * next_ref[...]).astype(BF16)
@@ -577,13 +582,34 @@
     pair, place_ref, grad_ref, mid_ref, mixed0_ref, mixed1_ref, mixed2_ref, mixed3_ref, *refs
 ):
     pieces = (len(refs) - 12) // 2
-    mine_refs, other_refs = refs[:pieces], refs[pieces : 2 * pieces]
-    (gain_ref, mine_grad_ref, other_grad_ref, mixed_grad0_ref, mixed_grad1_ref, mixed_grad2_ref,
-     mixed_grad3_ref, grad_mid_ref, gain_grad_ref, sums, mats, grads) = refs[2 * pieces :]
+    mats = refs[-2]
+    load_pieces(place_ref, refs[:pieces], refs[pieces : 2 * pieces], mats)
+    mixed_refs = (mixed0_ref, mixed1_ref, mixed2_ref, mixed3_ref)
+    back_step(pair, place_ref, grad_ref, mid_ref, mixed_refs, *refs[2 * pieces :])
+
+
+def token_last_kernel(
+    pair, place_ref, grad_ref, in_ref, mixed0_ref, mixed1_ref, mixed2_ref, mixed3_ref, *refs
+):
+    pieces = (len(refs) - 14) // 2
+    mats, sums = refs[-3], refs[-4]
+    load_pieces(place_ref, refs[:pieces], refs[pieces : 2 * pieces], mats)
+    mixed_refs = (mixed0_ref, mixed1_ref, mixed2_ref, mixed3_ref)
+    rest = refs[2 * pieces :]
+    gain_ref, out_ref, mid = rest[0], rest[9], rest[13]
+    forward_step(pair, mixed_refs, in_ref, gain_ref, mid, sums, mats)
+    out_ref[...] = sums[...].astype(BF16)
+    back_step(pair, place_ref, grad_ref, mid, mixed_refs, *rest[:9], *rest[10:13])
+
+
+def back_step(
+    pair, place_ref, grad_ref, mid_ref, mixed_refs, gain_ref, mine_grad_ref, other_grad_ref,
+    mixed_grad0_ref, mixed_grad1_ref, mixed_grad2_ref, mixed_grad3_ref, grad_mid_ref,
+    gain_grad_ref, sums, mats, grads,
+):
     parts = mats.shape[0]
-    width = mixed0_ref.shape[1] // 2
+    width = mixed_refs[0].shape[1] // 2
     units = pair // 2
-    load_pieces(place_ref, mine_refs, other_refs, mats)
     grad = grad_ref[...].astype(F32)
     grad_low = grad.astype(BF16)
     grad_flip = grad.T.astype(BF16)
@@ -621,7 +647,6 @@
     grad_mid_ref[...] = grad_mid
     mid_low = grad_mid.astype(BF16)
     mid_flip = grad_mid.T.astype(BF16)
-    mixed_refs = (mixed0_ref, mixed1_ref, mixed2_ref, mixed3_ref)
     mixed_grad_refs = (mixed_grad0_ref, mixed_grad1_ref, mixed_grad2_ref, mixed_grad3_ref)
     for part in range(parts):
         weight = mats[part, :, pair : pair + width]
@@ -656,6 +681,31 @@
     )(place, grad, mid, *mixed, *mine, *other, gain)
 
 
+def token_last(place, grad, layer_in, mixed, mine, other, gain, pair):
+    shape, rows = mine[0].shape, layer_in.shape
+    half = jax.ShapeDtypeStruct((4,) + shape, BF16)
+    mixed_grad = jax.ShapeDtypeStruct(mixed[0].shape, BF16)
+    return pl.pallas_call(
+        functools.partial(token_last_kernel, pair),
+        out_shape=(
+            half, half, mixed_grad, mixed_grad, mixed_grad, mixed_grad,
+            jax.ShapeDtypeStruct(rows, F32),
+            jax.ShapeDtypeStruct((1, rows[1]), F32),
+            jax.ShapeDtypeStruct(rows, BF16),
+        ),
+        in_specs=[SCALARS] + [WHOLE] * (7 + 2 * len(mine)),
+        scratch_shapes=[
+            pltpu.VMEM(rows, F32),
+            pltpu.VMEM((4, rows[1], shape[2]), BF16),
+            pltpu.VMEM((rows[1], shape[2]), BF16),
+            pltpu.VMEM(rows, F32),
+        ],
+        compiler_params=pltpu.CompilerParams(vmem_limit_bytes=VMEM_BYTES),
+        cost_estimate=cost(20),
+        name="token_last",
+    )(place, grad, layer_in, *mixed, *mine, *other, gain)
+
+
 def frequencies(theta_base, half_dim):
     return theta_base ** (-(jnp.arange(half_dim, dtype=F32) * 2.0) / (2.0 * half_dim))
 
@@ -764,11 +814,6 @@
     mixed, second_near = after((mixed, second_near))
     mixed, second_far = after((swap_tensor(mixed), to_far(*second_near)))
     mats = piece_halves((mats_second,) + second_near + second_far)
-    mid, second_out, _ = token_forward(
-        place, mixed, first_out, *mats, gain_rows[1][:, model:], gain_rows[1][:, :model], pair
-    )
-    saved_token[1] = (mid, mixed) + mats
-
     def token_step(layer, grad):
         mid, mixed, mine, other = saved_token[layer]
         return token_back(
@@ -796,7 +841,9 @@
     def qkv_blocks(kept, came):
         return [add_low(kept[slot], came[slot]) for slot in range(kept.shape[0])]
 
-    mine_grad, other_grad, *mixed_grad, grad_mid, gain_mlp = token_step(1, cotangent)
+    mine_grad, other_grad, *mixed_grad, grad_mid, gain_mlp, second_out = token_last(
+        place, cotangent, first_out, mixed, *mats, gain_rows[1][:, model:], pair
+    )
     mixed_grad = swap_tensor(mixed_grad)
     kept, came = half_sums(mine_grad, other_grad)
     mixed_grad, kept, came = after((mixed_grad, kept, came))
@@ -823,20 +870,24 @@
         second = [jnp.concatenate(block, 0) for block in zip(second, second_qkv)]
     mixed_grad, kept, came, second = after((mixed_grad, kept, came, second))
     far = far_terms(add_low(kept[3], came[3]))
+    came_early = scatter_dp(second, (1, 2))
     *parts, grad_projected = attend_step(0, mixed_grad)
-    parts, grad_projected, far, kept, came = after((parts, grad_projected, far, kept, came))
+    parts, grad_projected, far, kept, came, came_early, second = after(
+        (parts, grad_projected, far, kept, came, came_early, second)
+    )
 
     pair_terms = near_terms(add_low(kept[1], came[1]), add_low(kept[2], came[2]), *far)
     pair_terms, grad_projected = after((pair_terms, grad_projected))
-    near, second_came = to_near(pair_terms), scatter_dp(second)
+    near, came_late = to_near(pair_terms), scatter_dp(second, (3,))
     qkv_kept, qkv_came, gain_attn = weight_step(0, grad_projected)
     first_gain = jnp.concatenate([gain_attn, gain_mlp], 1)
     gain_sum = jnp.where(core == 0, first_gain, second_gain)
     gain_sum += swap_cores(jnp.where(core == 0, second_gain, first_gain))
     first_qkv = qkv_blocks(qkv_kept, qkv_came)
-    near, second_came, parts, gain_sum, first_qkv = after(
-        (near, second_came, parts, gain_sum, first_qkv)
-    )
+    near, came_late, parts, gain_sum, first_qkv = after(
+        (near, came_late, parts, gain_sum, first_qkv)
+    )
+    second_came = came_early + came_late
     first = slot_sums(kept, came, near)
     if four_dp():
         first = [jnp.concatenate(block, 0) for block in zip(first, first_qkv)]

time: 389 us -> 388 us (level)
  waiting for transfers between devices: 129 us -> 142 us
  starting transfers between devices: 93.5 us -> 84.9 us
    pallas_call x0 -> x1, Pallas kernels: none -> 19.7 us  [token_last(): pl.pallas_call(functools.partial(token_last_kernel, pair), out_shape=(hal...]
    ppermute x48, waiting for transfers between devices: 60 us -> 74.9 us  [to_mate(): return lax.ppermute(block, 'tensor', [(i, i ^ bit) for i in range(size)])]
    pallas_call x2 -> x1, Pallas kernels: 27.5 us -> 13.7 us  [token_back(): pl.pallas_call(functools.partial(token_back_kernel, pair), out_shape=(hal...]
    ppermute x14, starting transfers between devices: 35.3 us -> 26.5 us  [to_peer(): return lax.ppermute(block, 'dp', [(i, i ^ bit) for i in range(4)])]
    pallas_call x2 -> x1, Pallas kernels: 15.1 us -> 6.97 us  [token_forward(): pl.pallas_call(functools.partial(token_kernel, pair), out_shape=(jax.Shap...]
    unnamed x178 -> x186, local copies, waits for them, and re-layouts: 15 us -> 12.3 us
  transfers between devices with their start and end apart: 84 -> 84, of which waited for: 39 -> 44; matrix products, arithmetic and copies ran while one was open for 9% -> 9% of each run, Pallas kernels for 17% -> 17%
where the time goes in v5:
time: 388 us; the launch traced here: 383 us
  waiting for transfers between devices  142 us (37%)
  Pallas kernels  98.9 us (25%)
  starting transfers between devices  84.9 us (22%)
  other arithmetic  35.8 us (9%)
  local copies, waits for them, and re-layouts  18.3 us (5%)
    ppermute x48, waiting for transfers between devices, to_mate(): return lax.ppermute(block, 'tensor', [(i, i ^ bit) for i in range(size)])  74.9 us
    ppermute x14, waiting for transfers between devices, to_peer(): return lax.ppermute(block, 'dp', [(i, i ^ bit) for i in range(4)])  62.9 us
    ppermute x48, starting transfers between devices, to_mate(): return lax.ppermute(block, 'tensor', [(i, i ^ bit) for i in range(size)])  55.6 us
    pallas_call x2, Pallas kernels, attend_back(): pl.pallas_call(functools.partial(attend_back_kernel, span), out_shape=(pa...  29.3 us
    ppermute x14, starting transfers between devices, to_peer(): return lax.ppermute(block, 'dp', [(i, i ^ bit) for i in range(4)])  26.5 us
    pallas_call x2, Pallas kernels, attend(): pl.pallas_call(functools.partial(attend_kernel, span), out_shape=(mixed,...  22.2 us
    pallas_call x1, Pallas kernels, token_last(): pl.pallas_call(functools.partial(token_last_kernel, pair), out_shape=(hal...  19.7 us
    pallas_call x1, Pallas kernels, token_back(): pl.pallas_call(functools.partial(token_back_kernel, pair), out_shape=(hal...  13.7 us
  transfers between devices with their start and end apart: 84, of which 44 were waited for; matrix products, arithmetic and copies ran while one was open for 9% of the time, Pallas kernels for 17%

profile of v5, /device:TPU:0, one launch (start us, length us, event | category | flops | bytes accessed | tf_op | source)
XLA Modules:
  0.0 382.5 jit_solution(13249746345386879175)
XLA Ops:
  7.7 3.0 collective-permute-start.2
  12.4 1.6 collective-permute-start.6
  14.1 2.6 collective-permute-start.7
  16.9 5.2 %collective-permute-done.2.one_ref = bf16[320,768]{1,0:T(8,128)(2,1)S(1)} collective-permute-done((bf16[320,768]{1,0:T(8,128)(2,1)S(1)}, bf16[320,768]{1,0:T(8,128)(2,1)S(1)}, u32[]{:S(2)}, u32[]{:S(2)}) %collective-permute-start.2) | collective-permute-done | bytes 491552 | tf_op jit(solution)/shard_map/ppermute | solution.py:26
  26.1 1.7 collective-permute-start.5
  28.0 12.0 %collective-permute-done.7.block2_ref = bf16[144,1152]{1,0:T(8,128)(2,1)} collective-permute-done((bf16[144,1152]{1,0:T(8,128)(2,1)S(1)}, bf16[144,1152]{1,0:T(8,128)(2,1)}, u32[]{:S(2)}, u32[]{:S(2)}) %collective-permute-start.7) | collective-permute-done | bytes 331808 | tf_op jit(solution)/shard_map/ppermute | solution.py:107
  44.2 5.9 %collective-permute-start.12 = (bf16[144,1152]{1,0:T(8,128)(2,1)S(1)}, bf16[144,1152]{1,0:T(8,128)(2,1)S(1)}, u32[]{:S(2)}, u32[]{:S(2)}) collective-permute-start(bf16[144,1152]{1,0:T(8,128)(2,1)S(1)} %get-tuple-element.245.block0_ref), channel_id=1, source_target_pairs={{0,8},{8,0},{16,24},{24,16},{1,9},{9,1},{17,25},{25,17},{2,10},{10... | collective-permute-start | bytes 995336 | tf_op jit(solution)/shard_map/ppermute | solution.py:107
  51.1 8.6 %attend_local.1 = (bf16[160,384]{1,0:T(8,128)(2,1)S(1)}, bf16[160,384]{1,0:T(8,128)(2,1)S(1)}, bf16[160,384]{1,0:T(8,128)(2,1)S(1)}, bf16[160,384]{1,0:T(8,128)(...) custom-call(s32[6]{0:T(128)S(1)} %stack.69.place_ref, ...), custom_call_target="tpu_custom_call" | custom-call | flops 12650000384 | bytes 39600000 | tf_op jit(solution)/shard_map/attend_local/pallas_call | solution.py:377
  63.0 1.7 collective-permute-done.12.block1_ref
  64.6 2.5 collective-permute-done.13.block2_ref
  75.2 2.2 collective-permute-done.16.mixed3_ref
  77.4 5.1 %collective-permute-done.17.refs_3_ = bf16[2,96,1152]{2,1,0:T(8,128)(2,1)S(1)} collective-permute-done((bf16[2,96,1152]{2,1,0:T(8,128)(2,1)S(1)}, bf16[2,96,1152]{2,1,0:T(8,128)(2,1)S(1)}, u32[]{:S(2)}, u32[]{:S(2)}) %collective-permute-start.17) | collective-permute-done | bytes 442400 | tf_op jit(solution)/shard_map/ppermute | solution.py:26
  85.6 7.0 %token_forward.1 = (f32[320,768]{1,0:T(8,128)S(1)}, bf16[320,768]{1,0:T(8,128)(2,1)S(1)}, bf16[320,768]{1,0:T(8,128)(2,1)S(1)}) custom-call(s32[6]{0:T(128)S(1)} %stack.69.place_ref, bf16[160,384]{1,0:T(8,128)(2,1)S(1)} %get-tuple-element.234.mixed0_ref, bf16[160,384]{1,0:T(8,128)(2,1)S(1)} %collective-permute-done.14.mixed1_ref, ...), custom_call_target="tpu_custom_call" | custom-call | flops 11500000256 | bytes 36000000 | tf_op jit(solution)/shard_map/token_forward/pallas_call | solution.py:563
  94.3 2.5 collective-permute-start.26
  96.8 8.7 %collective-permute-done.26.block3_ref = bf16[144,1152]{1,0:T(8,128)(2,1)S(1)} collective-permute-done((bf16[144,1152]{1,0:T(8,128)(2,1)S(1)}, bf16[144,1152]{1,0:T(8,128)(2,1)S(1)}, u32[]{:S(2)}, u32[]{:S(2)}) %collective-permute-start.26) | collective-permute-done | bytes 331808 | tf_op jit(solution)/shard_map/ppermute | solution.py:107
  109.1 5.8 %collective-permute-done.27.head_ref = bf16[160,768]{1,0:T(8,128)(2,1)S(1)} collective-permute-done((bf16[160,768]{1,0:T(8,128)(2,1)S(1)}, bf16[160,768]{1,0:T(8,128)(2,1)S(1)}, u32[]{:S(2)}, u32[]{:S(2)}) %collective-permute-start.27) | collective-permute-done | bytes 245792 | tf_op jit(solution)/shard_map/ppermute | solution.py:26
  117.8 13.6 %attend_global.1 = (bf16[160,384]{1,0:T(8,128)(2,1)S(1)}, bf16[160,384]{1,0:T(8,128)(2,1)S(1)}, bf16[160,384]{1,0:T(8,128)(2,1)S(1)}, bf16[160,384]{1,0:T(8,128)...) custom-call(s32[6]{0:T(128)S(1)} %stack.69.place_ref, ...), custom_call_target="tpu_custom_call" | custom-call | flops 23000000512 | bytes 72000000 | tf_op jit(solution)/shard_map/attend_global/pallas_call | solution.py:377
  131.4 5.8 %collective-permute-done.30.refs_1_ = bf16[4,96,1152]{2,1,0:T(8,128)(2,1)S(1)} collective-permute-done((bf16[4,96,1152]{2,1,0:T(8,128)(2,1)S(1)}, bf16[4,96,1152]{2,1,0:T(8,128)(2,1)S(1)}, u32[]{:S(2)}, u32[]{:S(2)}) %collective-permute-start.30) | collective-permute-done | bytes 884768 | tf_op jit(solution)/shard_map/ppermute | solution.py:26
  143.5 3.0 collective-permute-done.33.mixed2_ref
  147.0 7.0 %collective-permute-done.35.refs_3_ = bf16[2,96,1152]{2,1,0:T(8,128)(2,1)S(1)} collective-permute-done((bf16[2,96,1152]{2,1,0:T(8,128)(2,1)S(1)}, bf16[2,96,1152]{2,1,0:T(8,128)(2,1)S(1)}, u32[]{:S(2)}, u32[]{:S(2)}) %collective-permute-start.35) | collective-permute-done | bytes 442400 | tf_op jit(solution)/shard_map/ppermute | solution.py:26
  157.3 19.7 %token_last.1 = (bf16[4,4,96,1152]{3,2,1,0:T(8,128)(2,1)S(1)}, bf16[4,4,96,1152]{3,2,1,0:T(8,128)(2,1)S(1)}, bf16[160,384]{1,0:T(8,128)(2,1)S(1)}, bf16[160,384]...) custom-call(s32[6]{0:T(128)S(1)} %stack.69.place_ref, ...), custom_call_target="tpu_custom_call" | custom-call | flops 23000000512 | bytes 72000000 | tf_op jit(solution)/shard_map/token_last/pallas_call | solution.py:688
  178.9 2.3 collective-permute-start.45
  181.2 2.6 collective-permute-done.43.grad1_ref
  183.9 2.6 collective-permute-done.45.grad3_ref
  190.8 19.3 %attend_back_global.1 = (bf16[320,768]{1,0:T(8,128)(2,1)S(1)}, bf16[160,768]{1,0:T(8,128)(2,1)}, bf16[160,768]{1,0:T(8,128)(2,1)S(1)}, bf16[160,768]{1,0:T(8,128...) custom-call(s32[6]{0:T(128)S(1)} %stack.69.place_ref, ...), custom_call_target="tpu_custom_call" | custom-call | flops 24149999616 | bytes 75600000 | tf_op jit(solution)/shard_map/attend_back_global/pallas_call | solution.py:485
  210.9 3.2 qkv_grad.2
  220.5 3.8 collective-permute-done.52
  230.2 4.5 %collective-permute-done.53 = bf16[160,768]{1,0:T(8,128)(2,1)S(1)} collective-permute-done((bf16[160,768]{1,0:T(8,128)(2,1)S(1)}, bf16[160,768]{1,0:T(8,128)(2,1)S(1)}, u32[]{:S(2)}, u32[]{:S(2)}) %collective-permute-start.53) | collective-permute-done | bytes 245792 | tf_op jit(solution)/shard_map/ppermute | solution.py:26
  239.4 13.7 %token_back.1 = (bf16[4,4,96,1152]{3,2,1,0:T(8,128)(2,1)S(1)}, bf16[4,4,96,1152]{3,2,1,0:T(8,128)(2,1)S(1)}, bf16[160,384]{1,0:T(8,128)(2,1)S(1)}, bf16[160,384]...) custom-call(s32[6]{0:T(128)S(1)} %stack.69.place_ref, ...), custom_call_target="tpu_custom_call" | custom-call | flops 23000000512 | bytes 72000000 | tf_op jit(solution)/shard_map/token_back/pallas_call | solution.py:665
  253.1 4.4 %collective-permute-done.56 = bf16[4,96,1152]{2,1,0:T(8,128)(2,1)S(1)} collective-permute-done((bf16[4,96,1152]{2,1,0:T(8,128)(2,1)S(1)}, bf16[4,96,1152]{2,1,0:T(8,128)(2,1)S(1)}, u32[]{:S(2)}, u32[]{:S(2)}) %collective-permute-start.56) | collective-permute-done | bytes 884768 | tf_op jit(solution)/shard_map/ppermute | solution.py:26
  261.9 1.8 collective-permute-start.60
  263.6 2.0 fusion.32
  271.6 6.9 %collective-permute-start.64 = (bf16[144,1152]{1,0:T(8,128)(2,1)S(1)}, bf16[144,1152]{1,0:T(8,128)(2,1)S(1)}, u32[]{:S(2)}, u32[]{:S(2)}) collective-permute-start(bf16[144,1152]{1,0:T(8,128)(2,1)S(1)} %pad_maximum_fusion.8), channel_id=1, source_target_pairs={{0,8},{8,0},{16,24},{24,16},{1,9},{9,1},{17,25},{25,17},{2,10},{10... | collective-permute-start | bytes 995336 | tf_op jit(solution)/shard_map/ppermute | solution.py:107
  279.3 10.0 %attend_back_local.1 = (bf16[320,768]{1,0:T(8,128)(2,1)S(1)}, bf16[160,768]{1,0:T(8,128)(2,1)S(1)}, bf16[160,768]{1,0:T(8,128)(2,1)S(1)}, bf16[160,768]{1,0:T(8,...) custom-call(s32[6]{0:T(128)S(1)} %stack.69.place_ref, ...), custom_call_target="tpu_custom_call" | custom-call | flops 12650000384 | bytes 39600000 | tf_op jit(solution)/shard_map/attend_back_local/pallas_call | solution.py:485
  289.4 2.2 collective-permute-done.64
  291.6 2.8 collective-permute-done.65
  297.5 2.5 qkv_grad.3
  305.8 2.3 collective-permute-start.68
  308.2 8.9 %collective-permute-done.68 = bf16[144,1152]{1,0:T(8,128)(2,1)S(1)} collective-permute-done((bf16[144,1152]{1,0:T(8,128)(2,1)}, bf16[144,1152]{1,0:T(8,128)(2,1)S(1)}, u32[]{:S(2)}, u32[]{:S(2)}) %collective-permute-start.68) | collective-permute-done | bytes 331808 | tf_op jit(solution)/shard_map/ppermute | solution.py:107
  317.1 8.1 %collective-permute-done.66 = bf16[4,96,1152]{2,1,0:T(8,128)(2,1)S(1)} collective-permute-done((bf16[4,96,1152]{2,1,0:T(8,128)(2,1)}, bf16[4,96,1152]{2,1,0:T(8,128)(2,1)S(1)}, u32[]{:S(2)}, u32[]{:S(2)}) %collective-permute-start.66) | collective-permute-done | bytes 884768 | tf_op jit(solution)/shard_map/ppermute | solution.py:26
  327.7 2.0 fusion.31
  329.7 2.4 collective-permute-start.80
  333.9 2.0 collective-permute-done.73
  342.4 16.7 %collective-permute-done.79 = bf16[144,1152]{1,0:T(8,128)(2,1)S(1)} collective-permute-done((bf16[144,1152]{1,0:T(8,128)(2,1)S(1)}, bf16[144,1152]{1,0:T(8,128)(2,1)S(1)}, u32[]{:S(2)}, u32[]{:S(2)}) %collective-permute-start.79) | collective-permute-done | bytes 331808 | tf_op jit(solution)/shard_map/ppermute | solution.py:107
  363.3 3.6 collective-permute-done.82
  367.1 2.3 maximum_select_fusion.2
  369.3 2.2 collective-permute-done.83
  379.2 3.0 maximum_select_fusion
  (431 shorter events, 116.8 us)
Async XLA Ops:
  7.7 14.4 %collective-permute-start.2 = (bf16[320,768]{1,0:T(8,128)(2,1)S(1)}, bf16[320,768]{1,0:T(8,128)(2,1)S(1)}, u32[]{:S(2)}, u32[]{:S(2)}) collective-permute-start(bf16[320,768]{1,0:T(8,128)(2,1)S(1)} %fusion.15.own_ref), channel_id=1, source_target_pairs={{0,1},{1,0},{2,3},{3,2},{4,5},{5,4},{6,7},{7,6},{8,9},{9,8},{10,11... | collective-permute-start | bytes 1474568 | tf_op jit(solution)/shard_map/ppermute | solution.py:26
  10.7 12.9 %collective-permute-start.3 = (bf16[320,768]{1,0:T(8,128)(2,1)S(1)}, bf16[320,768]{1,0:T(8,128)(2,1)S(1)}, u32[]{:S(2)}, u32[]{:S(2)}) collective-permute-start(bf16[320,768]{1,0:T(8,128)(2,1)S(1)} %fusion.15.own_ref), channel_id=1, source_target_pairs={{0,2},{1,3},{2,0},{3,1},{4,6},{5,7},{6,4},{7,5},{8,10},{9,11},{10,... | collective-permute-start | bytes 1474568 | tf_op jit(solution)/shard_map/ppermute | solution.py:26
  12.4 15.6 %collective-permute-start.6 = (bf16[144,1152]{1,0:T(8,128)(2,1)S(1)}, bf16[144,1152]{1,0:T(8,128)(2,1)}, u32[]{:S(2)}, u32[]{:S(2)}) collective-permute-start(bf16[144,1152]{1,0:T(8,128)(2,1)S(1)} %get-tuple-element.215.block0_ref), channel_id=1, source_target_pairs={{0,8},{8,0},{16,24},{24,16},{1,9},{9,1},{17,25},{25,17},{2,10},{10... | collective-permute-start | bytes 995336 | tf_op jit(solution)/shard_map/ppermute | solution.py:107
  14.1 26.0 %collective-permute-start.7 = (bf16[144,1152]{1,0:T(8,128)(2,1)S(1)}, bf16[144,1152]{1,0:T(8,128)(2,1)}, u32[]{:S(2)}, u32[]{:S(2)}) collective-permute-start(bf16[144,1152]{1,0:T(8,128)(2,1)S(1)} %get-tuple-element.215.block0_ref), channel_id=1, source_target_pairs={{0,16},{8,24},{16,0},{24,8},{1,17},{9,25},{17,1},{25,9},{2,18},{10... | collective-permute-start | bytes 995336 | tf_op jit(solution)/shard_map/ppermute | solution.py:107
  16.7 23.4 %collective-permute-start.8 = (bf16[144,1152]{1,0:T(8,128)(2,1)S(1)}, bf16[144,1152]{1,0:T(8,128)(2,1)}, u32[]{:S(2)}, u32[]{:S(2)}) collective-permute-start(bf16[144,1152]{1,0:T(8,128)(2,1)S(1)} %get-tuple-element.215.block0_ref), channel_id=1, source_target_pairs={{0,24},{8,16},{16,8},{24,0},{1,25},{9,17},{17,9},{25,1},{2,26},{10... | collective-permute-start | bytes 995336 | tf_op jit(solution)/shard_map/ppermute | solution.py:107
  25.1 15.0 %collective-permute-start.4 = (bf16[160,768]{1,0:T(8,128)(2,1)}, bf16[160,768]{1,0:T(8,128)(2,1)S(1)}, u32[]{:S(2)}, u32[]{:S(2)}) collective-permute-start(bf16[160,768]{1,0:T(8,128)(2,1)} %slice.363), channel_id=1, source_target_pairs={{0,1},{1,0},{2,3},{3,2},{4,5},{5,4},{6,7},{7,6},{8,9},{9,8},{10,11... | collective-permute-start | bytes 737288 | tf_op jit(solution)/shard_map/ppermute | solution.py:26
  26.1 13.9 %collective-permute-start.5 = (bf16[160,768]{1,0:T(8,128)(2,1)}, bf16[160,768]{1,0:T(8,128)(2,1)}, u32[]{:S(2)}, u32[]{:S(2)}) collective-permute-start(bf16[160,768]{1,0:T(8,128)(2,1)} %slice.364), channel_id=1, source_target_pairs={{0,2},{1,3},{2,0},{3,1},{4,6},{5,7},{6,4},{7,5},{8,10},{9,11},{10,... | collective-permute-start | bytes 737288 | tf_op jit(solution)/shard_map/ppermute | solution.py:26
  43.2 24.0 %collective-permute-start.10 = (bf16[4,96,1152]{2,1,0:T(8,128)(2,1)S(1)}, bf16[4,96,1152]{2,1,0:T(8,128)(2,1)S(1)}, u32[]{:S(2)}, u32[]{:S(2)}) collective-permute-start(bf16[4,96,1152]{2,1,0:T(8,128)(2,1)S(1)} %get-tuple-element.238.refs_0_), channel_id=1, source_target_pairs={{0,1},{1,0},{2,3},{3,2},{4,5},{5,4},{6,7},{7,6},{8,9},{9,8},{10,11... | collective-permute-start | bytes 2654216 | tf_op jit(solution)/shard_map/ppermute | solution.py:26
  43.7 23.4 %collective-permute-start.11 = (bf16[4,96,1152]{2,1,0:T(8,128)(2,1)S(1)}, bf16[4,96,1152]{2,1,0:T(8,128)(2,1)S(1)}, u32[]{:S(2)}, u32[]{:S(2)}) collective-permute-start(bf16[4,96,1152]{2,1,0:T(8,128)(2,1)S(1)} %get-tuple-element.238.refs_0_), channel_id=1, source_target_pairs={{0,2},{1,3},{2,0},{3,1},{4,6},{5,7},{6,4},{7,5},{8,10},{9,11},{10,... | collective-permute-start | bytes 2654216 | tf_op jit(solution)/shard_map/ppermute | solution.py:26
  44.2 20.4 %collective-permute-start.12 = (bf16[144,1152]{1,0:T(8,128)(2,1)S(1)}, bf16[144,1152]{1,0:T(8,128)(2,1)S(1)}, u32[]{:S(2)}, u32[]{:S(2)}) collective-permute-start(bf16[144,1152]{1,0:T(8,128)(2,1)S(1)} %get-tuple-element.245.block0_ref), channel_id=1, source_target_pairs={{0,8},{8,0},{16,24},{24,16},{1,9},{9,1},{17,25},{25,17},{2,10},{10... | collective-permute-start | bytes 995336 | tf_op jit(solution)/shard_map/ppermute | solution.py:107
  50.1 17.1 %collective-permute-start.13 = (bf16[144,1152]{1,0:T(8,128)(2,1)S(1)}, bf16[144,1152]{1,0:T(8,128)(2,1)S(1)}, u32[]{:S(2)}, u32[]{:S(2)}) collective-permute-start(bf16[144,1152]{1,0:T(8,128)(2,1)S(1)} %get-tuple-element.245.block0_ref), channel_id=1, source_target_pairs={{0,16},{8,24},{16,0},{24,8},{1,17},{9,25},{17,1},{25,9},{2,18},{10... | collective-permute-start | bytes 995336 | tf_op jit(solution)/shard_map/ppermute | solution.py:107
  70.8 11.8 %collective-permute-start.17 = (bf16[2,96,1152]{2,1,0:T(8,128)(2,1)S(1)}, bf16[2,96,1152]{2,1,0:T(8,128)(2,1)S(1)}, u32[]{:S(2)}, u32[]{:S(2)}) collective-permute-start(bf16[2,96,1152]{2,1,0:T(8,128)(2,1)S(1)} %slice.365), channel_id=1, source_target_pairs={{0,1},{1,0},{2,3},{3,2},{4,5},{5,4},{6,7},{7,6},{8,9},{9,8},{10,11... | collective-permute-start | bytes 1327112 | tf_op jit(solution)/shard_map/ppermute | solution.py:26
  72.4 10.7 %collective-permute-start.18 = (bf16[2,96,1152]{2,1,0:T(8,128)(2,1)S(1)}, bf16[2,96,1152]{2,1,0:T(8,128)(2,1)S(1)}, u32[]{:S(2)}, u32[]{:S(2)}) collective-permute-start(bf16[2,96,1152]{2,1,0:T(8,128)(2,1)S(1)} %slice.366), channel_id=1, source_target_pairs={{0,2},{1,3},{2,0},{3,1},{4,6},{5,7},{6,4},{7,5},{8,10},{9,11},{10,... | collective-permute-start | bytes 1327112 | tf_op jit(solution)/shard_map/ppermute | solution.py:26
  73.9 11.6 %collective-permute-start.20 = (bf16[4,96,1152]{2,1,0:T(8,128)(2,1)S(1)}, bf16[4,96,1152]{2,1,0:T(8,128)(2,1)S(1)}, u32[]{:S(2)}, u32[]{:S(2)}) collective-permute-start(bf16[4,96,1152]{2,1,0:T(8,128)(2,1)S(1)} %collective-permute-done.10.refs_1_), channel_id=1, source_target_pairs={{0,4},{4,0},{1,5},{5,1},{2,6},{6,2},{3,7},{7,3},{8,12},{12,8},{9,1... | collective-permute-start | bytes 2654216 | tf_op jit(solution)/shard_map/ppermute | solution.py:21
  75.2 10.3 %collective-permute-start.19 = (bf16[4,96,1152]{2,1,0:T(8,128)(2,1)S(1)}, bf16[4,96,1152]{2,1,0:T(8,128)(2,1)S(1)}, u32[]{:S(2)}, u32[]{:S(2)}) collective-permute-start(bf16[4,96,1152]{2,1,0:T(8,128)(2,1)S(1)} %get-tuple-element.238.refs_0_), channel_id=1, source_target_pairs={{0,4},{4,0},{1,5},{5,1},{2,6},{6,2},{3,7},{7,3},{8,12},{12,8},{9,1... | collective-permute-start | bytes 2654216 | tf_op jit(solution)/shard_map/ppermute | solution.py:21
  92.7 13.3 %collective-permute-start.24 = (bf16[320,768]{1,0:T(8,128)(2,1)S(1)}, bf16[320,768]{1,0:T(8,128)(2,1)S(1)}, u32[]{:S(2)}, u32[]{:S(2)}) collective-permute-start(bf16[320,768]{1,0:T(8,128)(2,1)S(1)} %get-tuple-element.242.own_ref), channel_id=1, source_target_pairs={{0,1},{1,0},{2,3},{3,2},{4,5},{5,4},{6,7},{7,6},{8,9},{9,8},{10,11... | collective-permute-start | bytes 1474568 | tf_op jit(solution)/shard_map/ppermute | solution.py:26
  93.3 13.0 %collective-permute-start.25 = (bf16[320,768]{1,0:T(8,128)(2,1)S(1)}, bf16[320,768]{1,0:T(8,128)(2,1)S(1)}, u32[]{:S(2)}, u32[]{:S(2)}) collective-permute-start(bf16[320,768]{1,0:T(8,128)(2,1)S(1)} %get-tuple-element.242.own_ref), channel_id=1, source_target_pairs={{0,2},{1,3},{2,0},{3,1},{4,6},{5,7},{6,4},{7,5},{8,10},{9,11},{10,... | collective-permute-start | bytes 1474568 | tf_op jit(solution)/shard_map/ppermute | solution.py:26
  94.3 11.2 %collective-permute-start.26 = (bf16[144,1152]{1,0:T(8,128)(2,1)S(1)}, bf16[144,1152]{1,0:T(8,128)(2,1)S(1)}, u32[]{:S(2)}, u32[]{:S(2)}) collective-permute-start(bf16[144,1152]{1,0:T(8,128)(2,1)S(1)} %get-tuple-element.245.block0_ref), channel_id=1, source_target_pairs={{0,24},{8,16},{16,8},{24,0},{1,25},{9,17},{17,9},{25,1},{2,26},{10... | collective-permute-start | bytes 995336 | tf_op jit(solution)/shard_map/ppermute | solution.py:107
  116.2 20.9 %collective-permute-start.30 = (bf16[4,96,1152]{2,1,0:T(8,128)(2,1)S(1)}, bf16[4,96,1152]{2,1,0:T(8,128)(2,1)S(1)}, u32[]{:S(2)}, u32[]{:S(2)}) collective-permute-start(bf16[4,96,1152]{2,1,0:T(8,128)(2,1)S(1)} %get-tuple-element.259.refs_0_), channel_id=1, source_target_pairs={{0,1},{1,0},{2,3},{3,2},{4,5},{5,4},{6,7},{7,6},{8,9},{9,8},{10,11... | collective-permute-start | bytes 2654216 | tf_op jit(solution)/shard_map/ppermute | solution.py:26
  116.8 20.7 %collective-permute-start.31 = (bf16[4,96,1152]{2,1,0:T(8,128)(2,1)S(1)}, bf16[4,96,1152]{2,1,0:T(8,128)(2,1)S(1)}, u32[]{:S(2)}, u32[]{:S(2)}) collective-permute-start(bf16[4,96,1152]{2,1,0:T(8,128)(2,1)S(1)} %get-tuple-element.259.refs_0_), channel_id=1, source_target_pairs={{0,2},{1,3},{2,0},{3,1},{4,6},{5,7},{6,4},{7,5},{8,10},{9,11},{10,... | collective-permute-start | bytes 2654216 | tf_op jit(solution)/shard_map/ppermute | solution.py:26
  140.9 13.1 %collective-permute-start.35 = (bf16[2,96,1152]{2,1,0:T(8,128)(2,1)S(1)}, bf16[2,96,1152]{2,1,0:T(8,128)(2,1)S(1)}, u32[]{:S(2)}, u32[]{:S(2)}) collective-permute-start(bf16[2,96,1152]{2,1,0:T(8,128)(2,1)S(1)} %slice.371), channel_id=1, source_target_pairs={{0,1},{1,0},{2,3},{3,2},{4,5},{5,4},{6,7},{7,6},{8,9},{9,8},{10,11... | collective-permute-start | bytes 1327112 | tf_op jit(solution)/shard_map/ppermute | solution.py:26
  142.5 12.3 %collective-permute-start.36 = (bf16[2,96,1152]{2,1,0:T(8,128)(2,1)S(1)}, bf16[2,96,1152]{2,1,0:T(8,128)(2,1)S(1)}, u32[]{:S(2)}, u32[]{:S(2)}) collective-permute-start(bf16[2,96,1152]{2,1,0:T(8,128)(2,1)S(1)} %slice.372), channel_id=1, source_target_pairs={{0,2},{1,3},{2,0},{3,1},{4,6},{5,7},{6,4},{7,5},{8,10},{9,11},{10,... | collective-permute-start | bytes 1327112 | tf_op jit(solution)/shard_map/ppermute | solution.py:26
  143.5 11.8 %collective-permute-start.37 = (bf16[4,96,1152]{2,1,0:T(8,128)(2,1)S(1)}, bf16[4,96,1152]{2,1,0:T(8,128)(2,1)S(1)}, u32[]{:S(2)}, u32[]{:S(2)}) collective-permute-start(bf16[4,96,1152]{2,1,0:T(8,128)(2,1)S(1)} %get-tuple-element.259.refs_0_), channel_id=1, source_target_pairs={{0,4},{4,0},{1,5},{5,1},{2,6},{6,2},{3,7},{7,3},{8,12},{12,8},{9,1... | collective-permute-start | bytes 2654216 | tf_op jit(solution)/shard_map/ppermute | solution.py:21
  146.5 10.7 %collective-permute-start.38 = (bf16[4,96,1152]{2,1,0:T(8,128)(2,1)S(1)}, bf16[4,96,1152]{2,1,0:T(8,128)(2,1)S(1)}, u32[]{:S(2)}, u32[]{:S(2)}) collective-permute-start(bf16[4,96,1152]{2,1,0:T(8,128)(2,1)S(1)} %collective-permute-done.30.refs_1_), channel_id=1, source_target_pairs={{0,4},{4,0},{1,5},{5,1},{2,6},{6,2},{3,7},{7,3},{8,12},{12,8},{9,1... | collective-permute-start | bytes 2654216 | tf_op jit(solution)/shard_map/ppermute | solution.py:21
  147.0 10.3 %collective-permute-start.39 = (bf16[4,96,1152]{2,1,0:T(8,128)(2,1)S(1)}, bf16[4,96,1152]{2,1,0:T(8,128)(2,1)S(1)}, u32[]{:S(2)}, u32[]{:S(2)}) collective-permute-start(bf16[4,96,1152]{2,1,0:T(8,128)(2,1)S(1)} %collective-permute-done.31.refs_2_), channel_id=1, source_target_pairs={{0,4},{4,0},{1,5},{5,1},{2,6},{6,2},{3,7},{7,3},{8,12},{12,8},{9,1... | collective-permute-start | bytes 2654216 | tf_op jit(solution)/shard_map/ppermute | solution.py:21
  188.4 22.5 %collective-permute-start.47 = (bf16[2,96,1152]{2,1,0:T(8,128)(2,1)S(1)}, bf16[2,96,1152]{2,1,0:T(8,128)(2,1)S(1)}, u32[]{:S(2)}, u32[]{:S(2)}) collective-permute-start(bf16[2,96,1152]{2,1,0:T(8,128)(2,1)S(1)} %get-tuple-element.465), channel_id=1, source_target_pairs={{0,1},{1,0},{2,3},{3,2},{4,5},{5,4},{6,7},{7,6},{8,9},{9,8},{10,11... | collective-permute-start | bytes 1327112 | tf_op jit(solution)/shard_map/ppermute | solution.py:26
  189.6 21.3 %collective-permute-start.48 = (bf16[2,96,1152]{2,1,0:T(8,128)(2,1)S(1)}, bf16[2,96,1152]{2,1,0:T(8,128)(2,1)S(1)}, u32[]{:S(2)}, u32[]{:S(2)}) collective-permute-start(bf16[2,96,1152]{2,1,0:T(8,128)(2,1)S(1)} %get-tuple-element.464), channel_id=1, source_target_pairs={{0,2},{1,3},{2,0},{3,1},{4,6},{5,7},{6,4},{7,5},{8,10},{9,11},{10,... | collective-permute-start | bytes 1327112 | tf_op jit(solution)/shard_map/ppermute | solution.py:26
  214.2 16.0 %collective-permute-start.54 = (bf16[4,48,1152]{2,1,0:T(8,128)(2,1)}, bf16[4,48,1152]{2,1,0:T(8,128)(2,1)}, u32[]{:S(2)}, u32[]{:S(2)}) collective-permute-start(bf16[4,48,1152]{2,1,0:T(8,128)(2,1)} %get-tuple-element.311), channel_id=1, source_target_pairs={{0,4},{4,0},{1,5},{5,1},{2,6},{6,2},{3,7},{7,3},{8,12},{12,8},{9,1... | collective-permute-start | bytes 1327112 | tf_op jit(solution)/shard_map/ppermute | solution.py:21
  215.8 10.5 %collective-permute-start.50 = (bf16[160,768]{1,0:T(8,128)(2,1)}, bf16[160,768]{1,0:T(8,128)(2,1)}, u32[]{:S(2)}, u32[]{:S(2)}) collective-permute-start(bf16[160,768]{1,0:T(8,128)(2,1)} %get-tuple-element.303), channel_id=1, source_target_pairs={{0,2},{1,3},{2,0},{3,1},{4,6},{5,7},{6,4},{7,5},{8,10},{9,11},{10,... | collective-permute-start | bytes 737288 | tf_op jit(solution)/shard_map/ppermute | solution.py:26
  216.9 12.2 %collective-permute-start.49 = (bf16[160,768]{1,0:T(8,128)(2,1)}, bf16[160,768]{1,0:T(8,128)(2,1)}, u32[]{:S(2)}, u32[]{:S(2)}) collective-permute-start(bf16[160,768]{1,0:T(8,128)(2,1)} %get-tuple-element.301), channel_id=1, source_target_pairs={{0,1},{1,0},{2,3},{3,2},{4,5},{5,4},{6,7},{7,6},{8,9},{9,8},{10,11... | collective-permute-start | bytes 737288 | tf_op jit(solution)/shard_map/ppermute | solution.py:26
  218.1 12.1 %collective-permute-start.55 = (bf16[160,768]{1,0:T(8,128)(2,1)}, bf16[160,768]{1,0:T(8,128)(2,1)}, u32[]{:S(2)}, u32[]{:S(2)}) collective-permute-start(bf16[160,768]{1,0:T(8,128)(2,1)} %get-tuple-element.312), channel_id=1, source_target_pairs={{0,2},{1,3},{2,0},{3,1},{4,6},{5,7},{6,4},{7,5},{8,10},{9,11},{10,... | collective-permute-start | bytes 737288 | tf_op jit(solution)/shard_map/ppermute | solution.py:26
  236.5 21.0 %collective-permute-start.56 = (bf16[4,96,1152]{2,1,0:T(8,128)(2,1)S(1)}, bf16[4,96,1152]{2,1,0:T(8,128)(2,1)S(1)}, u32[]{:S(2)}, u32[]{:S(2)}) collective-permute-start(bf16[4,96,1152]{2,1,0:T(8,128)(2,1)S(1)} %pad_maximum_fusion), channel_id=1, source_target_pairs={{0,1},{1,0},{2,3},{3,2},{4,5},{5,4},{6,7},{7,6},{8,9},{9,8},{10,11... | collective-permute-start | bytes 2654216 | tf_op jit(solution)/shard_map/ppermute | solution.py:26
  238.0 20.9 %collective-permute-start.57 = (bf16[4,96,1152]{2,1,0:T(8,128)(2,1)}, bf16[4,96,1152]{2,1,0:T(8,128)(2,1)S(1)}, u32[]{:S(2)}, u32[]{:S(2)}) collective-permute-start(bf16[4,96,1152]{2,1,0:T(8,128)(2,1)} %pad_maximum_fusion.1), channel_id=1, source_target_pairs={{0,2},{1,3},{2,0},{3,1},{4,6},{5,7},{6,4},{7,5},{8,10},{9,11},{10,... | collective-permute-start | bytes 2654216 | tf_op jit(solution)/shard_map/ppermute | solution.py:26
  258.9 9.9 %collective-permute-start.61 = (bf16[4,4,96,1152]{3,2,1,0:T(8,128)(2,1)S(1)}, bf16[4,4,96,1152]{3,2,1,0:T(8,128)(2,1)S(1)}, u32[]{:S(2)}, u32[]{:S(2)}) collective-permute-start(bf16[4,4,96,1152]{3,2,1,0:T(8,128)(2,1)S(1)} %get-tuple-element.333), channel_id=1, source_target_pairs={{0,4},{4,0},{1,5},{5,1},{2,6},{6,2},{3,7},{7,3},{8,12},{12,8},{9,1... | collective-permute-start | bytes 10616840 | tf_op jit(solution)/shard_map/ppermute | solution.py:21
  269.2 25.2 %collective-permute-start.62 = (bf16[2,96,1152]{2,1,0:T(8,128)(2,1)S(1)}, bf16[2,96,1152]{2,1,0:T(8,128)(2,1)S(1)}, u32[]{:S(2)}, u32[]{:S(2)}) collective-permute-start(bf16[2,96,1152]{2,1,0:T(8,128)(2,1)S(1)} %get-tuple-element.459), channel_id=1, source_target_pairs={{0,1},{1,0},{2,3},{3,2},{4,5},{5,4},{6,7},{7,6},{8,9},{9,8},{10,11... | collective-permute-start | bytes 1327112 | tf_op jit(solution)/shard_map/ppermute | solution.py:26
  270.7 23.7 %collective-permute-start.63 = (bf16[2,96,1152]{2,1,0:T(8,128)(2,1)S(1)}, bf16[2,96,1152]{2,1,0:T(8,128)(2,1)S(1)}, u32[]{:S(2)}, u32[]{:S(2)}) collective-permute-start(bf16[2,96,1152]{2,1,0:T(8,128)(2,1)S(1)} %get-tuple-element.458), channel_id=1, source_target_pairs={{0,2},{1,3},{2,0},{3,1},{4,6},{5,7},{6,4},{7,5},{8,10},{9,11},{10,... | collective-permute-start | bytes 1327112 | tf_op jit(solution)/shard_map/ppermute | solution.py:26
  271.6 20.0 %collective-permute-start.64 = (bf16[144,1152]{1,0:T(8,128)(2,1)S(1)}, bf16[144,1152]{1,0:T(8,128)(2,1)S(1)}, u32[]{:S(2)}, u32[]{:S(2)}) collective-permute-start(bf16[144,1152]{1,0:T(8,128)(2,1)S(1)} %pad_maximum_fusion.8), channel_id=1, source_target_pairs={{0,8},{8,0},{16,24},{24,16},{1,9},{9,1},{17,25},{25,17},{2,10},{10... | collective-permute-start | bytes 995336 | tf_op jit(solution)/shard_map/ppermute | solution.py:107
  278.5 15.9 %collective-permute-start.65 = (bf16[144,1152]{1,0:T(8,128)(2,1)S(1)}, bf16[144,1152]{1,0:T(8,128)(2,1)S(1)}, u32[]{:S(2)}, u32[]{:S(2)}) collective-permute-start(bf16[144,1152]{1,0:T(8,128)(2,1)S(1)} %pad_maximum_fusion.9), channel_id=1, source_target_pairs={{0,16},{8,24},{16,0},{24,8},{1,17},{9,25},{17,1},{25,9},{2,18},{10... | collective-permute-start | bytes 995336 | tf_op jit(solution)/shard_map/ppermute | solution.py:107
  303.3 21.8 %collective-permute-start.66 = (bf16[4,96,1152]{2,1,0:T(8,128)(2,1)}, bf16[4,96,1152]{2,1,0:T(8,128)(2,1)S(1)}, u32[]{:S(2)}, u32[]{:S(2)}) collective-permute-start(bf16[4,96,1152]{2,1,0:T(8,128)(2,1)} %pad_maximum_fusion.2), channel_id=1, source_target_pairs={{0,1},{1,0},{2,3},{3,2},{4,5},{5,4},{6,7},{7,6},{8,9},{9,8},{10,11... | collective-permute-start | bytes 2654216 | tf_op jit(solution)/shard_map/ppermute | solution.py:26
  304.6 21.6 %collective-permute-start.67 = (bf16[4,96,1152]{2,1,0:T(8,128)(2,1)}, bf16[4,96,1152]{2,1,0:T(8,128)(2,1)S(1)}, u32[]{:S(2)}, u32[]{:S(2)}) collective-permute-start(bf16[4,96,1152]{2,1,0:T(8,128)(2,1)} %pad_maximum_fusion.3), channel_id=1, source_target_pairs={{0,2},{1,3},{2,0},{3,1},{4,6},{5,7},{6,4},{7,5},{8,10},{9,11},{10,... | collective-permute-start | bytes 2654216 | tf_op jit(solution)/shard_map/ppermute | solution.py:26
  305.8 11.3 %collective-permute-start.68 = (bf16[144,1152]{1,0:T(8,128)(2,1)}, bf16[144,1152]{1,0:T(8,128)(2,1)S(1)}, u32[]{:S(2)}, u32[]{:S(2)}) collective-permute-start(bf16[144,1152]{1,0:T(8,128)(2,1)} %pad_maximum_fusion.10), channel_id=1, source_target_pairs={{0,24},{8,16},{16,8},{24,0},{1,25},{9,17},{17,9},{25,1},{2,26},{10... | collective-permute-start | bytes 995336 | tf_op jit(solution)/shard_map/ppermute | solution.py:107
  329.7 12.7 %collective-permute-start.80 = (bf16[144,1152]{1,0:T(8,128)(2,1)S(1)}, bf16[144,1152]{1,0:T(8,128)(2,1)S(1)}, u32[]{:S(2)}, u32[]{:S(2)}) collective-permute-start(bf16[144,1152]{1,0:T(8,128)(2,1)S(1)} %pad_maximum_fusion.13), channel_id=1, source_target_pairs={{0,24},{8,16},{16,8},{24,0},{1,25},{9,17},{17,9},{25,1},{2,26},{10... | collective-permute-start | bytes 995336 | tf_op jit(solution)/shard_map/ppermute | solution.py:107
  333.8 25.3 %collective-permute-start.79 = (bf16[144,1152]{1,0:T(8,128)(2,1)S(1)}, bf16[144,1152]{1,0:T(8,128)(2,1)S(1)}, u32[]{:S(2)}, u32[]{:S(2)}) collective-permute-start(bf16[144,1152]{1,0:T(8,128)(2,1)S(1)} %pad_maximum_fusion.12), channel_id=1, source_target_pairs={{0,16},{8,24},{16,0},{24,8},{1,17},{9,25},{17,1},{25,9},{2,18},{10... | collective-permute-start | bytes 995336 | tf_op jit(solution)/shard_map/ppermute | solution.py:107
  337.1 22.0 %collective-permute-start.74 = (bf16[320,768]{1,0:T(8,128)(2,1)S(1)}, bf16[320,768]{1,0:T(8,128)(2,1)S(1)}, u32[]{:S(2)}, u32[]{:S(2)}) collective-permute-start(bf16[320,768]{1,0:T(8,128)(2,1)S(1)} %pad_maximum_fusion.5), channel_id=1, source_target_pairs={{0,1},{1,0},{2,3},{3,2},{4,5},{5,4},{6,7},{7,6},{8,9},{9,8},{10,11... | collective-permute-start | bytes 1474568 | tf_op jit(solution)/shard_map/ppermute | solution.py:26
  338.8 20.3 %collective-permute-start.75 = (bf16[320,768]{1,0:T(8,128)(2,1)S(1)}, bf16[320,768]{1,0:T(8,128)(2,1)S(1)}, u32[]{:S(2)}, u32[]{:S(2)}) collective-permute-start(bf16[320,768]{1,0:T(8,128)(2,1)S(1)} %pad_maximum_fusion.6), channel_id=1, source_target_pairs={{0,2},{1,3},{2,0},{3,1},{4,6},{5,7},{6,4},{7,5},{8,10},{9,11},{10,... | collective-permute-start | bytes 1474568 | tf_op jit(solution)/shard_map/ppermute | solution.py:26
  340.0 19.2 %collective-permute-start.78 = (bf16[144,1152]{1,0:T(8,128)(2,1)S(1)}, bf16[144,1152]{1,0:T(8,128)(2,1)S(1)}, u32[]{:S(2)}, u32[]{:S(2)}) collective-permute-start(bf16[144,1152]{1,0:T(8,128)(2,1)S(1)} %pad_maximum_fusion.11), channel_id=1, source_target_pairs={{0,8},{8,0},{16,24},{24,16},{1,9},{9,1},{17,25},{25,17},{2,10},{10... | collective-permute-start | bytes 995336 | tf_op jit(solution)/shard_map/ppermute | solution.py:107
  342.4 24.7 %collective-permute-start.42 = (bf16[320,768]{1,0:T(8,128)(2,1)}, bf16[320,768]{1,0:T(8,128)(2,1)}, u32[]{:S(2)}, u32[]{:S(2)}) collective-permute-start(bf16[320,768]{1,0:T(8,128)(2,1)} %get-tuple-element.453), channel_id=1, source_target_pairs={{0,4},{4,0},{1,5},{5,1},{2,6},{6,2},{3,7},{7,3},{8,12},{12,8},{9,1... | collective-permute-start | bytes 1474568 | tf_op jit(solution)/shard_map/ppermute | solution.py:21
  362.3 16.9 %collective-permute-start.76 = (f32[320,768]{1,0:T(8,128)}, f32[320,768]{1,0:T(8,128)}, u32[]{:S(2)}, u32[]{:S(2)}) collective-permute-start(f32[320,768]{1,0:T(8,128)} %convert_select_fusion), channel_id=1, source_target_pairs={{0,4},{4,0},{1,5},{5,1},{2,6},{6,2},{3,7},{7,3},{8,12},{12,8},{9,1... | collective-permute-start | bytes 2949128 | tf_op jit(solution)/shard_map/ppermute | solution.py:21
  (127 other events, 1273.7 us)

commit v6 on v5

--- a/solution.py
+++ b/solution.py
@@ -906,11 +906,14 @@
     chunk = model * 2 // (4 * lax.axis_size("dp"))
     me = lax.axis_index("dp") * 4 + lax.axis_index("tensor")
     if four_dp():
-        gain_sum += to_peer(gain_sum, 1)
-        gain_sum += to_peer(gain_sum, 2)
+        rank = lax.axis_index("dp")
+        chunks = take(jnp.swapaxes(gain_sum.reshape(4, 4, chunk), 0, 1), lax.axis_index("tensor"))
+        gain_part = take(chunks, rank)
+        for bit in (1, 2, 3):
+            gain_part += to_peer(take(chunks, rank ^ bit), bit)
     else:
         gain_sum = lax.psum(gain_sum, "dp")
-    gain_part = lax.dynamic_slice_in_dim(gain_sum[0], me * chunk, chunk, 0)
+        gain_part = lax.dynamic_slice_in_dim(gain_sum[0], me * chunk, chunk, 0)
     first_grad = norm_step(0, add_up(parts[0], *rows_near), grad_mid)
     input_grads = (first_grad, second_grad)
 
@@ -933,7 +936,7 @@
     )
     grads_in = join_halves(
         jnp.where(core == 0, input_grads[0], input_grads[1]),
-        swap_cores(jnp.where(core == 0, input_grads[1], input_grads[0])),
+        swap_cores(jnp.where(core == 0, input_grads[1], input_grads[0]).astype(BF16)).astype(F32),
         0,
     )
     return (

time: 388 us -> 393 us (1.013)
  waiting for transfers between devices: 142 us -> 126 us
  local copies, waits for them, and re-layouts: 18.3 us -> 25.8 us
  other arithmetic: 35.8 us -> 41.6 us
  starting transfers between devices: 84.9 us -> 90.6 us
    ppermute x14 -> x15, waiting for transfers between devices: 62.9 us -> 51.3 us  [to_peer(): return lax.ppermute(block, 'dp', [(i, i ^ bit) for i in range(4)])]
    unnamed x186 -> x216, local copies, waits for them, and re-layouts: 12.3 us -> 17.7 us
    ppermute x14 -> x15, starting transfers between devices: 26.5 us -> 31.6 us  [to_peer(): return lax.ppermute(block, 'dp', [(i, i ^ bit) for i in range(4)])]
    ppermute x48, waiting for transfers between devices: 74.9 us -> 70.2 us  [to_mate(): return lax.ppermute(block, 'tensor', [(i, i ^ bit) for i in range(size)])]
  transfers between devices with their start and end apart: 84 -> 85, of which waited for: 44 -> 39; matrix products, arithmetic and copies ran while one was open for 9% -> 12% of each run, Pallas kernels for 17% -> 18%
where the time goes in v6:
time: 393 us; the launch traced here: 387 us
  waiting for transfers between devices  126 us (32%)
  Pallas kernels  101 us (26%)
  starting transfers between devices  90.6 us (23%)
  other arithmetic  41.6 us (11%)
  local copies, waits for them, and re-layouts  25.8 us (7%)
    ppermute x48, waiting for transfers between devices, to_mate(): return lax.ppermute(block, 'tensor', [(i, i ^ bit) for i in range(size)])  70.2 us
    ppermute x48, starting transfers between devices, to_mate(): return lax.ppermute(block, 'tensor', [(i, i ^ bit) for i in range(size)])  55.4 us
    ppermute x15, waiting for transfers between devices, to_peer(): return lax.ppermute(block, 'dp', [(i, i ^ bit) for i in range(4)])  51.3 us
    ppermute x15, starting transfers between devices, to_peer(): return lax.ppermute(block, 'dp', [(i, i ^ bit) for i in range(4)])  31.6 us
    pallas_call x2, Pallas kernels, attend_back(): pl.pallas_call(functools.partial(attend_back_kernel, span), out_shape=(pa...  29.3 us
    pallas_call x2, Pallas kernels, attend(): pl.pallas_call(functools.partial(attend_kernel, span), out_shape=(mixed,...  22.2 us
    pallas_call x1, Pallas kernels, token_last(): pl.pallas_call(functools.partial(token_last_kernel, pair), out_shape=(hal...  19.7 us
    unnamed x216, local copies, waits for them, and re-layouts  17.7 us
  transfers between devices with their start and end apart: 85, of which 39 were waited for; matrix products, arithmetic and copies ran while one was open for 12% of the time, Pallas kernels for 18%

profile of v6, /device:TPU:0, one launch (start us, length us, event | category | flops | bytes accessed | tf_op | source)
XLA Modules:
  0.0 387.2 jit_solution(17132489581316660031)
XLA Ops:
  7.7 3.0 collective-permute-start.2
  12.4 1.6 collective-permute-start.6
  14.1 2.6 collective-permute-start.7
  16.9 5.2 %collective-permute-done.2.one_ref = bf16[320,768]{1,0:T(8,128)(2,1)S(1)} collective-permute-done((bf16[320,768]{1,0:T(8,128)(2,1)S(1)}, bf16[320,768]{1,0:T(8,128)(2,1)S(1)}, u32[]{:S(2)}, u32[]{:S(2)}) %collective-permute-start.2) | collective-permute-done | bytes 491552 | tf_op jit(solution)/shard_map/ppermute | solution.py:26
  26.1 1.7 collective-permute-start.5
  28.0 12.0 %collective-permute-done.7.block2_ref = bf16[144,1152]{1,0:T(8,128)(2,1)} collective-permute-done((bf16[144,1152]{1,0:T(8,128)(2,1)S(1)}, bf16[144,1152]{1,0:T(8,128)(2,1)}, u32[]{:S(2)}, u32[]{:S(2)}) %collective-permute-start.7) | collective-permute-done | bytes 331808 | tf_op jit(solution)/shard_map/ppermute | solution.py:107
  44.2 5.9 %collective-permute-start.12 = (bf16[144,1152]{1,0:T(8,128)(2,1)S(1)}, bf16[144,1152]{1,0:T(8,128)(2,1)S(1)}, u32[]{:S(2)}, u32[]{:S(2)}) collective-permute-start(bf16[144,1152]{1,0:T(8,128)(2,1)S(1)} %get-tuple-element.245.block0_ref), channel_id=1, source_target_pairs={{0,8},{8,0},{16,24},{24,16},{1,9},{9,1},{17,25},{25,17},{2,10},{10... | collective-permute-start | bytes 995336 | tf_op jit(solution)/shard_map/ppermute | solution.py:107
  51.1 8.6 %attend_local.1 = (bf16[160,384]{1,0:T(8,128)(2,1)S(1)}, bf16[160,384]{1,0:T(8,128)(2,1)S(1)}, bf16[160,384]{1,0:T(8,128)(2,1)S(1)}, bf16[160,384]{1,0:T(8,128)(...) custom-call(s32[6]{0:T(128)S(1)} %stack.71.place_ref, ...), custom_call_target="tpu_custom_call" | custom-call | flops 12650000384 | bytes 39600000 | tf_op jit(solution)/shard_map/attend_local/pallas_call | solution.py:377
  64.6 2.5 collective-permute-done.13.block2_ref
  75.2 2.2 collective-permute-done.16.mixed3_ref
  77.4 5.1 %collective-permute-done.17.refs_3_ = bf16[2,96,1152]{2,1,0:T(8,128)(2,1)S(1)} collective-permute-done((bf16[2,96,1152]{2,1,0:T(8,128)(2,1)S(1)}, bf16[2,96,1152]{2,1,0:T(8,128)(2,1)S(1)}, u32[]{:S(2)}, u32[]{:S(2)}) %collective-permute-start.17) | collective-permute-done | bytes 442400 | tf_op jit(solution)/shard_map/ppermute | solution.py:26
  85.6 7.0 %token_forward.1 = (f32[320,768]{1,0:T(8,128)S(1)}, bf16[320,768]{1,0:T(8,128)(2,1)S(1)}, bf16[320,768]{1,0:T(8,128)(2,1)S(1)}) custom-call(s32[6]{0:T(128)S(1)} %stack.71.place_ref, bf16[160,384]{1,0:T(8,128)(2,1)S(1)} %get-tuple-element.234.mixed0_ref, bf16[160,384]{1,0:T(8,128)(2,1)S(1)} %collective-permute-done.14.mixed1_ref, ...), custom_call_target="tpu_custom_call" | custom-call | flops 11500000256 | bytes 36000000 | tf_op jit(solution)/shard_map/token_forward/pallas_call | solution.py:563
  94.4 2.5 collective-permute-start.26
  96.8 8.7 %collective-permute-done.26.block3_ref = bf16[144,1152]{1,0:T(8,128)(2,1)S(1)} collective-permute-done((bf16[144,1152]{1,0:T(8,128)(2,1)S(1)}, bf16[144,1152]{1,0:T(8,128)(2,1)S(1)}, u32[]{:S(2)}, u32[]{:S(2)}) %collective-permute-start.26) | collective-permute-done | bytes 331808 | tf_op jit(solution)/shard_map/ppermute | solution.py:107
  109.1 5.8 %collective-permute-done.27.head_ref = bf16[160,768]{1,0:T(8,128)(2,1)S(1)} collective-permute-done((bf16[160,768]{1,0:T(8,128)(2,1)S(1)}, bf16[160,768]{1,0:T(8,128)(2,1)S(1)}, u32[]{:S(2)}, u32[]{:S(2)}) %collective-permute-start.27) | collective-permute-done | bytes 245792 | tf_op jit(solution)/shard_map/ppermute | solution.py:26
  117.8 13.6 %attend_global.1 = (bf16[160,384]{1,0:T(8,128)(2,1)S(1)}, bf16[160,384]{1,0:T(8,128)(2,1)S(1)}, bf16[160,384]{1,0:T(8,128)(2,1)S(1)}, bf16[160,384]{1,0:T(8,128)...) custom-call(s32[6]{0:T(128)S(1)} %stack.71.place_ref, ...), custom_call_target="tpu_custom_call" | custom-call | flops 23000000512 | bytes 72000000 | tf_op jit(solution)/shard_map/attend_global/pallas_call | solution.py:377
  131.4 5.8 %collective-permute-done.30.refs_1_ = bf16[4,96,1152]{2,1,0:T(8,128)(2,1)S(1)} collective-permute-done((bf16[4,96,1152]{2,1,0:T(8,128)(2,1)S(1)}, bf16[4,96,1152]{2,1,0:T(8,128)(2,1)S(1)}, u32[]{:S(2)}, u32[]{:S(2)}) %collective-permute-start.30) | collective-permute-done | bytes 884768 | tf_op jit(solution)/shard_map/ppermute | solution.py:26
  143.5 3.0 collective-permute-done.33.mixed2_ref
  147.0 7.0 %collective-permute-done.35.refs_3_ = bf16[2,96,1152]{2,1,0:T(8,128)(2,1)S(1)} collective-permute-done((bf16[2,96,1152]{2,1,0:T(8,128)(2,1)S(1)}, bf16[2,96,1152]{2,1,0:T(8,128)(2,1)S(1)}, u32[]{:S(2)}, u32[]{:S(2)}) %collective-permute-start.35) | collective-permute-done | bytes 442400 | tf_op jit(solution)/shard_map/ppermute | solution.py:26
  157.3 19.7 %token_last.1 = (bf16[4,4,96,1152]{3,2,1,0:T(8,128)(2,1)S(1)}, bf16[4,4,96,1152]{3,2,1,0:T(8,128)(2,1)S(1)}, bf16[160,384]{1,0:T(8,128)(2,1)S(1)}, bf16[160,384]...) custom-call(s32[6]{0:T(128)S(1)} %stack.71.place_ref, ...), custom_call_target="tpu_custom_call" | custom-call | flops 23000000512 | bytes 72000000 | tf_op jit(solution)/shard_map/token_last/pallas_call | solution.py:688
  179.0 2.3 collective-permute-start.45
  181.2 2.6 collective-permute-done.43.grad1_ref
  183.9 2.6 collective-permute-done.45.grad3_ref
  190.8 19.3 %attend_back_global.1 = (bf16[320,768]{1,0:T(8,128)(2,1)S(1)}, bf16[160,768]{1,0:T(8,128)(2,1)}, bf16[160,768]{1,0:T(8,128)(2,1)S(1)}, bf16[160,768]{1,0:T(8,128...) custom-call(s32[6]{0:T(128)S(1)} %stack.71.place_ref, ...), custom_call_target="tpu_custom_call" | custom-call | flops 24149999616 | bytes 75600000 | tf_op jit(solution)/shard_map/attend_back_global/pallas_call | solution.py:485
  210.9 3.2 qkv_grad.2
  220.5 3.8 collective-permute-done.52
  230.2 4.5 %collective-permute-done.53 = bf16[160,768]{1,0:T(8,128)(2,1)S(1)} collective-permute-done((bf16[160,768]{1,0:T(8,128)(2,1)S(1)}, bf16[160,768]{1,0:T(8,128)(2,1)S(1)}, u32[]{:S(2)}, u32[]{:S(2)}) %collective-permute-start.53) | collective-permute-done | bytes 245792 | tf_op jit(solution)/shard_map/ppermute | solution.py:26
  239.4 15.4 %token_back.1 = (bf16[4,4,96,1152]{3,2,1,0:T(8,128)(2,1)S(1)}, bf16[4,4,96,1152]{3,2,1,0:T(8,128)(2,1)}, bf16[160,384]{1,0:T(8,128)(2,1)S(1)}, bf16[160,384]{1,0...) custom-call(s32[6]{0:T(128)S(1)} %stack.71.place_ref, ...), custom_call_target="tpu_custom_call" | custom-call | flops 23000000512 | bytes 72000000 | tf_op jit(solution)/shard_map/token_back/pallas_call | solution.py:665
  254.9 1.9 copy-done.3
  265.7 1.8 collective-permute-start.60
  267.5 2.1 fusion.33
  276.5 6.7 %collective-permute-start.64 = (bf16[144,1152]{1,0:T(8,128)(2,1)S(1)}, bf16[144,1152]{1,0:T(8,128)(2,1)S(1)}, u32[]{:S(2)}, u32[]{:S(2)}) collective-permute-start(bf16[144,1152]{1,0:T(8,128)(2,1)S(1)} %pad_maximum_fusion.8), channel_id=1, source_target_pairs={{0,8},{8,0},{16,24},{24,16},{1,9},{9,1},{17,25},{25,17},{2,10},{10... | collective-permute-start | bytes 995336 | tf_op jit(solution)/shard_map/ppermute | solution.py:107
  284.2 10.0 %attend_back_local.1 = (bf16[320,768]{1,0:T(8,128)(2,1)S(1)}, bf16[160,768]{1,0:T(8,128)(2,1)S(1)}, bf16[160,768]{1,0:T(8,128)(2,1)S(1)}, bf16[160,768]{1,0:T(8,...) custom-call(s32[6]{0:T(128)S(1)} %stack.71.place_ref, ...), custom_call_target="tpu_custom_call" | custom-call | flops 12650000384 | bytes 39600000 | tf_op jit(solution)/shard_map/attend_back_local/pallas_call | solution.py:485
  294.3 1.7 collective-permute-done.64
  296.0 2.5 collective-permute-done.65
  298.5 2.0 add_convert_fusion
  302.9 2.5 qkv_grad.3
  306.5 2.7 maximum_select_fusion.2
  312.2 2.4 collective-permute-start.68
  314.8 8.5 %collective-permute-done.68 = bf16[144,1152]{1,0:T(8,128)(2,1)S(1)} collective-permute-done((bf16[144,1152]{1,0:T(8,128)(2,1)S(1)}, bf16[144,1152]{1,0:T(8,128)(2,1)S(1)}, u32[]{:S(2)}, u32[]{:S(2)}) %collective-permute-start.68) | collective-permute-done | bytes 331808 | tf_op jit(solution)/shard_map/ppermute | solution.py:107
  323.3 8.1 %collective-permute-done.66 = bf16[4,96,1152]{2,1,0:T(8,128)(2,1)S(1)} collective-permute-done((bf16[4,96,1152]{2,1,0:T(8,128)(2,1)}, bf16[4,96,1152]{2,1,0:T(8,128)(2,1)S(1)}, u32[]{:S(2)}, u32[]{:S(2)}) %collective-permute-start.66) | collective-permute-done | bytes 884768 | tf_op jit(solution)/shard_map/ppermute | solution.py:26
  332.6 2.7 fusion.32
  335.4 2.4 collective-permute-start.80
  341.0 3.3 collective-permute-done.73
  351.0 14.0 %collective-permute-done.79 = bf16[144,1152]{1,0:T(8,128)(2,1)S(1)} collective-permute-done((bf16[144,1152]{1,0:T(8,128)(2,1)S(1)}, bf16[144,1152]{1,0:T(8,128)(2,1)S(1)}, u32[]{:S(2)}, u32[]{:S(2)}) %collective-permute-start.79) | collective-permute-done | bytes 331808 | tf_op jit(solution)/shard_map/ppermute | solution.py:107
  369.2 2.1 collective-permute-start.83
  371.3 2.3 collective-permute-start.84
  373.6 2.0 select_bitcast_fusion
  (466 shorter events, 125.7 us)
Async XLA Ops:
  7.7 14.4 %collective-permute-start.2 = (bf16[320,768]{1,0:T(8,128)(2,1)S(1)}, bf16[320,768]{1,0:T(8,128)(2,1)S(1)}, u32[]{:S(2)}, u32[]{:S(2)}) collective-permute-start(bf16[320,768]{1,0:T(8,128)(2,1)S(1)} %fusion.15.own_ref), channel_id=1, source_target_pairs={{0,1},{1,0},{2,3},{3,2},{4,5},{5,4},{6,7},{7,6},{8,9},{9,8},{10,11... | collective-permute-start | bytes 1474568 | tf_op jit(solution)/shard_map/ppermute | solution.py:26
  10.7 12.9 %collective-permute-start.3 = (bf16[320,768]{1,0:T(8,128)(2,1)S(1)}, bf16[320,768]{1,0:T(8,128)(2,1)S(1)}, u32[]{:S(2)}, u32[]{:S(2)}) collective-permute-start(bf16[320,768]{1,0:T(8,128)(2,1)S(1)} %fusion.15.own_ref), channel_id=1, source_target_pairs={{0,2},{1,3},{2,0},{3,1},{4,6},{5,7},{6,4},{7,5},{8,10},{9,11},{10,... | collective-permute-start | bytes 1474568 | tf_op jit(solution)/shard_map/ppermute | solution.py:26
  12.4 15.6 %collective-permute-start.6 = (bf16[144,1152]{1,0:T(8,128)(2,1)S(1)}, bf16[144,1152]{1,0:T(8,128)(2,1)}, u32[]{:S(2)}, u32[]{:S(2)}) collective-permute-start(bf16[144,1152]{1,0:T(8,128)(2,1)S(1)} %get-tuple-element.215.block0_ref), channel_id=1, source_target_pairs={{0,8},{8,0},{16,24},{24,16},{1,9},{9,1},{17,25},{25,17},{2,10},{10... | collective-permute-start | bytes 995336 | tf_op jit(solution)/shard_map/ppermute | solution.py:107
  14.1 26.0 %collective-permute-start.7 = (bf16[144,1152]{1,0:T(8,128)(2,1)S(1)}, bf16[144,1152]{1,0:T(8,128)(2,1)}, u32[]{:S(2)}, u32[]{:S(2)}) collective-permute-start(bf16[144,1152]{1,0:T(8,128)(2,1)S(1)} %get-tuple-element.215.block0_ref), channel_id=1, source_target_pairs={{0,16},{8,24},{16,0},{24,8},{1,17},{9,25},{17,1},{25,9},{2,18},{10... | collective-permute-start | bytes 995336 | tf_op jit(solution)/shard_map/ppermute | solution.py:107
  16.7 23.4 %collective-permute-start.8 = (bf16[144,1152]{1,0:T(8,128)(2,1)S(1)}, bf16[144,1152]{1,0:T(8,128)(2,1)}, u32[]{:S(2)}, u32[]{:S(2)}) collective-permute-start(bf16[144,1152]{1,0:T(8,128)(2,1)S(1)} %get-tuple-element.215.block0_ref), channel_id=1, source_target_pairs={{0,24},{8,16},{16,8},{24,0},{1,25},{9,17},{17,9},{25,1},{2,26},{10... | collective-permute-start | bytes 995336 | tf_op jit(solution)/shard_map/ppermute | solution.py:107
  25.1 15.0 %collective-permute-start.4 = (bf16[160,768]{1,0:T(8,128)(2,1)}, bf16[160,768]{1,0:T(8,128)(2,1)S(1)}, u32[]{:S(2)}, u32[]{:S(2)}) collective-permute-start(bf16[160,768]{1,0:T(8,128)(2,1)} %slice.363), channel_id=1, source_target_pairs={{0,1},{1,0},{2,3},{3,2},{4,5},{5,4},{6,7},{7,6},{8,9},{9,8},{10,11... | collective-permute-start | bytes 737288 | tf_op jit(solution)/shard_map/ppermute | solution.py:26
  26.1 13.9 %collective-permute-start.5 = (bf16[160,768]{1,0:T(8,128)(2,1)}, bf16[160,768]{1,0:T(8,128)(2,1)}, u32[]{:S(2)}, u32[]{:S(2)}) collective-permute-start(bf16[160,768]{1,0:T(8,128)(2,1)} %slice.364), channel_id=1, source_target_pairs={{0,2},{1,3},{2,0},{3,1},{4,6},{5,7},{6,4},{7,5},{8,10},{9,11},{10,... | collective-permute-start | bytes 737288 | tf_op jit(solution)/shard_map/ppermute | solution.py:26
  43.2 24.0 %collective-permute-start.10 = (bf16[4,96,1152]{2,1,0:T(8,128)(2,1)S(1)}, bf16[4,96,1152]{2,1,0:T(8,128)(2,1)S(1)}, u32[]{:S(2)}, u32[]{:S(2)}) collective-permute-start(bf16[4,96,1152]{2,1,0:T(8,128)(2,1)S(1)} %get-tuple-element.238.refs_0_), channel_id=1, source_target_pairs={{0,1},{1,0},{2,3},{3,2},{4,5},{5,4},{6,7},{7,6},{8,9},{9,8},{10,11... | collective-permute-start | bytes 2654216 | tf_op jit(solution)/shard_map/ppermute | solution.py:26
  43.7 23.4 %collective-permute-start.11 = (bf16[4,96,1152]{2,1,0:T(8,128)(2,1)S(1)}, bf16[4,96,1152]{2,1,0:T(8,128)(2,1)S(1)}, u32[]{:S(2)}, u32[]{:S(2)}) collective-permute-start(bf16[4,96,1152]{2,1,0:T(8,128)(2,1)S(1)} %get-tuple-element.238.refs_0_), channel_id=1, source_target_pairs={{0,2},{1,3},{2,0},{3,1},{4,6},{5,7},{6,4},{7,5},{8,10},{9,11},{10,... | collective-permute-start | bytes 2654216 | tf_op jit(solution)/shard_map/ppermute | solution.py:26
  44.2 20.4 %collective-permute-start.12 = (bf16[144,1152]{1,0:T(8,128)(2,1)S(1)}, bf16[144,1152]{1,0:T(8,128)(2,1)S(1)}, u32[]{:S(2)}, u32[]{:S(2)}) collective-permute-start(bf16[144,1152]{1,0:T(8,128)(2,1)S(1)} %get-tuple-element.245.block0_ref), channel_id=1, source_target_pairs={{0,8},{8,0},{16,24},{24,16},{1,9},{9,1},{17,25},{25,17},{2,10},{10... | collective-permute-start | bytes 995336 | tf_op jit(solution)/shard_map/ppermute | solution.py:107
  50.1 17.1 %collective-permute-start.13 = (bf16[144,1152]{1,0:T(8,128)(2,1)S(1)}, bf16[144,1152]{1,0:T(8,128)(2,1)S(1)}, u32[]{:S(2)}, u32[]{:S(2)}) collective-permute-start(bf16[144,1152]{1,0:T(8,128)(2,1)S(1)} %get-tuple-element.245.block0_ref), channel_id=1, source_target_pairs={{0,16},{8,24},{16,0},{24,8},{1,17},{9,25},{17,1},{25,9},{2,18},{10... | collective-permute-start | bytes 995336 | tf_op jit(solution)/shard_map/ppermute | solution.py:107
  70.8 11.8 %collective-permute-start.17 = (bf16[2,96,1152]{2,1,0:T(8,128)(2,1)S(1)}, bf16[2,96,1152]{2,1,0:T(8,128)(2,1)S(1)}, u32[]{:S(2)}, u32[]{:S(2)}) collective-permute-start(bf16[2,96,1152]{2,1,0:T(8,128)(2,1)S(1)} %slice.365), channel_id=1, source_target_pairs={{0,1},{1,0},{2,3},{3,2},{4,5},{5,4},{6,7},{7,6},{8,9},{9,8},{10,11... | collective-permute-start | bytes 1327112 | tf_op jit(solution)/shard_map/ppermute | solution.py:26
  72.4 10.7 %collective-permute-start.18 = (bf16[2,96,1152]{2,1,0:T(8,128)(2,1)S(1)}, bf16[2,96,1152]{2,1,0:T(8,128)(2,1)S(1)}, u32[]{:S(2)}, u32[]{:S(2)}) collective-permute-start(bf16[2,96,1152]{2,1,0:T(8,128)(2,1)S(1)} %slice.366), channel_id=1, source_target_pairs={{0,2},{1,3},{2,0},{3,1},{4,6},{5,7},{6,4},{7,5},{8,10},{9,11},{10,... | collective-permute-start | bytes 1327112 | tf_op jit(solution)/shard_map/ppermute | solution.py:26
  73.9 11.6 %collective-permute-start.20 = (bf16[4,96,1152]{2,1,0:T(8,128)(2,1)S(1)}, bf16[4,96,1152]{2,1,0:T(8,128)(2,1)S(1)}, u32[]{:S(2)}, u32[]{:S(2)}) collective-permute-start(bf16[4,96,1152]{2,1,0:T(8,128)(2,1)S(1)} %collective-permute-done.10.refs_1_), channel_id=1, source_target_pairs={{0,4},{4,0},{1,5},{5,1},{2,6},{6,2},{3,7},{7,3},{8,12},{12,8},{9,1... | collective-permute-start | bytes 2654216 | tf_op jit(solution)/shard_map/ppermute | solution.py:21
  75.2 10.3 %collective-permute-start.19 = (bf16[4,96,1152]{2,1,0:T(8,128)(2,1)S(1)}, bf16[4,96,1152]{2,1,0:T(8,128)(2,1)S(1)}, u32[]{:S(2)}, u32[]{:S(2)}) collective-permute-start(bf16[4,96,1152]{2,1,0:T(8,128)(2,1)S(1)} %get-tuple-element.238.refs_0_), channel_id=1, source_target_pairs={{0,4},{4,0},{1,5},{5,1},{2,6},{6,2},{3,7},{7,3},{8,12},{12,8},{9,1... | collective-permute-start | bytes 2654216 | tf_op jit(solution)/shard_map/ppermute | solution.py:21
  92.7 13.3 %collective-permute-start.24 = (bf16[320,768]{1,0:T(8,128)(2,1)S(1)}, bf16[320,768]{1,0:T(8,128)(2,1)S(1)}, u32[]{:S(2)}, u32[]{:S(2)}) collective-permute-start(bf16[320,768]{1,0:T(8,128)(2,1)S(1)} %get-tuple-element.242.own_ref), channel_id=1, source_target_pairs={{0,1},{1,0},{2,3},{3,2},{4,5},{5,4},{6,7},{7,6},{8,9},{9,8},{10,11... | collective-permute-start | bytes 1474568 | tf_op jit(solution)/shard_map/ppermute | solution.py:26
  93.3 13.0 %collective-permute-start.25 = (bf16[320,768]{1,0:T(8,128)(2,1)S(1)}, bf16[320,768]{1,0:T(8,128)(2,1)S(1)}, u32[]{:S(2)}, u32[]{:S(2)}) collective-permute-start(bf16[320,768]{1,0:T(8,128)(2,1)S(1)} %get-tuple-element.242.own_ref), channel_id=1, source_target_pairs={{0,2},{1,3},{2,0},{3,1},{4,6},{5,7},{6,4},{7,5},{8,10},{9,11},{10,... | collective-permute-start | bytes 1474568 | tf_op jit(solution)/shard_map/ppermute | solution.py:26
  94.4 11.2 %collective-permute-start.26 = (bf16[144,1152]{1,0:T(8,128)(2,1)S(1)}, bf16[144,1152]{1,0:T(8,128)(2,1)S(1)}, u32[]{:S(2)}, u32[]{:S(2)}) collective-permute-start(bf16[144,1152]{1,0:T(8,128)(2,1)S(1)} %get-tuple-element.245.block0_ref), channel_id=1, source_target_pairs={{0,24},{8,16},{16,8},{24,0},{1,25},{9,17},{17,9},{25,1},{2,26},{10... | collective-permute-start | bytes 995336 | tf_op jit(solution)/shard_map/ppermute | solution.py:107
  116.2 20.9 %collective-permute-start.30 = (bf16[4,96,1152]{2,1,0:T(8,128)(2,1)S(1)}, bf16[4,96,1152]{2,1,0:T(8,128)(2,1)S(1)}, u32[]{:S(2)}, u32[]{:S(2)}) collective-permute-start(bf16[4,96,1152]{2,1,0:T(8,128)(2,1)S(1)} %get-tuple-element.259.refs_0_), channel_id=1, source_target_pairs={{0,1},{1,0},{2,3},{3,2},{4,5},{5,4},{6,7},{7,6},{8,9},{9,8},{10,11... | collective-permute-start | bytes 2654216 | tf_op jit(solution)/shard_map/ppermute | solution.py:26
  116.8 20.7 %collective-permute-start.31 = (bf16[4,96,1152]{2,1,0:T(8,128)(2,1)S(1)}, bf16[4,96,1152]{2,1,0:T(8,128)(2,1)S(1)}, u32[]{:S(2)}, u32[]{:S(2)}) collective-permute-start(bf16[4,96,1152]{2,1,0:T(8,128)(2,1)S(1)} %get-tuple-element.259.refs_0_), channel_id=1, source_target_pairs={{0,2},{1,3},{2,0},{3,1},{4,6},{5,7},{6,4},{7,5},{8,10},{9,11},{10,... | collective-permute-start | bytes 2654216 | tf_op jit(solution)/shard_map/ppermute | solution.py:26
  140.9 13.1 %collective-permute-start.35 = (bf16[2,96,1152]{2,1,0:T(8,128)(2,1)S(1)}, bf16[2,96,1152]{2,1,0:T(8,128)(2,1)S(1)}, u32[]{:S(2)}, u32[]{:S(2)}) collective-permute-start(bf16[2,96,1152]{2,1,0:T(8,128)(2,1)S(1)} %slice.371), channel_id=1, source_target_pairs={{0,1},{1,0},{2,3},{3,2},{4,5},{5,4},{6,7},{7,6},{8,9},{9,8},{10,11... | collective-permute-start | bytes 1327112 | tf_op jit(solution)/shard_map/ppermute | solution.py:26
  142.5 12.3 %collective-permute-start.36 = (bf16[2,96,1152]{2,1,0:T(8,128)(2,1)S(1)}, bf16[2,96,1152]{2,1,0:T(8,128)(2,1)S(1)}, u32[]{:S(2)}, u32[]{:S(2)}) collective-permute-start(bf16[2,96,1152]{2,1,0:T(8,128)(2,1)S(1)} %slice.372), channel_id=1, source_target_pairs={{0,2},{1,3},{2,0},{3,1},{4,6},{5,7},{6,4},{7,5},{8,10},{9,11},{10,... | collective-permute-start | bytes 1327112 | tf_op jit(solution)/shard_map/ppermute | solution.py:26
  143.5 11.8 %collective-permute-start.37 = (bf16[4,96,1152]{2,1,0:T(8,128)(2,1)S(1)}, bf16[4,96,1152]{2,1,0:T(8,128)(2,1)S(1)}, u32[]{:S(2)}, u32[]{:S(2)}) collective-permute-start(bf16[4,96,1152]{2,1,0:T(8,128)(2,1)S(1)} %get-tuple-element.259.refs_0_), channel_id=1, source_target_pairs={{0,4},{4,0},{1,5},{5,1},{2,6},{6,2},{3,7},{7,3},{8,12},{12,8},{9,1... | collective-permute-start | bytes 2654216 | tf_op jit(solution)/shard_map/ppermute | solution.py:21
  146.5 10.7 %collective-permute-start.38 = (bf16[4,96,1152]{2,1,0:T(8,128)(2,1)S(1)}, bf16[4,96,1152]{2,1,0:T(8,128)(2,1)S(1)}, u32[]{:S(2)}, u32[]{:S(2)}) collective-permute-start(bf16[4,96,1152]{2,1,0:T(8,128)(2,1)S(1)} %collective-permute-done.30.refs_1_), channel_id=1, source_target_pairs={{0,4},{4,0},{1,5},{5,1},{2,6},{6,2},{3,7},{7,3},{8,12},{12,8},{9,1... | collective-permute-start | bytes 2654216 | tf_op jit(solution)/shard_map/ppermute | solution.py:21
  147.0 10.3 %collective-permute-start.39 = (bf16[4,96,1152]{2,1,0:T(8,128)(2,1)S(1)}, bf16[4,96,1152]{2,1,0:T(8,128)(2,1)S(1)}, u32[]{:S(2)}, u32[]{:S(2)}) collective-permute-start(bf16[4,96,1152]{2,1,0:T(8,128)(2,1)S(1)} %collective-permute-done.31.refs_2_), channel_id=1, source_target_pairs={{0,4},{4,0},{1,5},{5,1},{2,6},{6,2},{3,7},{7,3},{8,12},{12,8},{9,1... | collective-permute-start | bytes 2654216 | tf_op jit(solution)/shard_map/ppermute | solution.py:21
  188.4 22.5 %collective-permute-start.47 = (bf16[2,96,1152]{2,1,0:T(8,128)(2,1)S(1)}, bf16[2,96,1152]{2,1,0:T(8,128)(2,1)S(1)}, u32[]{:S(2)}, u32[]{:S(2)}) collective-permute-start(bf16[2,96,1152]{2,1,0:T(8,128)(2,1)S(1)} %get-tuple-element.465), channel_id=1, source_target_pairs={{0,1},{1,0},{2,3},{3,2},{4,5},{5,4},{6,7},{7,6},{8,9},{9,8},{10,11... | collective-permute-start | bytes 1327112 | tf_op jit(solution)/shard_map/ppermute | solution.py:26
  189.7 21.3 %collective-permute-start.48 = (bf16[2,96,1152]{2,1,0:T(8,128)(2,1)S(1)}, bf16[2,96,1152]{2,1,0:T(8,128)(2,1)S(1)}, u32[]{:S(2)}, u32[]{:S(2)}) collective-permute-start(bf16[2,96,1152]{2,1,0:T(8,128)(2,1)S(1)} %get-tuple-element.464), channel_id=1, source_target_pairs={{0,2},{1,3},{2,0},{3,1},{4,6},{5,7},{6,4},{7,5},{8,10},{9,11},{10,... | collective-permute-start | bytes 1327112 | tf_op jit(solution)/shard_map/ppermute | solution.py:26
  214.2 16.0 %collective-permute-start.54 = (bf16[4,48,1152]{2,1,0:T(8,128)(2,1)}, bf16[4,48,1152]{2,1,0:T(8,128)(2,1)}, u32[]{:S(2)}, u32[]{:S(2)}) collective-permute-start(bf16[4,48,1152]{2,1,0:T(8,128)(2,1)} %get-tuple-element.311), channel_id=1, source_target_pairs={{0,4},{4,0},{1,5},{5,1},{2,6},{6,2},{3,7},{7,3},{8,12},{12,8},{9,1... | collective-permute-start | bytes 1327112 | tf_op jit(solution)/shard_map/ppermute | solution.py:21
  215.8 10.5 %collective-permute-start.50 = (bf16[160,768]{1,0:T(8,128)(2,1)}, bf16[160,768]{1,0:T(8,128)(2,1)}, u32[]{:S(2)}, u32[]{:S(2)}) collective-permute-start(bf16[160,768]{1,0:T(8,128)(2,1)} %get-tuple-element.303), channel_id=1, source_target_pairs={{0,2},{1,3},{2,0},{3,1},{4,6},{5,7},{6,4},{7,5},{8,10},{9,11},{10,... | collective-permute-start | bytes 737288 | tf_op jit(solution)/shard_map/ppermute | solution.py:26
  216.9 12.2 %collective-permute-start.49 = (bf16[160,768]{1,0:T(8,128)(2,1)}, bf16[160,768]{1,0:T(8,128)(2,1)}, u32[]{:S(2)}, u32[]{:S(2)}) collective-permute-start(bf16[160,768]{1,0:T(8,128)(2,1)} %get-tuple-element.301), channel_id=1, source_target_pairs={{0,1},{1,0},{2,3},{3,2},{4,5},{5,4},{6,7},{7,6},{8,9},{9,8},{10,11... | collective-permute-start | bytes 737288 | tf_op jit(solution)/shard_map/ppermute | solution.py:26
  218.1 12.1 %collective-permute-start.55 = (bf16[160,768]{1,0:T(8,128)(2,1)}, bf16[160,768]{1,0:T(8,128)(2,1)}, u32[]{:S(2)}, u32[]{:S(2)}) collective-permute-start(bf16[160,768]{1,0:T(8,128)(2,1)} %get-tuple-element.312), channel_id=1, source_target_pairs={{0,2},{1,3},{2,0},{3,1},{4,6},{5,7},{6,4},{7,5},{8,10},{9,11},{10,... | collective-permute-start | bytes 737288 | tf_op jit(solution)/shard_map/ppermute | solution.py:26
  236.5 22.8 %collective-permute-start.56 = (bf16[4,96,1152]{2,1,0:T(8,128)(2,1)S(1)}, bf16[4,96,1152]{2,1,0:T(8,128)(2,1)S(1)}, u32[]{:S(2)}, u32[]{:S(2)}) collective-permute-start(bf16[4,96,1152]{2,1,0:T(8,128)(2,1)S(1)} %pad_maximum_fusion), channel_id=1, source_target_pairs={{0,1},{1,0},{2,3},{3,2},{4,5},{5,4},{6,7},{7,6},{8,9},{9,8},{10,11... | collective-permute-start | bytes 2654216 | tf_op jit(solution)/shard_map/ppermute | solution.py:26
  238.0 22.3 %collective-permute-start.57 = (bf16[4,96,1152]{2,1,0:T(8,128)(2,1)}, bf16[4,96,1152]{2,1,0:T(8,128)(2,1)S(1)}, u32[]{:S(2)}, u32[]{:S(2)}) collective-permute-start(bf16[4,96,1152]{2,1,0:T(8,128)(2,1)} %pad_maximum_fusion.1), channel_id=1, source_target_pairs={{0,2},{1,3},{2,0},{3,1},{4,6},{5,7},{6,4},{7,5},{8,10},{9,11},{10,... | collective-permute-start | bytes 2654216 | tf_op jit(solution)/shard_map/ppermute | solution.py:26
  261.2 11.2 %collective-permute-start.61 = (bf16[4,4,96,1152]{3,2,1,0:T(8,128)(2,1)}, bf16[4,4,96,1152]{3,2,1,0:T(8,128)(2,1)}, u32[]{:S(2)}, u32[]{:S(2)}) collective-permute-start(bf16[4,4,96,1152]{3,2,1,0:T(8,128)(2,1)} %get-tuple-element.333), channel_id=1, source_target_pairs={{0,4},{4,0},{1,5},{5,1},{2,6},{6,2},{3,7},{7,3},{8,12},{12,8},{9,1... | collective-permute-start | bytes 10616840 | tf_op jit(solution)/shard_map/ppermute | solution.py:21
  262.2 44.2 %collective-permute-start.42 = (bf16[320,768]{1,0:T(8,128)(2,1)}, bf16[320,768]{1,0:T(8,128)(2,1)}, u32[]{:S(2)}, u32[]{:S(2)}) collective-permute-start(bf16[320,768]{1,0:T(8,128)(2,1)} %get-tuple-element.453), channel_id=1, source_target_pairs={{0,4},{4,0},{1,5},{5,1},{2,6},{6,2},{3,7},{7,3},{8,12},{12,8},{9,1... | collective-permute-start | bytes 1474568 | tf_op jit(solution)/shard_map/ppermute | solution.py:21
  274.1 24.4 %collective-permute-start.62 = (bf16[2,96,1152]{2,1,0:T(8,128)(2,1)S(1)}, bf16[2,96,1152]{2,1,0:T(8,128)(2,1)S(1)}, u32[]{:S(2)}, u32[]{:S(2)}) collective-permute-start(bf16[2,96,1152]{2,1,0:T(8,128)(2,1)S(1)} %get-tuple-element.459), channel_id=1, source_target_pairs={{0,1},{1,0},{2,3},{3,2},{4,5},{5,4},{6,7},{7,6},{8,9},{9,8},{10,11... | collective-permute-start | bytes 1327112 | tf_op jit(solution)/shard_map/ppermute | solution.py:26
  275.4 23.1 %collective-permute-start.63 = (bf16[2,96,1152]{2,1,0:T(8,128)(2,1)S(1)}, bf16[2,96,1152]{2,1,0:T(8,128)(2,1)S(1)}, u32[]{:S(2)}, u32[]{:S(2)}) collective-permute-start(bf16[2,96,1152]{2,1,0:T(8,128)(2,1)S(1)} %get-tuple-element.458), channel_id=1, source_target_pairs={{0,2},{1,3},{2,0},{3,1},{4,6},{5,7},{6,4},{7,5},{8,10},{9,11},{10,... | collective-permute-start | bytes 1327112 | tf_op jit(solution)/shard_map/ppermute | solution.py:26
  276.5 19.5 %collective-permute-start.64 = (bf16[144,1152]{1,0:T(8,128)(2,1)S(1)}, bf16[144,1152]{1,0:T(8,128)(2,1)S(1)}, u32[]{:S(2)}, u32[]{:S(2)}) collective-permute-start(bf16[144,1152]{1,0:T(8,128)(2,1)S(1)} %pad_maximum_fusion.8), channel_id=1, source_target_pairs={{0,8},{8,0},{16,24},{24,16},{1,9},{9,1},{17,25},{25,17},{2,10},{10... | collective-permute-start | bytes 995336 | tf_op jit(solution)/shard_map/ppermute | solution.py:107
  283.2 15.3 %collective-permute-start.65 = (bf16[144,1152]{1,0:T(8,128)(2,1)S(1)}, bf16[144,1152]{1,0:T(8,128)(2,1)S(1)}, u32[]{:S(2)}, u32[]{:S(2)}) collective-permute-start(bf16[144,1152]{1,0:T(8,128)(2,1)S(1)} %pad_maximum_fusion.9), channel_id=1, source_target_pairs={{0,16},{8,24},{16,0},{24,8},{1,17},{9,25},{17,1},{25,9},{2,18},{10... | collective-permute-start | bytes 995336 | tf_op jit(solution)/shard_map/ppermute | solution.py:107
  309.6 21.8 %collective-permute-start.66 = (bf16[4,96,1152]{2,1,0:T(8,128)(2,1)}, bf16[4,96,1152]{2,1,0:T(8,128)(2,1)S(1)}, u32[]{:S(2)}, u32[]{:S(2)}) collective-permute-start(bf16[4,96,1152]{2,1,0:T(8,128)(2,1)} %pad_maximum_fusion.2), channel_id=1, source_target_pairs={{0,1},{1,0},{2,3},{3,2},{4,5},{5,4},{6,7},{7,6},{8,9},{9,8},{10,11... | collective-permute-start | bytes 2654216 | tf_op jit(solution)/shard_map/ppermute | solution.py:26
  311.3 21.3 %collective-permute-start.67 = (bf16[4,96,1152]{2,1,0:T(8,128)(2,1)S(1)}, bf16[4,96,1152]{2,1,0:T(8,128)(2,1)S(1)}, u32[]{:S(2)}, u32[]{:S(2)}) collective-permute-start(bf16[4,96,1152]{2,1,0:T(8,128)(2,1)S(1)} %copy-done.83), channel_id=1, source_target_pairs={{0,2},{1,3},{2,0},{3,1},{4,6},{5,7},{6,4},{7,5},{8,10},{9,11},{10,... | collective-permute-start | bytes 2654216 | tf_op jit(solution)/shard_map/ppermute | solution.py:26
  312.2 11.1 %collective-permute-start.68 = (bf16[144,1152]{1,0:T(8,128)(2,1)S(1)}, bf16[144,1152]{1,0:T(8,128)(2,1)S(1)}, u32[]{:S(2)}, u32[]{:S(2)}) collective-permute-start(bf16[144,1152]{1,0:T(8,128)(2,1)S(1)} %copy-done.88), channel_id=1, source_target_pairs={{0,24},{8,16},{16,8},{24,0},{1,25},{9,17},{17,9},{25,1},{2,26},{10... | collective-permute-start | bytes 995336 | tf_op jit(solution)/shard_map/ppermute | solution.py:107
  335.4 15.7 %collective-permute-start.80 = (bf16[144,1152]{1,0:T(8,128)(2,1)S(1)}, bf16[144,1152]{1,0:T(8,128)(2,1)S(1)}, u32[]{:S(2)}, u32[]{:S(2)}) collective-permute-start(bf16[144,1152]{1,0:T(8,128)(2,1)S(1)} %pad_maximum_fusion.13), channel_id=1, source_target_pairs={{0,24},{8,16},{16,8},{24,0},{1,25},{9,17},{17,9},{25,1},{2,26},{10... | collective-permute-start | bytes 995336 | tf_op jit(solution)/shard_map/ppermute | solution.py:107
  339.3 25.7 %collective-permute-start.79 = (bf16[144,1152]{1,0:T(8,128)(2,1)S(1)}, bf16[144,1152]{1,0:T(8,128)(2,1)S(1)}, u32[]{:S(2)}, u32[]{:S(2)}) collective-permute-start(bf16[144,1152]{1,0:T(8,128)(2,1)S(1)} %pad_maximum_fusion.12), channel_id=1, source_target_pairs={{0,16},{8,24},{16,0},{24,8},{1,17},{9,25},{17,1},{25,9},{2,18},{10... | collective-permute-start | bytes 995336 | tf_op jit(solution)/shard_map/ppermute | solution.py:107
  344.3 21.5 %collective-permute-start.78 = (bf16[144,1152]{1,0:T(8,128)(2,1)S(1)}, bf16[144,1152]{1,0:T(8,128)(2,1)}, u32[]{:S(2)}, u32[]{:S(2)}) collective-permute-start(bf16[144,1152]{1,0:T(8,128)(2,1)S(1)} %pad_maximum_fusion.11), channel_id=1, source_target_pairs={{0,8},{8,0},{16,24},{24,16},{1,9},{9,1},{17,25},{25,17},{2,10},{10... | collective-permute-start | bytes 995336 | tf_op jit(solution)/shard_map/ppermute | solution.py:107
  347.1 28.5 %collective-permute-start.74 = (bf16[320,768]{1,0:T(8,128)(2,1)}, bf16[320,768]{1,0:T(8,128)(2,1)S(1)}, u32[]{:S(2)}, u32[]{:S(2)}) collective-permute-start(bf16[320,768]{1,0:T(8,128)(2,1)} %pad_maximum_fusion.5), channel_id=1, source_target_pairs={{0,1},{1,0},{2,3},{3,2},{4,5},{5,4},{6,7},{7,6},{8,9},{9,8},{10,11... | collective-permute-start | bytes 1474568 | tf_op jit(solution)/shard_map/ppermute | solution.py:26
  349.5 26.2 %collective-permute-start.75 = (bf16[320,768]{1,0:T(8,128)(2,1)}, bf16[320,768]{1,0:T(8,128)(2,1)S(1)}, u32[]{:S(2)}, u32[]{:S(2)}) collective-permute-start(bf16[320,768]{1,0:T(8,128)(2,1)} %pad_maximum_fusion.6), channel_id=1, source_target_pairs={{0,2},{1,3},{2,0},{3,1},{4,6},{5,7},{6,4},{7,5},{8,10},{9,11},{10,... | collective-permute-start | bytes 1474568 | tf_op jit(solution)/shard_map/ppermute | solution.py:26
  369.2 9.9 %collective-permute-start.82 = (f32[96]{0:T(128)S(1)}, f32[96]{0:T(128)S(1)}, u32[]{:S(2)}, u32[]{:S(2)}) collective-permute-start(f32[96]{0:T(128)S(1)} %get-tuple-element.476), channel_id=1, source_target_pairs={{0,8},{8,0},{16,24},{24,16},{1,9},{9,1},{17,25},{25,17},{2,10},{10... | collective-permute-start | bytes 1160 | tf_op jit(solution)/shard_map/ppermute | solution.py:107
  (143 other events, 1283.1 us)
